TPU v7x, 32 devices: a whole 2x2x4 slice. The times are simulated.
32 devices in a mesh: row: 8 (over z, y), rep: 4 (over x, core).
Axes of the slice: x: 2, y: 2, z: 4, core: 2. Of those that a mesh axis runs over, the one named last changes fastest.
Arguments:
- node_features: bfloat16 [16384, 256], P('row'), may hold values from -6 to 6
- weight: bfloat16 [256, 256], replicated, may hold values from -0.375 to 0.375
- out_grad: bfloat16 [16384, 256], P(('row', 'rep')), may hold values from -6 to 6
- blocks: bfloat16 [6144, 128, 128], P(('row', 'rep')), may hold values from -0.109375 to 0.109375
- block_rows: int32 [6144], P(('row', 'rep')), may hold values from 0 to 15
- block_fetch: int32 [6144], P(('row', 'rep')), may hold values from 0 to 15, as said below
- fetch_lists: int32 [32, 8, 2], P(('row', 'rep')), may hold values from 0 to 15, as said below
- block_count: int32 [32], P(('row', 'rep')), may hold values from 27 to 192, as said below
Outputs:
- output: bfloat16 [16384, 256], P(('row', 'rep'))
- weight_grad: float32 [256, 256], replicated
- node_grad: float32 [16384, 256], P(('row', 'rep'))
Inputs may be any that keep to these rules, and one draw needn't show every extreme that they name: `fetch_lists`: each fetch list of one device and one source group holds 2 different node blocks, and all devices of one row group hold the same fetch lists. `block_fetch`: within each device, the first 16 slots name every value once. `block_count`: some device has all 192 slots live.
All inputs are finite; a program needn't handle non-finite values.
Results may differ from a plain program's by a relative error of at most 0.0056.
Values may be sent and summed in bfloat16 or wider, within the bound.
No kernel may reach another device: no remote copies, remote signals or barrier semaphores. Data moves between devices by JAX's collectives and lax.ppermute only.
A program may use at most 128 MiB of HBM per device.

v0:
```python
import jax
import jax.numpy as jnp
from jax import lax
from jax.sharding import PartitionSpec as P


def silu_grad(pre_act):
    sigmoid_part = jax.nn.sigmoid(pre_act)
    return sigmoid_part * (1.0 + pre_act * (1.0 - sigmoid_part))


def local(
    node_features, weight, out_grad, blocks, block_rows, block_fetch, fetch_lists, block_count
):
    row_count = lax.axis_size("row")
    rep_count = lax.axis_size("rep")
    band_rows, features = node_features.shape
    blk_size = blocks.shape[1]
    row_blocks = band_rows // blk_size
    share_cols = features // rep_count
    col_start = lax.axis_index("rep") * share_cols
    band_blocks = node_features.reshape(row_blocks, blk_size, features)
    requested = lax.all_to_all(fetch_lists[0], "row", split_axis=0, concat_axis=0, tiled=True)
    outgoing = band_blocks[requested]
    own_cols = lax.dynamic_slice_in_dim(outgoing, col_start, share_cols, 3)
    got_cols = lax.all_to_all(own_cols, "row", split_axis=0, concat_axis=0, tiled=True)
    arrived = lax.all_gather(got_cols, "rep", axis=3, tiled=True)
    live_mask = (jnp.arange(blocks.shape[0], dtype=jnp.int32) < block_count[0]).astype(blocks.dtype)
    live_blocks = blocks * live_mask[:, None, None]
    slot_rows = arrived.reshape(-1, blk_size, features)
    gathered = slot_rows[block_fetch]
    block_terms = jnp.einsum(
        "bkj,bjf->bkf", live_blocks, gathered, preferred_element_type=jnp.float32
    )
    partial_band = jax.ops.segment_sum(block_terms, block_rows, num_segments=row_blocks).reshape(
        band_rows, features
    )
    hidden_own = lax.psum_scatter(partial_band, "rep", scatter_dimension=0, tiled=True).astype(
        jnp.bfloat16
    )
    pre_act = jnp.dot(hidden_own, weight, preferred_element_type=jnp.float32)
    output = jax.nn.silu(pre_act).astype(jnp.bfloat16)
    pre_grad = (out_grad.astype(jnp.float32) * silu_grad(pre_act)).astype(jnp.bfloat16)
    local_grad = lax.dot_general(
        hidden_own, pre_grad, (((0,), (0,)), ((), ())), preferred_element_type=jnp.float32
    )
    own_input_grad = lax.dot_general(
        pre_grad, weight, (((1,), (1,)), ((), ())), preferred_element_type=jnp.float32
    ).astype(jnp.bfloat16)
    input_grad = lax.all_gather(own_input_grad, "rep", axis=0, tiled=True)
    factor = float(row_count * band_rows) ** (-0.5)
    weight_grad = lax.psum(local_grad, ("row", "rep")) * factor
    grad_blocks = input_grad.reshape(row_blocks, blk_size, features)
    picked = grad_blocks[block_rows]
    back_terms = jnp.einsum("bjk,bjf->bkf", live_blocks, picked, preferred_element_type=jnp.float32)
    outbound = jax.ops.segment_sum(
        back_terms, block_fetch, num_segments=slot_rows.shape[0]
    ).reshape(arrived.shape)
    reduced = lax.psum_scatter(outbound, "rep", scatter_dimension=3, tiled=True)
    returned = lax.all_to_all(reduced, "row", split_axis=0, concat_axis=0, tiled=True)
    grad_cols = jax.ops.segment_sum(
        returned.reshape(-1, blk_size, share_cols), requested.reshape(-1), num_segments=row_blocks
    )
    node_grad = lax.all_to_all(
        grad_cols.reshape(band_rows, share_cols), "rep", split_axis=0, concat_axis=1, tiled=True
    )
    return (output, weight_grad, node_grad)


def solution(mesh):
    in_specs = (
        P("row", None),
        P(),
        P(("row", "rep"), None),
        P(("row", "rep"), None, None),
        P(("row", "rep")),
        P(("row", "rep")),
        P(("row", "rep"), None, None),
        P(("row", "rep")),
    )
    out_specs = (P(("row", "rep"), None), P(), P(("row", "rep"), None))
    return jax.shard_map(local, mesh=mesh, in_specs=in_specs, out_specs=out_specs, check_vma=False)
```

profile of v0, /device:TPU:0, one launch (start us, length us, event | category | flops | bytes accessed | tf_op | source)
XLA Modules:
  0.0 431.3 jit_solution(17896839713746537105)
XLA Ops:
  7.2 1.4 copy.31
  8.6 7.3 %all-to-all-start = ((s32[8,1,2]{2,1,0:T(1,128)}), s32[8,1,2]{2,1,0:T(1,128)S(1)}, u32[]{:S(2)}, u32[]{:S(2)}) async-start(s32[8,1,2]{2,1,0:T(1,128)} %copy.31), calls=%async_computation | async-start | bytes 8192 | tf_op jit(solution)/shard_map/all_to_all | solution.py:23
  15.9 6.3 %all-to-all-done = s32[8,1,2]{2,1,0:T(1,128)S(1)} async-done(((s32[8,1,2]{2,1,0:T(1,128)}), s32[8,1,2]{2,1,0:T(1,128)S(1)}, u32[]{:S(2)}, u32[]{:S(2)}) %all-to-all-start) | async-done | bytes 96 | tf_op jit(solution)/shard_map/all_to_all | solution.py:23
  23.6 10.6 %all_to_all.41 = bf16[8,2,128,64]{2,3,1,0:T(8,128)(2,1)S(1)} all-to-all(bf16[8,2,128,64]{2,3,1,0:T(8,128)(2,1)S(1)} %copy.44), channel_id=1, replica_groups=mesh['row'=8,'rep'=4] {'row'}, dimensions={0} | all-to-all | bytes 524288 | tf_op jit(solution)/shard_map/all_to_all | solution.py:26
  36.6 14.0 %all-gather.3.cloned.1.call-done = bf16[8,2,128,256]{2,0,1,3:T(8,128)(2,1)} async-done(((bf16[8,2,128,64]{2,0,1,3:T(8,128)(2,1)}), bf16[8,2,128,256]{2,0,1,3:T(8,128)(2,1)}) %all-gather.3.cloned.1.call-update) | async-done | bytes 1048592 | tf_op jit(solution)/shard_map/all_gather | solution.py:27
  50.6 1.6 copy.36
  52.2 8.3 %gather_fusion.1 = bf16[192,128,256]{2,1,0:T(8,128)(2,1)} fusion(bf16[16,128,256]{2,1,0:T(8,128)(2,1)S(1)} %bitcast.28, s32[1024]{0:T(1024)S(1)} %pad_clamp_fusion.1), kind=kCustom, calls=%fused_computation.1 | custom fusion | bytes 25166592 | tf_op jit(solution)/shard_map/gather | solution.py:31
  60.5 18.2 %fusion.2 = f32[192,128,256]{2,1,0:T(8,128)} fusion(bf16[192,128,256]{2,1,0:T(8,128)(2,1)} %gather_fusion.1, bf16[192,128,128]{2,1,0:T(8,128)(2,1)} %param.11, bf16[192]{0:T(256)(128)(2,1)S(1)} %compare_convert_fusion), kind=kOutput, calls=%fused_computation.8 | convolution fusion | flops 1613758464 | bytes 44040576 | tf_op jit(solution)/shard_map/bkj,bjf->bkf/dot_general | solution.py:32
  78.9 36.1 %scatter_fusion = f32[16,128,256]{2,1,0:T(8,128)S(1)} fusion(f32[16,128,256]{2,1,0:T(8,128)S(1)} %broadcast.36.clone, s32[192]{0:T(256)S(1)} %copy-done.4, f32[192,128,256]{2,1,0:T(8,128)} %fusion.2), kind=kCustom, calls=%fused_computation.3 | custom fusion | flops 6291456 | bytes 75498240 | tf_op jit(solution)/shard_map/scatter-add | solution.py:35
  116.5 31.6 %reduce-scatter.3.cloned.1.call-done = f32[512,256]{1,0:T(8,128)} async-done(((f32[2048,256]{1,0:T(8,128)}), f32[512,256]{1,0:T(8,128)}) %reduce-scatter.3.cloned.1.call-update) | async-done | bytes 524304 | tf_op jit(solution)/shard_map/reduce_scatter | solution.py:38
  148.1 2.1 multiply_convert_fusion
  151.5 16.6 %all-gather.5.cloned.1.call-done = bf16[2048,256]{1,0:T(8,128)(2,1)} async-done(((bf16[512,256]{1,0:T(8,128)(2,1)}), bf16[2048,256]{1,0:T(8,128)(2,1)}) %all-gather.5.cloned.1.call-update) | async-done | bytes 1048592 | tf_op jit(solution)/shard_map/all_gather | solution.py:50
  168.2 9.5 %gather_fusion.2 = bf16[192,128,256]{2,1,0:T(8,128)(2,1)} fusion(bf16[16,128,256]{2,1,0:T(8,128)(2,1)} %bitcast.29, s32[1024]{0:T(1024)S(1)} %pad_clamp_fusion), kind=kCustom, calls=%fused_computation.2 | custom fusion | bytes 25166592 | tf_op jit(solution)/shard_map/gather | solution.py:54
  177.7 14.8 %fusion = f32[192,128,256]{2,1,0:T(8,128)} fusion(bf16[192,128,256]{2,1,0:T(8,128)(2,1)} %gather_fusion.2, bf16[192,128,128]{2,1,0:T(8,128)(2,1)} %param.11, bf16[192]{0:T(256)(128)(2,1)S(1)} %compare_convert_fusion), kind=kOutput, calls=%fused_computation.6 | convolution fusion | flops 1613758464 | bytes 44040576 | tf_op jit(solution)/shard_map/bjk,bjf->bkf/dot_general | solution.py:55
  192.7 36.2 %scatter_fusion.1 = f32[16,128,256]{2,1,0:T(8,128)S(1)} fusion(f32[16,128,256]{2,1,0:T(8,128)S(1)} %broadcast.36, s32[192]{0:T(256)S(1)} %copy-done.5, f32[192,128,256]{2,1,0:T(8,128)} %fusion), kind=kCustom, calls=%fused_computation.4 | custom fusion | flops 6291456 | bytes 75498240 | tf_op jit(solution)/shard_map/scatter-add | solution.py:56
  228.9 2.0 copy.38
  231.0 31.6 %reduce-scatter.5.cloned.1.call-done = f32[8,2,128,64]{2,0,1,3:T(8,128)} async-done(((f32[8,2,128,256]{2,0,1,3:T(8,128)}), f32[8,2,128,64]{2,0,1,3:T(8,128)}) %reduce-scatter.5.cloned.1.call-update) | async-done | bytes 524304 | tf_op jit(solution)/shard_map/reduce_scatter | solution.py:59
  262.6 2.0 copy.39
  264.6 5.5 %all-to-all-start.2 = ((f32[8,2,128,64]{2,3,1,0:T(8,128)}), f32[8,2,128,64]{2,3,1,0:T(8,128)S(1)}, u32[]{:S(2)}, u32[]{:S(2)}) async-start(f32[8,2,128,64]{2,3,1,0:T(8,128)} %copy.39), calls=%async_computation.4 | async-start | bytes 1048576 | tf_op jit(solution)/shard_map/all_to_all | solution.py:60
  271.4 13.2 %all-to-all-done.2 = f32[8,2,128,64]{2,3,1,0:T(8,128)S(1)} async-done(((f32[8,2,128,64]{2,3,1,0:T(8,128)}), f32[8,2,128,64]{2,3,1,0:T(8,128)S(1)}, u32[]{:S(2)}, u32[]{:S(2)}) %all-to-all-start.2) | async-done | bytes 524320 | tf_op jit(solution)/shard_map/all_to_all | solution.py:60
  287.5 3.5 all-to-all-start.3
  291.0 2.0 fusion.6
  293.0 129.1 %all-reduce.2.cloned.1.call-done = f32[256,256]{1,0:T(8,128)} async-done(((f32[256,256]{1,0:T(8,128)}), f32[256,256]{1,0:T(8,128)}) %all-reduce.2.cloned.1.call-update) | async-done | bytes 262160 | tf_op jit(solution)/shard_map/psum | solution.py:52
  422.1 1.7 broadcast_multiply_fusion
  (51 shorter events, 11.2 us)
Async XLA Ops:
  7.2 15.4 %copy-start = (bf16[2048,256]{1,0:T(8,128)(2,1)S(1)}, bf16[2048,256]{1,0:T(8,128)(2,1)}, u32[]{:S(2)}) copy-start(bf16[2048,256]{1,0:T(8,128)(2,1)} %param.8) | copy-start | bytes 3145732
  8.6 13.7 %all-to-all-start = ((s32[8,1,2]{2,1,0:T(1,128)}), s32[8,1,2]{2,1,0:T(1,128)S(1)}, u32[]{:S(2)}, u32[]{:S(2)}) async-start(s32[8,1,2]{2,1,0:T(1,128)} %copy.31), calls=%async_computation | async-start | bytes 8192 | tf_op jit(solution)/shard_map/all_to_all | solution.py:23
  15.9 34.7 %all-gather.3.cloned.1.call-start = ((), (), s32[]{:S(2)}) async-start(), calls=%async_computation.6 | async-start | bytes 1310720 | tf_op jit(solution)/shard_map/all_gather | solution.py:27
  35.2 113.0 %reduce-scatter.3.cloned.1.call-start = ((), (), s32[]{:S(2)}) async-start(), calls=%async_computation.7 | async-start | bytes 2621440 | tf_op jit(solution)/shard_map/reduce_scatter | solution.py:38
  60.5 18.4 %copy-start.4 = (s32[192]{0:T(256)S(1)}, s32[192]{0:T(256)}, u32[]{:S(2)}) copy-start(s32[192]{0:T(256)} %param.12) | copy-start | bytes 2308
  78.9 69.2 %copy-start.3 = (bf16[256,256]{1,0:T(8,128)(2,1)S(1)}, bf16[256,256]{1,0:T(8,128)(2,1)}, u32[]{:S(2)}) copy-start(bf16[256,256]{1,0:T(8,128)(2,1)} %param.9) | copy-start | bytes 393220
  78.9 69.2 %copy-start.6 = (bf16[512,256]{1,0:T(8,128)(2,1)S(1)}, bf16[512,256]{1,0:T(8,128)(2,1)}, u32[]{:S(2)}) copy-start(bf16[512,256]{1,0:T(8,128)(2,1)} %param.10) | copy-start | bytes 786436
  115.1 1.3 copy-start.2
  116.4 51.7 %all-gather.5.cloned.1.call-start = ((), (), s32[]{:S(2)}) async-start(), calls=%async_computation.9 | async-start | bytes 1310720 | tf_op jit(solution)/shard_map/all_gather | solution.py:50
  151.3 111.3 %reduce-scatter.5.cloned.1.call-start = ((), (), s32[]{:S(2)}) async-start(), calls=%async_computation.10 | async-start | bytes 2621440 | tf_op jit(solution)/shard_map/reduce_scatter | solution.py:59
  177.7 15.0 %copy-start.5 = (s32[192]{0:T(256)S(1)}, s32[192]{0:T(256)}, u32[]{:S(2)}) copy-start(s32[192]{0:T(256)} %param.13) | copy-start | bytes 2308
  192.7 232.1 %copy-start.1 = (bf16[2048,256]{1,0:T(8,128)(2,1)S(1)}, bf16[2048,256]{1,0:T(8,128)(2,1)}, u32[]{:S(2)}) copy-start(bf16[2048,256]{1,0:T(8,128)(2,1)} %param.8) | copy-start | bytes 3145732
  264.6 20.0 %all-to-all-start.2 = ((f32[8,2,128,64]{2,3,1,0:T(8,128)}), f32[8,2,128,64]{2,3,1,0:T(8,128)S(1)}, u32[]{:S(2)}, u32[]{:S(2)}) async-start(f32[8,2,128,64]{2,3,1,0:T(8,128)} %copy.39), calls=%async_computation.4 | async-start | bytes 1048576 | tf_op jit(solution)/shard_map/all_to_all | solution.py:60
  287.5 136.3 %all-to-all-start.3 = ((f32[4,512,64]{1,2,0:T(8,128)}), f32[4,512,64]{1,2,0:T(8,128)S(1)}, u32[]{:S(2)}, u32[]{:S(2)}) async-start(f32[4,512,64]{1,2,0:T(8,128)} %copy.41), calls=%async_computation.5 | async-start | bytes 1048576 | tf_op jit(solution)/shard_map/all_to_all | solution.py:64
  291.0 131.2 %all-reduce.2.cloned.1.call-start = ((), (), s32[]{:S(2)}) async-start(), calls=%async_computation.8 | async-start | bytes 524288 | tf_op jit(solution)/shard_map/psum | solution.py:52
Sparse Core Ops, SparseCore 0:
  35.3 15.2 all-gather.2
  116.6 31.5 reduce-scatter.2
  151.4 16.7 all-gather.4
  231.1 31.4 reduce-scatter.4
  297.6 124.5 all-reduce.1
where the time goes:
time: 433 us; the launch traced here: 431 us
  waiting for transfers between devices  243 us (56%)
  other arithmetic  76.7 us (18%)
  matrix products  38.1 us (9%)
  local copies, waits for them, and re-layouts  31.9 us (7%)
  starting transfers between devices  16.7 us (4%)
  between operations  14.6 us (3%)
  blocking collectives  10.6 us (2%)
    psum x1, waiting for transfers between devices, local(): weight_grad = lax.psum(local_grad, ('row', 'rep')) * factor  129 us
    scatter-add x1, other arithmetic, local(): jax.ops.segment_sum(back_terms, block_fetch, num_segments=slot_rows.shape...  36.2 us
    scatter-add x1, other arithmetic, local(): jax.ops.segment_sum(block_terms, block_rows, num_segments=row_blocks)  36.1 us
    reduce_scatter x1, waiting for transfers between devices, local(): reduced = lax.psum_scatter(outbound, 'rep', scatter_dimension=3, tiled=True)  31.6 us
    reduce_scatter x1, waiting for transfers between devices, local(): lax.psum_scatter(partial_band, 'rep', scatter_dimension=0, tiled=True)  31.6 us
    dot_general x1, matrix products, local(): jnp.einsum('bkj,bjf->bkf', live_blocks, gathered, preferred_element_type=...  18.2 us
    all_gather x1, waiting for transfers between devices, local(): input_grad = lax.all_gather(own_input_grad, 'rep', axis=0, tiled=True)  16.6 us
    dot_general x1, matrix products, local(): jnp.einsum('bjk,bjf->bkf', live_blocks, picked, preferred_element_type=jn...  14.8 us
  transfers between devices with their start and end apart: 8, of which 7 were waited for; matrix products, arithmetic and copies ran while one was open for 1% of the time, Pallas kernels for 0%

commit v1 on v0

v1 whole, which is shorter than its diff:
```python
import functools

import jax
import jax.numpy as jnp
from jax import lax
from jax.experimental import pallas as pl
from jax.experimental.pallas import tpu as pltpu
from jax.sharding import PartitionSpec as P

BF16 = jnp.bfloat16
F32 = jnp.float32
SLOT_GROUP = 16
COL_CHUNK = 16
ROW_TILE = 256
COL_TILE = 512
WHOLE = pl.BlockSpec(memory_space=pltpu.VMEM)
SMEM = pl.BlockSpec(memory_space=pltpu.SMEM)
ANY = pl.BlockSpec(memory_space=pl.ANY)


def params(*parts):
    size = sum(parts) + (6 << 20)
    return pltpu.CompilerParams(vmem_limit_bytes=min(size, 60 << 20))


def shape(dims, dtype):
    return jax.ShapeDtypeStruct(tuple(dims), dtype)


def dot(a, b, dims=((1,), (0,))):
    return lax.dot_general(a, b, (dims, ((), ())), preferred_element_type=F32)


def xor_perm(count, offset):
    return [(i, i ^ offset) for i in range(count)]


def densify_body(
    rows_ref, fetch_ref, count_ref, blocks_ref, out_ref, acc_ref, *, half, n_rep, n_hi, per_list, quarter
):
    r, q = lax.axis_index("row"), lax.axis_index("rep")
    chunk, step = pl.program_id(0), pl.program_id(1)
    group, blk = blocks_ref.shape[0], blocks_ref.shape[1]
    half_cells = acc_ref.shape[0]

    @pl.when(step == 0)
    def _():
        @pl.loop(0, half_cells)
        def _(i):
            acc_ref[i] = jnp.zeros(acc_ref.shape[1:], F32)

    live = count_ref[0]

    @pl.loop(0, group)
    def _(i):
        slot = step * group + i
        row = rows_ref[slot]
        fetch = fetch_ref[slot]
        j = lax.div(row, quarter) ^ q
        row_cell = (n_rep - 1 - j) * quarter + lax.rem(row, quarter) - half * half_cells
        k = lax.div(fetch, per_list) ^ r
        piece = (lax.rem(k, n_rep) ^ q) * n_hi + lax.div(k, n_rep)
        col_cell = piece * per_list + lax.rem(fetch, per_list) - chunk * COL_CHUNK
        here = (row_cell >= 0) & (row_cell < half_cells) & (col_cell >= 0) & (col_cell < COL_CHUNK)

        @pl.when(here & (slot < live))
        def _():
            cols = pl.ds(pl.multiple_of(col_cell * blk, blk), blk)
            acc_ref[row_cell, :, cols] += blocks_ref[i].astype(F32)

    @pl.when(step == pl.num_programs(1) - 1)
    def _():
        @pl.loop(0, half_cells)
        def _(i):
            out_ref[pl.ds(pl.multiple_of(i * blk, blk), blk), :] = acc_ref[i].astype(BF16)


def densify(block_rows, block_fetch, block_count, blocks, half, n_row, n_rep, per_list, row_blocks):
    slots, blk, _ = blocks.shape
    half_cells = row_blocks // 2
    cols = n_row * per_list * blk
    width = COL_CHUNK * blk
    body = functools.partial(
        densify_body,
        half=half,
        n_rep=n_rep,
        n_hi=n_row // n_rep,
        per_list=per_list,
        quarter=row_blocks // n_rep,
    )
    return pl.pallas_call(
        body,
        out_shape=shape((half_cells * blk, cols), BF16),
        grid_spec=pltpu.PrefetchScalarGridSpec(
            num_scalar_prefetch=3,
            grid=(cols // width, slots // SLOT_GROUP),
            in_specs=[pl.BlockSpec((SLOT_GROUP, blk, blk), lambda c, s, *_: (s, 0, 0))],
            out_specs=pl.BlockSpec((half_cells * blk, width), lambda c, s, *_: (0, c)),
            scratch_shapes=[pltpu.VMEM((half_cells, blk, width), F32)],
        ),
        compiler_params=params(half_cells * blk * width * 8, SLOT_GROUP * blk * blk * 4),
        cost_estimate=pl.CostEstimate(
            flops=slots * blk * blk, bytes_accessed=blocks.size * 2 + 8 * cols * half_cells * blk, transcendentals=0
        ),
        name=f"densify_{half}",
    )(block_rows, block_fetch, block_count, blocks)


def pack_body(*refs, n_hi, per_list, blk):
    lists = refs[:n_hi]
    features = refs[n_hi]
    outs = refs[n_hi + 1 : 2 * n_hi + 1]
    sems = refs[-1]
    r = lax.axis_index("row")
    copies = []
    for hi in range(n_hi):
        for c in range(per_list):
            b = lists[hi][0, r, c]
            copy = pltpu.make_async_copy(
                features.at[pl.ds(pl.multiple_of(b * blk, blk), blk)],
                outs[hi].at[pl.ds(c * blk, blk)],
                sems.at[hi * per_list + c],
            )
            copy.start()
            copies.append(copy)
    for copy in copies:
        copy.wait()


def pack(lists, features, per_list, blk):
    n_hi = len(lists)
    return pl.pallas_call(
        functools.partial(pack_body, n_hi=n_hi, per_list=per_list, blk=blk),
        out_shape=[shape((per_list * blk, features.shape[1]), BF16)] * n_hi,
        in_specs=[SMEM] * n_hi + [ANY],
        out_specs=[ANY] * n_hi,
        scratch_shapes=[pltpu.SemaphoreType.DMA((n_hi * per_list,))],
        compiler_params=params(0),
        name="pack",
    )(*lists, features)


def forward_body(*refs, n_pieces):
    pieces = refs[:n_pieces]
    adj_ref, send_ref, keep_ref = refs[n_pieces:]
    i = pl.program_id(0)
    depth = pieces[0].shape[0]
    total = dot(adj_ref[:, :depth], pieces[0][...])
    for n in range(1, n_pieces):
        total += dot(adj_ref[:, n * depth : (n + 1) * depth], pieces[n][...])

    half = pl.num_programs(0) // 2

    @pl.when(i < half)
    def _():
        send_ref[...] = total.astype(BF16)

    @pl.when(i >= half)
    def _():
        keep_ref[...] = total


def forward(pieces, adj):
    rows, cols = adj.shape
    features = pieces[0].shape[1]
    tiles = rows // ROW_TILE
    half = tiles // 2
    return pl.pallas_call(
        functools.partial(forward_body, n_pieces=len(pieces)),
        grid=(tiles,),
        out_shape=[shape((rows // 2, features), BF16), shape((rows // 2, features), F32)],
        in_specs=[pl.BlockSpec(x.shape, lambda i: (0, 0)) for x in pieces]
        + [pl.BlockSpec((ROW_TILE, cols), lambda i: (i, 0))],
        out_specs=[
            pl.BlockSpec((ROW_TILE, features), lambda i: (jnp.minimum(i, half - 1), 0)),
            pl.BlockSpec((ROW_TILE, features), lambda i: (jnp.maximum(i - half, 0), 0)),
        ],
        compiler_params=params(ROW_TILE * cols * 4, cols * features * 4),
        cost_estimate=pl.CostEstimate(
            flops=2 * rows * cols * features, bytes_accessed=adj.size * 2 + cols * features * 2, transcendentals=0
        ),
        name="forward",
    )(*pieces, adj)


def middle_body(
    keep_ref, near_ref, far_ref, weight_ref, cot_ref, out_ref, grad_ref, wsend_ref, w2_ref, w0_ref, acc_ref
):
    q = lax.axis_index("rep")
    hidden = (keep_ref[...] + near_ref[...].astype(F32) + far_ref[...].astype(F32)).astype(BF16)
    weight = weight_ref[...]
    pre_act = dot(hidden, weight)
    sig = jax.nn.sigmoid(pre_act)
    out_ref[...] = (pre_act * sig).astype(BF16)
    pre_grad = (cot_ref[...].astype(F32) * (sig * (1.0 + pre_act * (1.0 - sig)))).astype(BF16)
    grad_ref[...] = dot(weight, pre_grad, ((1,), (1,))).astype(BF16)
    acc_ref[...] = dot(hidden, pre_grad, ((0,), (0,)))
    part = w0_ref.shape[0]

    def piece(j):
        return acc_ref[pl.ds(pl.multiple_of((q ^ j) * part, part), part), :]

    wsend_ref[:part] = piece(3)
    wsend_ref[part:] = piece(1)
    w2_ref[...] = piece(2)
    w0_ref[...] = piece(0)


def middle(keep, near, far, weight, cot, n_rep):
    rows, features = keep.shape
    part = features // n_rep
    return pl.pallas_call(
        middle_body,
        out_shape=[
            shape((rows, features), BF16),
            shape((features, rows), BF16),
            shape((2 * part, features), F32),
            shape((part, features), F32),
            shape((part, features), F32),
        ],
        in_specs=[WHOLE] * 5,
        out_specs=[WHOLE] * 5,
        scratch_shapes=[pltpu.VMEM((features, features), F32)],
        compiler_params=params(12 << 20),
        cost_estimate=pl.CostEstimate(
            flops=6 * rows * features * features, bytes_accessed=rows * features * 14, transcendentals=rows * features
        ),
        name="middle",
    )(keep, near, far, weight, cot)


def back_first_body(odd_ref, even_ref, adj_ref, out_ref):
    rows = odd_ref.shape[1]
    out_ref[...] = dot(odd_ref[...], adj_ref[:rows]) + dot(even_ref[...], adj_ref[rows:])


def back_first(odd, even, adj):
    rows, cols = adj.shape
    features = odd.shape[0]
    return pl.pallas_call(
        back_first_body,
        grid=(cols // COL_TILE,),
        out_shape=shape((features, cols), F32),
        in_specs=[
            pl.BlockSpec(odd.shape, lambda i: (0, 0)),
            pl.BlockSpec(even.shape, lambda i: (0, 0)),
            pl.BlockSpec((rows, COL_TILE), lambda i: (0, i)),
        ],
        out_specs=pl.BlockSpec((features, COL_TILE), lambda i: (0, i)),
        compiler_params=params(4 << 20),
        cost_estimate=pl.CostEstimate(
            flops=2 * rows * cols * features, bytes_accessed=adj.size * 2 + cols * features * 4, transcendentals=0
        ),
        name="back_first",
    )(odd, even, adj)


def back_second_body(odd_ref, even_ref, adj_ref, first_ref, o3_ref, o2_ref, o1_ref, o0_ref, acc_ref):
    q = lax.axis_index("rep")
    rows = odd_ref.shape[1]
    acc_ref[...] = first_ref[...] + dot(odd_ref[...], adj_ref[:rows]) + dot(even_ref[...], adj_ref[rows:])
    part = o0_ref.shape[0]

    def piece(j):
        return acc_ref[pl.ds(pl.multiple_of((q ^ j) * part, part), part), :]

    o3_ref[...] = piece(3).astype(BF16)
    o2_ref[...] = piece(2)
    o1_ref[...] = piece(1).astype(BF16)
    o0_ref[...] = piece(0)


def back_second(odd, even, adj, first, n_rep):
    rows, cols = adj.shape
    features = odd.shape[0]
    part = features // n_rep
    per_piece = cols // n_rep // COL_TILE
    keep_spec = pl.BlockSpec((part, COL_TILE), lambda i: (0, i))
    send_spec = pl.BlockSpec(
        (part, COL_TILE), lambda i: (0, (lax.div(i, per_piece) ^ 1) * per_piece + lax.rem(i, per_piece))
    )
    return pl.pallas_call(
        back_second_body,
        grid=(cols // COL_TILE,),
        out_shape=[shape((part, cols), dtype) for dtype in (BF16, F32, BF16, F32)],
        in_specs=[
            pl.BlockSpec(odd.shape, lambda i: (0, 0)),
            pl.BlockSpec(even.shape, lambda i: (0, 0)),
            pl.BlockSpec((rows, COL_TILE), lambda i: (0, i)),
            pl.BlockSpec((features, COL_TILE), lambda i: (0, i)),
        ],
        out_specs=[send_spec, keep_spec, send_spec, keep_spec],
        scratch_shapes=[pltpu.VMEM((features, COL_TILE), F32)],
        compiler_params=params(6 << 20),
        cost_estimate=pl.CostEstimate(
            flops=2 * rows * cols * features, bytes_accessed=adj.size * 2 + cols * features * 7, transcendentals=0
        ),
        name="back_second",
    )(odd, even, adj, first)


def split_body(own_ref, near_ref, far_ref, *outs, n_rep, n_hi):
    q = lax.axis_index("rep")
    width = outs[0].shape[1]
    for k, out in enumerate(outs):
        j, hi = (k % n_rep) ^ q, k // n_rep
        cols = pl.ds(pl.multiple_of((j * n_hi + hi) * width, width), width)
        far_cols = pl.ds(pl.multiple_of(((j ^ 2) * n_hi + hi) * width, width), width)
        total = own_ref[:, cols] + near_ref[:, cols].astype(F32) + far_ref[:, far_cols].astype(F32)
        out[...] = total.astype(out.dtype)


def split(own, near, far, n_row, n_rep):
    part, cols = own.shape
    width = cols // n_row
    return pl.pallas_call(
        functools.partial(split_body, n_rep=n_rep, n_hi=n_row // n_rep),
        out_shape=[shape((part, width), F32 if k == 0 else BF16) for k in range(n_row)],
        in_specs=[WHOLE] * 3,
        out_specs=[WHOLE] * n_row,
        compiler_params=params(own.size * 12),
        cost_estimate=pl.CostEstimate(flops=2 * own.size, bytes_accessed=own.size * 10, transcendentals=0),
        name="split",
    )(own, near, far)


def collect_body(lists_ref, *refs, n_row, per_list, quarter, blk):
    messages = refs[:n_row]
    outs = refs[n_row:-1]
    acc_ref = refs[-1]
    r, q = lax.axis_index("row"), lax.axis_index("rep")
    acc_ref[...] = jnp.zeros(acc_ref.shape, F32)
    for k in range(n_row):
        for c in range(per_list):
            b = lists_ref[(r ^ k) * per_list + c]
            cell = (lax.div(b, quarter) ^ q) * quarter + lax.rem(b, quarter)
            cols = pl.ds(pl.multiple_of(cell * blk, blk), blk)
            acc_ref[:, cols] += messages[k][:, c * blk : (c + 1) * blk].astype(F32)
    width = outs[0].shape[1]
    for j, out in enumerate(outs):
        out[...] = acc_ref[:, j * width : (j + 1) * width].astype(out.dtype)


def collect(lists, messages, n_rep, per_list, row_blocks, blk):
    part = messages[0].shape[0]
    quarter = row_blocks // n_rep
    return pl.pallas_call(
        functools.partial(collect_body, n_row=len(messages), per_list=per_list, quarter=quarter, blk=blk),
        out_shape=[shape((part, quarter * blk), F32 if j == 0 else BF16) for j in range(n_rep)],
        in_specs=[SMEM] + [WHOLE] * len(messages),
        out_specs=[WHOLE] * n_rep,
        scratch_shapes=[pltpu.VMEM((part, row_blocks * blk), F32)],
        compiler_params=params(4 << 20),
        cost_estimate=pl.CostEstimate(
            flops=part * row_blocks * blk, bytes_accessed=part * row_blocks * blk * 5, transcendentals=0
        ),
        name="collect",
    )(lists, *messages)


def finish_body(*refs, n_rep, factor):
    grads = refs[:n_rep]
    weights = refs[n_rep : 2 * n_rep]
    node_ref, weight_ref, acc_ref = refs[2 * n_rep :]
    q = lax.axis_index("rep")
    part = grads[0].shape[0]
    for j in range(n_rep):
        rows = pl.ds(pl.multiple_of((q ^ j) * part, part), part)
        acc_ref[rows, :] = grads[j][...].astype(F32)
        weight_ref[rows, :] = weights[j][...] * factor
    node_ref[...] = acc_ref[...].T


def finish(grads, weights, factor):
    n_rep = len(grads)
    part, rows = grads[0].shape
    features = weights[0].shape[1]
    return pl.pallas_call(
        functools.partial(finish_body, n_rep=n_rep, factor=factor),
        out_shape=[shape((rows, part * n_rep), F32), shape((features, features), F32)],
        in_specs=[WHOLE] * (2 * n_rep),
        out_specs=[WHOLE] * 2,
        scratch_shapes=[pltpu.VMEM((part * n_rep, rows), F32)],
        compiler_params=params(6 << 20),
        cost_estimate=pl.CostEstimate(flops=0, bytes_accessed=rows * part * n_rep * 8, transcendentals=0),
        name="finish",
    )(*grads, *weights)


def local(
    node_features, weight, out_grad, blocks, block_rows, block_fetch, fetch_lists, block_count
):
    n_row = lax.axis_size("row")
    n_rep = lax.axis_size("rep")
    n_hi = n_row // n_rep
    band_rows, features = node_features.shape
    blk = blocks.shape[1]
    row_blocks = band_rows // blk
    per_list = fetch_lists.shape[2]

    def to_rep(x, j):
        return lax.ppermute(x, "rep", xor_perm(n_rep, j))

    def to_row(x, k):
        return lax.ppermute(x, "row", xor_perm(n_row, k))

    def spread(x, hi):
        perm = [
            (r * n_rep + q, (r ^ (hi * n_rep + q)) * n_rep + q) for r in range(n_row) for q in range(n_rep)
        ]
        return lax.ppermute(x, ("row", "rep"), perm)

    wanted = [spread(fetch_lists, hi) for hi in range(n_hi)]
    all_lists = lax.all_gather(fetch_lists[0], "row", axis=0, tiled=False)
    lists = lax.dynamic_index_in_dim(all_lists, lax.axis_index("row"), 1, keepdims=False).reshape(-1)

    outgoing = pack(wanted, node_features, per_list, blk)
    own = [spread(x, hi) for hi, x in enumerate(outgoing)]
    far = [to_rep(x, 2) for x in own]
    near = [to_rep(x, 1) for x in own]
    diag = [to_rep(x, 1) for x in far]
    pieces = own + near + far + diag

    adj_far, adj_near = [
        densify(block_rows, block_fetch, block_count, blocks, half, n_row, n_rep, per_list, row_blocks)
        for half in range(2)
    ]

    send3, keep2 = forward(pieces, adj_far)
    across = (keep2 + to_rep(send3, 1).astype(F32)).astype(BF16)
    arrived = to_rep(across, 2)
    send1, keep0 = forward(pieces, adj_near)
    output, grad0, wsend, w2, w0 = middle(keep0, to_rep(send1, 1), arrived, weight, out_grad, n_rep)

    grad2 = to_rep(grad0, 2)
    grad1 = to_rep(grad0, 1)
    grad3 = to_rep(grad2, 1)
    first = back_first(grad1, grad0, adj_near)
    o3, o2, o1, o0 = back_second(grad3, grad2, adj_far, first, n_rep)
    back_across = (o2 + to_rep(o3, 1).astype(F32)).astype(BF16)
    messages = split(o0, to_rep(o1, 1), to_rep(back_across, 2), n_row, n_rep)
    returned = [messages[0]] + [to_row(messages[k], k) for k in range(1, n_row)]
    grads = collect(lists, returned, n_rep, per_list, row_blocks, blk)

    part = features // n_rep
    got = to_rep(wsend, 1)
    w = w0 + got[part:] + to_rep(w2 + got[:part], 2)
    step = 1
    while step < n_row:
        w = w + to_row(w, step)
        step *= 2

    all_grads = [grads[0]] + [to_rep(grads[j], j) for j in range(1, n_rep)]
    all_w = [w] + [to_rep(w, j) for j in range(1, n_rep)]
    factor = float(n_row * band_rows) ** (-0.5)
    node_grad, weight_grad = finish(all_grads, all_w, factor)
    return (output, weight_grad, node_grad)


def solution(mesh):
    in_specs = (
        P("row", None),
        P(),
        P(("row", "rep"), None),
        P(("row", "rep"), None, None),
        P(("row", "rep")),
        P(("row", "rep")),
        P(("row", "rep"), None, None),
        P(("row", "rep")),
    )
    out_specs = (P(("row", "rep"), None), P(), P(("row", "rep"), None))
    return jax.shard_map(local, mesh=mesh, in_specs=in_specs, out_specs=out_specs, check_vma=False)
```

time: 433 us -> 136 us (0.31)
  waiting for transfers between devices: 243 us -> 27.8 us
  other arithmetic: 76.7 us -> 0.17 us
  matrix products: 38.1 us -> 0 us
  starting transfers between devices: 16.7 us -> 52.9 us
  Pallas kernels: 0 us -> 27.7 us
  local copies, waits for them, and re-layouts: 31.9 us -> 6.5 us
  between operations: 14.6 us -> 1.57 us
  blocking collectives: 10.6 us -> 19.4 us
    psum x1 -> x0, waiting for transfers between devices: 129 us -> none  [local(): weight_grad = lax.psum(local_grad, ('row', 'rep')) * factor]
    scatter-add x3 -> x0, other arithmetic: 73.7 us -> none  [the longest x1 36.2 us: local(): jax.ops.segment_sum(back_terms, block_fetch, num_segments=slot_rows.shape...]
    reduce_scatter x2 -> x0, waiting for transfers between devices: 63.3 us -> none  [the longest x1 31.6 us: local(): reduced = lax.psum_scatter(outbound, 'rep', scatter_dimension=3, tiled=True)]
    ppermute x0 -> x37, starting transfers between devices: none -> 52.9 us  [the longest x23 26 us: to_rep(): return lax.ppermute(x, 'rep', xor_perm(n_rep, j))]
    dot_general x5 -> x0, matrix products: 38.1 us -> none  [the longest x1 18.2 us: local(): jnp.einsum('bkj,bjf->bkf', live_blocks, gathered, preferred_element_type=...]
    all_gather x2 -> x0, waiting for transfers between devices: 30.7 us -> none  [the longest x1 16.6 us: local(): input_grad = lax.all_gather(own_input_grad, 'rep', axis=0, tiled=True)]
    ppermute x0 -> x37, waiting for transfers between devices: none -> 27.8 us  [the longest x23 20.8 us: to_rep(): return lax.ppermute(x, 'rep', xor_perm(n_rep, j))]
    pallas_call x0 -> x11, Pallas kernels: none -> 27.7 us  [the longest x2 15.1 us: densify(): pl.pallas_call(body, out_shape=shape((half_cells * blk, cols), BF16), gri...]
  transfers between devices with their start and end apart: 8 -> 37, of which waited for: 7 -> 11; matrix products, arithmetic and copies ran while one was open for 1% -> 0% of each run, Pallas kernels for 0% -> 17%
where the time goes in v1:
time: 136 us
  starting transfers between devices  52.9 us (39%)
  waiting for transfers between devices  27.8 us (20%)
  Pallas kernels  27.7 us (20%)
  blocking collectives  19.4 us (14%)
  local copies, waits for them, and re-layouts  6.5 us (5%)
  between operations  1.57 us (1%)
    ppermute x23, starting transfers between devices, to_rep(): return lax.ppermute(x, 'rep', xor_perm(n_rep, j))  26 us
    ppermute x23, waiting for transfers between devices, to_rep(): return lax.ppermute(x, 'rep', xor_perm(n_rep, j))  20.8 us
    all_gather x1, blocking collectives, local(): all_lists = lax.all_gather(fetch_lists[0], 'row', axis=0, tiled=False)  19.4 us
    ppermute x10, starting transfers between devices, to_row(): return lax.ppermute(x, 'row', xor_perm(n_row, k))  18.5 us
    pallas_call x2, Pallas kernels, densify(): pl.pallas_call(body, out_shape=shape((half_cells * blk, cols), BF16), gri...  15.1 us
    ppermute x4, starting transfers between devices, spread(): return lax.ppermute(x, ('row', 'rep'), perm)  8.4 us
    unnamed x15, local copies, waits for them, and re-layouts  6.14 us
    ppermute x10, waiting for transfers between devices, to_row(): return lax.ppermute(x, 'row', xor_perm(n_row, k))  5.39 us
  transfers between devices with their start and end apart: 37, of which 11 were waited for; matrix products, arithmetic and copies ran while one was open for 0% of the time, Pallas kernels for 17%

profile of v1, /device:TPU:0, one launch (start us, length us, event | category | flops | bytes accessed | tf_op | source)
XLA Modules:
  0.0 135.9 jit_solution(16503961226599513255)
XLA Ops:
  2.0 4.1 %collective-permute-start.1 = (s32[1,8,2]{2,1,0:T(8,128)S(1)}, s32[1,8,2]{2,1,0:T(8,128)S(1)}, u32[]{:S(2)}, u32[]{:S(2)}) collective-permute-start(s32[1,8,2]{2,1,0:T(8,128)S(1)} %copy.15), channel_id=1, source_target_pairs={{0,16},{1,21},{2,26},{3,31},{4,20},{5,17},{6,30},{7,27},{8,24},{9,... | collective-permute-start | bytes 200 | tf_op jit(solution)/shard_map/ppermute | solution.py:411
  10.7 3.0 %collective-permute-start.3 = (bf16[256,256]{1,0:T(8,128)(2,1)S(1)}, bf16[256,256]{1,0:T(8,128)(2,1)S(1)}, u32[]{:S(2)}, u32[]{:S(2)}) collective-permute-start(bf16[256,256]{1,0:T(8,128)(2,1)S(1)} %get-tuple-element.33), channel_id=1, source_target_pairs={{0,16},{1,21},{2,26},{3,31},{4,20},{5,17},{6,30},{7,27},{8,24},{9,... | collective-permute-start | bytes 393224 | tf_op jit(solution)/shard_map/ppermute | solution.py:411
  13.7 9.4 %collective-permute-start.6 = (bf16[256,256]{1,0:T(8,128)(2,1)S(1)}, bf16[256,256]{1,0:T(8,128)(2,1)S(1)}, u32[]{:S(2)}, u32[]{:S(2)}) collective-permute-start(bf16[256,256]{1,0:T(8,128)(2,1)S(1)} %collective-permute-done.2.refs_0_), channel_id=1, source_target_pairs={{0,2},{1,3},{2,0},{3,1},{4,6},{5,7},{6,4},{7,5},{8,10},{9,11},{10,... | collective-permute-start | bytes 393224 | tf_op jit(solution)/shard_map/ppermute | solution.py:402
  23.1 3.7 %collective-permute-start.7 = (bf16[256,256]{1,0:T(8,128)(2,1)S(1)}, bf16[256,256]{1,0:T(8,128)(2,1)S(1)}, u32[]{:S(2)}, u32[]{:S(2)}) collective-permute-start(bf16[256,256]{1,0:T(8,128)(2,1)S(1)} %collective-permute-done.3.refs_1_), channel_id=1, source_target_pairs={{0,2},{1,3},{2,0},{3,1},{4,6},{5,7},{6,4},{7,5},{8,10},{9,11},{10,... | collective-permute-start | bytes 393224 | tf_op jit(solution)/shard_map/ppermute | solution.py:402
  27.3 2.4 %collective-permute-done.7.refs_5_ = bf16[256,256]{1,0:T(8,128)(2,1)S(1)} collective-permute-done((bf16[256,256]{1,0:T(8,128)(2,1)S(1)}, bf16[256,256]{1,0:T(8,128)(2,1)S(1)}, u32[]{:S(2)}, u32[]{:S(2)}) %collective-permute-start.7) | collective-permute-done | bytes 131104 | tf_op jit(solution)/shard_map/ppermute | solution.py:402
  30.4 2.8 %copy-done = bf16[192,128,128]{2,1,0:T(8,128)(2,1)S(1)} copy-done((bf16[192,128,128]{2,1,0:T(8,128)(2,1)S(1)}, bf16[192,128,128]{2,1,0:T(8,128)(2,1)}, u32[]{:S(2)}) %copy-start) | copy-done | bytes 6291480
  34.5 7.5 %densify_0.1.refs_8_.adj_ref = bf16[1024,2048]{1,0:T(8,128)(2,1)S(1)} custom-call(s32[192]{0:T(256)S(1)} %copy-done.4, s32[192]{0:T(256)S(1)} %copy-done.5, s32[1]{0:T(128)S(6)} %copy.17.count_ref, bf16[192,128,128]{2,1,0:T(8,128)(2,1)S(1)} %copy-done), custom_call_target="tpu_custom_call" | custom-call | flops 3145728 | bytes 23068672 | tf_op jit(solution)/shard_map/densify_0/pallas_call | solution.py:91
  42.0 1.9 %forward.3 = (bf16[512,256]{1,0:T(8,128)(2,1)S(1)}, f32[512,256]{1,0:T(8,128)S(1)}) custom-call(bf16[256,256]{1,0:T(8,128)(2,1)S(1)} %collective-permute-done.2.refs_0_, bf16[256,256]{1,0:T(8,128)(2,1)S(1)} %collective-permute-done.3.refs_1_, bf16[256,256]{1,0:T(8,128)(2,1)S(1)} %collective-permute-done.4.refs_2_, ...), custom_call_target="tpu_custom_call" | custom-call | flops 1073741824 | bytes 5242880 | tf_op jit(solution)/shard_map/forward/pallas_call | solution.py:168
  44.4 7.6 %densify_1.1.refs_8_.adj_ref = bf16[1024,2048]{1,0:T(8,128)(2,1)S(1)} custom-call(s32[192]{0:T(256)S(1)} %copy-done.4, s32[192]{0:T(256)S(1)} %copy-done.5, s32[1]{0:T(128)S(6)} %copy.17.count_ref, bf16[192,128,128]{2,1,0:T(8,128)(2,1)S(1)} %copy-done), custom_call_target="tpu_custom_call" | custom-call | flops 3145728 | bytes 23068672 | tf_op jit(solution)/shard_map/densify_1/pallas_call | solution.py:91
  52.1 1.9 %forward.2 = (bf16[512,256]{1,0:T(8,128)(2,1)S(1)}, f32[512,256]{1,0:T(8,128)S(1)}) custom-call(bf16[256,256]{1,0:T(8,128)(2,1)S(1)} %collective-permute-done.2.refs_0_, bf16[256,256]{1,0:T(8,128)(2,1)S(1)} %collective-permute-done.3.refs_1_, bf16[256,256]{1,0:T(8,128)(2,1)S(1)} %collective-permute-done.4.refs_2_, ...), custom_call_target="tpu_custom_call" | custom-call | flops 1073741824 | bytes 5242880 | tf_op jit(solution)/shard_map/forward/pallas_call | solution.py:168
  54.1 2.7 %collective-permute-start.12 = (bf16[512,256]{1,0:T(8,128)(2,1)S(1)}, bf16[512,256]{1,0:T(8,128)(2,1)S(1)}, u32[]{:S(2)}, u32[]{:S(2)}) collective-permute-start(bf16[512,256]{1,0:T(8,128)(2,1)S(1)} %add_convert_fusion.1), channel_id=1, source_target_pairs={{0,2},{1,3},{2,0},{3,1},{4,6},{5,7},{6,4},{7,5},{8,10},{9,11},{10,... | collective-permute-start | bytes 786440 | tf_op jit(solution)/shard_map/ppermute | solution.py:402
  56.8 6.8 %collective-permute-done.12.far_ref = bf16[512,256]{1,0:T(8,128)(2,1)S(1)} collective-permute-done((bf16[512,256]{1,0:T(8,128)(2,1)S(1)}, bf16[512,256]{1,0:T(8,128)(2,1)S(1)}, u32[]{:S(2)}, u32[]{:S(2)}) %collective-permute-start.12) | collective-permute-done | bytes 262176 | tf_op jit(solution)/shard_map/ppermute | solution.py:402
  64.7 1.7 %collective-permute-start.13 = (bf16[256,512]{1,0:T(8,128)(2,1)S(1)}, bf16[256,512]{1,0:T(8,128)(2,1)S(1)}, u32[]{:S(2)}, u32[]{:S(2)}) collective-permute-start(bf16[256,512]{1,0:T(8,128)(2,1)S(1)} %get-tuple-element.39.even_ref), channel_id=1, source_target_pairs={{0,2},{1,3},{2,0},{3,1},{4,6},{5,7},{6,4},{7,5},{8,10},{9,11},{10,... | collective-permute-start | bytes 786440 | tf_op jit(solution)/shard_map/ppermute | solution.py:402
  66.4 6.2 %collective-permute-done.13.even_ref = bf16[256,512]{1,0:T(8,128)(2,1)S(1)} collective-permute-done((bf16[256,512]{1,0:T(8,128)(2,1)S(1)}, bf16[256,512]{1,0:T(8,128)(2,1)S(1)}, u32[]{:S(2)}, u32[]{:S(2)}) %collective-permute-start.13) | collective-permute-done | bytes 262176 | tf_op jit(solution)/shard_map/ppermute | solution.py:402
  73.2 2.3 %back_first.1.first_ref = f32[256,2048]{1,0:T(8,128)S(1)} custom-call(bf16[256,512]{1,0:T(8,128)(2,1)S(1)} %collective-permute-done.15.odd_ref, bf16[256,512]{1,0:T(8,128)(2,1)S(1)} %get-tuple-element.39.even_ref, bf16[1024,2048]{1,0:T(8,128)(2,1)S(1)} %densify_1.1.refs_8_.adj_ref), custom_call_target="tpu_custom_call" | custom-call | flops 1073741824 | bytes 6291456 | tf_op jit(solution)/shard_map/back_first/pallas_call | solution.py:240
  75.5 2.6 %back_second.1 = (bf16[64,2048]{1,0:T(8,128)(2,1)S(1)}, f32[64,2048]{1,0:T(8,128)S(1)}, bf16[64,2048]{1,0:T(8,128)(2,1)S(1)}, f32[64,2048]{1,0:T(8,128)S(1)}) custom-call(bf16[256,512]{1,0:T(8,128)(2,1)S(1)} %collective-permute-done.14.odd_ref, bf16[256,512]{1,0:T(8,128)(2,1)S(1)} %collective-permute-done.13.even_ref, ...), custom_call_target="tpu_custom_call" | custom-call | flops 1073741824 | bytes 7864320 | tf_op jit(solution)/shard_map/back_second/pallas_call | solution.py:282
  83.9 3.1 %collective-permute-done.31 = f32[64,256]{1,0:T(8,128)S(1)} collective-permute-done((f32[64,256]{1,0:T(8,128)S(1)}, f32[64,256]{1,0:T(8,128)S(1)}, u32[]{:S(2)}, u32[]{:S(2)}) %collective-permute-start.31) | collective-permute-done | bytes 65568 | tf_op jit(solution)/shard_map/ppermute | solution.py:405
  87.1 2.8 %collective-permute-start.32 = (f32[64,256]{1,0:T(8,128)S(1)}, f32[64,256]{1,0:T(8,128)S(1)}, u32[]{:S(2)}, u32[]{:S(2)}) collective-permute-start(f32[64,256]{1,0:T(8,128)S(1)} %add.34), channel_id=1, source_target_pairs={{0,8},{4,12},{8,0},{12,4},{16,24},{20,28},{24,16},{28,20},{1,9},{5... | collective-permute-start | bytes 196616 | tf_op jit(solution)/shard_map/ppermute | solution.py:405
  89.9 2.2 %collective-permute-done.32 = f32[64,256]{1,0:T(8,128)S(1)} collective-permute-done((f32[64,256]{1,0:T(8,128)S(1)}, f32[64,256]{1,0:T(8,128)S(1)}, u32[]{:S(2)}, u32[]{:S(2)}) %collective-permute-start.32) | collective-permute-done | bytes 65568 | tf_op jit(solution)/shard_map/ppermute | solution.py:405
  92.2 3.2 %collective-permute-start.33 = (f32[64,256]{1,0:T(8,128)S(1)}, f32[64,256]{1,0:T(8,128)S(1)}, u32[]{:S(2)}, u32[]{:S(2)}) collective-permute-start(f32[64,256]{1,0:T(8,128)S(1)} %add.35), channel_id=1, source_target_pairs={{0,16},{4,20},{8,24},{12,28},{16,0},{20,4},{24,8},{28,12},{1,17},{... | collective-permute-start | bytes 196616 | tf_op jit(solution)/shard_map/ppermute | solution.py:405
  100.7 1.8 %collective-permute-start.23 = (bf16[64,256]{1,0:T(8,128)(2,1)S(1)}, bf16[64,256]{1,0:T(8,128)(2,1)S(1)}, u32[]{:S(2)}, u32[]{:S(2)}) collective-permute-start(bf16[64,256]{1,0:T(8,128)(2,1)S(1)} %get-tuple-element.49), channel_id=1, source_target_pairs={{0,20},{4,16},{8,28},{12,24},{16,4},{20,0},{24,12},{28,8},{1,21},{... | collective-permute-start | bytes 98312 | tf_op jit(solution)/shard_map/ppermute | solution.py:405
  102.5 2.7 %collective-permute-start.24 = (bf16[64,256]{1,0:T(8,128)(2,1)S(1)}, bf16[64,256]{1,0:T(8,128)(2,1)S(1)}, u32[]{:S(2)}, u32[]{:S(2)}) collective-permute-start(bf16[64,256]{1,0:T(8,128)(2,1)S(1)} %get-tuple-element.50), channel_id=1, source_target_pairs={{0,24},{4,28},{8,16},{12,20},{16,8},{20,12},{24,0},{28,4},{1,25},{... | collective-permute-start | bytes 98312 | tf_op jit(solution)/shard_map/ppermute | solution.py:405
  106.8 19.4 %all_gather.3 = s32[8,8,2]{1,2,0:T(2,128)S(1)} all-gather(s32[1,8,2]{1,2,0:T(2,128)S(1)} %copy-done.6), channel_id=1, replica_groups=mesh['row'=8,'rep'=4] {'row'}, dimensions={0}, use_global_device_ids=true | all-gather | bytes 576 | tf_op jit(solution)/shard_map/all_gather | solution.py:414
  131.9 2.3 %collective-permute-done.27.refs_2_ = bf16[64,512]{1,0:T(8,128)(2,1)S(1)} collective-permute-done((bf16[64,512]{1,0:T(8,128)(2,1)S(1)}, bf16[64,512]{1,0:T(8,128)(2,1)S(1)}, u32[]{:S(2)}, u32[]{:S(2)}) %collective-permute-start.27) | collective-permute-done | bytes 65568 | tf_op jit(solution)/shard_map/ppermute | solution.py:402
  (86 shorter events, 30.5 us)
Async XLA Ops:
  2.0 5.7 %collective-permute-start.1 = (s32[1,8,2]{2,1,0:T(8,128)S(1)}, s32[1,8,2]{2,1,0:T(8,128)S(1)}, u32[]{:S(2)}, u32[]{:S(2)}) collective-permute-start(s32[1,8,2]{2,1,0:T(8,128)S(1)} %copy.15), channel_id=1, source_target_pairs={{0,16},{1,21},{2,26},{3,31},{4,20},{5,17},{6,30},{7,27},{8,24},{9,... | collective-permute-start | bytes 200 | tf_op jit(solution)/shard_map/ppermute | solution.py:411
  10.7 12.4 %collective-permute-start.3 = (bf16[256,256]{1,0:T(8,128)(2,1)S(1)}, bf16[256,256]{1,0:T(8,128)(2,1)S(1)}, u32[]{:S(2)}, u32[]{:S(2)}) collective-permute-start(bf16[256,256]{1,0:T(8,128)(2,1)S(1)} %get-tuple-element.33), channel_id=1, source_target_pairs={{0,16},{1,21},{2,26},{3,31},{4,20},{5,17},{6,30},{7,27},{8,24},{9,... | collective-permute-start | bytes 393224 | tf_op jit(solution)/shard_map/ppermute | solution.py:411
  13.7 13.6 %collective-permute-start.6 = (bf16[256,256]{1,0:T(8,128)(2,1)S(1)}, bf16[256,256]{1,0:T(8,128)(2,1)S(1)}, u32[]{:S(2)}, u32[]{:S(2)}) collective-permute-start(bf16[256,256]{1,0:T(8,128)(2,1)S(1)} %collective-permute-done.2.refs_0_), channel_id=1, source_target_pairs={{0,2},{1,3},{2,0},{3,1},{4,6},{5,7},{6,4},{7,5},{8,10},{9,11},{10,... | collective-permute-start | bytes 393224 | tf_op jit(solution)/shard_map/ppermute | solution.py:402
  23.1 6.6 %collective-permute-start.7 = (bf16[256,256]{1,0:T(8,128)(2,1)S(1)}, bf16[256,256]{1,0:T(8,128)(2,1)S(1)}, u32[]{:S(2)}, u32[]{:S(2)}) collective-permute-start(bf16[256,256]{1,0:T(8,128)(2,1)S(1)} %collective-permute-done.3.refs_1_), channel_id=1, source_target_pairs={{0,2},{1,3},{2,0},{3,1},{4,6},{5,7},{6,4},{7,5},{8,10},{9,11},{10,... | collective-permute-start | bytes 393224 | tf_op jit(solution)/shard_map/ppermute | solution.py:402
  26.8 15.2 %collective-permute-start.4 = (bf16[256,256]{1,0:T(8,128)(2,1)S(1)}, bf16[256,256]{1,0:T(8,128)(2,1)S(1)}, u32[]{:S(2)}, u32[]{:S(2)}) collective-permute-start(bf16[256,256]{1,0:T(8,128)(2,1)S(1)} %collective-permute-done.2.refs_0_), channel_id=1, source_target_pairs={{0,1},{1,0},{2,3},{3,2},{4,5},{5,4},{6,7},{7,6},{8,9},{9,8},{10,11... | collective-permute-start | bytes 393224 | tf_op jit(solution)/shard_map/ppermute | solution.py:402
  26.8 15.2 %collective-permute-start.5 = (bf16[256,256]{1,0:T(8,128)(2,1)S(1)}, bf16[256,256]{1,0:T(8,128)(2,1)S(1)}, u32[]{:S(2)}, u32[]{:S(2)}) collective-permute-start(bf16[256,256]{1,0:T(8,128)(2,1)S(1)} %collective-permute-done.3.refs_1_), channel_id=1, source_target_pairs={{0,1},{1,0},{2,3},{3,2},{4,5},{5,4},{6,7},{7,6},{8,9},{9,8},{10,11... | collective-permute-start | bytes 393224 | tf_op jit(solution)/shard_map/ppermute | solution.py:402
  27.3 14.7 %collective-permute-start.8 = (bf16[256,256]{1,0:T(8,128)(2,1)S(1)}, bf16[256,256]{1,0:T(8,128)(2,1)S(1)}, u32[]{:S(2)}, u32[]{:S(2)}) collective-permute-start(bf16[256,256]{1,0:T(8,128)(2,1)S(1)} %collective-permute-done.6.refs_4_), channel_id=1, source_target_pairs={{0,1},{1,0},{2,3},{3,2},{4,5},{5,4},{6,7},{7,6},{8,9},{9,8},{10,11... | collective-permute-start | bytes 393224 | tf_op jit(solution)/shard_map/ppermute | solution.py:402
  29.7 12.3 %collective-permute-start.9 = (bf16[256,256]{1,0:T(8,128)(2,1)S(1)}, bf16[256,256]{1,0:T(8,128)(2,1)S(1)}, u32[]{:S(2)}, u32[]{:S(2)}) collective-permute-start(bf16[256,256]{1,0:T(8,128)(2,1)S(1)} %collective-permute-done.7.refs_5_), channel_id=1, source_target_pairs={{0,1},{1,0},{2,3},{3,2},{4,5},{5,4},{6,7},{7,6},{8,9},{9,8},{10,11... | collective-permute-start | bytes 393224 | tf_op jit(solution)/shard_map/ppermute | solution.py:402
  43.9 10.1 %collective-permute-start.11 = (bf16[512,256]{1,0:T(8,128)(2,1)S(1)}, bf16[512,256]{1,0:T(8,128)(2,1)S(1)}, u32[]{:S(2)}, u32[]{:S(2)}) collective-permute-start(bf16[512,256]{1,0:T(8,128)(2,1)S(1)} %get-tuple-element.37), channel_id=1, source_target_pairs={{0,1},{1,0},{2,3},{3,2},{4,5},{5,4},{6,7},{7,6},{8,9},{9,8},{10,11... | collective-permute-start | bytes 786440 | tf_op jit(solution)/shard_map/ppermute | solution.py:402
  54.1 9.5 %collective-permute-start.12 = (bf16[512,256]{1,0:T(8,128)(2,1)S(1)}, bf16[512,256]{1,0:T(8,128)(2,1)S(1)}, u32[]{:S(2)}, u32[]{:S(2)}) collective-permute-start(bf16[512,256]{1,0:T(8,128)(2,1)S(1)} %add_convert_fusion.1), channel_id=1, source_target_pairs={{0,2},{1,3},{2,0},{3,1},{4,6},{5,7},{6,4},{7,5},{8,10},{9,11},{10,... | collective-permute-start | bytes 786440 | tf_op jit(solution)/shard_map/ppermute | solution.py:402
  64.7 8.0 %collective-permute-start.13 = (bf16[256,512]{1,0:T(8,128)(2,1)S(1)}, bf16[256,512]{1,0:T(8,128)(2,1)S(1)}, u32[]{:S(2)}, u32[]{:S(2)}) collective-permute-start(bf16[256,512]{1,0:T(8,128)(2,1)S(1)} %get-tuple-element.39.even_ref), channel_id=1, source_target_pairs={{0,2},{1,3},{2,0},{3,1},{4,6},{5,7},{6,4},{7,5},{8,10},{9,11},{10,... | collective-permute-start | bytes 786440 | tf_op jit(solution)/shard_map/ppermute | solution.py:402
  66.4 6.8 %collective-permute-start.15 = (bf16[256,512]{1,0:T(8,128)(2,1)S(1)}, bf16[256,512]{1,0:T(8,128)(2,1)S(1)}, u32[]{:S(2)}, u32[]{:S(2)}) collective-permute-start(bf16[256,512]{1,0:T(8,128)(2,1)S(1)} %get-tuple-element.39.even_ref), channel_id=1, source_target_pairs={{0,1},{1,0},{2,3},{3,2},{4,5},{5,4},{6,7},{7,6},{8,9},{9,8},{10,11... | collective-permute-start | bytes 786440 | tf_op jit(solution)/shard_map/ppermute | solution.py:402
  72.7 5.5 %collective-permute-start.29 = (f32[128,256]{1,0:T(8,128)S(1)}, f32[128,256]{1,0:T(8,128)S(1)}, u32[]{:S(2)}, u32[]{:S(2)}) collective-permute-start(f32[128,256]{1,0:T(8,128)S(1)} %get-tuple-element.57), channel_id=1, source_target_pairs={{0,1},{1,0},{2,3},{3,2},{4,5},{5,4},{6,7},{7,6},{8,9},{9,8},{10,11... | collective-permute-start | bytes 393224 | tf_op jit(solution)/shard_map/ppermute | solution.py:402
  79.7 15.6 %collective-permute-start.16 = (bf16[64,2048]{1,0:T(8,128)(2,1)S(1)}, bf16[64,2048]{1,0:T(8,128)(2,1)S(1)}, u32[]{:S(2)}, u32[]{:S(2)}) collective-permute-start(bf16[64,2048]{1,0:T(8,128)(2,1)S(1)} %get-tuple-element.41), channel_id=1, source_target_pairs={{0,1},{1,0},{2,3},{3,2},{4,5},{5,4},{6,7},{7,6},{8,9},{9,8},{10,11... | collective-permute-start | bytes 786440 | tf_op jit(solution)/shard_map/ppermute | solution.py:402
  80.0 15.3 %collective-permute-start.18 = (bf16[64,2048]{1,0:T(8,128)(2,1)S(1)}, bf16[64,2048]{1,0:T(8,128)(2,1)S(1)}, u32[]{:S(2)}, u32[]{:S(2)}) collective-permute-start(bf16[64,2048]{1,0:T(8,128)(2,1)S(1)} %add_convert_fusion), channel_id=1, source_target_pairs={{0,2},{1,3},{2,0},{3,1},{4,6},{5,7},{6,4},{7,5},{8,10},{9,11},{10,... | collective-permute-start | bytes 786440 | tf_op jit(solution)/shard_map/ppermute | solution.py:402
  92.2 6.8 %collective-permute-start.33 = (f32[64,256]{1,0:T(8,128)S(1)}, f32[64,256]{1,0:T(8,128)S(1)}, u32[]{:S(2)}, u32[]{:S(2)}) collective-permute-start(f32[64,256]{1,0:T(8,128)S(1)} %add.35), channel_id=1, source_target_pairs={{0,16},{4,20},{8,24},{12,28},{16,0},{20,4},{24,8},{28,12},{1,17},{... | collective-permute-start | bytes 196616 | tf_op jit(solution)/shard_map/ppermute | solution.py:405
  95.4 5.3 %collective-permute-start.19 = (bf16[64,256]{1,0:T(8,128)(2,1)S(1)}, bf16[64,256]{1,0:T(8,128)(2,1)S(1)}, u32[]{:S(2)}, u32[]{:S(2)}) collective-permute-start(bf16[64,256]{1,0:T(8,128)(2,1)S(1)} %get-tuple-element.45), channel_id=1, source_target_pairs={{0,4},{4,0},{8,12},{12,8},{16,20},{20,16},{24,28},{28,24},{1,5},{5... | collective-permute-start | bytes 98312 | tf_op jit(solution)/shard_map/ppermute | solution.py:405
  96.5 6.0 %collective-permute-start.20 = (bf16[64,256]{1,0:T(8,128)(2,1)S(1)}, bf16[64,256]{1,0:T(8,128)(2,1)S(1)}, u32[]{:S(2)}, u32[]{:S(2)}) collective-permute-start(bf16[64,256]{1,0:T(8,128)(2,1)S(1)} %get-tuple-element.46), channel_id=1, source_target_pairs={{0,8},{4,12},{8,0},{12,4},{16,24},{20,28},{24,16},{28,20},{1,9},{5... | collective-permute-start | bytes 98312 | tf_op jit(solution)/shard_map/ppermute | solution.py:405
  97.5 7.8 %collective-permute-start.21 = (bf16[64,256]{1,0:T(8,128)(2,1)S(1)}, bf16[64,256]{1,0:T(8,128)(2,1)S(1)}, u32[]{:S(2)}, u32[]{:S(2)}) collective-permute-start(bf16[64,256]{1,0:T(8,128)(2,1)S(1)} %get-tuple-element.47), channel_id=1, source_target_pairs={{0,12},{4,8},{8,4},{12,0},{16,28},{20,24},{24,20},{28,16},{1,13},{... | collective-permute-start | bytes 98312 | tf_op jit(solution)/shard_map/ppermute | solution.py:405
  99.0 31.5 %collective-permute-start.34 = (f32[64,256]{1,0:T(8,128)S(1)}, f32[64,256]{1,0:T(8,128)S(1)}, u32[]{:S(2)}, u32[]{:S(2)}) collective-permute-start(f32[64,256]{1,0:T(8,128)S(1)} %add.36.refs_4_), channel_id=1, source_target_pairs={{0,1},{1,0},{2,3},{3,2},{4,5},{5,4},{6,7},{7,6},{8,9},{9,8},{10,11... | collective-permute-start | bytes 196616 | tf_op jit(solution)/shard_map/ppermute | solution.py:402
  99.1 27.5 %collective-permute-start.22 = (bf16[64,256]{1,0:T(8,128)(2,1)S(1)}, bf16[64,256]{1,0:T(8,128)(2,1)S(1)}, u32[]{:S(2)}, u32[]{:S(2)}) collective-permute-start(bf16[64,256]{1,0:T(8,128)(2,1)S(1)} %get-tuple-element.48), channel_id=1, source_target_pairs={{0,16},{4,20},{8,24},{12,28},{16,0},{20,4},{24,8},{28,12},{1,17},{... | collective-permute-start | bytes 98312 | tf_op jit(solution)/shard_map/ppermute | solution.py:405
  100.7 26.8 %collective-permute-start.23 = (bf16[64,256]{1,0:T(8,128)(2,1)S(1)}, bf16[64,256]{1,0:T(8,128)(2,1)S(1)}, u32[]{:S(2)}, u32[]{:S(2)}) collective-permute-start(bf16[64,256]{1,0:T(8,128)(2,1)S(1)} %get-tuple-element.49), channel_id=1, source_target_pairs={{0,20},{4,16},{8,28},{12,24},{16,4},{20,0},{24,12},{28,8},{1,21},{... | collective-permute-start | bytes 98312 | tf_op jit(solution)/shard_map/ppermute | solution.py:405
  102.5 25.0 %collective-permute-start.24 = (bf16[64,256]{1,0:T(8,128)(2,1)S(1)}, bf16[64,256]{1,0:T(8,128)(2,1)S(1)}, u32[]{:S(2)}, u32[]{:S(2)}) collective-permute-start(bf16[64,256]{1,0:T(8,128)(2,1)S(1)} %get-tuple-element.50), channel_id=1, source_target_pairs={{0,24},{4,28},{8,16},{12,20},{16,8},{20,12},{24,0},{28,4},{1,25},{... | collective-permute-start | bytes 98312 | tf_op jit(solution)/shard_map/ppermute | solution.py:405
  105.2 22.3 %collective-permute-start.25 = (bf16[64,256]{1,0:T(8,128)(2,1)S(1)}, bf16[64,256]{1,0:T(8,128)(2,1)S(1)}, u32[]{:S(2)}, u32[]{:S(2)}) collective-permute-start(bf16[64,256]{1,0:T(8,128)(2,1)S(1)} %get-tuple-element.51), channel_id=1, source_target_pairs={{0,28},{4,24},{8,20},{12,16},{16,12},{20,8},{24,4},{28,0},{1,29},{... | collective-permute-start | bytes 98312 | tf_op jit(solution)/shard_map/ppermute | solution.py:405
  (20 other events, 111.4 us)

commit v2 on v1

--- a/solution.py
+++ b/solution.py
@@ -19,8 +19,7 @@
 
 
 def params(*parts):
-    size = sum(parts) + (6 << 20)
-    return pltpu.CompilerParams(vmem_limit_bytes=min(size, 60 << 20))
+    return pltpu.CompilerParams(vmem_limit_bytes=min(sum(parts) + (6 << 20), 62 << 20))
 
 
 def shape(dims, dtype):
@@ -36,43 +35,56 @@
 
 
 def densify_body(
-    rows_ref, fetch_ref, count_ref, blocks_ref, out_ref, acc_ref, *, half, n_rep, n_hi, per_list, quarter
+    rows_ref, fetch_ref, count_ref, blocks_ref, out_ref, acc_ref, held_ref, sems, *, half, n_rep, n_hi, per_list, quarter
 ):
     r, q = lax.axis_index("row"), lax.axis_index("rep")
-    chunk, step = pl.program_id(0), pl.program_id(1)
-    group, blk = blocks_ref.shape[0], blocks_ref.shape[1]
+    chunk = pl.program_id(0)
+    slots, blk = blocks_ref.shape[0], blocks_ref.shape[1]
+    groups = slots // SLOT_GROUP
     half_cells = acc_ref.shape[0]
 
-    @pl.when(step == 0)
+    def fetch_group(g):
+        part = pl.ds(g * SLOT_GROUP, SLOT_GROUP)
+        return pltpu.make_async_copy(blocks_ref.at[part], held_ref.at[part], sems.at[g])
+
+    @pl.when(chunk == 0)
     def _():
-        @pl.loop(0, half_cells)
+        @pl.loop(0, groups)
+        def _(g):
+            fetch_group(g).start()
+
+    @pl.loop(0, half_cells)
+    def _(i):
+        acc_ref[i] = jnp.zeros(acc_ref.shape[1:], F32)
+
+    live = count_ref[0]
+
+    @pl.loop(0, groups)
+    def _(g):
+        @pl.when(chunk == 0)
+        def _():
+            fetch_group(g).wait()
+
+        @pl.loop(0, SLOT_GROUP)
         def _(i):
-            acc_ref[i] = jnp.zeros(acc_ref.shape[1:], F32)
-
-    live = count_ref[0]
-
-    @pl.loop(0, group)
+            slot = g * SLOT_GROUP + i
+            row = rows_ref[slot]
+            fetch = fetch_ref[slot]
+            j = lax.div(row, quarter) ^ q
+            row_cell = (n_rep - 1 - j) * quarter + lax.rem(row, quarter) - half * half_cells
+            k = lax.div(fetch, per_list) ^ r
+            piece = (lax.rem(k, n_rep) ^ q) * n_hi + lax.div(k, n_rep)
+            col_cell = piece * per_list + lax.rem(fetch, per_list) - chunk * COL_CHUNK
+            here = (row_cell >= 0) & (row_cell < half_cells) & (col_cell >= 0) & (col_cell < COL_CHUNK)
+
+            @pl.when(here & (slot < live))
+            def _():
+                cols = pl.ds(pl.multiple_of(col_cell * blk, blk), blk)
+                acc_ref[row_cell, :, cols] += held_ref[slot].astype(F32)
+
+    @pl.loop(0, half_cells)
     def _(i):
-        slot = step * group + i
-        row = rows_ref[slot]
-        fetch = fetch_ref[slot]
-        j = lax.div(row, quarter) ^ q
-        row_cell = (n_rep - 1 - j) * quarter + lax.rem(row, quarter) - half * half_cells
-        k = lax.div(fetch, per_list) ^ r
-        piece = (lax.rem(k, n_rep) ^ q) * n_hi + lax.div(k, n_rep)
-        col_cell = piece * per_list + lax.rem(fetch, per_list) - chunk * COL_CHUNK
-        here = (row_cell >= 0) & (row_cell < half_cells) & (col_cell >= 0) & (col_cell < COL_CHUNK)
-
-        @pl.when(here & (slot < live))
-        def _():
-            cols = pl.ds(pl.multiple_of(col_cell * blk, blk), blk)
-            acc_ref[row_cell, :, cols] += blocks_ref[i].astype(F32)
-
-    @pl.when(step == pl.num_programs(1) - 1)
-    def _():
-        @pl.loop(0, half_cells)
-        def _(i):
-            out_ref[pl.ds(pl.multiple_of(i * blk, blk), blk), :] = acc_ref[i].astype(BF16)
+        out_ref[pl.ds(pl.multiple_of(i * blk, blk), blk), :] = acc_ref[i].astype(BF16)
 
 
 def densify(block_rows, block_fetch, block_count, blocks, half, n_row, n_rep, per_list, row_blocks):
@@ -93,12 +105,16 @@
         out_shape=shape((half_cells * blk, cols), BF16),
         grid_spec=pltpu.PrefetchScalarGridSpec(
             num_scalar_prefetch=3,
-            grid=(cols // width, slots // SLOT_GROUP),
-            in_specs=[pl.BlockSpec((SLOT_GROUP, blk, blk), lambda c, s, *_: (s, 0, 0))],
-            out_specs=pl.BlockSpec((half_cells * blk, width), lambda c, s, *_: (0, c)),
-            scratch_shapes=[pltpu.VMEM((half_cells, blk, width), F32)],
-        ),
-        compiler_params=params(half_cells * blk * width * 8, SLOT_GROUP * blk * blk * 4),
+            grid=(cols // width,),
+            in_specs=[pl.BlockSpec(memory_space=pltpu.HBM)],
+            out_specs=pl.BlockSpec((half_cells * blk, width), lambda c, *_: (0, c)),
+            scratch_shapes=[
+                pltpu.VMEM((half_cells, blk, width), F32),
+                pltpu.VMEM(blocks.shape, BF16),
+                pltpu.SemaphoreType.DMA((slots // SLOT_GROUP,)),
+            ],
+        ),
+        compiler_params=params((52 if half else 56) << 20),
         cost_estimate=pl.CostEstimate(
             flops=slots * blk * blk, bytes_accessed=blocks.size * 2 + 8 * cols * half_cells * blk, transcendentals=0
         ),
@@ -110,12 +126,13 @@
     lists = refs[:n_hi]
     features = refs[n_hi]
     outs = refs[n_hi + 1 : 2 * n_hi + 1]
-    sems = refs[-1]
+    own_list, sems = refs[2 * n_hi + 1 :]
     r = lax.axis_index("row")
     copies = []
     for hi in range(n_hi):
         for c in range(per_list):
             b = lists[hi][0, r, c]
+            own_list[hi * per_list + c] = b
             copy = pltpu.make_async_copy(
                 features.at[pl.ds(pl.multiple_of(b * blk, blk), blk)],
                 outs[hi].at[pl.ds(c * blk, blk)],
@@ -131,9 +148,9 @@
     n_hi = len(lists)
     return pl.pallas_call(
         functools.partial(pack_body, n_hi=n_hi, per_list=per_list, blk=blk),
-        out_shape=[shape((per_list * blk, features.shape[1]), BF16)] * n_hi,
-        in_specs=[SMEM] * n_hi + [ANY],
-        out_specs=[ANY] * n_hi,
+        out_shape=[shape((per_list * blk, features.shape[1]), BF16)] * n_hi + [shape((128,), jnp.int32)],
+        in_specs=[SMEM] * n_hi + [pl.BlockSpec(memory_space=pltpu.HBM)],
+        out_specs=[ANY] * n_hi + [SMEM],
         scratch_shapes=[pltpu.SemaphoreType.DMA((n_hi * per_list,))],
         compiler_params=params(0),
         name="pack",
@@ -229,34 +246,52 @@
     )(keep, near, far, weight, cot)
 
 
-def back_first_body(odd_ref, even_ref, adj_ref, out_ref):
+def back_first_body(odd_ref, even_ref, adj_ref, w2_ref, w0_ref, got_ref, out_ref, w2_out, w0_out):
     rows = odd_ref.shape[1]
+    part = w0_ref.shape[0]
+
+    @pl.when(pl.program_id(0) == 0)
+    def _():
+        w2_out[...] = w2_ref[...] + got_ref[:part]
+        w0_out[...] = w0_ref[...] + got_ref[part:]
+
     out_ref[...] = dot(odd_ref[...], adj_ref[:rows]) + dot(even_ref[...], adj_ref[rows:])
 
 
-def back_first(odd, even, adj):
+def back_first(odd, even, adj, w2, w0, got):
     rows, cols = adj.shape
     features = odd.shape[0]
+    w_spec = pl.BlockSpec(w0.shape, lambda i: (0, 0))
     return pl.pallas_call(
         back_first_body,
         grid=(cols // COL_TILE,),
-        out_shape=shape((features, cols), F32),
+        out_shape=[shape((features, cols), F32), shape(w0.shape, F32), shape(w0.shape, F32)],
         in_specs=[
             pl.BlockSpec(odd.shape, lambda i: (0, 0)),
             pl.BlockSpec(even.shape, lambda i: (0, 0)),
             pl.BlockSpec((rows, COL_TILE), lambda i: (0, i)),
+            w_spec,
+            w_spec,
+            pl.BlockSpec(got.shape, lambda i: (0, 0)),
         ],
-        out_specs=pl.BlockSpec((features, COL_TILE), lambda i: (0, i)),
+        out_specs=[pl.BlockSpec((features, COL_TILE), lambda i: (0, i)), w_spec, w_spec],
         compiler_params=params(4 << 20),
         cost_estimate=pl.CostEstimate(
             flops=2 * rows * cols * features, bytes_accessed=adj.size * 2 + cols * features * 4, transcendentals=0
         ),
         name="back_first",
-    )(odd, even, adj)
-
-
-def back_second_body(odd_ref, even_ref, adj_ref, first_ref, o3_ref, o2_ref, o1_ref, o0_ref, acc_ref):
+    )(odd, even, adj, w2, w0, got)
+
+
+def back_second_body(
+    odd_ref, even_ref, adj_ref, first_ref, w_ref, got_ref, o3_ref, o2_ref, o1_ref, o0_ref, w_out, acc_ref
+):
     q = lax.axis_index("rep")
+
+    @pl.when(pl.program_id(0) == 0)
+    def _():
+        w_out[...] = w_ref[...] + got_ref[...]
+
     rows = odd_ref.shape[1]
     acc_ref[...] = first_ref[...] + dot(odd_ref[...], adj_ref[:rows]) + dot(even_ref[...], adj_ref[rows:])
     part = o0_ref.shape[0]
@@ -270,37 +305,59 @@
     o0_ref[...] = piece(0)
 
 
-def back_second(odd, even, adj, first, n_rep):
+def back_second(odd, even, adj, first, w, got, n_rep):
     rows, cols = adj.shape
     features = odd.shape[0]
     part = features // n_rep
     per_piece = cols // n_rep // COL_TILE
     keep_spec = pl.BlockSpec((part, COL_TILE), lambda i: (0, i))
+    w_spec = pl.BlockSpec(w.shape, lambda i: (0, 0))
     send_spec = pl.BlockSpec(
         (part, COL_TILE), lambda i: (0, (lax.div(i, per_piece) ^ 1) * per_piece + lax.rem(i, per_piece))
     )
     return pl.pallas_call(
         back_second_body,
         grid=(cols // COL_TILE,),
-        out_shape=[shape((part, cols), dtype) for dtype in (BF16, F32, BF16, F32)],
+        out_shape=[shape((part, cols), dtype) for dtype in (BF16, F32, BF16, F32)] + [shape(w.shape, F32)],
         in_specs=[
             pl.BlockSpec(odd.shape, lambda i: (0, 0)),
             pl.BlockSpec(even.shape, lambda i: (0, 0)),
             pl.BlockSpec((rows, COL_TILE), lambda i: (0, i)),
             pl.BlockSpec((features, COL_TILE), lambda i: (0, i)),
+            w_spec,
+            w_spec,
         ],
-        out_specs=[send_spec, keep_spec, send_spec, keep_spec],
+        out_specs=[send_spec, keep_spec, send_spec, keep_spec, w_spec],
         scratch_shapes=[pltpu.VMEM((features, COL_TILE), F32)],
         compiler_params=params(6 << 20),
         cost_estimate=pl.CostEstimate(
             flops=2 * rows * cols * features, bytes_accessed=adj.size * 2 + cols * features * 7, transcendentals=0
         ),
         name="back_second",
-    )(odd, even, adj, first)
-
-
-def split_body(own_ref, near_ref, far_ref, *outs, n_rep, n_hi):
+    )(odd, even, adj, first, w, got)
+
+
+def across_body(keep_ref, near_ref, w_ref, got_ref, out_ref, w_out):
+    out_ref[...] = (keep_ref[...] + near_ref[...].astype(F32)).astype(BF16)
+    w_out[...] = w_ref[...] + got_ref[...]
+
+
+def across_sum(keep, near, w, got):
+    return pl.pallas_call(
+        across_body,
+        out_shape=[shape(keep.shape, BF16), shape(w.shape, F32)],
+        in_specs=[WHOLE] * 4,
+        out_specs=[WHOLE] * 2,
+        compiler_params=params(keep.size * 8),
+        cost_estimate=pl.CostEstimate(flops=keep.size, bytes_accessed=keep.size * 8, transcendentals=0),
+        name="across_sum",
+    )(keep, near, w, got)
+
+
+def split_body(own_ref, near_ref, far_ref, w_ref, got_ref, *outs, n_rep, n_hi):
     q = lax.axis_index("rep")
+    *outs, w_out = outs
+    w_out[...] = w_ref[...] + got_ref[...]
     width = outs[0].shape[1]
     for k, out in enumerate(outs):
         j, hi = (k % n_rep) ^ q, k // n_rep
@@ -310,52 +367,65 @@
         out[...] = total.astype(out.dtype)
 
 
-def split(own, near, far, n_row, n_rep):
+def split(own, near, far, w, got, n_row, n_rep):
     part, cols = own.shape
     width = cols // n_row
     return pl.pallas_call(
         functools.partial(split_body, n_rep=n_rep, n_hi=n_row // n_rep),
-        out_shape=[shape((part, width), F32 if k == 0 else BF16) for k in range(n_row)],
-        in_specs=[WHOLE] * 3,
-        out_specs=[WHOLE] * n_row,
+        out_shape=[shape((part, width), F32 if k == 0 else BF16) for k in range(n_row)] + [shape(w.shape, F32)],
+        in_specs=[WHOLE] * 5,
+        out_specs=[WHOLE] * (n_row + 1),
         compiler_params=params(own.size * 12),
         cost_estimate=pl.CostEstimate(flops=2 * own.size, bytes_accessed=own.size * 10, transcendentals=0),
         name="split",
-    )(own, near, far)
-
-
-def collect_body(lists_ref, *refs, n_row, per_list, quarter, blk):
-    messages = refs[:n_row]
-    outs = refs[n_row:-1]
-    acc_ref = refs[-1]
-    r, q = lax.axis_index("row"), lax.axis_index("rep")
+    )(own, near, far, w, got)
+
+
+def collect_body(*refs, n_row, n_rep, per_list, quarter, blk):
+    lists = refs[:n_rep]
+    messages = refs[n_rep : n_rep + n_row]
+    w_ref, got_ref = refs[n_rep + n_row : n_rep + n_row + 2]
+    outs = refs[n_rep + n_row + 2 : -2]
+    w_out, acc_ref = refs[-2:]
+    q = lax.axis_index("rep")
     acc_ref[...] = jnp.zeros(acc_ref.shape, F32)
     for k in range(n_row):
+        j = (k % n_rep) ^ q
         for c in range(per_list):
-            b = lists_ref[(r ^ k) * per_list + c]
+            at = k // n_rep * per_list + c
+            b = lists[0][at]
+            for other in range(1, n_rep):
+                b = jnp.where(j == other, lists[other][at], b)
             cell = (lax.div(b, quarter) ^ q) * quarter + lax.rem(b, quarter)
             cols = pl.ds(pl.multiple_of(cell * blk, blk), blk)
             acc_ref[:, cols] += messages[k][:, c * blk : (c + 1) * blk].astype(F32)
     width = outs[0].shape[1]
     for j, out in enumerate(outs):
         out[...] = acc_ref[:, j * width : (j + 1) * width].astype(out.dtype)
-
-
-def collect(lists, messages, n_rep, per_list, row_blocks, blk):
+    w_out[...] = (w_ref[...] + got_ref[...]).astype(w_out.dtype)
+
+
+def collect(lists, messages, w, got, per_list, row_blocks, blk, last):
+    n_rep = len(lists)
+    n_row = len(messages)
     part = messages[0].shape[0]
     quarter = row_blocks // n_rep
-    return pl.pallas_call(
-        functools.partial(collect_body, n_row=len(messages), per_list=per_list, quarter=quarter, blk=blk),
-        out_shape=[shape((part, quarter * blk), F32 if j == 0 else BF16) for j in range(n_rep)],
-        in_specs=[SMEM] + [WHOLE] * len(messages),
-        out_specs=[WHOLE] * n_rep,
+    body = functools.partial(
+        collect_body, n_row=n_row, n_rep=n_rep, per_list=per_list, quarter=quarter, blk=blk
+    )
+    return pl.pallas_call(
+        body,
+        out_shape=[shape((part, quarter * blk), F32 if j == 0 else BF16) for j in range(n_rep)]
+        + [shape(w.shape, BF16 if last else F32)],
+        in_specs=[SMEM] * n_rep + [WHOLE] * (n_row + 2),
+        out_specs=[WHOLE] * (n_rep + 1),
         scratch_shapes=[pltpu.VMEM((part, row_blocks * blk), F32)],
         compiler_params=params(4 << 20),
         cost_estimate=pl.CostEstimate(
             flops=part * row_blocks * blk, bytes_accessed=part * row_blocks * blk * 5, transcendentals=0
         ),
         name="collect",
-    )(lists, *messages)
+    )(*lists, *messages, w, got)
 
 
 def finish_body(*refs, n_rep, factor):
@@ -367,7 +437,7 @@
     for j in range(n_rep):
         rows = pl.ds(pl.multiple_of((q ^ j) * part, part), part)
         acc_ref[rows, :] = grads[j][...].astype(F32)
-        weight_ref[rows, :] = weights[j][...] * factor
+        weight_ref[rows, :] = weights[j][...].astype(F32) * factor
     node_ref[...] = acc_ref[...].T
 
 
@@ -410,46 +480,46 @@
         ]
         return lax.ppermute(x, ("row", "rep"), perm)
 
+    def after(x, *done):
+        return lax.optimization_barrier((x, *done))[0]
+
     wanted = [spread(fetch_lists, hi) for hi in range(n_hi)]
-    all_lists = lax.all_gather(fetch_lists[0], "row", axis=0, tiled=False)
-    lists = lax.dynamic_index_in_dim(all_lists, lax.axis_index("row"), 1, keepdims=False).reshape(-1)
-
-    outgoing = pack(wanted, node_features, per_list, blk)
+    adj_far, adj_near = [
+        densify(block_rows, block_fetch, block_count, blocks, half, n_row, n_rep, per_list, row_blocks)
+        for half in range(2)
+    ]
+    *outgoing, own_list = pack(after(wanted, adj_far), node_features, per_list, blk)
     own = [spread(x, hi) for hi, x in enumerate(outgoing)]
+    lists = [own_list] + [to_rep(own_list, j) for j in range(1, n_rep)]
+    own = after(own, adj_near, lists)
     far = [to_rep(x, 2) for x in own]
     near = [to_rep(x, 1) for x in own]
     diag = [to_rep(x, 1) for x in far]
     pieces = own + near + far + diag
 
-    adj_far, adj_near = [
-        densify(block_rows, block_fetch, block_count, blocks, half, n_row, n_rep, per_list, row_blocks)
-        for half in range(2)
-    ]
-
     send3, keep2 = forward(pieces, adj_far)
     across = (keep2 + to_rep(send3, 1).astype(F32)).astype(BF16)
     arrived = to_rep(across, 2)
-    send1, keep0 = forward(pieces, adj_near)
+    send1, keep0 = forward(pieces, after(adj_near, across))
+    arrived = after(arrived, keep0)
     output, grad0, wsend, w2, w0 = middle(keep0, to_rep(send1, 1), arrived, weight, out_grad, n_rep)
 
     grad2 = to_rep(grad0, 2)
     grad1 = to_rep(grad0, 1)
+    first, w2, w0 = back_first(grad1, grad0, adj_near, w2, w0, to_rep(wsend, 1))
+    grad2 = after(grad2, first)
     grad3 = to_rep(grad2, 1)
-    first = back_first(grad1, grad0, adj_near)
-    o3, o2, o1, o0 = back_second(grad3, grad2, adj_far, first, n_rep)
-    back_across = (o2 + to_rep(o3, 1).astype(F32)).astype(BF16)
-    messages = split(o0, to_rep(o1, 1), to_rep(back_across, 2), n_row, n_rep)
+    o3, o2, o1, o0, w = back_second(grad3, grad2, adj_far, first, w0, to_rep(w2, 2), n_rep)
+    back_across, w = across_sum(o2, to_rep(o3, 1), w, to_row(w, 1))
+    *messages, w = split(o0, to_rep(o1, 1), to_rep(back_across, 2), w, to_row(w, 2), n_row, n_rep)
     returned = [messages[0]] + [to_row(messages[k], k) for k in range(1, n_row)]
-    grads = collect(lists, returned, n_rep, per_list, row_blocks, blk)
-
-    part = features // n_rep
-    got = to_rep(wsend, 1)
-    w = w0 + got[part:] + to_rep(w2 + got[:part], 2)
-    step = 1
+    *grads, w = collect(lists, returned, w, to_row(w, 4), per_list, row_blocks, blk, n_row == 8)
+
+    step = 8
     while step < n_row:
         w = w + to_row(w, step)
         step *= 2
-
+    w = w.astype(BF16)
     all_grads = [grads[0]] + [to_rep(grads[j], j) for j in range(1, n_rep)]
     all_w = [w] + [to_rep(w, j) for j in range(1, n_rep)]
     factor = float(n_row * band_rows) ** (-0.5)

time: 136 us -> 118 us (0.87)
  blocking collectives: 19.4 us -> 0 us
  starting transfers between devices: 52.9 us -> 41.9 us
  waiting for transfers between devices: 27.8 us -> 38.4 us
  Pallas kernels: 27.7 us -> 34.3 us
  local copies, waits for them, and re-layouts: 6.5 us -> 0.78 us
    all_gather x1 -> x0, blocking collectives: 19.4 us -> none  [local(): all_lists = lax.all_gather(fetch_lists[0], 'row', axis=0, tiled=False)]
    ppermute x10, waiting for transfers between devices: 5.39 us -> 11.8 us  [to_row(): return lax.ppermute(x, 'row', xor_perm(n_row, k))]
    ppermute x23 -> x26, waiting for transfers between devices: 20.8 us -> 26.6 us  [to_rep(): return lax.ppermute(x, 'rep', xor_perm(n_rep, j))]
    pallas_call x2, Pallas kernels: 15.1 us -> 20.9 us  [densify(): pl.pallas_call(body, out_shape=shape((half_cells * blk, cols), BF16), gri...]
    unnamed x15 -> x11, local copies, waits for them, and re-layouts: 6.14 us -> 0.78 us
    ppermute x10, starting transfers between devices: 18.5 us -> 14 us  [to_row(): return lax.ppermute(x, 'row', xor_perm(n_row, k))]
    ppermute x23 -> x26, starting transfers between devices: 26 us -> 22.5 us  [to_rep(): return lax.ppermute(x, 'rep', xor_perm(n_rep, j))]
    ppermute x4, starting transfers between devices: 8.4 us -> 5.5 us  [spread(): return lax.ppermute(x, ('row', 'rep'), perm)]
  transfers between devices with their start and end apart: 37 -> 40, of which waited for: 11 -> 15; matrix products, arithmetic and copies ran while one was open for 0% -> 0% of each run, Pallas kernels for 17% -> 21%
where the time goes in v2:
time: 118 us; the launch traced here: 117 us
  starting transfers between devices  41.9 us (36%)
  waiting for transfers between devices  38.4 us (33%)
  Pallas kernels  34.3 us (29%)
  between operations  1.55 us (1%)
    ppermute x26, waiting for transfers between devices, to_rep(): return lax.ppermute(x, 'rep', xor_perm(n_rep, j))  26.6 us
    ppermute x26, starting transfers between devices, to_rep(): return lax.ppermute(x, 'rep', xor_perm(n_rep, j))  22.5 us
    pallas_call x2, Pallas kernels, densify(): pl.pallas_call(body, out_shape=shape((half_cells * blk, cols), BF16), gri...  20.9 us
    ppermute x10, starting transfers between devices, to_row(): return lax.ppermute(x, 'row', xor_perm(n_row, k))  14 us
    ppermute x10, waiting for transfers between devices, to_row(): return lax.ppermute(x, 'row', xor_perm(n_row, k))  11.8 us
    ppermute x4, starting transfers between devices, spread(): return lax.ppermute(x, ('row', 'rep'), perm)  5.5 us
    pallas_call x2, Pallas kernels, forward(): pl.pallas_call(functools.partial(forward_body, n_pieces=len(pieces)), gri...  3.79 us
    pallas_call x1, Pallas kernels, back_second(): pl.pallas_call(back_second_body, grid=(cols // COL_TILE,), out_shape=[sha...  2.61 us
  transfers between devices with their start and end apart: 40, of which 15 were waited for; matrix products, arithmetic and copies ran while one was open for 0% of the time, Pallas kernels for 21%

profile of v2, /device:TPU:0, one launch (start us, length us, event | category | flops | bytes accessed | tf_op | source)
XLA Modules:
  0.0 117.0 jit_solution(18283297725189506567)
XLA Ops:
  1.4 4.0 %collective-permute-start.1 = (s32[1,8,2]{2,1,0:T(8,128)S(1)}, s32[1,8,2]{2,1,0:T(8,128)S(1)}, u32[]{:S(2)}, u32[]{:S(2)}) collective-permute-start(s32[1,8,2]{2,1,0:T(8,128)S(1)} %copy.11), channel_id=1, source_target_pairs={{0,16},{1,21},{2,26},{3,31},{4,20},{5,17},{6,30},{7,27},{8,24},{9,... | collective-permute-start | bytes 200 | tf_op jit(solution)/shard_map/ppermute | solution.py:481
  6.7 10.5 %densify_0.1.refs_8_.adj_ref = bf16[1024,2048]{1,0:T(8,128)(2,1)} custom-call(s32[192]{0:T(256)} %rows_ref.3, s32[192]{0:T(256)} %fetch_ref.3, s32[1]{0:T(128)S(6)} %copy.13.count_ref, bf16[192,128,128]{2,1,0:T(8,128)(2,1)} %blocks_ref.3), custom_call_target="tpu_custom_call" | custom-call | flops 3145728 | bytes 23068672 | tf_op jit(solution)/shard_map/densify_0/pallas_call | solution.py:103
  19.8 7.4 %collective-permute-start.6 = (s32[128]{0:T(128)S(1)}, s32[128]{0:T(128)S(1)}, u32[]{:S(2)}, u32[]{:S(2)}) collective-permute-start(s32[128]{0:T(128)S(1)} %get-tuple-element.52.refs_0_), channel_id=1, source_target_pairs={{0,3},{1,2},{2,1},{3,0},{4,7},{5,6},{6,5},{7,4},{8,11},{9,10},{10,... | collective-permute-start | bytes 1544 | tf_op jit(solution)/shard_map/ppermute | solution.py:472
  27.4 10.3 %densify_1.1.refs_8_.adj_ref = bf16[1024,2048]{1,0:T(8,128)(2,1)} custom-call(s32[192]{0:T(256)} %rows_ref.3, s32[192]{0:T(256)} %fetch_ref.3, s32[1]{0:T(128)S(6)} %copy.13.count_ref, bf16[192,128,128]{2,1,0:T(8,128)(2,1)} %blocks_ref.3), custom_call_target="tpu_custom_call" | custom-call | flops 3145728 | bytes 23068672 | tf_op jit(solution)/shard_map/densify_1/pallas_call | solution.py:103
  37.8 2.4 %collective-permute-start.9 = (bf16[256,256]{1,0:T(8,128)(2,1)S(1)}, bf16[256,256]{1,0:T(8,128)(2,1)S(1)}, u32[]{:S(2)}, u32[]{:S(2)}) collective-permute-start(bf16[256,256]{1,0:T(8,128)(2,1)S(1)} %collective-permute-done.2.refs_0_), channel_id=1, source_target_pairs={{0,2},{1,3},{2,0},{3,1},{4,6},{5,7},{6,4},{7,5},{8,10},{9,11},{10,... | collective-permute-start | bytes 393224 | tf_op jit(solution)/shard_map/ppermute | solution.py:472
  40.8 3.8 %collective-permute-done.9.refs_4_ = bf16[256,256]{1,0:T(8,128)(2,1)S(1)} collective-permute-done((bf16[256,256]{1,0:T(8,128)(2,1)S(1)}, bf16[256,256]{1,0:T(8,128)(2,1)S(1)}, u32[]{:S(2)}, u32[]{:S(2)}) %collective-permute-start.9) | collective-permute-done | bytes 131104 | tf_op jit(solution)/shard_map/ppermute | solution.py:472
  44.5 2.5 %collective-permute-done.10.refs_5_ = bf16[256,256]{1,0:T(8,128)(2,1)S(1)} collective-permute-done((bf16[256,256]{1,0:T(8,128)(2,1)S(1)}, bf16[256,256]{1,0:T(8,128)(2,1)S(1)}, u32[]{:S(2)}, u32[]{:S(2)}) %collective-permute-start.10) | collective-permute-done | bytes 131104 | tf_op jit(solution)/shard_map/ppermute | solution.py:472
  48.3 1.9 %forward.2 = (bf16[512,256]{1,0:T(8,128)(2,1)S(1)}, f32[512,256]{1,0:T(8,128)S(1)}) custom-call(bf16[256,256]{1,0:T(8,128)(2,1)S(1)} %collective-permute-done.2.refs_0_, bf16[256,256]{1,0:T(8,128)(2,1)S(1)} %collective-permute-done.3.refs_1_, bf16[256,256]{1,0:T(8,128)(2,1)S(1)} %collective-permute-done.7.refs_2_, ...), custom_call_target="tpu_custom_call" | custom-call | flops 1073741824 | bytes 5242880 | tf_op jit(solution)/shard_map/forward/pallas_call | solution.py:185
  51.9 1.8 %collective-permute-start.15 = (bf16[512,256]{1,0:T(8,128)(2,1)S(1)}, bf16[512,256]{1,0:T(8,128)(2,1)S(1)}, u32[]{:S(2)}, u32[]{:S(2)}) collective-permute-start(bf16[512,256]{1,0:T(8,128)(2,1)S(1)} %add_convert_fusion), channel_id=1, source_target_pairs={{0,2},{1,3},{2,0},{3,1},{4,6},{5,7},{6,4},{7,5},{8,10},{9,11},{10,... | collective-permute-start | bytes 786440 | tf_op jit(solution)/shard_map/ppermute | solution.py:472
  53.7 1.9 %forward.3 = (bf16[512,256]{1,0:T(8,128)(2,1)S(1)}, f32[512,256]{1,0:T(8,128)S(1)}) custom-call(bf16[256,256]{1,0:T(8,128)(2,1)S(1)} %collective-permute-done.2.refs_0_, bf16[256,256]{1,0:T(8,128)(2,1)S(1)} %collective-permute-done.3.refs_1_, bf16[256,256]{1,0:T(8,128)(2,1)S(1)} %collective-permute-done.7.refs_2_, ...), custom_call_target="tpu_custom_call" | custom-call | flops 1073741824 | bytes 5242880 | tf_op jit(solution)/shard_map/forward/pallas_call | solution.py:185
  55.7 4.6 %collective-permute-done.15.far_ref = bf16[512,256]{1,0:T(8,128)(2,1)S(1)} collective-permute-done((bf16[512,256]{1,0:T(8,128)(2,1)S(1)}, bf16[512,256]{1,0:T(8,128)(2,1)S(1)}, u32[]{:S(2)}, u32[]{:S(2)}) %collective-permute-start.15) | collective-permute-done | bytes 262176 | tf_op jit(solution)/shard_map/ppermute | solution.py:472
  64.5 2.3 %back_first.1 = (f32[256,2048]{1,0:T(8,128)S(1)}, f32[64,256]{1,0:T(8,128)S(1)}, f32[64,256]{1,0:T(8,128)S(1)}) custom-call(bf16[256,512]{1,0:T(8,128)(2,1)S(1)} %collective-permute-done.17.odd_ref, bf16[256,512]{1,0:T(8,128)(2,1)S(1)} %get-tuple-element.62.even_ref, bf16[1024,2048]{1,0:T(8,128)(2,1)S(1)} %copy-done.1, ...), custom_call_target="tpu_custom_call" | custom-call | flops 1073741824 | bytes 6291456 | tf_op jit(solution)/shard_map/back_first/pallas_call | solution.py:265
  66.8 3.3 %collective-permute-done.16.even_ref = bf16[256,512]{1,0:T(8,128)(2,1)S(1)} collective-permute-done((bf16[256,512]{1,0:T(8,128)(2,1)S(1)}, bf16[256,512]{1,0:T(8,128)(2,1)S(1)}, u32[]{:S(2)}, u32[]{:S(2)}) %collective-permute-start.16) | collective-permute-done | bytes 262176 | tf_op jit(solution)/shard_map/ppermute | solution.py:472
  71.9 2.8 %collective-permute-done.20.got_ref = f32[64,256]{1,0:T(8,128)S(1)} collective-permute-done((f32[64,256]{1,0:T(8,128)S(1)}, f32[64,256]{1,0:T(8,128)S(1)}, u32[]{:S(2)}, u32[]{:S(2)}) %collective-permute-start.20) | collective-permute-done | bytes 65568 | tf_op jit(solution)/shard_map/ppermute | solution.py:472
  74.7 2.6 %back_second.1 = (bf16[64,2048]{1,0:T(8,128)(2,1)S(1)}, f32[64,2048]{1,0:T(8,128)S(1)}, bf16[64,2048]{1,0:T(8,128)(2,1)S(1)}, f32[64,2048]{1,0:T(8,128)S(1)}, f32[64,256]{1,0:T(8,128)S(1)}) custom-call(bf16[256,512]{1,0:T(8,128)(2,1)S(1)} %collective-permute-done.19.odd_ref, bf16[256,512]{1,0:T(8,128)(2,1)S(1)} %collective-permute-done.16.even_ref, ...), custom_call_target="tpu_custom_call" | custom-call | flops 1073741824 | bytes 7864320 | tf_op jit(solution)/shard_map/back_second/pallas_call | solution.py:318
  78.6 3.2 %collective-permute-done.23.got_ref = f32[64,256]{1,0:T(8,128)S(1)} collective-permute-done((f32[64,256]{1,0:T(8,128)S(1)}, f32[64,256]{1,0:T(8,128)S(1)}, u32[]{:S(2)}, u32[]{:S(2)}) %collective-permute-start.23) | collective-permute-done | bytes 65568 | tf_op jit(solution)/shard_map/ppermute | solution.py:475
  83.7 4.3 %collective-permute-done.25.got_ref = f32[64,256]{1,0:T(8,128)S(1)} collective-permute-done((f32[64,256]{1,0:T(8,128)S(1)}, f32[64,256]{1,0:T(8,128)S(1)}, u32[]{:S(2)}, u32[]{:S(2)}) %collective-permute-start.25) | collective-permute-done | bytes 65568 | tf_op jit(solution)/shard_map/ppermute | solution.py:475
  88.0 1.9 %collective-permute-done.24.far_ref = bf16[64,2048]{1,0:T(8,128)(2,1)S(1)} collective-permute-done((bf16[64,2048]{1,0:T(8,128)(2,1)S(1)}, bf16[64,2048]{1,0:T(8,128)(2,1)S(1)}, u32[]{:S(2)}, u32[]{:S(2)}) %collective-permute-start.24) | collective-permute-done | bytes 262176 | tf_op jit(solution)/shard_map/ppermute | solution.py:472
  91.2 2.3 %collective-permute-start.28 = (bf16[64,256]{1,0:T(8,128)(2,1)S(1)}, bf16[64,256]{1,0:T(8,128)(2,1)S(1)}, u32[]{:S(2)}, u32[]{:S(2)}) collective-permute-start(bf16[64,256]{1,0:T(8,128)(2,1)S(1)} %get-tuple-element.80), channel_id=1, source_target_pairs={{0,12},{4,8},{8,4},{12,0},{16,28},{20,24},{24,20},{28,16},{1,13},{... | collective-permute-start | bytes 98312 | tf_op jit(solution)/shard_map/ppermute | solution.py:475
  96.5 2.6 %collective-permute-start.30 = (bf16[64,256]{1,0:T(8,128)(2,1)S(1)}, bf16[64,256]{1,0:T(8,128)(2,1)S(1)}, u32[]{:S(2)}, u32[]{:S(2)}) collective-permute-start(bf16[64,256]{1,0:T(8,128)(2,1)S(1)} %get-tuple-element.82), channel_id=1, source_target_pairs={{0,20},{4,16},{8,28},{12,24},{16,4},{20,0},{24,12},{28,8},{1,21},{... | collective-permute-start | bytes 98312 | tf_op jit(solution)/shard_map/ppermute | solution.py:475
  100.6 2.3 %collective-permute-start.32 = (bf16[64,256]{1,0:T(8,128)(2,1)S(1)}, bf16[64,256]{1,0:T(8,128)(2,1)S(1)}, u32[]{:S(2)}, u32[]{:S(2)}) collective-permute-start(bf16[64,256]{1,0:T(8,128)(2,1)S(1)} %get-tuple-element.84), channel_id=1, source_target_pairs={{0,28},{4,24},{8,20},{12,16},{16,12},{20,8},{24,4},{28,0},{1,29},{... | collective-permute-start | bytes 98312 | tf_op jit(solution)/shard_map/ppermute | solution.py:475
  104.9 2.3 %collective-permute-done.32.refs_11_ = bf16[64,256]{1,0:T(8,128)(2,1)S(1)} collective-permute-done((bf16[64,256]{1,0:T(8,128)(2,1)S(1)}, bf16[64,256]{1,0:T(8,128)(2,1)S(1)}, u32[]{:S(2)}, u32[]{:S(2)}) %collective-permute-start.32) | collective-permute-done | bytes 32800 | tf_op jit(solution)/shard_map/ppermute | solution.py:475
  108.0 1.8 %collective-permute-start.34 = (bf16[64,512]{1,0:T(8,128)(2,1)S(1)}, bf16[64,512]{1,0:T(8,128)(2,1)S(1)}, u32[]{:S(2)}, u32[]{:S(2)}) collective-permute-start(bf16[64,512]{1,0:T(8,128)(2,1)S(1)} %get-tuple-element.87), channel_id=1, source_target_pairs={{0,1},{1,0},{2,3},{3,2},{4,5},{5,4},{6,7},{7,6},{8,9},{9,8},{10,11... | collective-permute-start | bytes 196616 | tf_op jit(solution)/shard_map/ppermute | solution.py:472
  112.0 3.9 %collective-permute-done.38.refs_6_ = bf16[64,256]{1,0:T(8,128)(2,1)S(1)} collective-permute-done((bf16[64,256]{1,0:T(8,128)(2,1)S(1)}, bf16[64,256]{1,0:T(8,128)(2,1)S(1)}, u32[]{:S(2)}, u32[]{:S(2)}) %collective-permute-start.38) | collective-permute-done | bytes 32800 | tf_op jit(solution)/shard_map/ppermute | solution.py:472
  (80 shorter events, 28.7 us)
Async XLA Ops:
  1.4 15.9 %collective-permute-start.1 = (s32[1,8,2]{2,1,0:T(8,128)S(1)}, s32[1,8,2]{2,1,0:T(8,128)S(1)}, u32[]{:S(2)}, u32[]{:S(2)}) collective-permute-start(s32[1,8,2]{2,1,0:T(8,128)S(1)} %copy.11), channel_id=1, source_target_pairs={{0,16},{1,21},{2,26},{3,31},{4,20},{5,17},{6,30},{7,27},{8,24},{9,... | collective-permute-start | bytes 200 | tf_op jit(solution)/shard_map/ppermute | solution.py:481
  5.4 11.9 %collective-permute-start = (s32[1,8,2]{2,1,0:T(8,128)S(1)}, s32[1,8,2]{2,1,0:T(8,128)S(1)}, u32[]{:S(2)}, u32[]{:S(2)}) collective-permute-start(s32[1,8,2]{2,1,0:T(8,128)S(1)} %copy.11), channel_id=1, source_target_pairs={{0,0},{1,5},{2,10},{3,15},{4,4},{5,1},{6,14},{7,11},{8,8},{9,13},{... | collective-permute-start | bytes 200 | tf_op jit(solution)/shard_map/ppermute | solution.py:481
  19.0 18.8 %collective-permute-start.2 = (bf16[256,256]{1,0:T(8,128)(2,1)S(1)}, bf16[256,256]{1,0:T(8,128)(2,1)S(1)}, u32[]{:S(2)}, u32[]{:S(2)}) collective-permute-start(bf16[256,256]{1,0:T(8,128)(2,1)S(1)} %get-tuple-element.50), channel_id=1, source_target_pairs={{0,0},{1,5},{2,10},{3,15},{4,4},{5,1},{6,14},{7,11},{8,8},{9,13},{... | collective-permute-start | bytes 393224 | tf_op jit(solution)/shard_map/ppermute | solution.py:481
  19.6 18.1 %collective-permute-start.3 = (bf16[256,256]{1,0:T(8,128)(2,1)S(1)}, bf16[256,256]{1,0:T(8,128)(2,1)S(1)}, u32[]{:S(2)}, u32[]{:S(2)}) collective-permute-start(bf16[256,256]{1,0:T(8,128)(2,1)S(1)} %get-tuple-element.51), channel_id=1, source_target_pairs={{0,16},{1,21},{2,26},{3,31},{4,20},{5,17},{6,30},{7,27},{8,24},{9,... | collective-permute-start | bytes 393224 | tf_op jit(solution)/shard_map/ppermute | solution.py:481
  19.8 17.9 %collective-permute-start.6 = (s32[128]{0:T(128)S(1)}, s32[128]{0:T(128)S(1)}, u32[]{:S(2)}, u32[]{:S(2)}) collective-permute-start(s32[128]{0:T(128)S(1)} %get-tuple-element.52.refs_0_), channel_id=1, source_target_pairs={{0,3},{1,2},{2,1},{3,0},{4,7},{5,6},{6,5},{7,4},{8,11},{9,10},{10,... | collective-permute-start | bytes 1544 | tf_op jit(solution)/shard_map/ppermute | solution.py:472
  27.2 10.5 %collective-permute-start.5 = (s32[128]{0:T(128)S(1)}, s32[128]{0:T(128)S(1)}, u32[]{:S(2)}, u32[]{:S(2)}) collective-permute-start(s32[128]{0:T(128)S(1)} %get-tuple-element.52.refs_0_), channel_id=1, source_target_pairs={{0,2},{1,3},{2,0},{3,1},{4,6},{5,7},{6,4},{7,5},{8,10},{9,11},{10,... | collective-permute-start | bytes 1544 | tf_op jit(solution)/shard_map/ppermute | solution.py:472
  27.2 10.5 %collective-permute-start.4 = (s32[128]{0:T(128)S(1)}, s32[128]{0:T(128)S(1)}, u32[]{:S(2)}, u32[]{:S(2)}) collective-permute-start(s32[128]{0:T(128)S(1)} %get-tuple-element.52.refs_0_), channel_id=1, source_target_pairs={{0,1},{1,0},{2,3},{3,2},{4,5},{5,4},{6,7},{7,6},{8,9},{9,8},{10,11... | collective-permute-start | bytes 1544 | tf_op jit(solution)/shard_map/ppermute | solution.py:472
  37.8 6.7 %collective-permute-start.9 = (bf16[256,256]{1,0:T(8,128)(2,1)S(1)}, bf16[256,256]{1,0:T(8,128)(2,1)S(1)}, u32[]{:S(2)}, u32[]{:S(2)}) collective-permute-start(bf16[256,256]{1,0:T(8,128)(2,1)S(1)} %collective-permute-done.2.refs_0_), channel_id=1, source_target_pairs={{0,2},{1,3},{2,0},{3,1},{4,6},{5,7},{6,4},{7,5},{8,10},{9,11},{10,... | collective-permute-start | bytes 393224 | tf_op jit(solution)/shard_map/ppermute | solution.py:472
  40.2 6.8 %collective-permute-start.10 = (bf16[256,256]{1,0:T(8,128)(2,1)S(1)}, bf16[256,256]{1,0:T(8,128)(2,1)S(1)}, u32[]{:S(2)}, u32[]{:S(2)}) collective-permute-start(bf16[256,256]{1,0:T(8,128)(2,1)S(1)} %collective-permute-done.3.refs_1_), channel_id=1, source_target_pairs={{0,2},{1,3},{2,0},{3,1},{4,6},{5,7},{6,4},{7,5},{8,10},{9,11},{10,... | collective-permute-start | bytes 393224 | tf_op jit(solution)/shard_map/ppermute | solution.py:472
  40.2 6.7 %collective-permute-start.7 = (bf16[256,256]{1,0:T(8,128)(2,1)S(1)}, bf16[256,256]{1,0:T(8,128)(2,1)S(1)}, u32[]{:S(2)}, u32[]{:S(2)}) collective-permute-start(bf16[256,256]{1,0:T(8,128)(2,1)S(1)} %collective-permute-done.2.refs_0_), channel_id=1, source_target_pairs={{0,1},{1,0},{2,3},{3,2},{4,5},{5,4},{6,7},{7,6},{8,9},{9,8},{10,11... | collective-permute-start | bytes 393224 | tf_op jit(solution)/shard_map/ppermute | solution.py:472
  40.3 6.7 %collective-permute-start.8 = (bf16[256,256]{1,0:T(8,128)(2,1)S(1)}, bf16[256,256]{1,0:T(8,128)(2,1)S(1)}, u32[]{:S(2)}, u32[]{:S(2)}) collective-permute-start(bf16[256,256]{1,0:T(8,128)(2,1)S(1)} %collective-permute-done.3.refs_1_), channel_id=1, source_target_pairs={{0,1},{1,0},{2,3},{3,2},{4,5},{5,4},{6,7},{7,6},{8,9},{9,8},{10,11... | collective-permute-start | bytes 393224 | tf_op jit(solution)/shard_map/ppermute | solution.py:472
  51.9 8.4 %collective-permute-start.15 = (bf16[512,256]{1,0:T(8,128)(2,1)S(1)}, bf16[512,256]{1,0:T(8,128)(2,1)S(1)}, u32[]{:S(2)}, u32[]{:S(2)}) collective-permute-start(bf16[512,256]{1,0:T(8,128)(2,1)S(1)} %add_convert_fusion), channel_id=1, source_target_pairs={{0,2},{1,3},{2,0},{3,1},{4,6},{5,7},{6,4},{7,5},{8,10},{9,11},{10,... | collective-permute-start | bytes 786440 | tf_op jit(solution)/shard_map/ppermute | solution.py:472
  61.4 8.7 %collective-permute-start.16 = (bf16[256,512]{1,0:T(8,128)(2,1)S(1)}, bf16[256,512]{1,0:T(8,128)(2,1)S(1)}, u32[]{:S(2)}, u32[]{:S(2)}) collective-permute-start(bf16[256,512]{1,0:T(8,128)(2,1)S(1)} %get-tuple-element.62.even_ref), channel_id=1, source_target_pairs={{0,2},{1,3},{2,0},{3,1},{4,6},{5,7},{6,4},{7,5},{8,10},{9,11},{10,... | collective-permute-start | bytes 786440 | tf_op jit(solution)/shard_map/ppermute | solution.py:472
  81.9 7.9 %collective-permute-start.24 = (bf16[64,2048]{1,0:T(8,128)(2,1)S(1)}, bf16[64,2048]{1,0:T(8,128)(2,1)S(1)}, u32[]{:S(2)}, u32[]{:S(2)}) collective-permute-start(bf16[64,2048]{1,0:T(8,128)(2,1)S(1)} %get-tuple-element.75), channel_id=1, source_target_pairs={{0,2},{1,3},{2,0},{3,1},{4,6},{5,7},{6,4},{7,5},{8,10},{9,11},{10,... | collective-permute-start | bytes 786440 | tf_op jit(solution)/shard_map/ppermute | solution.py:472
  90.0 6.5 %collective-permute-start.26 = (bf16[64,256]{1,0:T(8,128)(2,1)S(1)}, bf16[64,256]{1,0:T(8,128)(2,1)S(1)}, u32[]{:S(2)}, u32[]{:S(2)}) collective-permute-start(bf16[64,256]{1,0:T(8,128)(2,1)S(1)} %get-tuple-element.78), channel_id=1, source_target_pairs={{0,4},{4,0},{8,12},{12,8},{16,20},{20,16},{24,28},{28,24},{1,5},{5... | collective-permute-start | bytes 98312 | tf_op jit(solution)/shard_map/ppermute | solution.py:475
  91.1 8.0 %collective-permute-start.27 = (bf16[64,256]{1,0:T(8,128)(2,1)S(1)}, bf16[64,256]{1,0:T(8,128)(2,1)S(1)}, u32[]{:S(2)}, u32[]{:S(2)}) collective-permute-start(bf16[64,256]{1,0:T(8,128)(2,1)S(1)} %get-tuple-element.79), channel_id=1, source_target_pairs={{0,8},{4,12},{8,0},{12,4},{16,24},{20,28},{24,16},{28,20},{1,9},{5... | collective-permute-start | bytes 98312 | tf_op jit(solution)/shard_map/ppermute | solution.py:475
  91.2 9.3 %collective-permute-start.28 = (bf16[64,256]{1,0:T(8,128)(2,1)S(1)}, bf16[64,256]{1,0:T(8,128)(2,1)S(1)}, u32[]{:S(2)}, u32[]{:S(2)}) collective-permute-start(bf16[64,256]{1,0:T(8,128)(2,1)S(1)} %get-tuple-element.80), channel_id=1, source_target_pairs={{0,12},{4,8},{8,4},{12,0},{16,28},{20,24},{24,20},{28,16},{1,13},{... | collective-permute-start | bytes 98312 | tf_op jit(solution)/shard_map/ppermute | solution.py:475
  93.6 13.6 %collective-permute-start.33 = (f32[64,256]{1,0:T(8,128)S(1)}, f32[64,256]{1,0:T(8,128)S(1)}, u32[]{:S(2)}, u32[]{:S(2)}) collective-permute-start(f32[64,256]{1,0:T(8,128)S(1)} %get-tuple-element.85.refs_12_), channel_id=1, source_target_pairs={{0,16},{4,20},{8,24},{12,28},{16,0},{20,4},{24,8},{28,12},{1,17},{... | collective-permute-start | bytes 196616 | tf_op jit(solution)/shard_map/ppermute | solution.py:475
  95.2 7.7 %collective-permute-start.29 = (bf16[64,256]{1,0:T(8,128)(2,1)S(1)}, bf16[64,256]{1,0:T(8,128)(2,1)S(1)}, u32[]{:S(2)}, u32[]{:S(2)}) collective-permute-start(bf16[64,256]{1,0:T(8,128)(2,1)S(1)} %get-tuple-element.81), channel_id=1, source_target_pairs={{0,16},{4,20},{8,24},{12,28},{16,0},{20,4},{24,8},{28,12},{1,17},{... | collective-permute-start | bytes 98312 | tf_op jit(solution)/shard_map/ppermute | solution.py:475
  96.5 7.0 %collective-permute-start.30 = (bf16[64,256]{1,0:T(8,128)(2,1)S(1)}, bf16[64,256]{1,0:T(8,128)(2,1)S(1)}, u32[]{:S(2)}, u32[]{:S(2)}) collective-permute-start(bf16[64,256]{1,0:T(8,128)(2,1)S(1)} %get-tuple-element.82), channel_id=1, source_target_pairs={{0,20},{4,16},{8,28},{12,24},{16,4},{20,0},{24,12},{28,8},{1,21},{... | collective-permute-start | bytes 98312 | tf_op jit(solution)/shard_map/ppermute | solution.py:475
  100.6 6.6 %collective-permute-start.32 = (bf16[64,256]{1,0:T(8,128)(2,1)S(1)}, bf16[64,256]{1,0:T(8,128)(2,1)S(1)}, u32[]{:S(2)}, u32[]{:S(2)}) collective-permute-start(bf16[64,256]{1,0:T(8,128)(2,1)S(1)} %get-tuple-element.84), channel_id=1, source_target_pairs={{0,28},{4,24},{8,20},{12,16},{16,12},{20,8},{24,4},{28,0},{1,29},{... | collective-permute-start | bytes 98312 | tf_op jit(solution)/shard_map/ppermute | solution.py:475
  108.0 8.0 %collective-permute-start.34 = (bf16[64,512]{1,0:T(8,128)(2,1)S(1)}, bf16[64,512]{1,0:T(8,128)(2,1)S(1)}, u32[]{:S(2)}, u32[]{:S(2)}) collective-permute-start(bf16[64,512]{1,0:T(8,128)(2,1)S(1)} %get-tuple-element.87), channel_id=1, source_target_pairs={{0,1},{1,0},{2,3},{3,2},{4,5},{5,4},{6,7},{7,6},{8,9},{9,8},{10,11... | collective-permute-start | bytes 196616 | tf_op jit(solution)/shard_map/ppermute | solution.py:472
  109.9 6.1 %collective-permute-start.35 = (bf16[64,512]{1,0:T(8,128)(2,1)S(1)}, bf16[64,512]{1,0:T(8,128)(2,1)S(1)}, u32[]{:S(2)}, u32[]{:S(2)}) collective-permute-start(bf16[64,512]{1,0:T(8,128)(2,1)S(1)} %get-tuple-element.88), channel_id=1, source_target_pairs={{0,2},{1,3},{2,0},{3,1},{4,6},{5,7},{6,4},{7,5},{8,10},{9,11},{10,... | collective-permute-start | bytes 196616 | tf_op jit(solution)/shard_map/ppermute | solution.py:472
  110.1 5.8 %collective-permute-start.36 = (bf16[64,512]{1,0:T(8,128)(2,1)S(1)}, bf16[64,512]{1,0:T(8,128)(2,1)S(1)}, u32[]{:S(2)}, u32[]{:S(2)}) collective-permute-start(bf16[64,512]{1,0:T(8,128)(2,1)S(1)} %get-tuple-element.89), channel_id=1, source_target_pairs={{0,3},{1,2},{2,1},{3,0},{4,7},{5,6},{6,5},{7,4},{8,11},{9,10},{10,... | collective-permute-start | bytes 196616 | tf_op jit(solution)/shard_map/ppermute | solution.py:472
  (21 other events, 136.2 us)

commit v3 on v1

v3 whole, which is shorter than its diff:
```python
import functools

import jax
import jax.numpy as jnp
from jax import lax
from jax.experimental import pallas as pl
from jax.experimental.pallas import tpu as pltpu
from jax.sharding import PartitionSpec as P

BF16 = jnp.bfloat16
F32 = jnp.float32
COL_CHUNK = 16
ROW_TILE = 256
COL_TILE = 512
WHOLE = pl.BlockSpec(memory_space=pltpu.VMEM)
SMEM = pl.BlockSpec(memory_space=pltpu.SMEM)
ANY = pl.BlockSpec(memory_space=pl.ANY)


def params(*parts):
    return pltpu.CompilerParams(vmem_limit_bytes=min(sum(parts) + (6 << 20), 62 << 20))


def shape(dims, dtype):
    return jax.ShapeDtypeStruct(tuple(dims), dtype)


def dot(a, b, dims=((1,), (0,))):
    return lax.dot_general(a, b, (dims, ((), ())), preferred_element_type=F32)


def xor_perm(count, offset):
    return [(i, i ^ offset) for i in range(count)]


def densify_body(
    rows_ref, fetch_ref, count_ref, blocks_ref, out_ref, head_ref, next_ref, *, n_rep, n_hi, per_list, quarter
):
    chunk, row_cell = pl.program_id(0), pl.program_id(1)
    slots, blk = blocks_ref.shape[0], blocks_ref.shape[1]
    all_cols = n_rep * n_hi * per_list

    @pl.when((chunk == 0) & (row_cell == 0))
    def _():
        r, q = lax.axis_index("row"), lax.axis_index("rep")

        @pl.loop(0, n_rep * quarter * all_cols, unroll=16)
        def _(cell):
            head_ref[cell] = -1

        def link(slot):
            row, fetch = rows_ref[slot], fetch_ref[slot]
            j = lax.div(row, quarter) ^ q
            k = lax.div(fetch, per_list) ^ r
            piece = (lax.rem(k, n_rep) ^ q) * n_hi + lax.div(k, n_rep)
            col = piece * per_list + lax.rem(fetch, per_list)
            cell = ((n_rep - 1 - j) * quarter + lax.rem(row, quarter)) * all_cols + col
            next_ref[slot] = head_ref[cell]
            head_ref[cell] = slot

        pl.loop(0, count_ref[0])(link)

    for col in range(COL_CHUNK):
        first = head_ref[row_cell * all_cols + chunk * COL_CHUNK + col]
        place = (slice(None), slice(col * blk, (col + 1) * blk))

        @pl.when(first < 0)
        def _():
            out_ref[place] = jnp.zeros((blk, blk), BF16)

        @pl.when(first >= 0)
        def _():
            second = next_ref[first]

            @pl.when(second < 0)
            def _():
                out_ref[place] = blocks_ref[first]

            @pl.when(second >= 0)
            def _():
                def more(carry):
                    slot, total = carry
                    return next_ref[slot], total + blocks_ref[slot].astype(F32)

                start = (second, blocks_ref[first].astype(F32))
                _, total = lax.while_loop(lambda carry: carry[0] >= 0, more, start)
                out_ref[place] = total.astype(BF16)


def densify(block_rows, block_fetch, block_count, blocks, n_row, n_rep, per_list, row_blocks):
    slots, blk, _ = blocks.shape
    cols = n_row * per_list * blk
    width = COL_CHUNK * blk
    body = functools.partial(
        densify_body,
        n_rep=n_rep,
        n_hi=n_row // n_rep,
        per_list=per_list,
        quarter=row_blocks // n_rep,
    )
    return pl.pallas_call(
        body,
        out_shape=shape((row_blocks * blk, cols), BF16),
        grid_spec=pltpu.PrefetchScalarGridSpec(
            num_scalar_prefetch=3,
            grid=(cols // width, row_blocks),
            in_specs=[WHOLE],
            out_specs=pl.BlockSpec((blk, width), lambda c, i, *_: (i, c)),
            scratch_shapes=[
                pltpu.SMEM((row_blocks * n_row * per_list,), jnp.int32),
                pltpu.SMEM((slots,), jnp.int32),
            ],
        ),
        compiler_params=params(12 << 20),
        cost_estimate=pl.CostEstimate(
            flops=slots * blk * blk, bytes_accessed=blocks.size * 2 + 2 * cols * row_blocks * blk, transcendentals=0
        ),
        name="densify",
    )(block_rows, block_fetch, block_count, blocks)


def pack_body(*refs, n_hi, per_list, blk):
    lists = refs[:n_hi]
    features = refs[n_hi]
    outs = refs[n_hi + 1 : 2 * n_hi + 1]
    own_list, sems = refs[2 * n_hi + 1 :]
    r = lax.axis_index("row")
    copies = []
    for hi in range(n_hi):
        for c in range(per_list):
            b = lists[hi][0, r, c]
            own_list[hi * per_list + c] = b
            copy = pltpu.make_async_copy(
                features.at[pl.ds(pl.multiple_of(b * blk, blk), blk)],
                outs[hi].at[pl.ds(c * blk, blk)],
                sems.at[hi * per_list + c],
            )
            copy.start()
            copies.append(copy)
    for copy in copies:
        copy.wait()


def pack(lists, features, per_list, blk):
    n_hi = len(lists)
    return pl.pallas_call(
        functools.partial(pack_body, n_hi=n_hi, per_list=per_list, blk=blk),
        out_shape=[shape((per_list * blk, features.shape[1]), BF16)] * n_hi + [shape((128,), jnp.int32)],
        in_specs=[SMEM] * n_hi + [pl.BlockSpec(memory_space=pltpu.HBM)],
        out_specs=[ANY] * n_hi + [SMEM],
        scratch_shapes=[pltpu.SemaphoreType.DMA((n_hi * per_list,))],
        compiler_params=params(0),
        name="pack",
    )(*lists, features)


def forward_body(*refs, n_pieces):
    pieces = refs[:n_pieces]
    adj_ref, send_ref, keep_ref = refs[n_pieces:]
    i = pl.program_id(0)
    depth = pieces[0].shape[0]
    total = dot(adj_ref[:, :depth], pieces[0][...])
    for n in range(1, n_pieces):
        total += dot(adj_ref[:, n * depth : (n + 1) * depth], pieces[n][...])

    half = pl.num_programs(0) // 2

    @pl.when(i < half)
    def _():
        send_ref[...] = total.astype(BF16)

    @pl.when(i >= half)
    def _():
        keep_ref[...] = total


def forward(pieces, adj, half_index):
    rows, cols = adj.shape[0] // 2, adj.shape[1]
    features = pieces[0].shape[1]
    tiles = rows // ROW_TILE
    half = tiles // 2
    return pl.pallas_call(
        functools.partial(forward_body, n_pieces=len(pieces)),
        grid=(tiles,),
        out_shape=[shape((rows // 2, features), BF16), shape((rows // 2, features), F32)],
        in_specs=[pl.BlockSpec(x.shape, lambda i: (0, 0)) for x in pieces]
        + [pl.BlockSpec((ROW_TILE, cols), lambda i: (i + half_index * tiles, 0))],
        out_specs=[
            pl.BlockSpec((ROW_TILE, features), lambda i: (jnp.minimum(i, half - 1), 0)),
            pl.BlockSpec((ROW_TILE, features), lambda i: (jnp.maximum(i - half, 0), 0)),
        ],
        compiler_params=params(ROW_TILE * cols * 4, cols * features * 4),
        cost_estimate=pl.CostEstimate(
            flops=2 * rows * cols * features, bytes_accessed=adj.size + cols * features * 2, transcendentals=0
        ),
        name="forward",
    )(*pieces, adj)


def middle_body(
    keep_ref, near_ref, far_ref, weight_ref, cot_ref, out_ref, grad_ref, wsend_ref, wkeep_ref, acc_ref, *, factor
):
    q = lax.axis_index("rep")
    hidden = (keep_ref[...] + near_ref[...].astype(F32) + far_ref[...].astype(F32)).astype(BF16)
    weight = weight_ref[...]
    pre_act = dot(hidden, weight)
    sig = jax.nn.sigmoid(pre_act)
    out_ref[...] = (pre_act * sig).astype(BF16)
    pre_grad = (cot_ref[...].astype(F32) * (sig * (1.0 + pre_act * (1.0 - sig)))).astype(BF16)
    grad_ref[...] = dot(weight, pre_grad, ((1,), (1,))).astype(BF16)
    acc_ref[...] = dot(hidden, pre_grad, ((0,), (0,))) * factor
    part = wkeep_ref.shape[0] // 2
    for j in range(4):
        out = wsend_ref if j & 1 else wkeep_ref
        at = j // 2 * part
        out[at : at + part] = acc_ref[pl.ds(pl.multiple_of((q ^ j) * part, part), part), :]


def middle(keep, near, far, weight, cot, factor):
    rows, features = keep.shape
    return pl.pallas_call(
        functools.partial(middle_body, factor=factor),
        out_shape=[
            shape((rows, features), BF16),
            shape((features, rows), BF16),
            shape((features // 2, features), F32),
            shape((features // 2, features), F32),
        ],
        in_specs=[WHOLE] * 5,
        out_specs=[WHOLE] * 4,
        scratch_shapes=[pltpu.VMEM((features, features), F32)],
        compiler_params=params(12 << 20),
        cost_estimate=pl.CostEstimate(
            flops=6 * rows * features * features, bytes_accessed=rows * features * 14, transcendentals=rows * features
        ),
        name="middle",
    )(keep, near, far, weight, cot)


def back_first_body(odd_ref, even_ref, adj_ref, wkeep_ref, got_ref, out_ref, wsend_out, wkeep_out):
    rows = odd_ref.shape[1]
    part = wsend_out.shape[0]

    @pl.when(pl.program_id(0) == 0)
    def _():
        mine = lax.rem(lax.axis_index("row"), 2) ^ lax.div(lax.axis_index("rep"), 2)
        for out, at in ((wkeep_out, mine), (wsend_out, 1 - mine)):
            rows_here = pl.ds(pl.multiple_of(at * part, part), part)
            out[...] = wkeep_ref[rows_here, :] + got_ref[rows_here, :]

    out_ref[...] = dot(odd_ref[...], adj_ref[:rows]) + dot(even_ref[...], adj_ref[rows:])


def back_first(odd, even, adj, wkeep, got):
    rows, cols = adj.shape[0] // 2, adj.shape[1]
    features = odd.shape[0]
    return pl.pallas_call(
        back_first_body,
        grid=(cols // COL_TILE,),
        out_shape=[shape((features, cols), F32)] + [shape((wkeep.shape[0] // 2, features), F32)] * 2,
        in_specs=[
            pl.BlockSpec(odd.shape, lambda i: (0, 0)),
            pl.BlockSpec(even.shape, lambda i: (0, 0)),
            pl.BlockSpec((rows, COL_TILE), lambda i: (1, i)),
            pl.BlockSpec(wkeep.shape, lambda i: (0, 0)),
            pl.BlockSpec(wkeep.shape, lambda i: (0, 0)),
        ],
        out_specs=[pl.BlockSpec((features, COL_TILE), lambda i: (0, i))]
        + [pl.BlockSpec((wkeep.shape[0] // 2, features), lambda i: (0, 0))] * 2,
        compiler_params=params(4 << 20),
        cost_estimate=pl.CostEstimate(
            flops=2 * rows * cols * features, bytes_accessed=adj.size + cols * features * 4, transcendentals=0
        ),
        name="back_first",
    )(odd, even, adj, wkeep, got)


def back_second_body(odd_ref, even_ref, adj_ref, first_ref, o3_ref, o2_ref, o1_ref, o0_ref, acc_ref):
    q = lax.axis_index("rep")
    rows = odd_ref.shape[1]
    acc_ref[...] = first_ref[...] + dot(odd_ref[...], adj_ref[:rows]) + dot(even_ref[...], adj_ref[rows:])
    part = o0_ref.shape[0]

    def piece(j):
        return acc_ref[pl.ds(pl.multiple_of((q ^ j) * part, part), part), :]

    o3_ref[...] = piece(3).astype(BF16)
    o2_ref[...] = piece(2)
    o1_ref[...] = piece(1).astype(BF16)
    o0_ref[...] = piece(0)


def back_second(odd, even, adj, first, n_rep):
    rows, cols = adj.shape[0] // 2, adj.shape[1]
    features = odd.shape[0]
    part = features // n_rep
    per_piece = cols // n_rep // COL_TILE
    keep_spec = pl.BlockSpec((part, COL_TILE), lambda i: (0, i))
    send_spec = pl.BlockSpec(
        (part, COL_TILE), lambda i: (0, (lax.div(i, per_piece) ^ 1) * per_piece + lax.rem(i, per_piece))
    )
    return pl.pallas_call(
        back_second_body,
        grid=(cols // COL_TILE,),
        out_shape=[shape((part, cols), dtype) for dtype in (BF16, F32, BF16, F32)],
        in_specs=[
            pl.BlockSpec(odd.shape, lambda i: (0, 0)),
            pl.BlockSpec(even.shape, lambda i: (0, 0)),
            pl.BlockSpec((rows, COL_TILE), lambda i: (0, i)),
            pl.BlockSpec((features, COL_TILE), lambda i: (0, i)),
        ],
        out_specs=[send_spec, keep_spec, send_spec, keep_spec],
        scratch_shapes=[pltpu.VMEM((features, COL_TILE), F32)],
        compiler_params=params(6 << 20),
        cost_estimate=pl.CostEstimate(
            flops=2 * rows * cols * features, bytes_accessed=adj.size + cols * features * 7, transcendentals=0
        ),
        name="back_second",
    )(odd, even, adj, first)


def across_body(keep_ref, near_ref, w_ref, got_ref, *outs, n_rep, n_hi):
    *outs, w_out = outs
    width = keep_ref.shape[1] // (n_rep * n_hi)
    for half, out in enumerate(outs):
        for piece in range(n_rep * n_hi // 2):
            j, hi = piece // (n_hi // 2), piece % (n_hi // 2) + half * n_hi // 2
            cols = slice((j * n_hi + hi) * width, (j * n_hi + hi + 1) * width)
            total = keep_ref[:, cols] + near_ref[:, cols].astype(F32)
            out[:, piece * width : (piece + 1) * width] = total.astype(BF16)
    w_out[...] = w_ref[...] + got_ref[...]


def across_sum(keep, near, w, got, n_rep, n_hi):
    part, cols = keep.shape
    return pl.pallas_call(
        functools.partial(across_body, n_rep=n_rep, n_hi=n_hi),
        out_shape=[shape((part, cols // 2), BF16)] * 2 + [shape(w.shape, F32)],
        in_specs=[WHOLE] * 4,
        out_specs=[WHOLE] * 3,
        compiler_params=params(keep.size * 8),
        cost_estimate=pl.CostEstimate(flops=keep.size, bytes_accessed=keep.size * 8, transcendentals=0),
        name="across_sum",
    )(keep, near, w, got)


def split_body(own_ref, near_ref, far_ref, *outs, n_rep, n_hi, half):
    q = lax.axis_index("rep")
    width = outs[0].shape[1]
    for i, out in enumerate(outs):
        low, hi = i % n_rep, i // n_rep
        j = low ^ q
        cols = pl.ds(pl.multiple_of((j * n_hi + hi + half * n_hi // 2) * width, width), width)
        far_cols = pl.ds(pl.multiple_of(((j ^ 2) * (n_hi // 2) + hi) * width, width), width)
        total = own_ref[:, cols] + near_ref[:, cols].astype(F32) + far_ref[:, far_cols].astype(F32)
        out[...] = total.astype(out.dtype)


def split(own, near, far, half, n_row, n_rep):
    part, cols = own.shape
    width = cols // n_row
    count = n_row // 2
    return pl.pallas_call(
        functools.partial(split_body, n_rep=n_rep, n_hi=n_row // n_rep, half=half),
        out_shape=[shape((part, width), F32 if half * count + i == 0 else BF16) for i in range(count)],
        in_specs=[WHOLE] * 3,
        out_specs=[WHOLE] * count,
        compiler_params=params(own.size * 10),
        cost_estimate=pl.CostEstimate(flops=own.size, bytes_accessed=own.size * 5, transcendentals=0),
        name=f"split_{half}",
    )(own, near, far)


def collect_body(*refs, n_row, n_rep, per_list, quarter, blk):
    lists = refs[:n_rep]
    messages = refs[n_rep : n_rep + n_row]
    outs = refs[n_rep + n_row : -1]
    acc_ref = refs[-1]
    q = lax.axis_index("rep")
    acc_ref[...] = jnp.zeros(acc_ref.shape, F32)
    for k in range(n_row):
        j = (k % n_rep) ^ q
        for c in range(per_list):
            at = k // n_rep * per_list + c
            b = lists[0][at]
            for other in range(1, n_rep):
                b = jnp.where(j == other, lists[other][at], b)
            cell = (lax.div(b, quarter) ^ q) * quarter + lax.rem(b, quarter)
            cols = pl.ds(pl.multiple_of(cell * blk, blk), blk)
            acc_ref[:, cols] += messages[k][:, c * blk : (c + 1) * blk].astype(F32)
    width = outs[0].shape[1]
    for j, out in enumerate(outs):
        out[...] = acc_ref[:, j * width : (j + 1) * width].astype(out.dtype)


def collect(lists, messages, per_list, row_blocks, blk):
    n_rep = len(lists)
    n_row = len(messages)
    part = messages[0].shape[0]
    quarter = row_blocks // n_rep
    body = functools.partial(
        collect_body, n_row=n_row, n_rep=n_rep, per_list=per_list, quarter=quarter, blk=blk
    )
    return pl.pallas_call(
        body,
        out_shape=[shape((part, quarter * blk), F32 if j == 0 else BF16) for j in range(n_rep)],
        in_specs=[SMEM] * n_rep + [WHOLE] * n_row,
        out_specs=[WHOLE] * n_rep,
        scratch_shapes=[pltpu.VMEM((part, row_blocks * blk), F32)],
        compiler_params=params(4 << 20),
        cost_estimate=pl.CostEstimate(
            flops=part * row_blocks * blk, bytes_accessed=part * row_blocks * blk * 5, transcendentals=0
        ),
        name="collect",
    )(*lists, *messages)


def finish_body(*refs, n_rep):
    grads = refs[:n_rep]
    weights = refs[n_rep : 2 * n_rep]
    node_ref, weight_ref, acc_ref = refs[2 * n_rep :]
    q = lax.axis_index("rep")
    part = grads[0].shape[0]
    first = lax.rem(q, 2) + 2 * lax.rem(lax.axis_index("row"), 2)
    for j in range(n_rep):
        acc_ref[pl.ds(pl.multiple_of((q ^ j) * part, part), part), :] = grads[j][...].astype(F32)
        weight_ref[pl.ds(pl.multiple_of((first ^ j) * part, part), part), :] = weights[j][...]
    node_ref[...] = acc_ref[...].T


def finish(grads, weights):
    n_rep = len(grads)
    part, rows = grads[0].shape
    features = weights[0].shape[1]
    return pl.pallas_call(
        functools.partial(finish_body, n_rep=n_rep),
        out_shape=[shape((rows, part * n_rep), F32), shape((features, features), F32)],
        in_specs=[WHOLE] * (2 * n_rep),
        out_specs=[WHOLE] * 2,
        scratch_shapes=[pltpu.VMEM((part * n_rep, rows), F32)],
        compiler_params=params(6 << 20),
        cost_estimate=pl.CostEstimate(flops=0, bytes_accessed=rows * part * n_rep * 8, transcendentals=0),
        name="finish",
    )(*grads, *weights)


def local(
    node_features, weight, out_grad, blocks, block_rows, block_fetch, fetch_lists, block_count
):
    n_row = lax.axis_size("row")
    n_rep = lax.axis_size("rep")
    n_hi = n_row // n_rep
    band_rows, features = node_features.shape
    blk = blocks.shape[1]
    row_blocks = band_rows // blk
    per_list = fetch_lists.shape[2]

    def to_rep(x, j):
        return lax.ppermute(x, "rep", xor_perm(n_rep, j))

    def to_row(x, k):
        return lax.ppermute(x, "row", xor_perm(n_row, k))

    def spread(x, hi):
        perm = [
            (r * n_rep + q, (r ^ (hi * n_rep + q)) * n_rep + q) for r in range(n_row) for q in range(n_rep)
        ]
        return lax.ppermute(x, ("row", "rep"), perm)

    def after(x, *done):
        return lax.optimization_barrier((x, *done))[0]

    wanted = [spread(fetch_lists, hi) for hi in range(n_hi)]
    *outgoing, own_list = pack(wanted, node_features, per_list, blk)
    own = [spread(x, hi) for hi, x in enumerate(outgoing)]
    adj = densify(
        block_rows, block_fetch, after(block_count, outgoing), blocks, n_row, n_rep, per_list, row_blocks
    )
    own[0] = after(own[0], adj)
    far = [to_rep(x, 2) for x in own]
    near = [to_rep(x, 1) for x in own]
    diag = [to_rep(x, 1) for x in far]
    pieces = own + near + far + diag

    send3, keep2 = forward(pieces, adj, 0)
    across = (keep2 + to_rep(send3, 1).astype(F32)).astype(BF16)
    arrived = to_rep(across, 2)
    send1, keep0 = forward(pieces, after(adj, across), 1)
    own_list = after(own_list, keep0)
    lists = [own_list] + [to_rep(own_list, j) for j in range(1, n_rep)]
    arrived = after(arrived, keep0, lists)
    factor = float(n_row * band_rows) ** (-0.5)
    output, grad0, wsend, wkeep = middle(keep0, to_rep(send1, 1), arrived, weight, out_grad, factor)

    grad2 = to_rep(grad0, 2)
    grad1 = to_rep(grad0, 1)
    first, wsend, wkeep = back_first(grad1, grad0, adj, wkeep, to_rep(wsend, 1))
    grad2 = after(grad2, first)
    grad3 = to_rep(grad2, 1)
    o3, o2, o1, o0 = back_second(grad3, grad2, adj, first, n_rep)
    to_low, to_high, w = across_sum(o2, to_rep(o3, 1), wkeep, to_row(wsend, 1), n_rep, n_hi)
    o1 = to_rep(o1, 1)
    from_high = to_rep(to_high, 2)
    from_low = to_rep(to_low, 2)
    w = w + to_row(w, 2)
    got = to_row(w, 4)
    high = split(o0, o1, from_high, 1, n_row, n_rep)
    half = n_row // 2
    back_high = [to_row(x, half + i) for i, x in enumerate(high)]
    w = w + after(got, high)
    step = 8
    while step < n_row:
        w = w + to_row(w, step)
        step *= 2
    low = split(o0, o1, after(from_low, back_high[:-1]), 0, n_row, n_rep)
    returned = [low[0]] + [to_row(low[i], i) for i in range(1, half)] + back_high
    w = w + to_rep(w, 2)
    grads = collect(lists, after(returned, w), per_list, row_blocks, blk)
    other = to_row(w, 1)
    weights = [w, to_rep(w, 1), other, to_rep(other, 1)]
    node_grad, weight_grad = finish(
        [grads[0]] + [to_rep(grads[j], j) for j in range(1, n_rep)], weights
    )
    return (output, weight_grad, node_grad)


def solution(mesh):
    in_specs = (
        P("row", None),
        P(),
        P(("row", "rep"), None),
        P(("row", "rep"), None, None),
        P(("row", "rep")),
        P(("row", "rep")),
        P(("row", "rep"), None, None),
        P(("row", "rep")),
    )
    out_specs = (P(("row", "rep"), None), P(), P(("row", "rep"), None))
    return jax.shard_map(local, mesh=mesh, in_specs=in_specs, out_specs=out_specs, check_vma=False)
```

time: 136 us -> 108 us (0.79)
  blocking collectives: 19.4 us -> 0 us
  starting transfers between devices: 52.9 us -> 43.7 us
  waiting for transfers between devices: 27.8 us -> 36.4 us
  Pallas kernels: 27.7 us -> 19.6 us
    all_gather x1 -> x0, blocking collectives: 19.4 us -> none  [local(): all_lists = lax.all_gather(fetch_lists[0], 'row', axis=0, tiled=False)]
    ppermute x10 -> x11, waiting for transfers between devices: 5.39 us -> 15.6 us  [to_row(): return lax.ppermute(x, 'row', xor_perm(n_row, k))]
    pallas_call x6, Pallas kernels: 20.2 us -> 11.5 us  [the longest x1 6.24 us: densify(): pl.pallas_call(body, out_shape=shape((row_blocks * blk, cols), BF16), gri...]
    ppermute x23 -> x26, starting transfers between devices: 26 us -> 21 us  [to_rep(): return lax.ppermute(x, 'rep', xor_perm(n_rep, j))]
    ppermute x10 -> x11, starting transfers between devices: 18.5 us -> 14.4 us  [to_row(): return lax.ppermute(x, 'row', xor_perm(n_row, k))]
    ppermute x23 -> x26, waiting for transfers between devices: 20.8 us -> 19.9 us  [to_rep(): return lax.ppermute(x, 'rep', xor_perm(n_rep, j))]
    unnamed x15 -> x13, local copies, waits for them, and re-layouts: 6.14 us -> 6.13 us
  transfers between devices with their start and end apart: 37 -> 41, of which waited for: 11 -> 20; matrix products, arithmetic and copies ran while one was open for 0% -> 0% of each run, Pallas kernels for 17% -> 11%
where the time goes in v3:
time: 108 us
  starting transfers between devices  43.7 us (40%)
  waiting for transfers between devices  36.4 us (34%)
  Pallas kernels  19.6 us (18%)
  local copies, waits for them, and re-layouts  6.13 us (6%)
  between operations  1.52 us (1%)
    ppermute x26, starting transfers between devices, to_rep(): return lax.ppermute(x, 'rep', xor_perm(n_rep, j))  21 us
    ppermute x26, waiting for transfers between devices, to_rep(): return lax.ppermute(x, 'rep', xor_perm(n_rep, j))  19.9 us
    ppermute x11, waiting for transfers between devices, to_row(): return lax.ppermute(x, 'row', xor_perm(n_row, k))  15.6 us
    ppermute x11, starting transfers between devices, to_row(): return lax.ppermute(x, 'row', xor_perm(n_row, k))  14.4 us
    ppermute x4, starting transfers between devices, spread(): return lax.ppermute(x, ('row', 'rep'), perm)  8.34 us
    pallas_call x1, Pallas kernels, densify(): pl.pallas_call(body, out_shape=shape((row_blocks * blk, cols), BF16), gri...  6.24 us
    unnamed x13, local copies, waits for them, and re-layouts  6.13 us
    pallas_call x2, Pallas kernels, forward(): pl.pallas_call(functools.partial(forward_body, n_pieces=len(pieces)), gri...  3.82 us
  transfers between devices with their start and end apart: 41, of which 20 were waited for; matrix products, arithmetic and copies ran while one was open for 0% of the time, Pallas kernels for 11%

profile of v3, /device:TPU:0, one launch (start us, length us, event | category | flops | bytes accessed | tf_op | source)
XLA Modules:
  0.0 107.5 jit_solution(16637584417127079820)
XLA Ops:
  1.4 4.0 %collective-permute-start.1 = (s32[1,8,2]{2,1,0:T(8,128)S(1)}, s32[1,8,2]{2,1,0:T(8,128)S(1)}, u32[]{:S(2)}, u32[]{:S(2)}) collective-permute-start(s32[1,8,2]{2,1,0:T(8,128)S(1)} %copy.11), channel_id=1, source_target_pairs={{0,16},{1,21},{2,26},{3,31},{4,20},{5,17},{6,30},{7,27},{8,24},{9,... | collective-permute-start | bytes 200 | tf_op jit(solution)/shard_map/ppermute | solution.py:468
  10.6 3.0 %collective-permute-start.3 = (bf16[256,256]{1,0:T(8,128)(2,1)S(1)}, bf16[256,256]{1,0:T(8,128)(2,1)S(1)}, u32[]{:S(2)}, u32[]{:S(2)}) collective-permute-start(bf16[256,256]{1,0:T(8,128)(2,1)S(1)} %get-tuple-element.55), channel_id=1, source_target_pairs={{0,16},{1,21},{2,26},{3,31},{4,20},{5,17},{6,30},{7,27},{8,24},{9,... | collective-permute-start | bytes 393224 | tf_op jit(solution)/shard_map/ppermute | solution.py:468
  14.2 2.8 %copy-done = bf16[192,128,128]{2,1,0:T(8,128)(2,1)S(1)} copy-done((bf16[192,128,128]{2,1,0:T(8,128)(2,1)S(1)}, bf16[192,128,128]{2,1,0:T(8,128)(2,1)}, u32[]{:S(2)}) %copy-start) | copy-done | bytes 6291480
  18.4 6.2 %densify.1.refs_8_.adj_ref = bf16[2048,2048]{1,0:T(8,128)(2,1)S(1)} custom-call(s32[192]{0:T(256)S(1)} %copy-done.4, s32[192]{0:T(256)S(1)} %copy-done.5, s32[1]{0:T(128)S(6)} %copy.13.count_ref, bf16[192,128,128]{2,1,0:T(8,128)(2,1)S(1)} %copy-done), custom_call_target="tpu_custom_call" | custom-call | flops 3145728 | bytes 14680064 | tf_op jit(solution)/shard_map/densify/pallas_call | solution.py:101
  24.6 8.9 %collective-permute-start.7 = (bf16[256,256]{1,0:T(8,128)(2,1)S(1)}, bf16[256,256]{1,0:T(8,128)(2,1)S(1)}, u32[]{:S(2)}, u32[]{:S(2)}) collective-permute-start(bf16[256,256]{1,0:T(8,128)(2,1)S(1)} %collective-permute-done.3.refs_1_), channel_id=1, source_target_pairs={{0,2},{1,3},{2,0},{3,1},{4,6},{5,7},{6,4},{7,5},{8,10},{9,11},{10,... | collective-permute-start | bytes 393224 | tf_op jit(solution)/shard_map/ppermute | solution.py:459
  34.2 3.7 %collective-permute-done.7.refs_5_ = bf16[256,256]{1,0:T(8,128)(2,1)S(1)} collective-permute-done((bf16[256,256]{1,0:T(8,128)(2,1)S(1)}, bf16[256,256]{1,0:T(8,128)(2,1)S(1)}, u32[]{:S(2)}, u32[]{:S(2)}) %collective-permute-start.7) | collective-permute-done | bytes 131104 | tf_op jit(solution)/shard_map/ppermute | solution.py:459
  40.7 1.9 %forward.2 = (bf16[512,256]{1,0:T(8,128)(2,1)S(1)}, f32[512,256]{1,0:T(8,128)S(1)}) custom-call(bf16[256,256]{1,0:T(8,128)(2,1)S(1)} %collective-permute-done.2.refs_0_, bf16[256,256]{1,0:T(8,128)(2,1)S(1)} %collective-permute-done.3.refs_1_, bf16[256,256]{1,0:T(8,128)(2,1)S(1)} %collective-permute-done.4.refs_2_, ...), custom_call_target="tpu_custom_call" | custom-call | flops 1073741824 | bytes 5242880 | tf_op jit(solution)/shard_map/forward/pallas_call | solution.py:182
  44.3 1.8 %collective-permute-start.12 = (bf16[512,256]{1,0:T(8,128)(2,1)S(1)}, bf16[512,256]{1,0:T(8,128)(2,1)S(1)}, u32[]{:S(2)}, u32[]{:S(2)}) collective-permute-start(bf16[512,256]{1,0:T(8,128)(2,1)S(1)} %add_convert_fusion), channel_id=1, source_target_pairs={{0,2},{1,3},{2,0},{3,1},{4,6},{5,7},{6,4},{7,5},{8,10},{9,11},{10,... | collective-permute-start | bytes 786440 | tf_op jit(solution)/shard_map/ppermute | solution.py:459
  46.1 1.9 %forward.3 = (bf16[512,256]{1,0:T(8,128)(2,1)S(1)}, f32[512,256]{1,0:T(8,128)S(1)}) custom-call(bf16[256,256]{1,0:T(8,128)(2,1)S(1)} %collective-permute-done.2.refs_0_, bf16[256,256]{1,0:T(8,128)(2,1)S(1)} %collective-permute-done.3.refs_1_, bf16[256,256]{1,0:T(8,128)(2,1)S(1)} %collective-permute-done.4.refs_2_, ...), custom_call_target="tpu_custom_call" | custom-call | flops 1073741824 | bytes 5242880 | tf_op jit(solution)/shard_map/forward/pallas_call | solution.py:182
  48.5 1.7 %collective-permute-start.14 = (s32[128]{0:T(128)S(1)}, s32[128]{0:T(128)S(1)}, u32[]{:S(2)}, u32[]{:S(2)}) collective-permute-start(s32[128]{0:T(128)S(1)} %get-tuple-element.64.refs_0_), channel_id=1, source_target_pairs={{0,2},{1,3},{2,0},{3,1},{4,6},{5,7},{6,4},{7,5},{8,10},{9,11},{10,... | collective-permute-start | bytes 1544 | tf_op jit(solution)/shard_map/ppermute | solution.py:459
  50.3 1.8 %collective-permute-done.15.refs_3_ = s32[128]{0:T(128)S(1)} collective-permute-done((s32[128]{0:T(128)S(1)}, s32[128]{0:T(128)S(1)}, u32[]{:S(2)}, u32[]{:S(2)}) %collective-permute-start.15) | collective-permute-done | bytes 544 | tf_op jit(solution)/shard_map/ppermute | solution.py:459
  54.0 1.7 %collective-permute-start.16 = (bf16[256,512]{1,0:T(8,128)(2,1)S(1)}, bf16[256,512]{1,0:T(8,128)(2,1)S(1)}, u32[]{:S(2)}, u32[]{:S(2)}) collective-permute-start(bf16[256,512]{1,0:T(8,128)(2,1)S(1)} %get-tuple-element.67.even_ref), channel_id=1, source_target_pairs={{0,2},{1,3},{2,0},{3,1},{4,6},{5,7},{6,4},{7,5},{8,10},{9,11},{10,... | collective-permute-start | bytes 786440 | tf_op jit(solution)/shard_map/ppermute | solution.py:459
  57.1 2.3 %back_first.1 = (f32[256,2048]{1,0:T(8,128)S(1)}, f32[64,256]{1,0:T(8,128)S(1)}, f32[64,256]{1,0:T(8,128)S(1)}) custom-call(bf16[256,512]{1,0:T(8,128)(2,1)S(1)} %collective-permute-done.17.odd_ref, bf16[256,512]{1,0:T(8,128)(2,1)S(1)} %get-tuple-element.67.even_ref, bf16[2048,2048]{1,0:T(8,128)(2,1)S(1)} %densify.1.refs_8_.adj_ref, ...), custom_call_target="tpu_custom_call" | custom-call | flops 1073741824 | bytes 6291456 | tf_op jit(solution)/shard_map/back_first/pallas_call | solution.py:257
  59.4 3.3 %collective-permute-done.16.even_ref = bf16[256,512]{1,0:T(8,128)(2,1)S(1)} collective-permute-done((bf16[256,512]{1,0:T(8,128)(2,1)S(1)}, bf16[256,512]{1,0:T(8,128)(2,1)S(1)}, u32[]{:S(2)}, u32[]{:S(2)}) %collective-permute-start.16) | collective-permute-done | bytes 262176 | tf_op jit(solution)/shard_map/ppermute | solution.py:459
  64.2 2.6 %back_second.1 = (bf16[64,2048]{1,0:T(8,128)(2,1)S(1)}, f32[64,2048]{1,0:T(8,128)S(1)}, bf16[64,2048]{1,0:T(8,128)(2,1)S(1)}, f32[64,2048]{1,0:T(8,128)S(1)}) custom-call(bf16[256,512]{1,0:T(8,128)(2,1)S(1)} %collective-permute-done.19.odd_ref, bf16[256,512]{1,0:T(8,128)(2,1)S(1)} %collective-permute-done.16.even_ref, ...), custom_call_target="tpu_custom_call" | custom-call | flops 1073741824 | bytes 7864320 | tf_op jit(solution)/shard_map/back_second/pallas_call | solution.py:302
  67.3 4.3 %collective-permute-done.22.got_ref = f32[64,256]{1,0:T(8,128)S(1)} collective-permute-done((f32[64,256]{1,0:T(8,128)S(1)}, f32[64,256]{1,0:T(8,128)S(1)}, u32[]{:S(2)}, u32[]{:S(2)}) %collective-permute-start.22) | collective-permute-done | bytes 65568 | tf_op jit(solution)/shard_map/ppermute | solution.py:462
  71.7 1.8 %collective-permute-start.24 = (bf16[64,1024]{1,0:T(8,128)(2,1)S(1)}, bf16[64,1024]{1,0:T(8,128)(2,1)S(1)}, u32[]{:S(2)}, u32[]{:S(2)}) collective-permute-start(bf16[64,1024]{1,0:T(8,128)(2,1)S(1)} %get-tuple-element.79), channel_id=1, source_target_pairs={{0,2},{1,3},{2,0},{3,1},{4,6},{5,7},{6,4},{7,5},{8,10},{9,11},{10,... | collective-permute-start | bytes 393224 | tf_op jit(solution)/shard_map/ppermute | solution.py:459
  74.6 3.2 %collective-permute-done.32 = f32[64,256]{1,0:T(8,128)S(1)} collective-permute-done((f32[64,256]{1,0:T(8,128)S(1)}, f32[64,256]{1,0:T(8,128)S(1)}, u32[]{:S(2)}, u32[]{:S(2)}) %collective-permute-start.32) | collective-permute-done | bytes 65568 | tf_op jit(solution)/shard_map/ppermute | solution.py:462
  79.6 4.1 %collective-permute-done.33 = f32[64,256]{1,0:T(8,128)S(1)} collective-permute-done((f32[64,256]{1,0:T(8,128)S(1)}, f32[64,256]{1,0:T(8,128)S(1)}, u32[]{:S(2)}, u32[]{:S(2)}) %collective-permute-start.33) | collective-permute-done | bytes 65568 | tf_op jit(solution)/shard_map/ppermute | solution.py:462
  84.8 2.2 %collective-permute-start.26 = (bf16[64,256]{1,0:T(8,128)(2,1)S(1)}, bf16[64,256]{1,0:T(8,128)(2,1)S(1)}, u32[]{:S(2)}, u32[]{:S(2)}) collective-permute-start(bf16[64,256]{1,0:T(8,128)(2,1)S(1)} %get-tuple-element.81), channel_id=1, source_target_pairs={{0,20},{4,16},{8,28},{12,24},{16,4},{20,0},{24,12},{28,8},{1,21},{... | collective-permute-start | bytes 98312 | tf_op jit(solution)/shard_map/ppermute | solution.py:462
  87.0 3.6 %collective-permute-start.27 = (bf16[64,256]{1,0:T(8,128)(2,1)S(1)}, bf16[64,256]{1,0:T(8,128)(2,1)S(1)}, u32[]{:S(2)}, u32[]{:S(2)}) collective-permute-start(bf16[64,256]{1,0:T(8,128)(2,1)S(1)} %get-tuple-element.82), channel_id=1, source_target_pairs={{0,24},{4,28},{8,16},{12,20},{16,8},{20,12},{24,0},{28,4},{1,25},{... | collective-permute-start | bytes 98312 | tf_op jit(solution)/shard_map/ppermute | solution.py:462
  95.1 1.7 %collective-permute-start.30 = (bf16[64,256]{1,0:T(8,128)(2,1)S(1)}, bf16[64,256]{1,0:T(8,128)(2,1)S(1)}, u32[]{:S(2)}, u32[]{:S(2)}) collective-permute-start(bf16[64,256]{1,0:T(8,128)(2,1)S(1)} %get-tuple-element.87), channel_id=1, source_target_pairs={{0,12},{4,8},{8,4},{12,0},{16,28},{20,24},{24,20},{28,16},{1,13},{... | collective-permute-start | bytes 98312 | tf_op jit(solution)/shard_map/ppermute | solution.py:462
  98.2 1.8 %collective-permute-done.30.refs_7_ = bf16[64,256]{1,0:T(8,128)(2,1)S(1)} collective-permute-done((bf16[64,256]{1,0:T(8,128)(2,1)S(1)}, bf16[64,256]{1,0:T(8,128)(2,1)S(1)}, u32[]{:S(2)}, u32[]{:S(2)}) %collective-permute-start.30) | collective-permute-done | bytes 32800 | tf_op jit(solution)/shard_map/ppermute | solution.py:462
  103.0 2.4 %collective-permute-done.36.refs_2_ = bf16[64,512]{1,0:T(8,128)(2,1)S(1)} collective-permute-done((bf16[64,512]{1,0:T(8,128)(2,1)S(1)}, bf16[64,512]{1,0:T(8,128)(2,1)S(1)}, u32[]{:S(2)}, u32[]{:S(2)}) %collective-permute-start.36) | collective-permute-done | bytes 65568 | tf_op jit(solution)/shard_map/ppermute | solution.py:459
  (87 shorter events, 33.2 us)
Async XLA Ops:
  1.4 5.6 %collective-permute-start.1 = (s32[1,8,2]{2,1,0:T(8,128)S(1)}, s32[1,8,2]{2,1,0:T(8,128)S(1)}, u32[]{:S(2)}, u32[]{:S(2)}) collective-permute-start(s32[1,8,2]{2,1,0:T(8,128)S(1)} %copy.11), channel_id=1, source_target_pairs={{0,16},{1,21},{2,26},{3,31},{4,20},{5,17},{6,30},{7,27},{8,24},{9,... | collective-permute-start | bytes 200 | tf_op jit(solution)/shard_map/ppermute | solution.py:468
  9.9 14.7 %collective-permute-start.2 = (bf16[256,256]{1,0:T(8,128)(2,1)S(1)}, bf16[256,256]{1,0:T(8,128)(2,1)S(1)}, u32[]{:S(2)}, u32[]{:S(2)}) collective-permute-start(bf16[256,256]{1,0:T(8,128)(2,1)S(1)} %get-tuple-element.54), channel_id=1, source_target_pairs={{0,0},{1,5},{2,10},{3,15},{4,4},{5,1},{6,14},{7,11},{8,8},{9,13},{... | collective-permute-start | bytes 393224 | tf_op jit(solution)/shard_map/ppermute | solution.py:468
  10.6 14.0 %collective-permute-start.3 = (bf16[256,256]{1,0:T(8,128)(2,1)S(1)}, bf16[256,256]{1,0:T(8,128)(2,1)S(1)}, u32[]{:S(2)}, u32[]{:S(2)}) collective-permute-start(bf16[256,256]{1,0:T(8,128)(2,1)S(1)} %get-tuple-element.55), channel_id=1, source_target_pairs={{0,16},{1,21},{2,26},{3,31},{4,20},{5,17},{6,30},{7,27},{8,24},{9,... | collective-permute-start | bytes 393224 | tf_op jit(solution)/shard_map/ppermute | solution.py:468
  24.6 13.3 %collective-permute-start.7 = (bf16[256,256]{1,0:T(8,128)(2,1)S(1)}, bf16[256,256]{1,0:T(8,128)(2,1)S(1)}, u32[]{:S(2)}, u32[]{:S(2)}) collective-permute-start(bf16[256,256]{1,0:T(8,128)(2,1)S(1)} %collective-permute-done.3.refs_1_), channel_id=1, source_target_pairs={{0,2},{1,3},{2,0},{3,1},{4,6},{5,7},{6,4},{7,5},{8,10},{9,11},{10,... | collective-permute-start | bytes 393224 | tf_op jit(solution)/shard_map/ppermute | solution.py:459
  33.6 5.8 %collective-permute-start.6 = (bf16[256,256]{1,0:T(8,128)(2,1)S(1)}, bf16[256,256]{1,0:T(8,128)(2,1)S(1)}, u32[]{:S(2)}, u32[]{:S(2)}) collective-permute-start(bf16[256,256]{1,0:T(8,128)(2,1)S(1)} %collective-permute-done.2.refs_0_), channel_id=1, source_target_pairs={{0,2},{1,3},{2,0},{3,1},{4,6},{5,7},{6,4},{7,5},{8,10},{9,11},{10,... | collective-permute-start | bytes 393224 | tf_op jit(solution)/shard_map/ppermute | solution.py:459
  33.6 5.7 %collective-permute-start.4 = (bf16[256,256]{1,0:T(8,128)(2,1)S(1)}, bf16[256,256]{1,0:T(8,128)(2,1)S(1)}, u32[]{:S(2)}, u32[]{:S(2)}) collective-permute-start(bf16[256,256]{1,0:T(8,128)(2,1)S(1)} %collective-permute-done.2.refs_0_), channel_id=1, source_target_pairs={{0,1},{1,0},{2,3},{3,2},{4,5},{5,4},{6,7},{7,6},{8,9},{9,8},{10,11... | collective-permute-start | bytes 393224 | tf_op jit(solution)/shard_map/ppermute | solution.py:459
  33.7 5.7 %collective-permute-start.5 = (bf16[256,256]{1,0:T(8,128)(2,1)S(1)}, bf16[256,256]{1,0:T(8,128)(2,1)S(1)}, u32[]{:S(2)}, u32[]{:S(2)}) collective-permute-start(bf16[256,256]{1,0:T(8,128)(2,1)S(1)} %collective-permute-done.3.refs_1_), channel_id=1, source_target_pairs={{0,1},{1,0},{2,3},{3,2},{4,5},{5,4},{6,7},{7,6},{8,9},{9,8},{10,11... | collective-permute-start | bytes 393224 | tf_op jit(solution)/shard_map/ppermute | solution.py:459
  44.3 8.5 %collective-permute-start.12 = (bf16[512,256]{1,0:T(8,128)(2,1)S(1)}, bf16[512,256]{1,0:T(8,128)(2,1)S(1)}, u32[]{:S(2)}, u32[]{:S(2)}) collective-permute-start(bf16[512,256]{1,0:T(8,128)(2,1)S(1)} %add_convert_fusion), channel_id=1, source_target_pairs={{0,2},{1,3},{2,0},{3,1},{4,6},{5,7},{6,4},{7,5},{8,10},{9,11},{10,... | collective-permute-start | bytes 786440 | tf_op jit(solution)/shard_map/ppermute | solution.py:459
  48.0 4.8 %collective-permute-start.11 = (bf16[512,256]{1,0:T(8,128)(2,1)S(1)}, bf16[512,256]{1,0:T(8,128)(2,1)S(1)}, u32[]{:S(2)}, u32[]{:S(2)}) collective-permute-start(bf16[512,256]{1,0:T(8,128)(2,1)S(1)} %get-tuple-element.62), channel_id=1, source_target_pairs={{0,1},{1,0},{2,3},{3,2},{4,5},{5,4},{6,7},{7,6},{8,9},{9,8},{10,11... | collective-permute-start | bytes 786440 | tf_op jit(solution)/shard_map/ppermute | solution.py:459
  54.0 8.7 %collective-permute-start.16 = (bf16[256,512]{1,0:T(8,128)(2,1)S(1)}, bf16[256,512]{1,0:T(8,128)(2,1)S(1)}, u32[]{:S(2)}, u32[]{:S(2)}) collective-permute-start(bf16[256,512]{1,0:T(8,128)(2,1)S(1)} %get-tuple-element.67.even_ref), channel_id=1, source_target_pairs={{0,2},{1,3},{2,0},{3,1},{4,6},{5,7},{6,4},{7,5},{8,10},{9,11},{10,... | collective-permute-start | bytes 786440 | tf_op jit(solution)/shard_map/ppermute | solution.py:459
  66.8 4.8 %collective-permute-start.21 = (bf16[64,2048]{1,0:T(8,128)(2,1)S(1)}, bf16[64,2048]{1,0:T(8,128)(2,1)S(1)}, u32[]{:S(2)}, u32[]{:S(2)}) collective-permute-start(bf16[64,2048]{1,0:T(8,128)(2,1)S(1)} %get-tuple-element.75), channel_id=1, source_target_pairs={{0,1},{1,0},{2,3},{3,2},{4,5},{5,4},{6,7},{7,6},{8,9},{9,8},{10,11... | collective-permute-start | bytes 786440 | tf_op jit(solution)/shard_map/ppermute | solution.py:459
  67.0 12.6 %collective-permute-start.20 = (bf16[64,2048]{1,0:T(8,128)(2,1)S(1)}, bf16[64,2048]{1,0:T(8,128)(2,1)S(1)}, u32[]{:S(2)}, u32[]{:S(2)}) collective-permute-start(bf16[64,2048]{1,0:T(8,128)(2,1)S(1)} %get-tuple-element.73), channel_id=1, source_target_pairs={{0,1},{1,0},{2,3},{3,2},{4,5},{5,4},{6,7},{7,6},{8,9},{9,8},{10,11... | collective-permute-start | bytes 786440 | tf_op jit(solution)/shard_map/ppermute | solution.py:459
  71.7 7.9 %collective-permute-start.24 = (bf16[64,1024]{1,0:T(8,128)(2,1)S(1)}, bf16[64,1024]{1,0:T(8,128)(2,1)S(1)}, u32[]{:S(2)}, u32[]{:S(2)}) collective-permute-start(bf16[64,1024]{1,0:T(8,128)(2,1)S(1)} %get-tuple-element.79), channel_id=1, source_target_pairs={{0,2},{1,3},{2,0},{3,1},{4,6},{5,7},{6,4},{7,5},{8,10},{9,11},{10,... | collective-permute-start | bytes 393224 | tf_op jit(solution)/shard_map/ppermute | solution.py:459
  77.7 6.0 %collective-permute-start.33 = (f32[64,256]{1,0:T(8,128)S(1)}, f32[64,256]{1,0:T(8,128)S(1)}, u32[]{:S(2)}, u32[]{:S(2)}) collective-permute-start(f32[64,256]{1,0:T(8,128)S(1)} %add.13), channel_id=1, source_target_pairs={{0,16},{4,20},{8,24},{12,28},{16,0},{20,4},{24,8},{28,12},{1,17},{... | collective-permute-start | bytes 196616 | tf_op jit(solution)/shard_map/ppermute | solution.py:462
  79.0 11.8 %collective-permute-start.23 = (bf16[64,1024]{1,0:T(8,128)(2,1)S(1)}, bf16[64,1024]{1,0:T(8,128)(2,1)S(1)}, u32[]{:S(2)}, u32[]{:S(2)}) collective-permute-start(bf16[64,1024]{1,0:T(8,128)(2,1)S(1)} %get-tuple-element.78), channel_id=1, source_target_pairs={{0,2},{1,3},{2,0},{3,1},{4,6},{5,7},{6,4},{7,5},{8,10},{9,11},{10,... | collective-permute-start | bytes 393224 | tf_op jit(solution)/shard_map/ppermute | solution.py:459
  83.7 6.9 %collective-permute-start.34 = (f32[64,256]{1,0:T(8,128)S(1)}, f32[64,256]{1,0:T(8,128)S(1)}, u32[]{:S(2)}, u32[]{:S(2)}) collective-permute-start(f32[64,256]{1,0:T(8,128)S(1)} %add.14), channel_id=1, source_target_pairs={{0,2},{1,3},{2,0},{3,1},{4,6},{5,7},{6,4},{7,5},{8,10},{9,11},{10,... | collective-permute-start | bytes 196616 | tf_op jit(solution)/shard_map/ppermute | solution.py:459
  83.8 8.5 %collective-permute-start.25 = (bf16[64,256]{1,0:T(8,128)(2,1)S(1)}, bf16[64,256]{1,0:T(8,128)(2,1)S(1)}, u32[]{:S(2)}, u32[]{:S(2)}) collective-permute-start(bf16[64,256]{1,0:T(8,128)(2,1)S(1)} %get-tuple-element.80), channel_id=1, source_target_pairs={{0,16},{4,20},{8,24},{12,28},{16,0},{20,4},{24,8},{28,12},{1,17},{... | collective-permute-start | bytes 98312 | tf_op jit(solution)/shard_map/ppermute | solution.py:462
  84.8 7.6 %collective-permute-start.26 = (bf16[64,256]{1,0:T(8,128)(2,1)S(1)}, bf16[64,256]{1,0:T(8,128)(2,1)S(1)}, u32[]{:S(2)}, u32[]{:S(2)}) collective-permute-start(bf16[64,256]{1,0:T(8,128)(2,1)S(1)} %get-tuple-element.81), channel_id=1, source_target_pairs={{0,20},{4,16},{8,28},{12,24},{16,4},{20,0},{24,12},{28,8},{1,21},{... | collective-permute-start | bytes 98312 | tf_op jit(solution)/shard_map/ppermute | solution.py:462
  87.0 6.3 %collective-permute-start.27 = (bf16[64,256]{1,0:T(8,128)(2,1)S(1)}, bf16[64,256]{1,0:T(8,128)(2,1)S(1)}, u32[]{:S(2)}, u32[]{:S(2)}) collective-permute-start(bf16[64,256]{1,0:T(8,128)(2,1)S(1)} %get-tuple-element.82), channel_id=1, source_target_pairs={{0,24},{4,28},{8,16},{12,20},{16,8},{20,12},{24,0},{28,4},{1,25},{... | collective-permute-start | bytes 98312 | tf_op jit(solution)/shard_map/ppermute | solution.py:462
  90.6 12.1 %collective-permute-start.39 = (f32[64,256]{1,0:T(8,128)S(1)}, f32[64,256]{1,0:T(8,128)S(1)}, u32[]{:S(2)}, u32[]{:S(2)}) collective-permute-start(f32[64,256]{1,0:T(8,128)S(1)} %add.15.refs_4_), channel_id=1, source_target_pairs={{0,4},{4,0},{8,12},{12,8},{16,20},{20,16},{24,28},{28,24},{1,5},{5... | collective-permute-start | bytes 196616 | tf_op jit(solution)/shard_map/ppermute | solution.py:462
  90.8 6.7 %collective-permute-start.31 = (bf16[64,256]{1,0:T(8,128)(2,1)S(1)}, bf16[64,256]{1,0:T(8,128)(2,1)S(1)}, u32[]{:S(2)}, u32[]{:S(2)}) collective-permute-start(bf16[64,256]{1,0:T(8,128)(2,1)S(1)} %get-tuple-element.88), channel_id=1, source_target_pairs={{0,28},{4,24},{8,20},{12,16},{16,12},{20,8},{24,4},{28,0},{1,29},{... | collective-permute-start | bytes 98312 | tf_op jit(solution)/shard_map/ppermute | solution.py:462
  95.1 4.8 %collective-permute-start.30 = (bf16[64,256]{1,0:T(8,128)(2,1)S(1)}, bf16[64,256]{1,0:T(8,128)(2,1)S(1)}, u32[]{:S(2)}, u32[]{:S(2)}) collective-permute-start(bf16[64,256]{1,0:T(8,128)(2,1)S(1)} %get-tuple-element.87), channel_id=1, source_target_pairs={{0,12},{4,8},{8,4},{12,0},{16,28},{20,24},{24,20},{28,16},{1,13},{... | collective-permute-start | bytes 98312 | tf_op jit(solution)/shard_map/ppermute | solution.py:462
  97.5 8.9 %collective-permute-start.38 = (f32[64,256]{1,0:T(8,128)S(1)}, f32[64,256]{1,0:T(8,128)S(1)}, u32[]{:S(2)}, u32[]{:S(2)}) collective-permute-start(f32[64,256]{1,0:T(8,128)S(1)} %add.15.refs_4_), channel_id=1, source_target_pairs={{0,1},{1,0},{2,3},{3,2},{4,5},{5,4},{6,7},{7,6},{8,9},{9,8},{10,11... | collective-permute-start | bytes 196616 | tf_op jit(solution)/shard_map/ppermute | solution.py:459
  100.8 4.6 %collective-permute-start.36 = (bf16[64,512]{1,0:T(8,128)(2,1)S(1)}, bf16[64,512]{1,0:T(8,128)(2,1)S(1)}, u32[]{:S(2)}, u32[]{:S(2)}) collective-permute-start(bf16[64,512]{1,0:T(8,128)(2,1)S(1)} %get-tuple-element.101), channel_id=1, source_target_pairs={{0,2},{1,3},{2,0},{3,1},{4,6},{5,7},{6,4},{7,5},{8,10},{9,11},{10,... | collective-permute-start | bytes 196616 | tf_op jit(solution)/shard_map/ppermute | solution.py:459
  (23 other events, 75.8 us)

commit v4 on v3

--- a/solution.py
+++ b/solution.py
@@ -21,6 +21,9 @@
     return pltpu.CompilerParams(vmem_limit_bytes=min(sum(parts) + (6 << 20), 62 << 20))
 
 
+WIDE = pltpu.CompilerParams(vmem_limit_bytes=46 << 20)
+
+
 def shape(dims, dtype):
     return jax.ShapeDtypeStruct(tuple(dims), dtype)
 
@@ -33,63 +36,82 @@
     return [(i, i ^ offset) for i in range(count)]
 
 
+def div_rem(x, n):
+    if n & (n - 1) == 0:
+        return x >> (n.bit_length() - 1), x & (n - 1)
+    return lax.div(x, n), lax.rem(x, n)
+
+
 def densify_body(
-    rows_ref, fetch_ref, count_ref, blocks_ref, out_ref, head_ref, next_ref, *, n_rep, n_hi, per_list, quarter
+    rows_ref, fetch_ref, count_ref, blocks_ref, out_ref, held, first, second, older, wide_at, wide_cell, wide_next, sem,
+    *, n_rep, n_hi, per_list, quarter
 ):
     chunk, row_cell = pl.program_id(0), pl.program_id(1)
     slots, blk = blocks_ref.shape[0], blocks_ref.shape[1]
     all_cols = n_rep * n_hi * per_list
+    chunks = all_cols // COL_CHUNK
+    deep = n_hi // 2
 
     @pl.when((chunk == 0) & (row_cell == 0))
     def _():
         r, q = lax.axis_index("row"), lax.axis_index("rep")
+        copy = pltpu.make_async_copy(blocks_ref, held.at[pl.ds(0, slots)], sem)
+        copy.start()
+        held[slots] = jnp.zeros((blk, blk), BF16)
 
         @pl.loop(0, n_rep * quarter * all_cols, unroll=16)
         def _(cell):
-            head_ref[cell] = -1
-
-        def link(slot):
-            row, fetch = rows_ref[slot], fetch_ref[slot]
-            j = lax.div(row, quarter) ^ q
-            k = lax.div(fetch, per_list) ^ r
-            piece = (lax.rem(k, n_rep) ^ q) * n_hi + lax.div(k, n_rep)
-            col = piece * per_list + lax.rem(fetch, per_list)
-            cell = ((n_rep - 1 - j) * quarter + lax.rem(row, quarter)) * all_cols + col
-            next_ref[slot] = head_ref[cell]
-            head_ref[cell] = slot
-
-        pl.loop(0, count_ref[0])(link)
+            first[cell] = slots
+            second[cell] = slots
+
+        @pl.loop(0, n_rep * quarter * chunks, unroll=16)
+        def _(at):
+            wide_at[at] = -1
+
+        def link(slot, wide):
+            row_high, row_low = div_rem(rows_ref[slot], quarter)
+            source, c = div_rem(fetch_ref[slot], per_list)
+            hi, low = div_rem(source ^ r, n_rep)
+            half, hi = div_rem(hi, deep)
+            row = (n_rep - 1 - (row_high ^ q)) * quarter + row_low
+            col = ((half * n_rep + (low ^ q)) * deep + hi) * per_list + c
+            cell = row * all_cols + col
+            at = row * chunks + div_rem(col, COL_CHUNK)[0]
+            one, two, begin = first[cell], second[cell], wide_at[at]
+            first[cell] = slot
+            second[cell] = one
+            older[slot] = one
+            full = two != slots
+            wide_cell[wide] = cell
+            wide_next[wide] = begin
+            wide_at[at] = jnp.where(full, wide, begin)
+            return wide + full.astype(jnp.int32)
+
+        lax.fori_loop(0, count_ref[0], link, jnp.int32(0))
+        copy.wait()
 
     for col in range(COL_CHUNK):
-        first = head_ref[row_cell * all_cols + chunk * COL_CHUNK + col]
-        place = (slice(None), slice(col * blk, (col + 1) * blk))
-
-        @pl.when(first < 0)
-        def _():
-            out_ref[place] = jnp.zeros((blk, blk), BF16)
-
-        @pl.when(first >= 0)
-        def _():
-            second = next_ref[first]
-
-            @pl.when(second < 0)
-            def _():
-                out_ref[place] = blocks_ref[first]
-
-            @pl.when(second >= 0)
-            def _():
-                def more(carry):
-                    slot, total = carry
-                    return next_ref[slot], total + blocks_ref[slot].astype(F32)
-
-                start = (second, blocks_ref[first].astype(F32))
-                _, total = lax.while_loop(lambda carry: carry[0] >= 0, more, start)
-                out_ref[place] = total.astype(BF16)
+        cell = row_cell * all_cols + chunk * COL_CHUNK + col
+        out_ref[:, col * blk : (col + 1) * blk] = held[first[cell]] + held[second[cell]]
+
+    def redo(wide):
+        cell = wide_cell[wide]
+
+        def more(carry):
+            slot, total = carry
+            return older[slot], total + held[slot].astype(F32)
+
+        _, total = lax.while_loop(lambda carry: carry[0] < slots, more, (first[cell], jnp.zeros((blk, blk), F32)))
+        col = cell - row_cell * all_cols - chunk * COL_CHUNK
+        out_ref[:, pl.ds(pl.multiple_of(col * blk, blk), blk)] = total.astype(BF16)
+        return wide_next[wide]
+
+    lax.while_loop(lambda wide: wide >= 0, redo, wide_at[row_cell * chunks + chunk])
 
 
 def densify(block_rows, block_fetch, block_count, blocks, n_row, n_rep, per_list, row_blocks):
     slots, blk, _ = blocks.shape
-    cols = n_row * per_list * blk
+    all_cols = n_row * per_list
     width = COL_CHUNK * blk
     body = functools.partial(
         densify_body,
@@ -98,22 +120,24 @@
         per_list=per_list,
         quarter=row_blocks // n_rep,
     )
+    smem = [row_blocks * all_cols] * 2 + [slots, row_blocks * all_cols // COL_CHUNK, slots, slots]
     return pl.pallas_call(
         body,
-        out_shape=shape((row_blocks * blk, cols), BF16),
+        out_shape=shape((row_blocks * blk, all_cols * blk), BF16),
         grid_spec=pltpu.PrefetchScalarGridSpec(
             num_scalar_prefetch=3,
-            grid=(cols // width, row_blocks),
-            in_specs=[WHOLE],
+            grid=(all_cols // COL_CHUNK, row_blocks),
+            in_specs=[pl.BlockSpec(memory_space=pltpu.HBM)],
             out_specs=pl.BlockSpec((blk, width), lambda c, i, *_: (i, c)),
-            scratch_shapes=[
-                pltpu.SMEM((row_blocks * n_row * per_list,), jnp.int32),
-                pltpu.SMEM((slots,), jnp.int32),
-            ],
-        ),
-        compiler_params=params(12 << 20),
+            scratch_shapes=[pltpu.VMEM((slots + 1, blk, blk), BF16)]
+            + [pltpu.SMEM((n,), jnp.int32) for n in smem]
+            + [pltpu.SemaphoreType.DMA],
+        ),
+        compiler_params=pltpu.CompilerParams(vmem_limit_bytes=52 << 20),
         cost_estimate=pl.CostEstimate(
-            flops=slots * blk * blk, bytes_accessed=blocks.size * 2 + 2 * cols * row_blocks * blk, transcendentals=0
+            flops=slots * blk * blk,
+            bytes_accessed=blocks.size * 2 + 2 * all_cols * row_blocks * blk * blk,
+            transcendentals=0,
         ),
         name="densify",
     )(block_rows, block_fetch, block_count, blocks)
@@ -189,7 +213,7 @@
             pl.BlockSpec((ROW_TILE, features), lambda i: (jnp.minimum(i, half - 1), 0)),
             pl.BlockSpec((ROW_TILE, features), lambda i: (jnp.maximum(i - half, 0), 0)),
         ],
-        compiler_params=params(ROW_TILE * cols * 4, cols * features * 4),
+        compiler_params=WIDE,
         cost_estimate=pl.CostEstimate(
             flops=2 * rows * cols * features, bytes_accessed=adj.size + cols * features * 2, transcendentals=0
         ),
@@ -267,7 +291,7 @@
         ],
         out_specs=[pl.BlockSpec((features, COL_TILE), lambda i: (0, i))]
         + [pl.BlockSpec((wkeep.shape[0] // 2, features), lambda i: (0, 0))] * 2,
-        compiler_params=params(4 << 20),
+        compiler_params=WIDE,
         cost_estimate=pl.CostEstimate(
             flops=2 * rows * cols * features, bytes_accessed=adj.size + cols * features * 4, transcendentals=0
         ),
@@ -275,94 +299,66 @@
     )(odd, even, adj, wkeep, got)
 
 
-def back_second_body(odd_ref, even_ref, adj_ref, first_ref, o3_ref, o2_ref, o1_ref, o0_ref, acc_ref):
+def back_second_body(odd_ref, even_ref, adj_ref, first_ref, send_ref, keep_ref, acc_ref):
     q = lax.axis_index("rep")
     rows = odd_ref.shape[1]
     acc_ref[...] = first_ref[...] + dot(odd_ref[...], adj_ref[:rows]) + dot(even_ref[...], adj_ref[rows:])
-    part = o0_ref.shape[0]
-
-    def piece(j):
-        return acc_ref[pl.ds(pl.multiple_of((q ^ j) * part, part), part), :]
-
-    o3_ref[...] = piece(3).astype(BF16)
-    o2_ref[...] = piece(2)
-    o1_ref[...] = piece(1).astype(BF16)
-    o0_ref[...] = piece(0)
-
-
-def back_second(odd, even, adj, first, n_rep):
-    rows, cols = adj.shape[0] // 2, adj.shape[1]
+    part = send_ref.shape[0] // 2
+    for j in range(4):
+        out = send_ref if j & 1 else keep_ref
+        at = (3 - j) // 2 * part
+        piece = acc_ref[pl.ds(pl.multiple_of((q ^ j) * part, part), part), :]
+        out[at : at + part] = piece.astype(out.dtype)
+
+
+def back_second(odd, even, adj, first, half, n_rep, per_piece):
+    rows, cols = adj.shape[0] // 2, adj.shape[1] // 2
     features = odd.shape[0]
-    part = features // n_rep
-    per_piece = cols // n_rep // COL_TILE
-    keep_spec = pl.BlockSpec((part, COL_TILE), lambda i: (0, i))
-    send_spec = pl.BlockSpec(
-        (part, COL_TILE), lambda i: (0, (lax.div(i, per_piece) ^ 1) * per_piece + lax.rem(i, per_piece))
-    )
+    width = cols // n_rep // per_piece
+    tiles = cols // width
     return pl.pallas_call(
         back_second_body,
-        grid=(cols // COL_TILE,),
-        out_shape=[shape((part, cols), dtype) for dtype in (BF16, F32, BF16, F32)],
+        grid=(tiles,),
+        out_shape=[shape((features // 2, cols), BF16), shape((features // 2, cols), F32)],
         in_specs=[
             pl.BlockSpec(odd.shape, lambda i: (0, 0)),
             pl.BlockSpec(even.shape, lambda i: (0, 0)),
-            pl.BlockSpec((rows, COL_TILE), lambda i: (0, i)),
-            pl.BlockSpec((features, COL_TILE), lambda i: (0, i)),
+            pl.BlockSpec((rows, width), lambda i: (0, i + half * tiles)),
+            pl.BlockSpec((features, width), lambda i: (0, i + half * tiles)),
         ],
-        out_specs=[send_spec, keep_spec, send_spec, keep_spec],
-        scratch_shapes=[pltpu.VMEM((features, COL_TILE), F32)],
-        compiler_params=params(6 << 20),
+        out_specs=[
+            pl.BlockSpec(
+                (features // 2, width), lambda i: (0, (lax.div(i, per_piece) ^ 1) * per_piece + lax.rem(i, per_piece))
+            ),
+            pl.BlockSpec((features // 2, width), lambda i: (0, i)),
+        ],
+        scratch_shapes=[pltpu.VMEM((features, width), F32)],
+        compiler_params=WIDE,
         cost_estimate=pl.CostEstimate(
-            flops=2 * rows * cols * features, bytes_accessed=adj.size + cols * features * 7, transcendentals=0
-        ),
-        name="back_second",
+            flops=2 * rows * cols * features, bytes_accessed=rows * cols * 2 + cols * features * 7, transcendentals=0
+        ),
+        name=f"back_second_{half}",
     )(odd, even, adj, first)
 
 
-def across_body(keep_ref, near_ref, w_ref, got_ref, *outs, n_rep, n_hi):
-    *outs, w_out = outs
-    width = keep_ref.shape[1] // (n_rep * n_hi)
-    for half, out in enumerate(outs):
-        for piece in range(n_rep * n_hi // 2):
-            j, hi = piece // (n_hi // 2), piece % (n_hi // 2) + half * n_hi // 2
-            cols = slice((j * n_hi + hi) * width, (j * n_hi + hi + 1) * width)
-            total = keep_ref[:, cols] + near_ref[:, cols].astype(F32)
-            out[:, piece * width : (piece + 1) * width] = total.astype(BF16)
-    w_out[...] = w_ref[...] + got_ref[...]
-
-
-def across_sum(keep, near, w, got, n_rep, n_hi):
-    part, cols = keep.shape
-    return pl.pallas_call(
-        functools.partial(across_body, n_rep=n_rep, n_hi=n_hi),
-        out_shape=[shape((part, cols // 2), BF16)] * 2 + [shape(w.shape, F32)],
-        in_specs=[WHOLE] * 4,
-        out_specs=[WHOLE] * 3,
-        compiler_params=params(keep.size * 8),
-        cost_estimate=pl.CostEstimate(flops=keep.size, bytes_accessed=keep.size * 8, transcendentals=0),
-        name="across_sum",
-    )(keep, near, w, got)
-
-
-def split_body(own_ref, near_ref, far_ref, *outs, n_rep, n_hi, half):
+def split_body(own_ref, near_ref, far_ref, *outs, n_rep, deep):
     q = lax.axis_index("rep")
-    width = outs[0].shape[1]
+    part, width = outs[0].shape
     for i, out in enumerate(outs):
         low, hi = i % n_rep, i // n_rep
         j = low ^ q
-        cols = pl.ds(pl.multiple_of((j * n_hi + hi + half * n_hi // 2) * width, width), width)
-        far_cols = pl.ds(pl.multiple_of(((j ^ 2) * (n_hi // 2) + hi) * width, width), width)
-        total = own_ref[:, cols] + near_ref[:, cols].astype(F32) + far_ref[:, far_cols].astype(F32)
+        cols = pl.ds(pl.multiple_of((j * deep + hi) * width, width), width)
+        far_cols = pl.ds(pl.multiple_of(((j ^ 2) * deep + hi) * width, width), width)
+        total = own_ref[part:, cols] + near_ref[part:, cols].astype(F32) + far_ref[:, far_cols].astype(F32)
         out[...] = total.astype(out.dtype)
 
 
-def split(own, near, far, half, n_row, n_rep):
-    part, cols = own.shape
-    width = cols // n_row
-    count = n_row // 2
-    return pl.pallas_call(
-        functools.partial(split_body, n_rep=n_rep, n_hi=n_row // n_rep, half=half),
-        out_shape=[shape((part, width), F32 if half * count + i == 0 else BF16) for i in range(count)],
+def split(own, near, far, half, n_rep, deep):
+    part, cols = far.shape
+    count = n_rep * deep
+    return pl.pallas_call(
+        functools.partial(split_body, n_rep=n_rep, deep=deep),
+        out_shape=[shape((part, cols // count), F32 if half + i == 0 else BF16) for i in range(count)],
         in_specs=[WHOLE] * 3,
         out_specs=[WHOLE] * count,
         compiler_params=params(own.size * 10),
@@ -480,7 +476,9 @@
     far = [to_rep(x, 2) for x in own]
     near = [to_rep(x, 1) for x in own]
     diag = [to_rep(x, 1) for x in far]
-    pieces = own + near + far + diag
+    deep = n_hi // 2
+    by_rep = [own, near, far, diag]
+    pieces = [by_rep[j][half * deep + i] for half in range(2) for j in range(n_rep) for i in range(deep)]
 
     send3, keep2 = forward(pieces, adj, 0)
     across = (keep2 + to_rep(send3, 1).astype(F32)).astype(BF16)
@@ -495,26 +493,35 @@
     grad2 = to_rep(grad0, 2)
     grad1 = to_rep(grad0, 1)
     first, wsend, wkeep = back_first(grad1, grad0, adj, wkeep, to_rep(wsend, 1))
+    w = wkeep + to_row(wsend, 1)
     grad2 = after(grad2, first)
-    grad3 = to_rep(grad2, 1)
-    o3, o2, o1, o0 = back_second(grad3, grad2, adj, first, n_rep)
-    to_low, to_high, w = across_sum(o2, to_rep(o3, 1), wkeep, to_row(wsend, 1), n_rep, n_hi)
-    o1 = to_rep(o1, 1)
-    from_high = to_rep(to_high, 2)
-    from_low = to_rep(to_low, 2)
-    w = w + to_row(w, 2)
+    grad3 = after(to_rep(grad2, 1), w)
+    got = to_row(w, 2)
+    send_high, keep_high = back_second(grad3, grad2, adj, first, 1, n_rep, deep)
+    near_high = to_rep(send_high, 1)
+    send_low, keep_low = back_second(grad3, grad2, adj, after(first, send_high), 0, n_rep, deep)
+    near_low = to_rep(send_low, 1)
+    part = features // n_rep
+
+    def across_sum(keep, near):
+        return (keep[:part] + near[:part].astype(F32)).astype(BF16)
+
+    far_high = to_rep(across_sum(keep_high, after(near_high, send_low)), 2)
+    far_low = to_rep(across_sum(keep_low, near_low), 2)
+    w = w + got
     got = to_row(w, 4)
-    high = split(o0, o1, from_high, 1, n_row, n_rep)
-    half = n_row // 2
-    back_high = [to_row(x, half + i) for i, x in enumerate(high)]
+    high = split(keep_high, near_high, far_high, 1, n_rep, deep)
+    half_rows = n_row // 2
+    back_high = [to_row(x, half_rows + i) for i, x in enumerate(high)]
     w = w + after(got, high)
     step = 8
     while step < n_row:
         w = w + to_row(w, step)
         step *= 2
-    low = split(o0, o1, after(from_low, back_high[:-1]), 0, n_row, n_rep)
-    returned = [low[0]] + [to_row(low[i], i) for i in range(1, half)] + back_high
-    w = w + to_rep(w, 2)
+    got = to_rep(w, 2)
+    low = split(keep_low, near_low, after(far_low, back_high[:-1]), 0, n_rep, deep)
+    w = w + after(got, low)
+    returned = [low[0]] + [to_row(low[i], i) for i in range(1, half_rows)] + back_high
     grads = collect(lists, after(returned, w), per_list, row_blocks, blk)
     other = to_row(w, 1)
     weights = [w, to_rep(w, 1), other, to_rep(other, 1)]

time: 108 us -> 116 us (1.074)
  Pallas kernels: 19.6 us -> 35.5 us
  waiting for transfers between devices: 36.4 us -> 26.6 us
  starting transfers between devices: 43.7 us -> 48.8 us
  local copies, waits for them, and re-layouts: 6.13 us -> 3.35 us
    pallas_call x5, Pallas kernels: 8.95 us -> 19 us  [the longest x1 12.4 us: densify(): pl.pallas_call(body, out_shape=shape((row_blocks * blk, all_cols * blk),...]
    ppermute x26, waiting for transfers between devices: 19.9 us -> 14.9 us  [to_rep(): return lax.ppermute(x, 'rep', xor_perm(n_rep, j))]
    ppermute x11, waiting for transfers between devices: 15.6 us -> 10.7 us  [to_row(): return lax.ppermute(x, 'row', xor_perm(n_row, k))]
    pallas_call x2, Pallas kernels: 3.82 us -> 7.91 us  [forward(): pl.pallas_call(functools.partial(forward_body, n_pieces=len(pieces)), gri...]
    ppermute x26, starting transfers between devices: 21 us -> 24.3 us  [to_rep(): return lax.ppermute(x, 'rep', xor_perm(n_rep, j))]
    unnamed x13 -> x11, local copies, waits for them, and re-layouts: 6.13 us -> 3.35 us
    ppermute x11, starting transfers between devices: 14.4 us -> 16.2 us  [to_row(): return lax.ppermute(x, 'row', xor_perm(n_row, k))]
    pallas_call x1, Pallas kernels: 2.31 us -> 4 us  [back_first(): pl.pallas_call(back_first_body, grid=(cols // COL_TILE,), out_shape=[shap...]
  transfers between devices with their start and end apart: 41 -> 41, of which waited for: 20 -> 16; matrix products, arithmetic and copies ran while one was open for 0% -> 0% of each run, Pallas kernels for 11% -> 21%
where the time goes in v4:
time: 116 us
  starting transfers between devices  48.8 us (42%)
  Pallas kernels  35.5 us (31%)
  waiting for transfers between devices  26.6 us (23%)
  local copies, waits for them, and re-layouts  3.35 us (3%)
  between operations  1.54 us (1%)
    ppermute x26, starting transfers between devices, to_rep(): return lax.ppermute(x, 'rep', xor_perm(n_rep, j))  24.3 us
    ppermute x11, starting transfers between devices, to_row(): return lax.ppermute(x, 'row', xor_perm(n_row, k))  16.2 us
    ppermute x26, waiting for transfers between devices, to_rep(): return lax.ppermute(x, 'rep', xor_perm(n_rep, j))  14.9 us
    pallas_call x1, Pallas kernels, densify(): pl.pallas_call(body, out_shape=shape((row_blocks * blk, all_cols * blk),...  12.4 us
    ppermute x11, waiting for transfers between devices, to_row(): return lax.ppermute(x, 'row', xor_perm(n_row, k))  10.7 us
    ppermute x4, starting transfers between devices, spread(): return lax.ppermute(x, ('row', 'rep'), perm)  8.34 us
    pallas_call x2, Pallas kernels, forward(): pl.pallas_call(functools.partial(forward_body, n_pieces=len(pieces)), gri...  7.91 us
    pallas_call x2, Pallas kernels, back_second(): pl.pallas_call(back_second_body, grid=(tiles,), out_shape=[shape((feature...  6.5 us
  transfers between devices with their start and end apart: 41, of which 16 were waited for; matrix products, arithmetic and copies ran while one was open for 0% of the time, Pallas kernels for 21%

profile of v4, /device:TPU:0, one launch (start us, length us, event | category | flops | bytes accessed | tf_op | source)
XLA Modules:
  0.0 116.0 jit_solution(1533422194604100266)
XLA Ops:
  1.4 4.0 %collective-permute-start.1 = (s32[1,8,2]{2,1,0:T(8,128)S(1)}, s32[1,8,2]{2,1,0:T(8,128)S(1)}, u32[]{:S(2)}, u32[]{:S(2)}) collective-permute-start(s32[1,8,2]{2,1,0:T(8,128)S(1)} %copy.11), channel_id=1, source_target_pairs={{0,16},{1,21},{2,26},{3,31},{4,20},{5,17},{6,30},{7,27},{8,24},{9,... | collective-permute-start | bytes 200 | tf_op jit(solution)/shard_map/ppermute | solution.py:464
  10.6 3.0 %collective-permute-start.6 = (bf16[256,256]{1,0:T(8,128)(2,1)S(1)}, bf16[256,256]{1,0:T(8,128)(2,1)S(1)}, u32[]{:S(2)}, u32[]{:S(2)}) collective-permute-start(bf16[256,256]{1,0:T(8,128)(2,1)S(1)} %get-tuple-element.56), channel_id=1, source_target_pairs={{0,16},{1,21},{2,26},{3,31},{4,20},{5,17},{6,30},{7,27},{8,24},{9,... | collective-permute-start | bytes 393224 | tf_op jit(solution)/shard_map/ppermute | solution.py:464
  15.6 12.4 %densify.1.refs_8_.adj_ref = bf16[2048,2048]{1,0:T(8,128)(2,1)} custom-call(s32[192]{0:T(256)S(1)} %copy-done.3, s32[192]{0:T(256)S(1)} %copy-done.4, s32[1]{0:T(128)S(6)} %copy.13.count_ref, bf16[192,128,128]{2,1,0:T(8,128)(2,1)} %blocks_ref.1), custom_call_target="tpu_custom_call" | custom-call | flops 3145728 | bytes 14680064 | tf_op jit(solution)/shard_map/densify/pallas_call | solution.py:124
  28.0 4.6 %collective-permute-start.8 = (bf16[256,256]{1,0:T(8,128)(2,1)S(1)}, bf16[256,256]{1,0:T(8,128)(2,1)S(1)}, u32[]{:S(2)}, u32[]{:S(2)}) collective-permute-start(bf16[256,256]{1,0:T(8,128)(2,1)S(1)} %collective-permute-done.6.refs_4_), channel_id=1, source_target_pairs={{0,2},{1,3},{2,0},{3,1},{4,6},{5,7},{6,4},{7,5},{8,10},{9,11},{10,... | collective-permute-start | bytes 393224 | tf_op jit(solution)/shard_map/ppermute | solution.py:455
  32.7 2.6 %collective-permute-start.3 = (bf16[256,256]{1,0:T(8,128)(2,1)S(1)}, bf16[256,256]{1,0:T(8,128)(2,1)S(1)}, u32[]{:S(2)}, u32[]{:S(2)}) collective-permute-start(bf16[256,256]{1,0:T(8,128)(2,1)S(1)} %collective-permute-done.2.refs_0_), channel_id=1, source_target_pairs={{0,1},{1,0},{2,3},{3,2},{4,5},{5,4},{6,7},{7,6},{8,9},{9,8},{10,11... | collective-permute-start | bytes 393224 | tf_op jit(solution)/shard_map/ppermute | solution.py:455
  35.5 3.4 %collective-permute-start.9 = (bf16[256,256]{1,0:T(8,128)(2,1)S(1)}, bf16[256,256]{1,0:T(8,128)(2,1)S(1)}, u32[]{:S(2)}, u32[]{:S(2)}) collective-permute-start(bf16[256,256]{1,0:T(8,128)(2,1)S(1)} %collective-permute-done.8.refs_6_), channel_id=1, source_target_pairs={{0,1},{1,0},{2,3},{3,2},{4,5},{5,4},{6,7},{7,6},{8,9},{9,8},{10,11... | collective-permute-start | bytes 393224 | tf_op jit(solution)/shard_map/ppermute | solution.py:455
  41.2 4.0 %forward.2 = (bf16[512,256]{1,0:T(8,128)(2,1)S(1)}, f32[512,256]{1,0:T(8,128)S(1)}) custom-call(bf16[256,256]{1,0:T(8,128)(2,1)S(1)} %collective-permute-done.2.refs_0_, bf16[256,256]{1,0:T(8,128)(2,1)S(1)} %collective-permute-done.3.refs_1_, bf16[256,256]{1,0:T(8,128)(2,1)S(1)} %collective-permute-done.4.refs_2_, ...), custom_call_target="tpu_custom_call" | custom-call | flops 1073741824 | bytes 5242880 | tf_op jit(solution)/shard_map/forward/pallas_call | solution.py:206
  48.3 4.0 %forward.3 = (bf16[512,256]{1,0:T(8,128)(2,1)S(1)}, f32[512,256]{1,0:T(8,128)S(1)}) custom-call(bf16[256,256]{1,0:T(8,128)(2,1)S(1)} %collective-permute-done.2.refs_0_, bf16[256,256]{1,0:T(8,128)(2,1)S(1)} %collective-permute-done.3.refs_1_, bf16[256,256]{1,0:T(8,128)(2,1)S(1)} %collective-permute-done.4.refs_2_, ...), custom_call_target="tpu_custom_call" | custom-call | flops 1073741824 | bytes 5242880 | tf_op jit(solution)/shard_map/forward/pallas_call | solution.py:206
  60.5 4.0 %back_first.1 = (f32[256,2048]{1,0:T(8,128)S(1)}, f32[64,256]{1,0:T(8,128)S(1)}, f32[64,256]{1,0:T(8,128)S(1)}) custom-call(bf16[256,512]{1,0:T(8,128)(2,1)S(1)} %collective-permute-done.17.odd_ref, bf16[256,512]{1,0:T(8,128)(2,1)S(1)} %get-tuple-element.68.even_ref, bf16[2048,2048]{1,0:T(8,128)(2,1)} %densify.1.refs_8_.adj_ref, ...), custom_call_target="tpu_custom_call" | custom-call | flops 1073741824 | bytes 6291456 | tf_op jit(solution)/shard_map/back_first/pallas_call | solution.py:281
  64.5 2.0 %collective-permute-done.16.even_ref = bf16[256,512]{1,0:T(8,128)(2,1)S(1)} collective-permute-done((bf16[256,512]{1,0:T(8,128)(2,1)S(1)}, bf16[256,512]{1,0:T(8,128)(2,1)S(1)}, u32[]{:S(2)}, u32[]{:S(2)}) %collective-permute-start.16) | collective-permute-done | bytes 262176 | tf_op jit(solution)/shard_map/ppermute | solution.py:455
  66.5 1.8 %collective-permute-start.20 = (f32[64,256]{1,0:T(8,128)S(1)}, f32[64,256]{1,0:T(8,128)S(1)}, u32[]{:S(2)}, u32[]{:S(2)}) collective-permute-start(f32[64,256]{1,0:T(8,128)S(1)} %get-tuple-element.74), channel_id=1, source_target_pairs={{0,4},{4,0},{8,12},{12,8},{16,20},{20,16},{24,28},{28,24},{1,5},{5... | collective-permute-start | bytes 196616 | tf_op jit(solution)/shard_map/ppermute | solution.py:458
  68.3 2.8 %collective-permute-done.20 = f32[64,256]{1,0:T(8,128)S(1)} collective-permute-done((f32[64,256]{1,0:T(8,128)S(1)}, f32[64,256]{1,0:T(8,128)S(1)}, u32[]{:S(2)}, u32[]{:S(2)}) %collective-permute-start.20) | collective-permute-done | bytes 65568 | tf_op jit(solution)/shard_map/ppermute | solution.py:458
  71.1 3.3 %back_second_1.1 = (bf16[128,1024]{1,0:T(8,128)(2,1)S(1)}, f32[128,1024]{1,0:T(8,128)S(1)}) custom-call(bf16[256,512]{1,0:T(8,128)(2,1)S(1)} %collective-permute-done.19.odd_ref, bf16[256,512]{1,0:T(8,128)(2,1)S(1)} %collective-permute-done.16.even_ref, bf16[2048,2048]{1,0:T(8,128)(2,1)} %densify.1.refs_8_.adj_ref, f32[256,2048]{1,0:T(8,128)S(1)} %get-tuple-element.77.first_ref), custom_call_target="tpu_custom_call" | custom-call | flops 536870912 | bytes 3932160 | tf_op jit(solution)/shard_map/back_second_1/pallas_call | solution.py:319
  75.5 3.2 %back_second_0.1 = (bf16[128,1024]{1,0:T(8,128)(2,1)S(1)}, f32[128,1024]{1,0:T(8,128)S(1)}) custom-call(bf16[256,512]{1,0:T(8,128)(2,1)S(1)} %collective-permute-done.19.odd_ref, bf16[256,512]{1,0:T(8,128)(2,1)S(1)} %collective-permute-done.16.even_ref, bf16[2048,2048]{1,0:T(8,128)(2,1)} %densify.1.refs_8_.adj_ref, f32[256,2048]{1,0:T(8,128)S(1)} %get-tuple-element.77.first_ref), custom_call_target="tpu_custom_call" | custom-call | flops 536870912 | bytes 3932160 | tf_op jit(solution)/shard_map/back_second_0/pallas_call | solution.py:319
  79.0 4.2 %collective-permute-start.33 = (f32[64,256]{1,0:T(8,128)S(1)}, f32[64,256]{1,0:T(8,128)S(1)}, u32[]{:S(2)}, u32[]{:S(2)}) collective-permute-start(f32[64,256]{1,0:T(8,128)S(1)} %add.25), channel_id=1, source_target_pairs={{0,16},{4,20},{8,24},{12,28},{16,0},{20,4},{24,8},{28,12},{1,17},{... | collective-permute-start | bytes 196616 | tf_op jit(solution)/shard_map/ppermute | solution.py:458
  83.2 1.8 %collective-permute-start.24 = (bf16[64,1024]{1,0:T(8,128)(2,1)S(1)}, bf16[64,1024]{1,0:T(8,128)(2,1)S(1)}, u32[]{:S(2)}, u32[]{:S(2)}) collective-permute-start(bf16[64,1024]{1,0:T(8,128)(2,1)S(1)} %add_convert_fusion.1), channel_id=1, source_target_pairs={{0,2},{1,3},{2,0},{3,1},{4,6},{5,7},{6,4},{7,5},{8,10},{9,11},{10,... | collective-permute-start | bytes 393224 | tf_op jit(solution)/shard_map/ppermute | solution.py:455
  85.4 4.2 %collective-permute-done.24.far_ref = bf16[64,1024]{1,0:T(8,128)(2,1)S(1)} collective-permute-done((bf16[64,1024]{1,0:T(8,128)(2,1)S(1)}, bf16[64,1024]{1,0:T(8,128)(2,1)S(1)}, u32[]{:S(2)}, u32[]{:S(2)}) %collective-permute-start.24) | collective-permute-done | bytes 131104 | tf_op jit(solution)/shard_map/ppermute | solution.py:455
  89.7 1.8 %collective-permute-start.34 = (f32[64,256]{1,0:T(8,128)S(1)}, f32[64,256]{1,0:T(8,128)S(1)}, u32[]{:S(2)}, u32[]{:S(2)}) collective-permute-start(f32[64,256]{1,0:T(8,128)S(1)} %add.26), channel_id=1, source_target_pairs={{0,2},{1,3},{2,0},{3,1},{4,6},{5,7},{6,4},{7,5},{8,10},{9,11},{10,... | collective-permute-start | bytes 196616 | tf_op jit(solution)/shard_map/ppermute | solution.py:455
  91.5 2.6 %collective-permute-start.26 = (bf16[64,256]{1,0:T(8,128)(2,1)S(1)}, bf16[64,256]{1,0:T(8,128)(2,1)S(1)}, u32[]{:S(2)}, u32[]{:S(2)}) collective-permute-start(bf16[64,256]{1,0:T(8,128)(2,1)S(1)} %get-tuple-element.83), channel_id=1, source_target_pairs={{0,20},{4,16},{8,28},{12,24},{16,4},{20,0},{24,12},{28,8},{1,21},{... | collective-permute-start | bytes 98312 | tf_op jit(solution)/shard_map/ppermute | solution.py:458
  94.9 2.5 %collective-permute-done.25.refs_8_ = bf16[64,256]{1,0:T(8,128)(2,1)S(1)} collective-permute-done((bf16[64,256]{1,0:T(8,128)(2,1)S(1)}, bf16[64,256]{1,0:T(8,128)(2,1)S(1)}, u32[]{:S(2)}, u32[]{:S(2)}) %collective-permute-start.25) | collective-permute-done | bytes 32800 | tf_op jit(solution)/shard_map/ppermute | solution.py:458
  97.4 2.5 %collective-permute-done.27.refs_10_ = bf16[64,256]{1,0:T(8,128)(2,1)S(1)} collective-permute-done((bf16[64,256]{1,0:T(8,128)(2,1)S(1)}, bf16[64,256]{1,0:T(8,128)(2,1)S(1)}, u32[]{:S(2)}, u32[]{:S(2)}) %collective-permute-start.27) | collective-permute-done | bytes 32800 | tf_op jit(solution)/shard_map/ppermute | solution.py:458
  103.8 2.0 %collective-permute-start.30 = (bf16[64,256]{1,0:T(8,128)(2,1)S(1)}, bf16[64,256]{1,0:T(8,128)(2,1)S(1)}, u32[]{:S(2)}, u32[]{:S(2)}) collective-permute-start(bf16[64,256]{1,0:T(8,128)(2,1)S(1)} %get-tuple-element.89), channel_id=1, source_target_pairs={{0,12},{4,8},{8,4},{12,0},{16,28},{20,24},{24,20},{28,16},{1,13},{... | collective-permute-start | bytes 98312 | tf_op jit(solution)/shard_map/ppermute | solution.py:458
  105.8 2.7 %collective-permute-done.31.refs_11_ = bf16[64,256]{1,0:T(8,128)(2,1)S(1)} collective-permute-done((bf16[64,256]{1,0:T(8,128)(2,1)S(1)}, bf16[64,256]{1,0:T(8,128)(2,1)S(1)}, u32[]{:S(2)}, u32[]{:S(2)}) %collective-permute-start.31) | collective-permute-done | bytes 32800 | tf_op jit(solution)/shard_map/ppermute | solution.py:458
  111.9 2.8 %collective-permute-done.36.refs_2_ = bf16[64,512]{1,0:T(8,128)(2,1)S(1)} collective-permute-done((bf16[64,512]{1,0:T(8,128)(2,1)S(1)}, bf16[64,512]{1,0:T(8,128)(2,1)S(1)}, u32[]{:S(2)}, u32[]{:S(2)}) %collective-permute-start.36) | collective-permute-done | bytes 65568 | tf_op jit(solution)/shard_map/ppermute | solution.py:455
  (88 shorter events, 32.4 us)
Async XLA Ops:
  1.4 5.6 %collective-permute-start.1 = (s32[1,8,2]{2,1,0:T(8,128)S(1)}, s32[1,8,2]{2,1,0:T(8,128)S(1)}, u32[]{:S(2)}, u32[]{:S(2)}) collective-permute-start(s32[1,8,2]{2,1,0:T(8,128)S(1)} %copy.11), channel_id=1, source_target_pairs={{0,16},{1,21},{2,26},{3,31},{4,20},{5,17},{6,30},{7,27},{8,24},{9,... | collective-permute-start | bytes 200 | tf_op jit(solution)/shard_map/ppermute | solution.py:464
  9.9 18.1 %collective-permute-start.2 = (bf16[256,256]{1,0:T(8,128)(2,1)S(1)}, bf16[256,256]{1,0:T(8,128)(2,1)S(1)}, u32[]{:S(2)}, u32[]{:S(2)}) collective-permute-start(bf16[256,256]{1,0:T(8,128)(2,1)S(1)} %get-tuple-element.55), channel_id=1, source_target_pairs={{0,0},{1,5},{2,10},{3,15},{4,4},{5,1},{6,14},{7,11},{8,8},{9,13},{... | collective-permute-start | bytes 393224 | tf_op jit(solution)/shard_map/ppermute | solution.py:464
  10.6 17.5 %collective-permute-start.6 = (bf16[256,256]{1,0:T(8,128)(2,1)S(1)}, bf16[256,256]{1,0:T(8,128)(2,1)S(1)}, u32[]{:S(2)}, u32[]{:S(2)}) collective-permute-start(bf16[256,256]{1,0:T(8,128)(2,1)S(1)} %get-tuple-element.56), channel_id=1, source_target_pairs={{0,16},{1,21},{2,26},{3,31},{4,20},{5,17},{6,30},{7,27},{8,24},{9,... | collective-permute-start | bytes 393224 | tf_op jit(solution)/shard_map/ppermute | solution.py:464
  28.0 7.5 %collective-permute-start.8 = (bf16[256,256]{1,0:T(8,128)(2,1)S(1)}, bf16[256,256]{1,0:T(8,128)(2,1)S(1)}, u32[]{:S(2)}, u32[]{:S(2)}) collective-permute-start(bf16[256,256]{1,0:T(8,128)(2,1)S(1)} %collective-permute-done.6.refs_4_), channel_id=1, source_target_pairs={{0,2},{1,3},{2,0},{3,1},{4,6},{5,7},{6,4},{7,5},{8,10},{9,11},{10,... | collective-permute-start | bytes 393224 | tf_op jit(solution)/shard_map/ppermute | solution.py:455
  32.6 6.4 %collective-permute-start.4 = (bf16[256,256]{1,0:T(8,128)(2,1)S(1)}, bf16[256,256]{1,0:T(8,128)(2,1)S(1)}, u32[]{:S(2)}, u32[]{:S(2)}) collective-permute-start(bf16[256,256]{1,0:T(8,128)(2,1)S(1)} %collective-permute-done.2.refs_0_), channel_id=1, source_target_pairs={{0,2},{1,3},{2,0},{3,1},{4,6},{5,7},{6,4},{7,5},{8,10},{9,11},{10,... | collective-permute-start | bytes 393224 | tf_op jit(solution)/shard_map/ppermute | solution.py:455
  32.7 7.5 %collective-permute-start.3 = (bf16[256,256]{1,0:T(8,128)(2,1)S(1)}, bf16[256,256]{1,0:T(8,128)(2,1)S(1)}, u32[]{:S(2)}, u32[]{:S(2)}) collective-permute-start(bf16[256,256]{1,0:T(8,128)(2,1)S(1)} %collective-permute-done.2.refs_0_), channel_id=1, source_target_pairs={{0,1},{1,0},{2,3},{3,2},{4,5},{5,4},{6,7},{7,6},{8,9},{9,8},{10,11... | collective-permute-start | bytes 393224 | tf_op jit(solution)/shard_map/ppermute | solution.py:455
  35.2 5.0 %collective-permute-start.7 = (bf16[256,256]{1,0:T(8,128)(2,1)S(1)}, bf16[256,256]{1,0:T(8,128)(2,1)S(1)}, u32[]{:S(2)}, u32[]{:S(2)}) collective-permute-start(bf16[256,256]{1,0:T(8,128)(2,1)S(1)} %collective-permute-done.6.refs_4_), channel_id=1, source_target_pairs={{0,1},{1,0},{2,3},{3,2},{4,5},{5,4},{6,7},{7,6},{8,9},{9,8},{10,11... | collective-permute-start | bytes 393224 | tf_op jit(solution)/shard_map/ppermute | solution.py:455
  46.8 9.8 %collective-permute-start.12 = (bf16[512,256]{1,0:T(8,128)(2,1)S(1)}, bf16[512,256]{1,0:T(8,128)(2,1)S(1)}, u32[]{:S(2)}, u32[]{:S(2)}) collective-permute-start(bf16[512,256]{1,0:T(8,128)(2,1)S(1)} %add_convert_fusion), channel_id=1, source_target_pairs={{0,2},{1,3},{2,0},{3,1},{4,6},{5,7},{6,4},{7,5},{8,10},{9,11},{10,... | collective-permute-start | bytes 786440 | tf_op jit(solution)/shard_map/ppermute | solution.py:455
  57.7 8.7 %collective-permute-start.16 = (bf16[256,512]{1,0:T(8,128)(2,1)S(1)}, bf16[256,512]{1,0:T(8,128)(2,1)S(1)}, u32[]{:S(2)}, u32[]{:S(2)}) collective-permute-start(bf16[256,512]{1,0:T(8,128)(2,1)S(1)} %get-tuple-element.68.even_ref), channel_id=1, source_target_pairs={{0,2},{1,3},{2,0},{3,1},{4,6},{5,7},{6,4},{7,5},{8,10},{9,11},{10,... | collective-permute-start | bytes 786440 | tf_op jit(solution)/shard_map/ppermute | solution.py:455
  74.3 8.8 %collective-permute-start.23 = (bf16[128,1024]{1,0:T(8,128)(2,1)S(1)}, bf16[128,1024]{1,0:T(8,128)(2,1)S(1)}, u32[]{:S(2)}, u32[]{:S(2)}) collective-permute-start(bf16[128,1024]{1,0:T(8,128)(2,1)S(1)} %get-tuple-element.76), channel_id=1, source_target_pairs={{0,1},{1,0},{2,3},{3,2},{4,5},{5,4},{6,7},{7,6},{8,9},{9,8},{10,11... | collective-permute-start | bytes 786440 | tf_op jit(solution)/shard_map/ppermute | solution.py:455
  78.7 6.3 %collective-permute-start.21 = (bf16[128,1024]{1,0:T(8,128)(2,1)S(1)}, bf16[128,1024]{1,0:T(8,128)(2,1)S(1)}, u32[]{:S(2)}, u32[]{:S(2)}) collective-permute-start(bf16[128,1024]{1,0:T(8,128)(2,1)S(1)} %get-tuple-element.79), channel_id=1, source_target_pairs={{0,1},{1,0},{2,3},{3,2},{4,5},{5,4},{6,7},{7,6},{8,9},{9,8},{10,11... | collective-permute-start | bytes 786440 | tf_op jit(solution)/shard_map/ppermute | solution.py:455
  79.0 10.7 %collective-permute-start.33 = (f32[64,256]{1,0:T(8,128)S(1)}, f32[64,256]{1,0:T(8,128)S(1)}, u32[]{:S(2)}, u32[]{:S(2)}) collective-permute-start(f32[64,256]{1,0:T(8,128)S(1)} %add.25), channel_id=1, source_target_pairs={{0,16},{4,20},{8,24},{12,28},{16,0},{20,4},{24,8},{28,12},{1,17},{... | collective-permute-start | bytes 196616 | tf_op jit(solution)/shard_map/ppermute | solution.py:458
  83.2 6.4 %collective-permute-start.24 = (bf16[64,1024]{1,0:T(8,128)(2,1)S(1)}, bf16[64,1024]{1,0:T(8,128)(2,1)S(1)}, u32[]{:S(2)}, u32[]{:S(2)}) collective-permute-start(bf16[64,1024]{1,0:T(8,128)(2,1)S(1)} %add_convert_fusion.1), channel_id=1, source_target_pairs={{0,2},{1,3},{2,0},{3,1},{4,6},{5,7},{6,4},{7,5},{8,10},{9,11},{10,... | collective-permute-start | bytes 393224 | tf_op jit(solution)/shard_map/ppermute | solution.py:455
  85.1 9.8 %collective-permute-start.22 = (bf16[64,1024]{1,0:T(8,128)(2,1)S(1)}, bf16[64,1024]{1,0:T(8,128)(2,1)S(1)}, u32[]{:S(2)}, u32[]{:S(2)}) collective-permute-start(bf16[64,1024]{1,0:T(8,128)(2,1)S(1)} %add_convert_fusion.2), channel_id=1, source_target_pairs={{0,2},{1,3},{2,0},{3,1},{4,6},{5,7},{6,4},{7,5},{8,10},{9,11},{10,... | collective-permute-start | bytes 393224 | tf_op jit(solution)/shard_map/ppermute | solution.py:455
  89.7 10.3 %collective-permute-start.34 = (f32[64,256]{1,0:T(8,128)S(1)}, f32[64,256]{1,0:T(8,128)S(1)}, u32[]{:S(2)}, u32[]{:S(2)}) collective-permute-start(f32[64,256]{1,0:T(8,128)S(1)} %add.26), channel_id=1, source_target_pairs={{0,2},{1,3},{2,0},{3,1},{4,6},{5,7},{6,4},{7,5},{8,10},{9,11},{10,... | collective-permute-start | bytes 196616 | tf_op jit(solution)/shard_map/ppermute | solution.py:455
  91.5 5.9 %collective-permute-start.25 = (bf16[64,256]{1,0:T(8,128)(2,1)S(1)}, bf16[64,256]{1,0:T(8,128)(2,1)S(1)}, u32[]{:S(2)}, u32[]{:S(2)}) collective-permute-start(bf16[64,256]{1,0:T(8,128)(2,1)S(1)} %get-tuple-element.82), channel_id=1, source_target_pairs={{0,16},{4,20},{8,24},{12,28},{16,0},{20,4},{24,8},{28,12},{1,17},{... | collective-permute-start | bytes 98312 | tf_op jit(solution)/shard_map/ppermute | solution.py:458
  91.5 5.9 %collective-permute-start.26 = (bf16[64,256]{1,0:T(8,128)(2,1)S(1)}, bf16[64,256]{1,0:T(8,128)(2,1)S(1)}, u32[]{:S(2)}, u32[]{:S(2)}) collective-permute-start(bf16[64,256]{1,0:T(8,128)(2,1)S(1)} %get-tuple-element.83), channel_id=1, source_target_pairs={{0,20},{4,16},{8,28},{12,24},{16,4},{20,0},{24,12},{28,8},{1,21},{... | collective-permute-start | bytes 98312 | tf_op jit(solution)/shard_map/ppermute | solution.py:458
  94.2 5.7 %collective-permute-start.27 = (bf16[64,256]{1,0:T(8,128)(2,1)S(1)}, bf16[64,256]{1,0:T(8,128)(2,1)S(1)}, u32[]{:S(2)}, u32[]{:S(2)}) collective-permute-start(bf16[64,256]{1,0:T(8,128)(2,1)S(1)} %get-tuple-element.84), channel_id=1, source_target_pairs={{0,24},{4,28},{8,16},{12,20},{16,8},{20,12},{24,0},{28,4},{1,25},{... | collective-permute-start | bytes 98312 | tf_op jit(solution)/shard_map/ppermute | solution.py:458
  100.0 11.5 %collective-permute-start.39 = (f32[64,256]{1,0:T(8,128)S(1)}, f32[64,256]{1,0:T(8,128)S(1)}, u32[]{:S(2)}, u32[]{:S(2)}) collective-permute-start(f32[64,256]{1,0:T(8,128)S(1)} %add.27.refs_4_), channel_id=1, source_target_pairs={{0,4},{4,0},{8,12},{12,8},{16,20},{20,16},{24,28},{28,24},{1,5},{5... | collective-permute-start | bytes 196616 | tf_op jit(solution)/shard_map/ppermute | solution.py:458
  101.8 6.6 %collective-permute-start.31 = (bf16[64,256]{1,0:T(8,128)(2,1)S(1)}, bf16[64,256]{1,0:T(8,128)(2,1)S(1)}, u32[]{:S(2)}, u32[]{:S(2)}) collective-permute-start(bf16[64,256]{1,0:T(8,128)(2,1)S(1)} %get-tuple-element.90), channel_id=1, source_target_pairs={{0,28},{4,24},{8,20},{12,16},{16,12},{20,8},{24,4},{28,0},{1,29},{... | collective-permute-start | bytes 98312 | tf_op jit(solution)/shard_map/ppermute | solution.py:458
  102.3 6.2 %collective-permute-start.28 = (bf16[64,256]{1,0:T(8,128)(2,1)S(1)}, bf16[64,256]{1,0:T(8,128)(2,1)S(1)}, u32[]{:S(2)}, u32[]{:S(2)}) collective-permute-start(bf16[64,256]{1,0:T(8,128)(2,1)S(1)} %get-tuple-element.87), channel_id=1, source_target_pairs={{0,4},{4,0},{8,12},{12,8},{16,20},{20,16},{24,28},{28,24},{1,5},{5... | collective-permute-start | bytes 98312 | tf_op jit(solution)/shard_map/ppermute | solution.py:458
  103.8 5.0 %collective-permute-start.30 = (bf16[64,256]{1,0:T(8,128)(2,1)S(1)}, bf16[64,256]{1,0:T(8,128)(2,1)S(1)}, u32[]{:S(2)}, u32[]{:S(2)}) collective-permute-start(bf16[64,256]{1,0:T(8,128)(2,1)S(1)} %get-tuple-element.89), channel_id=1, source_target_pairs={{0,12},{4,8},{8,4},{12,0},{16,28},{20,24},{24,20},{28,16},{1,13},{... | collective-permute-start | bytes 98312 | tf_op jit(solution)/shard_map/ppermute | solution.py:458
  108.4 6.5 %collective-permute-start.38 = (f32[64,256]{1,0:T(8,128)S(1)}, f32[64,256]{1,0:T(8,128)S(1)}, u32[]{:S(2)}, u32[]{:S(2)}) collective-permute-start(f32[64,256]{1,0:T(8,128)S(1)} %add.27.refs_4_), channel_id=1, source_target_pairs={{0,1},{1,0},{2,3},{3,2},{4,5},{5,4},{6,7},{7,6},{8,9},{9,8},{10,11... | collective-permute-start | bytes 196616 | tf_op jit(solution)/shard_map/ppermute | solution.py:455
  109.8 4.9 %collective-permute-start.36 = (bf16[64,512]{1,0:T(8,128)(2,1)S(1)}, bf16[64,512]{1,0:T(8,128)(2,1)S(1)}, u32[]{:S(2)}, u32[]{:S(2)}) collective-permute-start(bf16[64,512]{1,0:T(8,128)(2,1)S(1)} %get-tuple-element.103), channel_id=1, source_target_pairs={{0,2},{1,3},{2,0},{3,1},{4,6},{5,7},{6,4},{7,5},{8,10},{9,11},{10,... | collective-permute-start | bytes 196616 | tf_op jit(solution)/shard_map/ppermute | solution.py:455
  (22 other events, 82.0 us)

commit v5 on v4

--- a/solution.py
+++ b/solution.py
@@ -21,9 +21,6 @@
     return pltpu.CompilerParams(vmem_limit_bytes=min(sum(parts) + (6 << 20), 62 << 20))
 
 
-WIDE = pltpu.CompilerParams(vmem_limit_bytes=46 << 20)
-
-
 def shape(dims, dtype):
     return jax.ShapeDtypeStruct(tuple(dims), dtype)
 
@@ -43,11 +40,11 @@
 
 
 def densify_body(
-    rows_ref, fetch_ref, count_ref, blocks_ref, out_ref, held, first, second, older, wide_at, wide_cell, wide_next, sem,
+    rows_ref, fetch_ref, count_ref, held, out_ref, first, second, older, wide_at, wide_cell, wide_next,
     *, n_rep, n_hi, per_list, quarter
 ):
     chunk, row_cell = pl.program_id(0), pl.program_id(1)
-    slots, blk = blocks_ref.shape[0], blocks_ref.shape[1]
+    slots, blk = held.shape[0], held.shape[1]
     all_cols = n_rep * n_hi * per_list
     chunks = all_cols // COL_CHUNK
     deep = n_hi // 2
@@ -55,10 +52,6 @@
     @pl.when((chunk == 0) & (row_cell == 0))
     def _():
         r, q = lax.axis_index("row"), lax.axis_index("rep")
-        copy = pltpu.make_async_copy(blocks_ref, held.at[pl.ds(0, slots)], sem)
-        copy.start()
-        held[slots] = jnp.zeros((blk, blk), BF16)
-
         @pl.loop(0, n_rep * quarter * all_cols, unroll=16)
         def _(cell):
             first[cell] = slots
@@ -88,11 +81,15 @@
             return wide + full.astype(jnp.int32)
 
         lax.fori_loop(0, count_ref[0], link, jnp.int32(0))
-        copy.wait()
+
+    zero = jnp.zeros((blk, blk), BF16)
+
+    def block(slot):
+        return jnp.where(slot < slots, held[jnp.minimum(slot, slots - 1)], zero)
 
     for col in range(COL_CHUNK):
         cell = row_cell * all_cols + chunk * COL_CHUNK + col
-        out_ref[:, col * blk : (col + 1) * blk] = held[first[cell]] + held[second[cell]]
+        out_ref[:, col * blk : (col + 1) * blk] = block(first[cell]) + block(second[cell])
 
     def redo(wide):
         cell = wide_cell[wide]
@@ -127,13 +124,11 @@
         grid_spec=pltpu.PrefetchScalarGridSpec(
             num_scalar_prefetch=3,
             grid=(all_cols // COL_CHUNK, row_blocks),
-            in_specs=[pl.BlockSpec(memory_space=pltpu.HBM)],
+            in_specs=[WHOLE],
             out_specs=pl.BlockSpec((blk, width), lambda c, i, *_: (i, c)),
-            scratch_shapes=[pltpu.VMEM((slots + 1, blk, blk), BF16)]
-            + [pltpu.SMEM((n,), jnp.int32) for n in smem]
-            + [pltpu.SemaphoreType.DMA],
-        ),
-        compiler_params=pltpu.CompilerParams(vmem_limit_bytes=52 << 20),
+            scratch_shapes=[pltpu.SMEM((n,), jnp.int32) for n in smem],
+        ),
+        compiler_params=params(blocks.size * 2, blk * width * 4),
         cost_estimate=pl.CostEstimate(
             flops=slots * blk * blk,
             bytes_accessed=blocks.size * 2 + 2 * all_cols * row_blocks * blk * blk,
@@ -173,7 +168,7 @@
         in_specs=[SMEM] * n_hi + [pl.BlockSpec(memory_space=pltpu.HBM)],
         out_specs=[ANY] * n_hi + [SMEM],
         scratch_shapes=[pltpu.SemaphoreType.DMA((n_hi * per_list,))],
-        compiler_params=params(0),
+        compiler_params=pltpu.CompilerParams(vmem_limit_bytes=53 << 20),
         name="pack",
     )(*lists, features)
 
@@ -213,7 +208,7 @@
             pl.BlockSpec((ROW_TILE, features), lambda i: (jnp.minimum(i, half - 1), 0)),
             pl.BlockSpec((ROW_TILE, features), lambda i: (jnp.maximum(i - half, 0), 0)),
         ],
-        compiler_params=WIDE,
+        compiler_params=params(ROW_TILE * cols * 4, cols * features * 4),
         cost_estimate=pl.CostEstimate(
             flops=2 * rows * cols * features, bytes_accessed=adj.size + cols * features * 2, transcendentals=0
         ),
@@ -222,33 +217,54 @@
 
 
 def middle_body(
-    keep_ref, near_ref, far_ref, weight_ref, cot_ref, out_ref, grad_ref, wsend_ref, wkeep_ref, acc_ref, *, factor
+    keep_ref, near_ref, far_ref, weight_ref, cot_ref, out_ref, near_out, far_out, wkeep_ref, acc_ref, *, factor
 ):
     q = lax.axis_index("rep")
     hidden = (keep_ref[...] + near_ref[...].astype(F32) + far_ref[...].astype(F32)).astype(BF16)
     weight = weight_ref[...]
     pre_act = dot(hidden, weight)
     sig = jax.nn.sigmoid(pre_act)
+    pre_grad = (cot_ref[...].astype(F32) * (sig * (1.0 + pre_act * (1.0 - sig)))).astype(BF16)
+    features, rows = weight.shape[0], hidden.shape[0]
+    input_grad = dot(weight, pre_grad, ((1,), (1,))).astype(BF16)
+    near_out[:features] = input_grad
+    far_out[:features] = input_grad
     out_ref[...] = (pre_act * sig).astype(BF16)
-    pre_grad = (cot_ref[...].astype(F32) * (sig * (1.0 + pre_act * (1.0 - sig)))).astype(BF16)
-    grad_ref[...] = dot(weight, pre_grad, ((1,), (1,))).astype(BF16)
     acc_ref[...] = dot(hidden, pre_grad, ((0,), (0,))) * factor
-    part = wkeep_ref.shape[0] // 2
-    for j in range(4):
-        out = wsend_ref if j & 1 else wkeep_ref
-        at = j // 2 * part
-        out[at : at + part] = acc_ref[pl.ds(pl.multiple_of((q ^ j) * part, part), part), :]
-
-
-def middle(keep, near, far, weight, cot, factor):
+    part = wkeep_ref.shape[0]
+    wkeep_ref[...] = acc_ref[pl.ds(pl.multiple_of(q * part, part), part), :]
+    for j, out, at in ((1, near_out, 0), (2, far_out, 0), (3, far_out, 1)):
+        fold_in(out, features, at, acc_ref[pl.ds(pl.multiple_of((q ^ j) * part, part), part), :])
+
+
+def fold_in(ref, base, at, piece):
+    part, features = piece.shape
+    folds = ref.shape[1] // features
+    depth = part // folds
+    for i in range(folds):
+        ref[base + at * depth : base + (at + 1) * depth, i * features : (i + 1) * features] = piece[
+            i * depth : (i + 1) * depth
+        ].astype(ref.dtype)
+
+
+def fold_out(ref, base, at, part, features):
+    folds = ref.shape[1] // features
+    depth = part // folds
+    rows = ref[base + at * depth : base + (at + 1) * depth, :].astype(F32)
+    return jnp.concatenate([rows[:, i * features : (i + 1) * features] for i in range(folds)], axis=0)
+
+
+def middle(keep, near, far, weight, cot, n_rep, factor):
     rows, features = keep.shape
+    part = features // n_rep
+    extra = part * features // rows
     return pl.pallas_call(
         functools.partial(middle_body, factor=factor),
         out_shape=[
             shape((rows, features), BF16),
-            shape((features, rows), BF16),
-            shape((features // 2, features), F32),
-            shape((features // 2, features), F32),
+            shape((features + extra, rows), BF16),
+            shape((features + 2 * extra, rows), BF16),
+            shape((part, features), F32),
         ],
         in_specs=[WHOLE] * 5,
         out_specs=[WHOLE] * 4,
@@ -261,48 +277,39 @@
     )(keep, near, far, weight, cot)
 
 
-def back_first_body(odd_ref, even_ref, adj_ref, wkeep_ref, got_ref, out_ref, wsend_out, wkeep_out):
-    rows = odd_ref.shape[1]
-    part = wsend_out.shape[0]
+def back_first_body(odd_ref, even_ref, adj_ref, wkeep_ref, out_ref, w_out):
+    features, rows = out_ref.shape[0], odd_ref.shape[1]
+    out_ref[...] = dot(odd_ref[:features], adj_ref[:rows]) + dot(even_ref[:features], adj_ref[rows:])
 
     @pl.when(pl.program_id(0) == 0)
     def _():
-        mine = lax.rem(lax.axis_index("row"), 2) ^ lax.div(lax.axis_index("rep"), 2)
-        for out, at in ((wkeep_out, mine), (wsend_out, 1 - mine)):
-            rows_here = pl.ds(pl.multiple_of(at * part, part), part)
-            out[...] = wkeep_ref[rows_here, :] + got_ref[rows_here, :]
-
-    out_ref[...] = dot(odd_ref[...], adj_ref[:rows]) + dot(even_ref[...], adj_ref[rows:])
-
-
-def back_first(odd, even, adj, wkeep, got):
+        w_out[...] = wkeep_ref[...] + fold_out(odd_ref, features, 0, *w_out.shape)
+
+
+def back_first(odd, even, adj, wkeep):
     rows, cols = adj.shape[0] // 2, adj.shape[1]
-    features = odd.shape[0]
+    features = wkeep.shape[1]
+    whole = lambda x: pl.BlockSpec(x.shape, lambda i: (0, 0))
     return pl.pallas_call(
         back_first_body,
         grid=(cols // COL_TILE,),
-        out_shape=[shape((features, cols), F32)] + [shape((wkeep.shape[0] // 2, features), F32)] * 2,
-        in_specs=[
-            pl.BlockSpec(odd.shape, lambda i: (0, 0)),
-            pl.BlockSpec(even.shape, lambda i: (0, 0)),
-            pl.BlockSpec((rows, COL_TILE), lambda i: (1, i)),
-            pl.BlockSpec(wkeep.shape, lambda i: (0, 0)),
-            pl.BlockSpec(wkeep.shape, lambda i: (0, 0)),
-        ],
-        out_specs=[pl.BlockSpec((features, COL_TILE), lambda i: (0, i))]
-        + [pl.BlockSpec((wkeep.shape[0] // 2, features), lambda i: (0, 0))] * 2,
-        compiler_params=WIDE,
+        out_shape=[shape((features, cols), F32), shape(wkeep.shape, F32)],
+        in_specs=[whole(odd), whole(even), pl.BlockSpec((rows, COL_TILE), lambda i: (1, i)), whole(wkeep)],
+        out_specs=[pl.BlockSpec((features, COL_TILE), lambda i: (0, i)), whole(wkeep)],
+        compiler_params=params(4 << 20),
         cost_estimate=pl.CostEstimate(
             flops=2 * rows * cols * features, bytes_accessed=adj.size + cols * features * 4, transcendentals=0
         ),
         name="back_first",
-    )(odd, even, adj, wkeep, got)
-
-
-def back_second_body(odd_ref, even_ref, adj_ref, first_ref, send_ref, keep_ref, acc_ref):
+    )(odd, even, adj, wkeep)
+
+
+def back_second_body(odd_ref, even_ref, adj_ref, first_ref, w_ref, send_ref, keep_ref, w_out, acc_ref):
     q = lax.axis_index("rep")
-    rows = odd_ref.shape[1]
-    acc_ref[...] = first_ref[...] + dot(odd_ref[...], adj_ref[:rows]) + dot(even_ref[...], adj_ref[rows:])
+    features, rows = first_ref.shape[0], odd_ref.shape[1]
+    acc_ref[...] = (
+        first_ref[...] + dot(odd_ref[:features], adj_ref[:rows]) + dot(even_ref[:features], adj_ref[rows:])
+    )
     part = send_ref.shape[0] // 2
     for j in range(4):
         out = send_ref if j & 1 else keep_ref
@@ -310,35 +317,46 @@
         piece = acc_ref[pl.ds(pl.multiple_of((q ^ j) * part, part), part), :]
         out[at : at + part] = piece.astype(out.dtype)
 
-
-def back_second(odd, even, adj, first, half, n_rep, per_piece):
+    @pl.when(pl.program_id(0) == 0)
+    def _():
+        w_out[...] = (
+            w_ref[...]
+            + fold_out(even_ref, features, 0, *w_out.shape)
+            + fold_out(odd_ref, features, 1, *w_out.shape)
+        )
+
+
+def back_second(odd, even, adj, first, w, half, n_rep, per_piece):
     rows, cols = adj.shape[0] // 2, adj.shape[1] // 2
-    features = odd.shape[0]
+    features = first.shape[0]
     width = cols // n_rep // per_piece
     tiles = cols // width
+    whole = lambda x: pl.BlockSpec(x.shape, lambda i: (0, 0))
     return pl.pallas_call(
         back_second_body,
         grid=(tiles,),
-        out_shape=[shape((features // 2, cols), BF16), shape((features // 2, cols), F32)],
+        out_shape=[shape((features // 2, cols), BF16), shape((features // 2, cols), F32), shape(w.shape, F32)],
         in_specs=[
-            pl.BlockSpec(odd.shape, lambda i: (0, 0)),
-            pl.BlockSpec(even.shape, lambda i: (0, 0)),
+            whole(odd),
+            whole(even),
             pl.BlockSpec((rows, width), lambda i: (0, i + half * tiles)),
             pl.BlockSpec((features, width), lambda i: (0, i + half * tiles)),
+            whole(w),
         ],
         out_specs=[
             pl.BlockSpec(
                 (features // 2, width), lambda i: (0, (lax.div(i, per_piece) ^ 1) * per_piece + lax.rem(i, per_piece))
             ),
             pl.BlockSpec((features // 2, width), lambda i: (0, i)),
+            whole(w),
         ],
         scratch_shapes=[pltpu.VMEM((features, width), F32)],
-        compiler_params=WIDE,
+        compiler_params=params(4 << 20),
         cost_estimate=pl.CostEstimate(
             flops=2 * rows * cols * features, bytes_accessed=rows * cols * 2 + cols * features * 7, transcendentals=0
         ),
         name=f"back_second_{half}",
-    )(odd, even, adj, first)
+    )(odd, even, adj, first, w)
 
 
 def split_body(own_ref, near_ref, far_ref, *outs, n_rep, deep):
@@ -370,8 +388,9 @@
 def collect_body(*refs, n_row, n_rep, per_list, quarter, blk):
     lists = refs[:n_rep]
     messages = refs[n_rep : n_rep + n_row]
-    outs = refs[n_rep + n_row : -1]
-    acc_ref = refs[-1]
+    w_ref, got_ref = refs[n_rep + n_row : n_rep + n_row + 2]
+    outs = refs[n_rep + n_row + 2 : -2]
+    w_out, acc_ref = refs[-2:]
     q = lax.axis_index("rep")
     acc_ref[...] = jnp.zeros(acc_ref.shape, F32)
     for k in range(n_row):
@@ -385,11 +404,16 @@
             cols = pl.ds(pl.multiple_of(cell * blk, blk), blk)
             acc_ref[:, cols] += messages[k][:, c * blk : (c + 1) * blk].astype(F32)
     width = outs[0].shape[1]
+    part = acc_ref.shape[0]
+    w = (w_ref[...] + got_ref[...]).astype(BF16)
+    w_out[...] = w
     for j, out in enumerate(outs):
-        out[...] = acc_ref[:, j * width : (j + 1) * width].astype(out.dtype)
-
-
-def collect(lists, messages, per_list, row_blocks, blk):
+        out[:part] = acc_ref[:, j * width : (j + 1) * width].astype(out.dtype)
+        if j:
+            fold_in(out, part, 0, w)
+
+
+def collect(lists, messages, w, got, per_list, row_blocks, blk):
     n_rep = len(lists)
     n_row = len(messages)
     part = messages[0].shape[0]
@@ -399,45 +423,46 @@
     )
     return pl.pallas_call(
         body,
-        out_shape=[shape((part, quarter * blk), F32 if j == 0 else BF16) for j in range(n_rep)],
-        in_specs=[SMEM] * n_rep + [WHOLE] * n_row,
-        out_specs=[WHOLE] * n_rep,
+        out_shape=[shape((part, quarter * blk), F32)]
+        + [shape((part + w.size // (quarter * blk), quarter * blk), BF16)] * (n_rep - 1)
+        + [shape(w.shape, BF16)],
+        in_specs=[SMEM] * n_rep + [WHOLE] * (n_row + 2),
+        out_specs=[WHOLE] * (n_rep + 1),
         scratch_shapes=[pltpu.VMEM((part, row_blocks * blk), F32)],
         compiler_params=params(4 << 20),
         cost_estimate=pl.CostEstimate(
             flops=part * row_blocks * blk, bytes_accessed=part * row_blocks * blk * 5, transcendentals=0
         ),
         name="collect",
-    )(*lists, *messages)
+    )(*lists, *messages, w, got)
 
 
 def finish_body(*refs, n_rep):
     grads = refs[:n_rep]
-    weights = refs[n_rep : 2 * n_rep]
-    node_ref, weight_ref, acc_ref = refs[2 * n_rep :]
+    w_ref, node_ref, weight_ref, acc_ref = refs[n_rep:]
     q = lax.axis_index("rep")
-    part = grads[0].shape[0]
-    first = lax.rem(q, 2) + 2 * lax.rem(lax.axis_index("row"), 2)
+    part = w_ref.shape[0]
     for j in range(n_rep):
-        acc_ref[pl.ds(pl.multiple_of((q ^ j) * part, part), part), :] = grads[j][...].astype(F32)
-        weight_ref[pl.ds(pl.multiple_of((first ^ j) * part, part), part), :] = weights[j][...]
+        rows = pl.ds(pl.multiple_of((q ^ j) * part, part), part)
+        acc_ref[rows, :] = grads[j][:part].astype(F32)
+        weight_ref[rows, :] = fold_out(grads[j], part, 0, *w_ref.shape) if j else w_ref[...].astype(F32)
     node_ref[...] = acc_ref[...].T
 
 
-def finish(grads, weights):
+def finish(grads, w):
     n_rep = len(grads)
     part, rows = grads[0].shape
-    features = weights[0].shape[1]
+    features = w.shape[1]
     return pl.pallas_call(
         functools.partial(finish_body, n_rep=n_rep),
         out_shape=[shape((rows, part * n_rep), F32), shape((features, features), F32)],
-        in_specs=[WHOLE] * (2 * n_rep),
+        in_specs=[WHOLE] * (n_rep + 1),
         out_specs=[WHOLE] * 2,
         scratch_shapes=[pltpu.VMEM((part * n_rep, rows), F32)],
         compiler_params=params(6 << 20),
         cost_estimate=pl.CostEstimate(flops=0, bytes_accessed=rows * part * n_rep * 8, transcendentals=0),
         name="finish",
-    )(*grads, *weights)
+    )(*grads, w)
 
 
 def local(
@@ -488,18 +513,16 @@
     lists = [own_list] + [to_rep(own_list, j) for j in range(1, n_rep)]
     arrived = after(arrived, keep0, lists)
     factor = float(n_row * band_rows) ** (-0.5)
-    output, grad0, wsend, wkeep = middle(keep0, to_rep(send1, 1), arrived, weight, out_grad, factor)
-
-    grad2 = to_rep(grad0, 2)
+    output, grad0, to_far, w = middle(keep0, to_rep(send1, 1), arrived, weight, out_grad, n_rep, factor)
+
+    grad2 = to_rep(to_far, 2)
     grad1 = to_rep(grad0, 1)
-    first, wsend, wkeep = back_first(grad1, grad0, adj, wkeep, to_rep(wsend, 1))
-    w = wkeep + to_row(wsend, 1)
+    first, w = back_first(grad1, grad0, adj, w)
     grad2 = after(grad2, first)
-    grad3 = after(to_rep(grad2, 1), w)
-    got = to_row(w, 2)
-    send_high, keep_high = back_second(grad3, grad2, adj, first, 1, n_rep, deep)
+    grad3 = to_rep(grad2, 1)
+    send_high, keep_high, w = back_second(grad3, grad2, adj, first, w, 1, n_rep, deep)
     near_high = to_rep(send_high, 1)
-    send_low, keep_low = back_second(grad3, grad2, adj, after(first, send_high), 0, n_rep, deep)
+    send_low, keep_low, _ = back_second(grad3, grad2, adj, after(first, send_high), w, 0, n_rep, deep)
     near_low = to_rep(send_low, 1)
     part = features // n_rep
 
@@ -508,8 +531,7 @@
 
     far_high = to_rep(across_sum(keep_high, after(near_high, send_low)), 2)
     far_low = to_rep(across_sum(keep_low, near_low), 2)
-    w = w + got
-    got = to_row(w, 4)
+    got = to_row(w, 1)
     high = split(keep_high, near_high, far_high, 1, n_rep, deep)
     half_rows = n_row // 2
     back_high = [to_row(x, half_rows + i) for i, x in enumerate(high)]
@@ -518,16 +540,12 @@
     while step < n_row:
         w = w + to_row(w, step)
         step *= 2
-    got = to_rep(w, 2)
+    got = to_row(w, 2)
     low = split(keep_low, near_low, after(far_low, back_high[:-1]), 0, n_rep, deep)
     w = w + after(got, low)
     returned = [low[0]] + [to_row(low[i], i) for i in range(1, half_rows)] + back_high
-    grads = collect(lists, after(returned, w), per_list, row_blocks, blk)
-    other = to_row(w, 1)
-    weights = [w, to_rep(w, 1), other, to_rep(other, 1)]
-    node_grad, weight_grad = finish(
-        [grads[0]] + [to_rep(grads[j], j) for j in range(1, n_rep)], weights
-    )
+    *grads, w = collect(lists, returned, w, to_row(w, 4), per_list, row_blocks, blk)
+    node_grad, weight_grad = finish([grads[0]] + [to_rep(grads[j], j) for j in range(1, n_rep)], w)
     return (output, weight_grad, node_grad)
 
 

time: 116 us -> 107 us (0.922)
  Pallas kernels: 35.5 us -> 24.9 us
  waiting for transfers between devices: 26.6 us -> 35.7 us
  starting transfers between devices: 48.8 us -> 39.9 us
  local copies, waits for them, and re-layouts: 3.35 us -> 4.9 us
    ppermute x26 -> x22, waiting for transfers between devices: 14.9 us -> 28 us  [to_rep(): return lax.ppermute(x, 'rep', xor_perm(n_rep, j))]
    ppermute x26 -> x22, starting transfers between devices: 24.3 us -> 16.9 us  [to_rep(): return lax.ppermute(x, 'rep', xor_perm(n_rep, j))]
    pallas_call x2, Pallas kernels: 7.91 us -> 3.67 us  [forward(): pl.pallas_call(functools.partial(forward_body, n_pieces=len(pieces)), gri...]
    ppermute x11 -> x10, waiting for transfers between devices: 10.7 us -> 6.76 us  [to_row(): return lax.ppermute(x, 'row', xor_perm(n_row, k))]
    pallas_call x1, Pallas kernels: 12.4 us -> 9.36 us  [densify(): pl.pallas_call(body, out_shape=shape((row_blocks * blk, all_cols * blk),...]
    pallas_call x2, Pallas kernels: 6.5 us -> 4.33 us  [back_second(): pl.pallas_call(back_second_body, grid=(tiles,), out_shape=[shape((feature...]
    pallas_call x1, Pallas kernels: 4 us -> 2.27 us  [back_first(): pl.pallas_call(back_first_body, grid=(cols // COL_TILE,), out_shape=[shap...]
    unnamed x11, local copies, waits for them, and re-layouts: 3.35 us -> 4.9 us
  transfers between devices with their start and end apart: 41 -> 36, of which waited for: 16 -> 18; matrix products, arithmetic and copies ran while one was open for 0% -> 0% of each run, Pallas kernels for 21% -> 15%
where the time goes in v5:
time: 107 us
  starting transfers between devices  39.9 us (37%)
  waiting for transfers between devices  35.7 us (33%)
  Pallas kernels  24.9 us (23%)
  local copies, waits for them, and re-layouts  4.9 us (5%)
  between operations  1.52 us (1%)
    ppermute x22, waiting for transfers between devices, to_rep(): return lax.ppermute(x, 'rep', xor_perm(n_rep, j))  28 us
    ppermute x22, starting transfers between devices, to_rep(): return lax.ppermute(x, 'rep', xor_perm(n_rep, j))  16.9 us
    ppermute x10, starting transfers between devices, to_row(): return lax.ppermute(x, 'row', xor_perm(n_row, k))  14.7 us
    pallas_call x1, Pallas kernels, densify(): pl.pallas_call(body, out_shape=shape((row_blocks * blk, all_cols * blk),...  9.36 us
    ppermute x4, starting transfers between devices, spread(): return lax.ppermute(x, ('row', 'rep'), perm)  8.34 us
    ppermute x10, waiting for transfers between devices, to_row(): return lax.ppermute(x, 'row', xor_perm(n_row, k))  6.76 us
    unnamed x11, local copies, waits for them, and re-layouts  4.9 us
    pallas_call x2, Pallas kernels, back_second(): pl.pallas_call(back_second_body, grid=(tiles,), out_shape=[shape((feature...  4.33 us
  transfers between devices with their start and end apart: 36, of which 18 were waited for; matrix products, arithmetic and copies ran while one was open for 0% of the time, Pallas kernels for 15%

profile of v5, /device:TPU:0, one launch (start us, length us, event | category | flops | bytes accessed | tf_op | source)
XLA Modules:
  0.0 107.0 jit_solution(372741166257608937)
XLA Ops:
  1.4 4.0 %collective-permute-start.1 = (s32[1,8,2]{2,1,0:T(8,128)S(1)}, s32[1,8,2]{2,1,0:T(8,128)S(1)}, u32[]{:S(2)}, u32[]{:S(2)}) collective-permute-start(s32[1,8,2]{2,1,0:T(8,128)S(1)} %copy.11), channel_id=1, source_target_pairs={{0,16},{1,21},{2,26},{3,31},{4,20},{5,17},{6,30},{7,27},{8,24},{9,... | collective-permute-start | bytes 200 | tf_op jit(solution)/shard_map/ppermute | solution.py:489
  7.0 2.2 %pack.1 = (bf16[256,256]{1,0:T(8,128)(2,1)S(1)}, bf16[256,256]{1,0:T(8,128)(2,1)S(1)}, s32[128]{0:T(128)S(1)}) custom-call(s32[1,8,2]{2,1,0:T(8,128)S(1)} %collective-permute-done.refs_0_, s32[1,8,2]{2,1,0:T(8,128)S(1)} %collective-permute-done.1.refs_1_, bf16[2048,256]{1,0:T(8,128)(2,1)} %refs_2_.1), custom_call_target="tpu_custom_call" | custom-call | tf_op jit(solution)/shard_map/pack/pallas_call | solution.py:165
  9.9 3.0 %collective-permute-start.6 = (bf16[256,256]{1,0:T(8,128)(2,1)S(1)}, bf16[256,256]{1,0:T(8,128)(2,1)S(1)}, u32[]{:S(2)}, u32[]{:S(2)}) collective-permute-start(bf16[256,256]{1,0:T(8,128)(2,1)S(1)} %get-tuple-element.48), channel_id=1, source_target_pairs={{0,16},{1,21},{2,26},{3,31},{4,20},{5,17},{6,30},{7,27},{8,24},{9,... | collective-permute-start | bytes 393224 | tf_op jit(solution)/shard_map/ppermute | solution.py:489
  13.6 2.8 %copy-done = bf16[192,128,128]{2,1,0:T(8,128)(2,1)S(1)} copy-done((bf16[192,128,128]{2,1,0:T(8,128)(2,1)S(1)}, bf16[192,128,128]{2,1,0:T(8,128)(2,1)}, u32[]{:S(2)}) %copy-start) | copy-done | bytes 6291480
  17.7 9.4 %densify.1.refs_8_.adj_ref = bf16[2048,2048]{1,0:T(8,128)(2,1)S(1)} custom-call(s32[192]{0:T(256)S(1)} %copy-done.3, s32[192]{0:T(256)S(1)} %copy-done.4, s32[1]{0:T(128)S(6)} %copy.13.count_ref, bf16[192,128,128]{2,1,0:T(8,128)(2,1)S(1)} %copy-done), custom_call_target="tpu_custom_call" | custom-call | flops 3145728 | bytes 14680064 | tf_op jit(solution)/shard_map/densify/pallas_call | solution.py:121
  27.1 4.4 %collective-permute-start.8 = (bf16[256,256]{1,0:T(8,128)(2,1)S(1)}, bf16[256,256]{1,0:T(8,128)(2,1)S(1)}, u32[]{:S(2)}, u32[]{:S(2)}) collective-permute-start(bf16[256,256]{1,0:T(8,128)(2,1)S(1)} %collective-permute-done.6.refs_4_), channel_id=1, source_target_pairs={{0,2},{1,3},{2,0},{3,1},{4,6},{5,7},{6,4},{7,5},{8,10},{9,11},{10,... | collective-permute-start | bytes 393224 | tf_op jit(solution)/shard_map/ppermute | solution.py:480
  32.2 3.5 %collective-permute-done.8.refs_6_ = bf16[256,256]{1,0:T(8,128)(2,1)S(1)} collective-permute-done((bf16[256,256]{1,0:T(8,128)(2,1)S(1)}, bf16[256,256]{1,0:T(8,128)(2,1)S(1)}, u32[]{:S(2)}, u32[]{:S(2)}) %collective-permute-start.8) | collective-permute-done | bytes 131104 | tf_op jit(solution)/shard_map/ppermute | solution.py:480
  36.2 2.3 %collective-permute-done.4.refs_2_ = bf16[256,256]{1,0:T(8,128)(2,1)S(1)} collective-permute-done((bf16[256,256]{1,0:T(8,128)(2,1)S(1)}, bf16[256,256]{1,0:T(8,128)(2,1)S(1)}, u32[]{:S(2)}, u32[]{:S(2)}) %collective-permute-start.4) | collective-permute-done | bytes 131104 | tf_op jit(solution)/shard_map/ppermute | solution.py:480
  39.9 1.8 %forward.2 = (bf16[512,256]{1,0:T(8,128)(2,1)S(1)}, f32[512,256]{1,0:T(8,128)S(1)}) custom-call(bf16[256,256]{1,0:T(8,128)(2,1)S(1)} %collective-permute-done.2.refs_0_, bf16[256,256]{1,0:T(8,128)(2,1)S(1)} %collective-permute-done.3.refs_1_, bf16[256,256]{1,0:T(8,128)(2,1)S(1)} %collective-permute-done.4.refs_2_, ...), custom_call_target="tpu_custom_call" | custom-call | flops 1073741824 | bytes 5242880 | tf_op jit(solution)/shard_map/forward/pallas_call | solution.py:201
  43.4 2.2 %collective-permute-start.12 = (bf16[512,256]{1,0:T(8,128)(2,1)S(1)}, bf16[512,256]{1,0:T(8,128)(2,1)S(1)}, u32[]{:S(2)}, u32[]{:S(2)}) collective-permute-start(bf16[512,256]{1,0:T(8,128)(2,1)S(1)} %add_convert_fusion), channel_id=1, source_target_pairs={{0,2},{1,3},{2,0},{3,1},{4,6},{5,7},{6,4},{7,5},{8,10},{9,11},{10,... | collective-permute-start | bytes 786440 | tf_op jit(solution)/shard_map/ppermute | solution.py:480
  45.6 1.8 %forward.3 = (bf16[512,256]{1,0:T(8,128)(2,1)S(1)}, f32[512,256]{1,0:T(8,128)S(1)}) custom-call(bf16[256,256]{1,0:T(8,128)(2,1)S(1)} %collective-permute-done.2.refs_0_, bf16[256,256]{1,0:T(8,128)(2,1)S(1)} %collective-permute-done.3.refs_1_, bf16[256,256]{1,0:T(8,128)(2,1)S(1)} %collective-permute-done.4.refs_2_, ...), custom_call_target="tpu_custom_call" | custom-call | flops 1073741824 | bytes 5242880 | tf_op jit(solution)/shard_map/forward/pallas_call | solution.py:201
  47.6 2.0 %collective-permute-start.14 = (s32[128]{0:T(128)S(1)}, s32[128]{0:T(128)S(1)}, u32[]{:S(2)}, u32[]{:S(2)}) collective-permute-start(s32[128]{0:T(128)S(1)} %get-tuple-element.57.refs_0_), channel_id=1, source_target_pairs={{0,2},{1,3},{2,0},{3,1},{4,6},{5,7},{6,4},{7,5},{8,10},{9,11},{10,... | collective-permute-start | bytes 1544 | tf_op jit(solution)/shard_map/ppermute | solution.py:480
  49.7 2.1 %collective-permute-done.15.refs_3_ = s32[128]{0:T(128)S(1)} collective-permute-done((s32[128]{0:T(128)S(1)}, s32[128]{0:T(128)S(1)}, u32[]{:S(2)}, u32[]{:S(2)}) %collective-permute-start.15) | collective-permute-done | bytes 544 | tf_op jit(solution)/shard_map/ppermute | solution.py:480
  55.2 2.3 %back_first.1 = (f32[256,2048]{1,0:T(8,128)S(1)}, f32[64,256]{1,0:T(8,128)S(1)}) custom-call(bf16[288,512]{1,0:T(8,128)(2,1)S(1)} %collective-permute-done.17.odd_ref, bf16[288,512]{1,0:T(8,128)(2,1)S(1)} %get-tuple-element.61.even_ref, bf16[2048,2048]{1,0:T(8,128)(2,1)S(1)} %densify.1.refs_8_.adj_ref, f32[64,256]{1,0:T(8,128)S(1)} %get-tuple-element.62.wkeep_ref), custom_call_target="tpu_custom_call" | custom-call | flops 1073741824 | bytes 6291456 | tf_op jit(solution)/shard_map/back_first/pallas_call | solution.py:293
  57.5 6.1 %collective-permute-done.16.even_ref = bf16[320,512]{1,0:T(8,128)(2,1)S(1)} collective-permute-done((bf16[320,512]{1,0:T(8,128)(2,1)S(1)}, bf16[320,512]{1,0:T(8,128)(2,1)S(1)}, u32[]{:S(2)}, u32[]{:S(2)}) %collective-permute-start.16) | collective-permute-done | bytes 327712 | tf_op jit(solution)/shard_map/ppermute | solution.py:480
  65.1 1.9 %back_second_1.1 = (bf16[128,1024]{1,0:T(8,128)(2,1)S(1)}, f32[128,1024]{1,0:T(8,128)S(1)}, f32[64,256]{1,0:T(8,128)S(1)}) custom-call(bf16[320,512]{1,0:T(8,128)(2,1)S(1)} %collective-permute-done.18.odd_ref, bf16[320,512]{1,0:T(8,128)(2,1)S(1)} %collective-permute-done.16.even_ref, bf16[2048,2048]{1,0:T(8,128)(2,1)S(1)} %densify.1.refs_8_.adj_ref, ...), custom_call_target="tpu_custom_call" | custom-call | flops 536870912 | bytes 3932160 | tf_op jit(solution)/shard_map/back_second_1/pallas_call | solution.py:335
  67.2 2.5 %back_second_0.1 = (bf16[128,1024]{1,0:T(8,128)(2,1)S(1)}, f32[128,1024]{1,0:T(8,128)S(1)}, f32[64,256]{1,0:T(8,128)}) custom-call(bf16[320,512]{1,0:T(8,128)(2,1)S(1)} %collective-permute-done.18.odd_ref, bf16[320,512]{1,0:T(8,128)(2,1)S(1)} %collective-permute-done.16.even_ref, bf16[2048,2048]{1,0:T(8,128)(2,1)S(1)} %densify.1.refs_8_.adj_ref, ...), custom_call_target="tpu_custom_call" | custom-call | flops 536870912 | bytes 3932160 | tf_op jit(solution)/shard_map/back_second_0/pallas_call | solution.py:335
  71.5 1.9 %collective-permute-start.22 = (bf16[64,1024]{1,0:T(8,128)(2,1)S(1)}, bf16[64,1024]{1,0:T(8,128)(2,1)S(1)}, u32[]{:S(2)}, u32[]{:S(2)}) collective-permute-start(bf16[64,1024]{1,0:T(8,128)(2,1)S(1)} %add_convert_fusion.1), channel_id=1, source_target_pairs={{0,2},{1,3},{2,0},{3,1},{4,6},{5,7},{6,4},{7,5},{8,10},{9,11},{10,... | collective-permute-start | bytes 393224 | tf_op jit(solution)/shard_map/ppermute | solution.py:480
  73.7 4.2 %collective-permute-done.22.far_ref = bf16[64,1024]{1,0:T(8,128)(2,1)S(1)} collective-permute-done((bf16[64,1024]{1,0:T(8,128)(2,1)S(1)}, bf16[64,1024]{1,0:T(8,128)(2,1)S(1)}, u32[]{:S(2)}, u32[]{:S(2)}) %collective-permute-start.22) | collective-permute-done | bytes 131104 | tf_op jit(solution)/shard_map/ppermute | solution.py:480
  78.0 1.8 %collective-permute-start.31 = (f32[64,256]{1,0:T(8,128)S(1)}, f32[64,256]{1,0:T(8,128)S(1)}, u32[]{:S(2)}, u32[]{:S(2)}) collective-permute-start(f32[64,256]{1,0:T(8,128)S(1)} %add.18), channel_id=1, source_target_pairs={{0,8},{4,12},{8,0},{12,4},{16,24},{20,28},{24,16},{28,20},{1,9},{5... | collective-permute-start | bytes 196616 | tf_op jit(solution)/shard_map/ppermute | solution.py:483
  82.5 2.4 %collective-permute-start.25 = (bf16[64,256]{1,0:T(8,128)(2,1)S(1)}, bf16[64,256]{1,0:T(8,128)(2,1)S(1)}, u32[]{:S(2)}, u32[]{:S(2)}) collective-permute-start(bf16[64,256]{1,0:T(8,128)(2,1)S(1)} %get-tuple-element.75), channel_id=1, source_target_pairs={{0,24},{4,28},{8,16},{12,20},{16,8},{20,12},{24,0},{28,4},{1,25},{... | collective-permute-start | bytes 98312 | tf_op jit(solution)/shard_map/ppermute | solution.py:483
  90.8 2.0 %collective-permute-start.26 = (bf16[64,256]{1,0:T(8,128)(2,1)S(1)}, bf16[64,256]{1,0:T(8,128)(2,1)S(1)}, u32[]{:S(2)}, u32[]{:S(2)}) collective-permute-start(bf16[64,256]{1,0:T(8,128)(2,1)S(1)} %get-tuple-element.78), channel_id=1, source_target_pairs={{0,4},{4,0},{8,12},{12,8},{16,20},{20,16},{24,28},{28,24},{1,5},{5... | collective-permute-start | bytes 98312 | tf_op jit(solution)/shard_map/ppermute | solution.py:483
  99.0 1.9 %collective-permute-start.34 = (bf16[96,512]{1,0:T(8,128)(2,1)S(1)}, bf16[96,512]{1,0:T(8,128)(2,1)S(1)}, u32[]{:S(2)}, u32[]{:S(2)}) collective-permute-start(bf16[96,512]{1,0:T(8,128)(2,1)S(1)} %get-tuple-element.86), channel_id=1, source_target_pairs={{0,2},{1,3},{2,0},{3,1},{4,6},{5,7},{6,4},{7,5},{8,10},{9,11},{10,... | collective-permute-start | bytes 294920 | tf_op jit(solution)/shard_map/ppermute | solution.py:480
  100.9 3.7 %collective-permute-done.34.refs_2_ = bf16[96,512]{1,0:T(8,128)(2,1)S(1)} collective-permute-done((bf16[96,512]{1,0:T(8,128)(2,1)S(1)}, bf16[96,512]{1,0:T(8,128)(2,1)S(1)}, u32[]{:S(2)}, u32[]{:S(2)}) %collective-permute-start.34) | collective-permute-done | bytes 98336 | tf_op jit(solution)/shard_map/ppermute | solution.py:480
  (76 shorter events, 33.5 us)
Async XLA Ops:
  1.4 5.6 %collective-permute-start.1 = (s32[1,8,2]{2,1,0:T(8,128)S(1)}, s32[1,8,2]{2,1,0:T(8,128)S(1)}, u32[]{:S(2)}, u32[]{:S(2)}) collective-permute-start(s32[1,8,2]{2,1,0:T(8,128)S(1)} %copy.11), channel_id=1, source_target_pairs={{0,16},{1,21},{2,26},{3,31},{4,20},{5,17},{6,30},{7,27},{8,24},{9,... | collective-permute-start | bytes 200 | tf_op jit(solution)/shard_map/ppermute | solution.py:489
  9.3 17.8 %collective-permute-start.2 = (bf16[256,256]{1,0:T(8,128)(2,1)S(1)}, bf16[256,256]{1,0:T(8,128)(2,1)S(1)}, u32[]{:S(2)}, u32[]{:S(2)}) collective-permute-start(bf16[256,256]{1,0:T(8,128)(2,1)S(1)} %get-tuple-element.47), channel_id=1, source_target_pairs={{0,0},{1,5},{2,10},{3,15},{4,4},{5,1},{6,14},{7,11},{8,8},{9,13},{... | collective-permute-start | bytes 393224 | tf_op jit(solution)/shard_map/ppermute | solution.py:489
  9.9 17.2 %collective-permute-start.6 = (bf16[256,256]{1,0:T(8,128)(2,1)S(1)}, bf16[256,256]{1,0:T(8,128)(2,1)S(1)}, u32[]{:S(2)}, u32[]{:S(2)}) collective-permute-start(bf16[256,256]{1,0:T(8,128)(2,1)S(1)} %get-tuple-element.48), channel_id=1, source_target_pairs={{0,16},{1,21},{2,26},{3,31},{4,20},{5,17},{6,30},{7,27},{8,24},{9,... | collective-permute-start | bytes 393224 | tf_op jit(solution)/shard_map/ppermute | solution.py:489
  27.1 8.6 %collective-permute-start.8 = (bf16[256,256]{1,0:T(8,128)(2,1)S(1)}, bf16[256,256]{1,0:T(8,128)(2,1)S(1)}, u32[]{:S(2)}, u32[]{:S(2)}) collective-permute-start(bf16[256,256]{1,0:T(8,128)(2,1)S(1)} %collective-permute-done.6.refs_4_), channel_id=1, source_target_pairs={{0,2},{1,3},{2,0},{3,1},{4,6},{5,7},{6,4},{7,5},{8,10},{9,11},{10,... | collective-permute-start | bytes 393224 | tf_op jit(solution)/shard_map/ppermute | solution.py:480
  31.5 7.0 %collective-permute-start.4 = (bf16[256,256]{1,0:T(8,128)(2,1)S(1)}, bf16[256,256]{1,0:T(8,128)(2,1)S(1)}, u32[]{:S(2)}, u32[]{:S(2)}) collective-permute-start(bf16[256,256]{1,0:T(8,128)(2,1)S(1)} %collective-permute-done.2.refs_0_), channel_id=1, source_target_pairs={{0,2},{1,3},{2,0},{3,1},{4,6},{5,7},{6,4},{7,5},{8,10},{9,11},{10,... | collective-permute-start | bytes 393224 | tf_op jit(solution)/shard_map/ppermute | solution.py:480
  31.6 7.0 %collective-permute-start.3 = (bf16[256,256]{1,0:T(8,128)(2,1)S(1)}, bf16[256,256]{1,0:T(8,128)(2,1)S(1)}, u32[]{:S(2)}, u32[]{:S(2)}) collective-permute-start(bf16[256,256]{1,0:T(8,128)(2,1)S(1)} %collective-permute-done.2.refs_0_), channel_id=1, source_target_pairs={{0,1},{1,0},{2,3},{3,2},{4,5},{5,4},{6,7},{7,6},{8,9},{9,8},{10,11... | collective-permute-start | bytes 393224 | tf_op jit(solution)/shard_map/ppermute | solution.py:480
  32.2 6.4 %collective-permute-start.7 = (bf16[256,256]{1,0:T(8,128)(2,1)S(1)}, bf16[256,256]{1,0:T(8,128)(2,1)S(1)}, u32[]{:S(2)}, u32[]{:S(2)}) collective-permute-start(bf16[256,256]{1,0:T(8,128)(2,1)S(1)} %collective-permute-done.6.refs_4_), channel_id=1, source_target_pairs={{0,1},{1,0},{2,3},{3,2},{4,5},{5,4},{6,7},{7,6},{8,9},{9,8},{10,11... | collective-permute-start | bytes 393224 | tf_op jit(solution)/shard_map/ppermute | solution.py:480
  43.4 8.9 %collective-permute-start.12 = (bf16[512,256]{1,0:T(8,128)(2,1)S(1)}, bf16[512,256]{1,0:T(8,128)(2,1)S(1)}, u32[]{:S(2)}, u32[]{:S(2)}) collective-permute-start(bf16[512,256]{1,0:T(8,128)(2,1)S(1)} %add_convert_fusion), channel_id=1, source_target_pairs={{0,2},{1,3},{2,0},{3,1},{4,6},{5,7},{6,4},{7,5},{8,10},{9,11},{10,... | collective-permute-start | bytes 786440 | tf_op jit(solution)/shard_map/ppermute | solution.py:480
  47.4 4.9 %collective-permute-start.11 = (bf16[512,256]{1,0:T(8,128)(2,1)S(1)}, bf16[512,256]{1,0:T(8,128)(2,1)S(1)}, u32[]{:S(2)}, u32[]{:S(2)}) collective-permute-start(bf16[512,256]{1,0:T(8,128)(2,1)S(1)} %get-tuple-element.55), channel_id=1, source_target_pairs={{0,1},{1,0},{2,3},{3,2},{4,5},{5,4},{6,7},{7,6},{8,9},{9,8},{10,11... | collective-permute-start | bytes 786440 | tf_op jit(solution)/shard_map/ppermute | solution.py:480
  47.6 4.6 %collective-permute-start.14 = (s32[128]{0:T(128)S(1)}, s32[128]{0:T(128)S(1)}, u32[]{:S(2)}, u32[]{:S(2)}) collective-permute-start(s32[128]{0:T(128)S(1)} %get-tuple-element.57.refs_0_), channel_id=1, source_target_pairs={{0,2},{1,3},{2,0},{3,1},{4,6},{5,7},{6,4},{7,5},{8,10},{9,11},{10,... | collective-permute-start | bytes 1544 | tf_op jit(solution)/shard_map/ppermute | solution.py:480
  53.4 10.1 %collective-permute-start.16 = (bf16[320,512]{1,0:T(8,128)(2,1)S(1)}, bf16[320,512]{1,0:T(8,128)(2,1)S(1)}, u32[]{:S(2)}, u32[]{:S(2)}) collective-permute-start(bf16[320,512]{1,0:T(8,128)(2,1)S(1)} %get-tuple-element.60), channel_id=1, source_target_pairs={{0,2},{1,3},{2,0},{3,1},{4,6},{5,7},{6,4},{7,5},{8,10},{9,11},{10,... | collective-permute-start | bytes 983048 | tf_op jit(solution)/shard_map/ppermute | solution.py:480
  70.1 7.9 %collective-permute-start.30 = (f32[64,256]{1,0:T(8,128)S(1)}, f32[64,256]{1,0:T(8,128)S(1)}, u32[]{:S(2)}, u32[]{:S(2)}) collective-permute-start(f32[64,256]{1,0:T(8,128)S(1)} %get-tuple-element.68.w_ref), channel_id=1, source_target_pairs={{0,4},{4,0},{8,12},{12,8},{16,20},{20,16},{24,28},{28,24},{1,5},{5... | collective-permute-start | bytes 196616 | tf_op jit(solution)/shard_map/ppermute | solution.py:483
  71.5 6.4 %collective-permute-start.22 = (bf16[64,1024]{1,0:T(8,128)(2,1)S(1)}, bf16[64,1024]{1,0:T(8,128)(2,1)S(1)}, u32[]{:S(2)}, u32[]{:S(2)}) collective-permute-start(bf16[64,1024]{1,0:T(8,128)(2,1)S(1)} %add_convert_fusion.1), channel_id=1, source_target_pairs={{0,2},{1,3},{2,0},{3,1},{4,6},{5,7},{6,4},{7,5},{8,10},{9,11},{10,... | collective-permute-start | bytes 393224 | tf_op jit(solution)/shard_map/ppermute | solution.py:480
  73.4 11.6 %collective-permute-start.20 = (bf16[64,1024]{1,0:T(8,128)(2,1)S(1)}, bf16[64,1024]{1,0:T(8,128)(2,1)S(1)}, u32[]{:S(2)}, u32[]{:S(2)}) collective-permute-start(bf16[64,1024]{1,0:T(8,128)(2,1)S(1)} %add_convert_fusion.2), channel_id=1, source_target_pairs={{0,2},{1,3},{2,0},{3,1},{4,6},{5,7},{6,4},{7,5},{8,10},{9,11},{10,... | collective-permute-start | bytes 393224 | tf_op jit(solution)/shard_map/ppermute | solution.py:480
  78.0 10.3 %collective-permute-start.31 = (f32[64,256]{1,0:T(8,128)S(1)}, f32[64,256]{1,0:T(8,128)S(1)}, u32[]{:S(2)}, u32[]{:S(2)}) collective-permute-start(f32[64,256]{1,0:T(8,128)S(1)} %add.18), channel_id=1, source_target_pairs={{0,8},{4,12},{8,0},{12,4},{16,24},{20,28},{24,16},{28,20},{1,9},{5... | collective-permute-start | bytes 196616 | tf_op jit(solution)/shard_map/ppermute | solution.py:483
  79.8 5.6 %collective-permute-start.23 = (bf16[64,256]{1,0:T(8,128)(2,1)S(1)}, bf16[64,256]{1,0:T(8,128)(2,1)S(1)}, u32[]{:S(2)}, u32[]{:S(2)}) collective-permute-start(bf16[64,256]{1,0:T(8,128)(2,1)S(1)} %get-tuple-element.73), channel_id=1, source_target_pairs={{0,16},{4,20},{8,24},{12,28},{16,0},{20,4},{24,8},{28,12},{1,17},{... | collective-permute-start | bytes 98312 | tf_op jit(solution)/shard_map/ppermute | solution.py:483
  81.0 5.7 %collective-permute-start.24 = (bf16[64,256]{1,0:T(8,128)(2,1)S(1)}, bf16[64,256]{1,0:T(8,128)(2,1)S(1)}, u32[]{:S(2)}, u32[]{:S(2)}) collective-permute-start(bf16[64,256]{1,0:T(8,128)(2,1)S(1)} %get-tuple-element.74), channel_id=1, source_target_pairs={{0,20},{4,16},{8,28},{12,24},{16,4},{20,0},{24,12},{28,8},{1,21},{... | collective-permute-start | bytes 98312 | tf_op jit(solution)/shard_map/ppermute | solution.py:483
  82.5 5.7 %collective-permute-start.25 = (bf16[64,256]{1,0:T(8,128)(2,1)S(1)}, bf16[64,256]{1,0:T(8,128)(2,1)S(1)}, u32[]{:S(2)}, u32[]{:S(2)}) collective-permute-start(bf16[64,256]{1,0:T(8,128)(2,1)S(1)} %get-tuple-element.75), channel_id=1, source_target_pairs={{0,24},{4,28},{8,16},{12,20},{16,8},{20,12},{24,0},{28,4},{1,25},{... | collective-permute-start | bytes 98312 | tf_op jit(solution)/shard_map/ppermute | solution.py:483
  88.3 9.8 %collective-permute-start.32 = (f32[64,256]{1,0:T(8,128)S(1)}, f32[64,256]{1,0:T(8,128)S(1)}, u32[]{:S(2)}, u32[]{:S(2)}) collective-permute-start(f32[64,256]{1,0:T(8,128)S(1)} %add.19.refs_12_), channel_id=1, source_target_pairs={{0,16},{4,20},{8,24},{12,28},{16,0},{20,4},{24,8},{28,12},{1,17},{... | collective-permute-start | bytes 196616 | tf_op jit(solution)/shard_map/ppermute | solution.py:483
  89.5 6.7 %collective-permute-start.29 = (bf16[64,256]{1,0:T(8,128)(2,1)S(1)}, bf16[64,256]{1,0:T(8,128)(2,1)S(1)}, u32[]{:S(2)}, u32[]{:S(2)}) collective-permute-start(bf16[64,256]{1,0:T(8,128)(2,1)S(1)} %get-tuple-element.81), channel_id=1, source_target_pairs={{0,28},{4,24},{8,20},{12,16},{16,12},{20,8},{24,4},{28,0},{1,29},{... | collective-permute-start | bytes 98312 | tf_op jit(solution)/shard_map/ppermute | solution.py:483
  90.8 5.4 %collective-permute-start.26 = (bf16[64,256]{1,0:T(8,128)(2,1)S(1)}, bf16[64,256]{1,0:T(8,128)(2,1)S(1)}, u32[]{:S(2)}, u32[]{:S(2)}) collective-permute-start(bf16[64,256]{1,0:T(8,128)(2,1)S(1)} %get-tuple-element.78), channel_id=1, source_target_pairs={{0,4},{4,0},{8,12},{12,8},{16,20},{20,16},{24,28},{28,24},{1,5},{5... | collective-permute-start | bytes 98312 | tf_op jit(solution)/shard_map/ppermute | solution.py:483
  93.3 4.8 %collective-permute-start.28 = (bf16[64,256]{1,0:T(8,128)(2,1)S(1)}, bf16[64,256]{1,0:T(8,128)(2,1)S(1)}, u32[]{:S(2)}, u32[]{:S(2)}) collective-permute-start(bf16[64,256]{1,0:T(8,128)(2,1)S(1)} %get-tuple-element.80), channel_id=1, source_target_pairs={{0,12},{4,8},{8,4},{12,0},{16,28},{20,24},{24,20},{28,16},{1,13},{... | collective-permute-start | bytes 98312 | tf_op jit(solution)/shard_map/ppermute | solution.py:483
  99.0 5.6 %collective-permute-start.34 = (bf16[96,512]{1,0:T(8,128)(2,1)S(1)}, bf16[96,512]{1,0:T(8,128)(2,1)S(1)}, u32[]{:S(2)}, u32[]{:S(2)}) collective-permute-start(bf16[96,512]{1,0:T(8,128)(2,1)S(1)} %get-tuple-element.86), channel_id=1, source_target_pairs={{0,2},{1,3},{2,0},{3,1},{4,6},{5,7},{6,4},{7,5},{8,10},{9,11},{10,... | collective-permute-start | bytes 294920 | tf_op jit(solution)/shard_map/ppermute | solution.py:480
  100.8 5.1 %collective-permute-start.35 = (bf16[96,512]{1,0:T(8,128)(2,1)S(1)}, bf16[96,512]{1,0:T(8,128)(2,1)S(1)}, u32[]{:S(2)}, u32[]{:S(2)}) collective-permute-start(bf16[96,512]{1,0:T(8,128)(2,1)S(1)} %get-tuple-element.87), channel_id=1, source_target_pairs={{0,3},{1,2},{2,1},{3,0},{4,7},{5,6},{6,5},{7,4},{8,11},{9,10},{10,... | collective-permute-start | bytes 294920 | tf_op jit(solution)/shard_map/ppermute | solution.py:480
  (17 other events, 57.0 us)

commit v6 on v5

v6 whole, which is shorter than its diff:
```python
import functools

import jax
import jax.numpy as jnp
from jax import lax
from jax.experimental import pallas as pl
from jax.experimental.pallas import tpu as pltpu
from jax.sharding import PartitionSpec as P

BF16 = jnp.bfloat16
F32 = jnp.float32
COL_CHUNK = 16
ROW_TILE = 256
COL_TILE = 512
WHOLE = pl.BlockSpec(memory_space=pltpu.VMEM)
SMEM = pl.BlockSpec(memory_space=pltpu.SMEM)
ANY = pl.BlockSpec(memory_space=pl.ANY)


def params(*parts):
    return pltpu.CompilerParams(vmem_limit_bytes=min(sum(parts) + (6 << 20), 62 << 20))


def shape(dims, dtype):
    return jax.ShapeDtypeStruct(tuple(dims), dtype)


def dot(a, b, dims=((1,), (0,))):
    return lax.dot_general(a, b, (dims, ((), ())), preferred_element_type=F32)


def xor_perm(count, offset):
    return [(i, i ^ offset) for i in range(count)]


def div_rem(x, n):
    if n & (n - 1) == 0:
        return x >> (n.bit_length() - 1), x & (n - 1)
    return lax.div(x, n), lax.rem(x, n)


class Table:
    def __init__(self, slots, cells):
        self.groups = cells // COL_CHUNK
        self.first = 0
        self.second = cells
        self.older = 2 * cells
        self.wide_at = self.older + slots + 1
        self.wide_cell = self.wide_at + self.groups
        self.wide_next = self.wide_cell + slots
        self.size = -(-(self.wide_next + slots) // 128) * 128


def lists_body(rows_ref, fetch_ref, count_ref, out_ref, *, slots, n_rep, n_hi, per_list, quarter):
    r, q = lax.axis_index("row"), lax.axis_index("rep")
    all_cols = n_rep * n_hi * per_list
    chunks = all_cols // COL_CHUNK
    deep = n_hi // 2
    t = Table(slots, n_rep * quarter * all_cols)

    @pl.loop(0, t.older, unroll=16)
    def _(at):
        out_ref[at] = slots

    @pl.loop(0, t.groups, unroll=16)
    def _(at):
        out_ref[t.wide_at + at] = -1

    out_ref[t.older + slots] = slots

    def link(slot, wide):
        row_high, row_low = div_rem(rows_ref[slot], quarter)
        source, c = div_rem(fetch_ref[slot], per_list)
        hi, low = div_rem(source ^ r, n_rep)
        half, hi = div_rem(hi, deep)
        row = (n_rep - 1 - (row_high ^ q)) * quarter + row_low
        col = ((half * n_rep + (low ^ q)) * deep + hi) * per_list + c
        cell = row * all_cols + col
        at = t.wide_at + row * chunks + div_rem(col, COL_CHUNK)[0]
        one, two, begin = out_ref[t.first + cell], out_ref[t.second + cell], out_ref[at]
        out_ref[t.first + cell] = slot
        out_ref[t.second + cell] = one
        out_ref[t.older + slot] = one
        full = two != slots
        out_ref[t.wide_cell + wide] = cell
        out_ref[t.wide_next + wide] = begin
        out_ref[at] = jnp.where(full, wide, begin)
        return wide + full.astype(jnp.int32)

    lax.fori_loop(0, count_ref[0], link, jnp.int32(0))


def slot_lists(block_rows, block_fetch, block_count, n_row, n_rep, per_list, row_blocks):
    slots = block_rows.shape[0]
    body = functools.partial(
        lists_body,
        slots=slots,
        n_rep=n_rep,
        n_hi=n_row // n_rep,
        per_list=per_list,
        quarter=row_blocks // n_rep,
    )
    return pl.pallas_call(
        body,
        out_shape=shape((Table(slots, row_blocks * n_row * per_list).size,), jnp.int32),
        in_specs=[SMEM] * 3,
        out_specs=SMEM,
        compiler_params=pltpu.CompilerParams(vmem_limit_bytes=56 << 20),
        cost_estimate=pl.CostEstimate(flops=3 << 30, bytes_accessed=8 * slots, transcendentals=0),
        name="slot_lists",
    )(block_rows, block_fetch, block_count)


def densify_body(table_ref, held, out_ref, *, all_cols, row_blocks):
    chunk, row_cell = pl.program_id(0), pl.program_id(1)
    slots, blk = held.shape[0], held.shape[1]
    t = Table(slots, row_blocks * all_cols)
    zero = jnp.zeros((blk, blk), BF16)

    def block(slot):
        return jnp.where(slot < slots, held[jnp.minimum(slot, slots - 1)], zero)

    for col in range(COL_CHUNK):
        cell = row_cell * all_cols + chunk * COL_CHUNK + col
        total = block(table_ref[t.first + cell]) + block(table_ref[t.second + cell])
        out_ref[:, col * blk : (col + 1) * blk] = total

    def redo(wide):
        cell = table_ref[t.wide_cell + wide]
        two = table_ref[t.second + cell]
        three = table_ref[t.older + two]
        four = table_ref[t.older + three]
        total = held[table_ref[t.first + cell]].astype(F32) + held[two].astype(F32)
        total = total + (held[three].astype(F32) + block(four).astype(F32))
        col = cell - row_cell * all_cols - chunk * COL_CHUNK
        place = (slice(None), pl.ds(pl.multiple_of(col * blk, blk), blk))
        out_ref[place] = total.astype(BF16)
        five = table_ref[t.older + four]

        @pl.when(five < slots)
        def _():
            def more(carry):
                slot, total = carry
                return table_ref[t.older + slot], total + held[slot].astype(F32)

            _, rest = lax.while_loop(lambda carry: carry[0] < slots, more, (five, total))
            out_ref[place] = rest.astype(BF16)

        return table_ref[t.wide_next + wide]

    begin = table_ref[t.wide_at + row_cell * (all_cols // COL_CHUNK) + chunk]
    lax.while_loop(lambda wide: wide >= 0, redo, begin)


def densify(table, blocks, n_row, per_list, row_blocks):
    slots, blk, _ = blocks.shape
    all_cols = n_row * per_list
    width = COL_CHUNK * blk
    return pl.pallas_call(
        functools.partial(densify_body, all_cols=all_cols, row_blocks=row_blocks),
        out_shape=shape((row_blocks * blk, all_cols * blk), BF16),
        grid_spec=pltpu.PrefetchScalarGridSpec(
            num_scalar_prefetch=1,
            grid=(all_cols // COL_CHUNK, row_blocks),
            in_specs=[WHOLE],
            out_specs=pl.BlockSpec((blk, width), lambda c, i, *_: (i, c)),
        ),
        compiler_params=params(blocks.size * 2, blk * width * 4),
        cost_estimate=pl.CostEstimate(
            flops=slots * blk * blk,
            bytes_accessed=blocks.size * 2 + 2 * all_cols * row_blocks * blk * blk,
            transcendentals=0,
        ),
        name="densify",
    )(table, blocks)


def pack_body(*refs, n_hi, per_list, blk):
    lists = refs[:n_hi]
    features = refs[n_hi]
    outs = refs[n_hi + 1 : 2 * n_hi + 1]
    own_list, sems = refs[2 * n_hi + 1 :]
    r = lax.axis_index("row")
    copies = []
    for hi in range(n_hi):
        for c in range(per_list):
            b = lists[hi][0, r, c]
            own_list[hi * per_list + c] = b
            copy = pltpu.make_async_copy(
                features.at[pl.ds(pl.multiple_of(b * blk, blk), blk)],
                outs[hi].at[pl.ds(c * blk, blk)],
                sems.at[hi * per_list + c],
            )
            copy.start()
            copies.append(copy)
    for copy in copies:
        copy.wait()


def pack(lists, features, per_list, blk):
    n_hi = len(lists)
    return pl.pallas_call(
        functools.partial(pack_body, n_hi=n_hi, per_list=per_list, blk=blk),
        out_shape=[shape((per_list * blk, features.shape[1]), BF16)] * n_hi + [shape((128,), jnp.int32)],
        in_specs=[SMEM] * n_hi + [pl.BlockSpec(memory_space=pltpu.HBM)],
        out_specs=[ANY] * n_hi + [SMEM],
        scratch_shapes=[pltpu.SemaphoreType.DMA((n_hi * per_list,))],
        compiler_params=pltpu.CompilerParams(vmem_limit_bytes=53 << 20),
        name="pack",
    )(*lists, features)


def forward_body(*refs, n_rep):
    pieces = refs[:n_rep]
    adj_ref, send_ref, keep_ref = refs[n_rep:]
    i = pl.program_id(0)
    depth = pieces[0].shape[0] // 2
    total = 0.0
    for half in range(2):
        for j in range(n_rep):
            at = (half * n_rep + j) * depth
            total += dot(adj_ref[:, at : at + depth], pieces[j][half * depth : (half + 1) * depth])

    half = pl.num_programs(0) // 2

    @pl.when(i < half)
    def _():
        send_ref[...] = total.astype(BF16)

    @pl.when(i >= half)
    def _():
        keep_ref[...] = total


def forward(pieces, adj, half_index):
    rows, cols = adj.shape[0] // 2, adj.shape[1]
    features = pieces[0].shape[1]
    tiles = rows // ROW_TILE
    half = tiles // 2
    return pl.pallas_call(
        functools.partial(forward_body, n_rep=len(pieces)),
        grid=(tiles,),
        out_shape=[shape((rows // 2, features), BF16), shape((rows // 2, features), F32)],
        in_specs=[pl.BlockSpec(x.shape, lambda i: (0, 0)) for x in pieces]
        + [pl.BlockSpec((ROW_TILE, cols), lambda i: (i + half_index * tiles, 0))],
        out_specs=[
            pl.BlockSpec((ROW_TILE, features), lambda i: (jnp.minimum(i, half - 1), 0)),
            pl.BlockSpec((ROW_TILE, features), lambda i: (jnp.maximum(i - half, 0), 0)),
        ],
        compiler_params=params(ROW_TILE * cols * 4, cols * features * 4),
        cost_estimate=pl.CostEstimate(
            flops=2 * rows * cols * features, bytes_accessed=adj.size + cols * features * 2, transcendentals=0
        ),
        name="forward",
    )(*pieces, adj)


def middle_body(
    keep_ref, near_ref, far_ref, weight_ref, cot_ref, out_ref, near_out, far_out, wkeep_ref, acc_ref, *, factor
):
    q = lax.axis_index("rep")
    hidden = (keep_ref[...] + near_ref[...].astype(F32) + far_ref[...].astype(F32)).astype(BF16)
    weight = weight_ref[...]
    pre_act = dot(hidden, weight)
    sig = jax.nn.sigmoid(pre_act)
    pre_grad = (cot_ref[...].astype(F32) * (sig * (1.0 + pre_act * (1.0 - sig)))).astype(BF16)
    features, rows = weight.shape[0], hidden.shape[0]
    input_grad = dot(weight, pre_grad, ((1,), (1,))).astype(BF16)
    near_out[:features] = input_grad
    far_out[...] = input_grad
    out_ref[...] = (pre_act * sig).astype(BF16)
    acc_ref[...] = dot(hidden, pre_grad, ((0,), (0,))) * factor
    part = wkeep_ref.shape[0] // 2
    for j in range(4):
        piece = acc_ref[pl.ds(pl.multiple_of((q ^ j) * part, part), part), :]
        if j & 1:
            fold_in(near_out, features, j // 2, piece)
        else:
            wkeep_ref[j // 2 * part : (j // 2 + 1) * part] = piece


def fold_in(ref, base, at, piece):
    part, features = piece.shape
    folds = ref.shape[1] // features
    depth = part // folds
    for i in range(folds):
        ref[base + at * depth : base + (at + 1) * depth, i * features : (i + 1) * features] = piece[
            i * depth : (i + 1) * depth
        ].astype(ref.dtype)


def fold_out(ref, base, at, part, features):
    folds = ref.shape[1] // features
    depth = part // folds
    rows = ref[base + at * depth : base + (at + 1) * depth, :].astype(F32)
    return jnp.concatenate([rows[:, i * features : (i + 1) * features] for i in range(folds)], axis=0)


def middle(keep, near, far, weight, cot, n_rep, factor):
    rows, features = keep.shape
    part = features // n_rep
    extra = part * features // rows
    return pl.pallas_call(
        functools.partial(middle_body, factor=factor),
        out_shape=[
            shape((rows, features), BF16),
            shape((features + 2 * extra, rows), BF16),
            shape((features, rows), BF16),
            shape((2 * part, features), F32),
        ],
        in_specs=[WHOLE] * 5,
        out_specs=[WHOLE] * 4,
        scratch_shapes=[pltpu.VMEM((features, features), F32)],
        compiler_params=params(12 << 20),
        cost_estimate=pl.CostEstimate(
            flops=6 * rows * features * features, bytes_accessed=rows * features * 14, transcendentals=rows * features
        ),
        name="middle",
    )(keep, near, far, weight, cot)


def back_first_body(odd_ref, even_ref, adj_ref, wkeep_ref, out_ref, wsend_out, wkeep_out):
    features, rows = out_ref.shape[0], odd_ref.shape[1]
    out_ref[...] = dot(odd_ref[:features], adj_ref[:rows]) + dot(even_ref[...], adj_ref[rows:])

    @pl.when(pl.program_id(0) == 0)
    def _():
        part = wkeep_out.shape[0]
        mine = (lax.rem(lax.axis_index("row"), 2) ^ lax.div(lax.axis_index("rep"), 2)) == 0
        zero = wkeep_ref[:part] + fold_out(odd_ref, features, 0, *wkeep_out.shape)
        two = wkeep_ref[part:] + fold_out(odd_ref, features, 1, *wkeep_out.shape)
        wkeep_out[...] = jnp.where(mine, zero, two)
        wsend_out[...] = jnp.where(mine, two, zero)


def back_first(odd, even, adj, wkeep):
    rows, cols = adj.shape[0] // 2, adj.shape[1]
    features = wkeep.shape[1]
    whole = lambda x: pl.BlockSpec(x.shape, lambda i: (0, 0))
    part = wkeep.shape[0] // 2
    return pl.pallas_call(
        back_first_body,
        grid=(cols // COL_TILE,),
        out_shape=[shape((features, cols), F32)] + [shape((part, features), F32)] * 2,
        in_specs=[whole(odd), whole(even), pl.BlockSpec((rows, COL_TILE), lambda i: (1, i)), whole(wkeep)],
        out_specs=[pl.BlockSpec((features, COL_TILE), lambda i: (0, i))]
        + [pl.BlockSpec((part, features), lambda i: (0, 0))] * 2,
        compiler_params=params(4 << 20),
        cost_estimate=pl.CostEstimate(
            flops=2 * rows * cols * features, bytes_accessed=adj.size + cols * features * 4, transcendentals=0
        ),
        name="back_first",
    )(odd, even, adj, wkeep)


def back_second_body(odd_ref, even_ref, adj_ref, first_ref, send_ref, keep_ref, acc_ref):
    q = lax.axis_index("rep")
    rows = odd_ref.shape[1]
    acc_ref[...] = first_ref[...] + dot(odd_ref[...], adj_ref[:rows]) + dot(even_ref[...], adj_ref[rows:])
    part = send_ref.shape[0] // 2
    for j in range(4):
        out = send_ref if j & 1 else keep_ref
        at = (3 - j) // 2 * part
        piece = acc_ref[pl.ds(pl.multiple_of((q ^ j) * part, part), part), :]
        out[at : at + part] = piece.astype(out.dtype)


def back_second(odd, even, adj, first, half, n_rep, per_piece):
    rows, cols = adj.shape[0] // 2, adj.shape[1] // 2
    features = first.shape[0]
    width = cols // n_rep // per_piece
    tiles = cols // width
    whole = lambda x: pl.BlockSpec(x.shape, lambda i: (0, 0))
    return pl.pallas_call(
        back_second_body,
        grid=(tiles,),
        out_shape=[shape((features // 2, cols), BF16), shape((features // 2, cols), F32)],
        in_specs=[
            whole(odd),
            whole(even),
            pl.BlockSpec((rows, width), lambda i: (0, i + half * tiles)),
            pl.BlockSpec((features, width), lambda i: (0, i + half * tiles)),
        ],
        out_specs=[
            pl.BlockSpec(
                (features // 2, width), lambda i: (0, (lax.div(i, per_piece) ^ 1) * per_piece + lax.rem(i, per_piece))
            ),
            pl.BlockSpec((features // 2, width), lambda i: (0, i)),
        ],
        scratch_shapes=[pltpu.VMEM((features, width), F32)],
        compiler_params=params(4 << 20),
        cost_estimate=pl.CostEstimate(
            flops=2 * rows * cols * features, bytes_accessed=rows * cols * 2 + cols * features * 7, transcendentals=0
        ),
        name=f"back_second_{half}",
    )(odd, even, adj, first)


def split_body(own_ref, near_ref, far_ref, *refs, n_rep, deep, half):
    q = lax.axis_index("rep")
    w, outs = (None, refs) if half else (refs[0], refs[1:])
    part, width = outs[0].shape
    for i, out in enumerate(outs):
        low, hi = i % n_rep, i // n_rep
        j = low ^ q
        cols = pl.ds(pl.multiple_of((j * deep + hi) * width, width), width)
        far_cols = pl.ds(pl.multiple_of(((j ^ 2) * deep + hi) * width, width), width)
        total = own_ref[part:, cols] + near_ref[part:, cols].astype(F32) + far_ref[:, far_cols].astype(F32)
        out[:part] = total.astype(out.dtype)
    if w is not None:
        fold_in(outs[1], part, 0, w[...])


def split(own, near, far, w, half, n_rep, deep):
    part, cols = far.shape
    count = n_rep * deep
    width = cols // count
    out_shape = [shape((part, width), BF16) for i in range(count)]
    if not half:
        out_shape[0] = shape((part, width), F32)
        out_shape[1] = shape((part + w.size // width, width), BF16)
    extra = [] if half else [w]
    return pl.pallas_call(
        functools.partial(split_body, n_rep=n_rep, deep=deep, half=half),
        out_shape=out_shape,
        in_specs=[WHOLE] * (3 + len(extra)),
        out_specs=[WHOLE] * count,
        compiler_params=params(own.size * 10),
        cost_estimate=pl.CostEstimate(flops=own.size, bytes_accessed=own.size * 5, transcendentals=0),
        name=f"split_{half}",
    )(own, near, far, *extra)


def collect_body(*refs, n_row, n_rep, per_list, quarter, blk):
    lists = refs[:n_rep]
    messages = refs[n_rep : n_rep + n_row]
    w_ref = refs[n_rep + n_row]
    outs = refs[n_rep + n_row + 1 : -3]
    w_out, other_out, acc_ref = refs[-3:]
    q = lax.axis_index("rep")
    acc_ref[...] = jnp.zeros(acc_ref.shape, F32)
    for k in range(n_row):
        j = (k % n_rep) ^ q
        for c in range(per_list):
            at = k // n_rep * per_list + c
            b = lists[0][at]
            for other in range(1, n_rep):
                b = jnp.where(j == other, lists[other][at], b)
            cell = (lax.div(b, quarter) ^ q) * quarter + lax.rem(b, quarter)
            cols = pl.ds(pl.multiple_of(cell * blk, blk), blk)
            acc_ref[:, cols] += messages[k][: acc_ref.shape[0], c * blk : (c + 1) * blk].astype(F32)
    width = outs[0].shape[1]
    part = acc_ref.shape[0]
    w_out[...] = w_ref[...].astype(BF16)
    other_out[...] = fold_out(messages[1], part, 0, *w_ref.shape).astype(BF16)
    for j, out in enumerate(outs):
        out[:part] = acc_ref[:, j * width : (j + 1) * width].astype(out.dtype)
    fold_in(outs[1], part, 0, w_out[...])
    fold_in(outs[1], part, 1, other_out[...])


def collect(lists, messages, w, per_list, row_blocks, blk):
    n_rep = len(lists)
    n_row = len(messages)
    part = messages[0].shape[0]
    quarter = row_blocks // n_rep
    body = functools.partial(
        collect_body, n_row=n_row, n_rep=n_rep, per_list=per_list, quarter=quarter, blk=blk
    )
    return pl.pallas_call(
        body,
        out_shape=[
            shape((part, quarter * blk), F32),
            shape((part + 2 * w.size // (quarter * blk), quarter * blk), BF16),
        ]
        + [shape((part, quarter * blk), BF16)] * (n_rep - 2)
        + [shape(w.shape, BF16)] * 2,
        in_specs=[SMEM] * n_rep + [WHOLE] * (n_row + 1),
        out_specs=[WHOLE] * (n_rep + 2),
        scratch_shapes=[pltpu.VMEM((part, row_blocks * blk), F32)],
        compiler_params=params(4 << 20),
        cost_estimate=pl.CostEstimate(
            flops=part * row_blocks * blk, bytes_accessed=part * row_blocks * blk * 5, transcendentals=0
        ),
        name="collect",
    )(*lists, *messages, w)


def finish_body(*refs, n_rep):
    grads = refs[:n_rep]
    w_ref, other_ref, node_ref, weight_ref, acc_ref = refs[n_rep:]
    q = lax.axis_index("rep")
    part = w_ref.shape[0]
    for j in range(n_rep):
        acc_ref[pl.ds(pl.multiple_of((q ^ j) * part, part), part), :] = grads[j][:part].astype(F32)
    mine = lax.rem(q, 2) + 2 * lax.rem(lax.axis_index("row"), 2)
    near = [fold_out(grads[1], part, at, *w_ref.shape) for at in range(2)]
    for j, piece in enumerate((w_ref[...].astype(F32), near[0], other_ref[...].astype(F32), near[1])):
        weight_ref[pl.ds(pl.multiple_of((mine ^ j) * part, part), part), :] = piece
    node_ref[...] = acc_ref[...].T


def finish(grads, w, other):
    n_rep = len(grads)
    part, rows = grads[0].shape
    features = w.shape[1]
    return pl.pallas_call(
        functools.partial(finish_body, n_rep=n_rep),
        out_shape=[shape((rows, part * n_rep), F32), shape((features, features), F32)],
        in_specs=[WHOLE] * (n_rep + 2),
        out_specs=[WHOLE] * 2,
        scratch_shapes=[pltpu.VMEM((part * n_rep, rows), F32)],
        compiler_params=params(6 << 20),
        cost_estimate=pl.CostEstimate(flops=0, bytes_accessed=rows * part * n_rep * 8, transcendentals=0),
        name="finish",
    )(*grads, w, other)


def local(
    node_features, weight, out_grad, blocks, block_rows, block_fetch, fetch_lists, block_count
):
    n_row = lax.axis_size("row")
    n_rep = lax.axis_size("rep")
    n_hi = n_row // n_rep
    band_rows, features = node_features.shape
    blk = blocks.shape[1]
    row_blocks = band_rows // blk
    per_list = fetch_lists.shape[2]

    def to_rep(x, j):
        return lax.ppermute(x, "rep", xor_perm(n_rep, j))

    def to_row(x, k):
        return lax.ppermute(x, "row", xor_perm(n_row, k))

    def spread(x, hi):
        perm = [
            (r * n_rep + q, (r ^ (hi * n_rep + q)) * n_rep + q) for r in range(n_row) for q in range(n_rep)
        ]
        return lax.ppermute(x, ("row", "rep"), perm)

    def after(x, *done):
        return lax.optimization_barrier((x, *done))[0]

    wanted = [spread(fetch_lists, hi) for hi in range(n_hi)]
    *outgoing, own_list = pack(wanted, node_features, per_list, blk)
    own = [spread(x, hi) for hi, x in enumerate(outgoing)]
    table = slot_lists(
        block_rows, block_fetch, after(block_count, outgoing), n_row, n_rep, per_list, row_blocks
    )
    adj = densify(table, blocks, n_row, per_list, row_blocks)
    deep = n_hi // 2
    own = after(jnp.concatenate(own, axis=0), adj)
    far = to_rep(own, 2)
    pieces = [own, to_rep(own, 1), far, to_rep(far, 1)]

    send3, keep2 = forward(pieces, adj, 0)
    across = (keep2 + to_rep(send3, 1).astype(F32)).astype(BF16)
    arrived = to_rep(across, 2)
    send1, keep0 = forward(pieces, after(adj, across), 1)
    own_list = after(own_list, keep0)
    lists = [own_list] + [to_rep(own_list, j) for j in range(1, n_rep)]
    arrived = after(arrived, keep0, lists)
    factor = float(n_row * band_rows) ** (-0.5)
    output, to_near, grad0, wkeep = middle(keep0, to_rep(send1, 1), arrived, weight, out_grad, n_rep, factor)

    grad2 = to_rep(grad0, 2)
    first, wsend, w = back_first(to_rep(to_near, 1), grad0, adj, wkeep)
    w = w + to_row(wsend, 1)
    grad2 = after(grad2, first, w)
    grad3 = to_rep(grad2, 1)
    got = to_rep(w, 2)
    send_high, keep_high = back_second(grad3, grad2, adj, first, 1, n_rep, deep)
    send_high = after(send_high, got)
    near_high = to_rep(send_high, 1)
    send_low, keep_low = back_second(grad3, grad2, adj, after(first, send_high), 0, n_rep, deep)
    near_low = to_rep(send_low, 1)
    w = w + got
    got = to_row(w, 2)
    part = features // n_rep

    def across_sum(keep, near):
        return (keep[:part] + near[:part].astype(F32)).astype(BF16)

    far_high = to_rep(across_sum(keep_high, after(near_high, send_low, got)), 2)
    across = across_sum(keep_low, near_low)
    far_low = to_rep(across, 2)
    w = w + got
    got = to_row(after(w, across), 4)
    high = split(keep_high, near_high, after(far_high, got), None, 1, n_rep, deep)
    w = w + got
    step = 8
    while step < n_row:
        w = w + to_row(w, step)
        step *= 2
    half_rows = n_row // 2
    back_high = [to_row(x, half_rows + i) for i, x in enumerate(high)]
    low = split(keep_low, near_low, after(far_low, back_high[:2]), w, 0, n_rep, deep)
    returned = [low[0]] + [to_row(low[i], i) for i in range(1, half_rows)] + back_high
    *grads, w, other = collect(lists, returned, w, per_list, row_blocks, blk)
    node_grad, weight_grad = finish([grads[0]] + [to_rep(grads[j], j) for j in range(1, n_rep)], w, other)
    return (output, weight_grad, node_grad)


def solution(mesh):
    in_specs = (
        P("row", None),
        P(),
        P(("row", "rep"), None),
        P(("row", "rep"), None, None),
        P(("row", "rep")),
        P(("row", "rep")),
        P(("row", "rep"), None, None),
        P(("row", "rep")),
    )
    out_specs = (P(("row", "rep"), None), P(), P(("row", "rep"), None))
    return jax.shard_map(local, mesh=mesh, in_specs=in_specs, out_specs=out_specs, check_vma=False)
```

time: 107 us -> 102 us (0.953)
  local copies, waits for them, and re-layouts: 4.9 us -> 1.47 us
  starting transfers between devices: 39.9 us -> 42.9 us
  waiting for transfers between devices: 35.7 us -> 32.8 us
  Pallas kernels: 24.9 us -> 22.2 us
    ppermute x22 -> x20, waiting for transfers between devices: 28 us -> 19.4 us  [to_rep(): return lax.ppermute(x, 'rep', xor_perm(n_rep, j))]
    ppermute x10, waiting for transfers between devices: 6.76 us -> 13.1 us  [to_row(): return lax.ppermute(x, 'row', xor_perm(n_row, k))]
    unnamed x11, local copies, waits for them, and re-layouts: 4.9 us -> 1.47 us
    ppermute x10, starting transfers between devices: 14.7 us -> 18 us  [to_row(): return lax.ppermute(x, 'row', xor_perm(n_row, k))]
    pallas_call x6 -> x7, Pallas kernels: 13.9 us -> 11.6 us  [the longest x1 4.29 us: densify(): pl.pallas_call(functools.partial(densify_body, all_cols=all_cols, row_blo...]
    ppermute x22 -> x20, starting transfers between devices: 16.9 us -> 16.8 us  [to_rep(): return lax.ppermute(x, 'rep', xor_perm(n_rep, j))]
  transfers between devices with their start and end apart: 36 -> 34, of which waited for: 18 -> 20; matrix products, arithmetic and copies ran while one was open for 0% -> 0% of each run, Pallas kernels for 15% -> 15%
where the time goes in v6:
time: 102 us; the launch traced here: 101 us
  starting transfers between devices  42.9 us (42%)
  waiting for transfers between devices  32.8 us (32%)
  Pallas kernels  22.2 us (22%)
  between operations  1.55 us (2%)
  local copies, waits for them, and re-layouts  1.47 us (1%)
    ppermute x20, waiting for transfers between devices, to_rep(): return lax.ppermute(x, 'rep', xor_perm(n_rep, j))  19.4 us
    ppermute x10, starting transfers between devices, to_row(): return lax.ppermute(x, 'row', xor_perm(n_row, k))  18 us
    ppermute x20, starting transfers between devices, to_rep(): return lax.ppermute(x, 'rep', xor_perm(n_rep, j))  16.8 us
    ppermute x10, waiting for transfers between devices, to_row(): return lax.ppermute(x, 'row', xor_perm(n_row, k))  13.1 us
    ppermute x4, starting transfers between devices, spread(): return lax.ppermute(x, ('row', 'rep'), perm)  8.04 us
    pallas_call x1, Pallas kernels, densify(): pl.pallas_call(functools.partial(densify_body, all_cols=all_cols, row_blo...  4.29 us
    pallas_call x2, Pallas kernels, forward(): pl.pallas_call(functools.partial(forward_body, n_rep=len(pieces)), grid=(...  3.67 us
    pallas_call x2, Pallas kernels, back_second(): pl.pallas_call(back_second_body, grid=(tiles,), out_shape=[shape((feature...  3.67 us
  transfers between devices with their start and end apart: 34, of which 20 were waited for; matrix products, arithmetic and copies ran while one was open for 0% of the time, Pallas kernels for 15%

profile of v6, /device:TPU:0, one launch (start us, length us, event | category | flops | bytes accessed | tf_op | source)
XLA Modules:
  0.0 101.0 jit_solution(16899261833068888253)
XLA Ops:
  1.4 4.0 %collective-permute-start.1 = (s32[1,8,2]{2,1,0:T(8,128)S(1)}, s32[1,8,2]{2,1,0:T(8,128)S(1)}, u32[]{:S(2)}, u32[]{:S(2)}) collective-permute-start(s32[1,8,2]{2,1,0:T(8,128)S(1)} %copy.11), channel_id=1, source_target_pairs={{0,16},{1,21},{2,26},{3,31},{4,20},{5,17},{6,30},{7,27},{8,24},{9,... | collective-permute-start | bytes 200 | tf_op jit(solution)/shard_map/ppermute | solution.py:540
  7.0 2.5 %pack.1 = (bf16[256,256]{1,0:T(8,128)(2,1)S(1)}, bf16[256,256]{1,0:T(8,128)(2,1)S(1)}, s32[128]{0:T(128)S(1)}) custom-call(s32[1,8,2]{2,1,0:T(8,128)S(1)} %collective-permute-done.refs_0_, s32[1,8,2]{2,1,0:T(8,128)S(1)} %collective-permute-done.1.refs_1_, bf16[2048,256]{1,0:T(8,128)(2,1)} %refs_2_.1), custom_call_target="tpu_custom_call" | custom-call | tf_op jit(solution)/shard_map/pack/pallas_call | solution.py:202
  10.2 2.7 %collective-permute-start.3 = (bf16[256,256]{1,0:T(8,128)(2,1)S(1)}, bf16[256,256]{1,0:T(8,128)(2,1)S(1)}, u32[]{:S(2)}, u32[]{:S(2)}) collective-permute-start(bf16[256,256]{1,0:T(8,128)(2,1)S(1)} %get-tuple-element.50), channel_id=1, source_target_pairs={{0,16},{1,21},{2,26},{3,31},{4,20},{5,17},{6,30},{7,27},{8,24},{9,... | collective-permute-start | bytes 393224 | tf_op jit(solution)/shard_map/ppermute | solution.py:540
  12.9 2.7 %slot_lists.1.table_ref = s32[1152]{0:T(1024)} custom-call(s32[192]{0:T(256)} %rows_ref.1, s32[192]{0:T(256)} %fetch_ref.1, s32[1]{0:T(128)S(6)} %copy.13.count_ref), custom_call_target="tpu_custom_call" | custom-call | flops 3221225472 | bytes 1536 | tf_op jit(solution)/shard_map/slot_lists/pallas_call | solution.py:103
  16.4 4.3 %densify.1.refs_4_.adj_ref = bf16[2048,2048]{1,0:T(8,128)(2,1)S(1)} custom-call(s32[1152]{0:T(1024)S(1)} %copy-done.2, bf16[192,128,128]{2,1,0:T(8,128)(2,1)S(1)} %bitcast.1), custom_call_target="tpu_custom_call" | custom-call | flops 3145728 | bytes 14680064 | tf_op jit(solution)/shard_map/densify/pallas_call | solution.py:159
  20.7 6.9 %collective-permute-start.5 = (bf16[512,256]{1,0:T(8,128)(2,1)S(1)}, bf16[512,256]{1,0:T(8,128)(2,1)S(1)}, u32[]{:S(2)}, u32[]{:S(2)}) collective-permute-start(bf16[512,256]{1,0:T(8,128)(2,1)S(1)} %pad_maximum_fusion.refs_0_), channel_id=1, source_target_pairs={{0,2},{1,3},{2,0},{3,1},{4,6},{5,7},{6,4},{7,5},{8,10},{9,11},{10,... | collective-permute-start | bytes 786440 | tf_op jit(solution)/shard_map/ppermute | solution.py:531
  27.7 6.5 %collective-permute-done.5.refs_2_ = bf16[512,256]{1,0:T(8,128)(2,1)S(1)} collective-permute-done((bf16[512,256]{1,0:T(8,128)(2,1)S(1)}, bf16[512,256]{1,0:T(8,128)(2,1)S(1)}, u32[]{:S(2)}, u32[]{:S(2)}) %collective-permute-start.5) | collective-permute-done | bytes 262176 | tf_op jit(solution)/shard_map/ppermute | solution.py:531
  35.7 1.8 %forward.2 = (bf16[512,256]{1,0:T(8,128)(2,1)S(1)}, f32[512,256]{1,0:T(8,128)S(1)}) custom-call(bf16[512,256]{1,0:T(8,128)(2,1)S(1)} %pad_maximum_fusion.refs_0_, bf16[512,256]{1,0:T(8,128)(2,1)S(1)} %collective-permute-done.4.refs_1_, bf16[512,256]{1,0:T(8,128)(2,1)S(1)} %collective-permute-done.5.refs_2_, ...), custom_call_target="tpu_custom_call" | custom-call | flops 1073741824 | bytes 5242880 | tf_op jit(solution)/shard_map/forward/pallas_call | solution.py:240
  39.9 1.8 %forward.3 = (bf16[512,256]{1,0:T(8,128)(2,1)S(1)}, f32[512,256]{1,0:T(8,128)S(1)}) custom-call(bf16[512,256]{1,0:T(8,128)(2,1)S(1)} %pad_maximum_fusion.refs_0_, bf16[512,256]{1,0:T(8,128)(2,1)S(1)} %collective-permute-done.4.refs_1_, bf16[512,256]{1,0:T(8,128)(2,1)S(1)} %collective-permute-done.5.refs_2_, ...), custom_call_target="tpu_custom_call" | custom-call | flops 1073741824 | bytes 5242880 | tf_op jit(solution)/shard_map/forward/pallas_call | solution.py:240
  44.0 2.8 %collective-permute-done.12.refs_3_ = s32[128]{0:T(128)S(1)} collective-permute-done((s32[128]{0:T(128)S(1)}, s32[128]{0:T(128)S(1)}, u32[]{:S(2)}, u32[]{:S(2)}) %collective-permute-start.12) | collective-permute-done | bytes 544 | tf_op jit(solution)/shard_map/ppermute | solution.py:531
  50.4 2.3 %back_first.1 = (f32[256,2048]{1,0:T(8,128)S(1)}, f32[64,256]{1,0:T(8,128)S(1)}, f32[64,256]{1,0:T(8,128)S(1)}) custom-call(bf16[320,512]{1,0:T(8,128)(2,1)S(1)} %collective-permute-done.14.odd_ref, bf16[256,512]{1,0:T(8,128)(2,1)S(1)} %get-tuple-element.62.even_ref, bf16[2048,2048]{1,0:T(8,128)(2,1)S(1)} %densify.1.refs_4_.adj_ref, ...), custom_call_target="tpu_custom_call" | custom-call | flops 1073741824 | bytes 6291456 | tf_op jit(solution)/shard_map/back_first/pallas_call | solution.py:341
  52.7 2.2 %collective-permute-start.15 = (f32[64,256]{1,0:T(8,128)S(1)}, f32[64,256]{1,0:T(8,128)S(1)}, u32[]{:S(2)}, u32[]{:S(2)}) collective-permute-start(f32[64,256]{1,0:T(8,128)S(1)} %get-tuple-element.67), channel_id=1, source_target_pairs={{0,4},{4,0},{8,12},{12,8},{16,20},{20,16},{24,28},{28,24},{1,5},{5... | collective-permute-start | bytes 196616 | tf_op jit(solution)/shard_map/ppermute | solution.py:534
  54.9 2.4 %collective-permute-done.15 = f32[64,256]{1,0:T(8,128)S(1)} collective-permute-done((f32[64,256]{1,0:T(8,128)S(1)}, f32[64,256]{1,0:T(8,128)S(1)}, u32[]{:S(2)}, u32[]{:S(2)}) %collective-permute-start.15) | collective-permute-done | bytes 65568 | tf_op jit(solution)/shard_map/ppermute | solution.py:534
  59.0 1.8 %back_second_1.1 = (bf16[128,1024]{1,0:T(8,128)(2,1)S(1)}, f32[128,1024]{1,0:T(8,128)S(1)}) custom-call(bf16[256,512]{1,0:T(8,128)(2,1)S(1)} %collective-permute-done.16.odd_ref, bf16[256,512]{1,0:T(8,128)(2,1)S(1)} %collective-permute-done.13.even_ref, bf16[2048,2048]{1,0:T(8,128)(2,1)S(1)} %densify.1.refs_4_.adj_ref, ...), custom_call_target="tpu_custom_call" | custom-call | flops 536870912 | bytes 3932160 | tf_op jit(solution)/shard_map/back_second_1/pallas_call | solution.py:374
  62.0 2.0 %collective-permute-start.21 = (f32[64,256]{1,0:T(8,128)S(1)}, f32[64,256]{1,0:T(8,128)S(1)}, u32[]{:S(2)}, u32[]{:S(2)}) collective-permute-start(f32[64,256]{1,0:T(8,128)S(1)} %add.24), channel_id=1, source_target_pairs={{0,8},{4,12},{8,0},{12,4},{16,24},{20,28},{24,16},{28,20},{1,9},{5... | collective-permute-start | bytes 196616 | tf_op jit(solution)/shard_map/ppermute | solution.py:534
  64.1 1.8 %back_second_0.1 = (bf16[128,1024]{1,0:T(8,128)(2,1)S(1)}, f32[128,1024]{1,0:T(8,128)S(1)}) custom-call(bf16[256,512]{1,0:T(8,128)(2,1)S(1)} %collective-permute-done.16.odd_ref, bf16[256,512]{1,0:T(8,128)(2,1)S(1)} %collective-permute-done.13.even_ref, bf16[2048,2048]{1,0:T(8,128)(2,1)S(1)} %densify.1.refs_4_.adj_ref, ...), custom_call_target="tpu_custom_call" | custom-call | flops 536870912 | bytes 3932160 | tf_op jit(solution)/shard_map/back_second_0/pallas_call | solution.py:374
  66.9 1.8 %collective-permute-start.22 = (bf16[64,1024]{1,0:T(8,128)(2,1)S(1)}, bf16[64,1024]{1,0:T(8,128)(2,1)S(1)}, u32[]{:S(2)}, u32[]{:S(2)}) collective-permute-start(bf16[64,1024]{1,0:T(8,128)(2,1)S(1)} %add_convert_fusion.1), channel_id=1, source_target_pairs={{0,2},{1,3},{2,0},{3,1},{4,6},{5,7},{6,4},{7,5},{8,10},{9,11},{10,... | collective-permute-start | bytes 393224 | tf_op jit(solution)/shard_map/ppermute | solution.py:531
  69.4 2.2 %collective-permute-start.23 = (f32[64,256]{1,0:T(8,128)S(1)}, f32[64,256]{1,0:T(8,128)S(1)}, u32[]{:S(2)}, u32[]{:S(2)}) collective-permute-start(f32[64,256]{1,0:T(8,128)S(1)} %add.26), channel_id=1, source_target_pairs={{0,16},{4,20},{8,24},{12,28},{16,0},{20,4},{24,8},{28,12},{1,17},{... | collective-permute-start | bytes 196616 | tf_op jit(solution)/shard_map/ppermute | solution.py:534
  71.6 4.1 %collective-permute-done.23 = f32[64,256]{1,0:T(8,128)S(1)} collective-permute-done((f32[64,256]{1,0:T(8,128)S(1)}, f32[64,256]{1,0:T(8,128)S(1)}, u32[]{:S(2)}, u32[]{:S(2)}) %collective-permute-start.23) | collective-permute-done | bytes 65568 | tf_op jit(solution)/shard_map/ppermute | solution.py:534
  77.0 2.1 %collective-permute-start.25 = (bf16[64,256]{1,0:T(8,128)(2,1)S(1)}, bf16[64,256]{1,0:T(8,128)(2,1)S(1)}, u32[]{:S(2)}, u32[]{:S(2)}) collective-permute-start(bf16[64,256]{1,0:T(8,128)(2,1)S(1)} %get-tuple-element.79), channel_id=1, source_target_pairs={{0,20},{4,16},{8,28},{12,24},{16,4},{20,0},{24,12},{28,8},{1,21},{... | collective-permute-start | bytes 98312 | tf_op jit(solution)/shard_map/ppermute | solution.py:534
  80.9 1.9 %collective-permute-done.25.refs_9_ = bf16[64,256]{1,0:T(8,128)(2,1)S(1)} collective-permute-done((bf16[64,256]{1,0:T(8,128)(2,1)S(1)}, bf16[64,256]{1,0:T(8,128)(2,1)S(1)}, u32[]{:S(2)}, u32[]{:S(2)}) %collective-permute-start.25) | collective-permute-done | bytes 32800 | tf_op jit(solution)/shard_map/ppermute | solution.py:534
  85.0 3.2 %collective-permute-start.30 = (bf16[64,256]{1,0:T(8,128)(2,1)S(1)}, bf16[64,256]{1,0:T(8,128)(2,1)S(1)}, u32[]{:S(2)}, u32[]{:S(2)}) collective-permute-start(bf16[64,256]{1,0:T(8,128)(2,1)S(1)} %get-tuple-element.86), channel_id=1, source_target_pairs={{0,28},{4,24},{8,20},{12,16},{16,12},{20,8},{24,4},{28,0},{1,29},{... | collective-permute-start | bytes 98312 | tf_op jit(solution)/shard_map/ppermute | solution.py:534
  88.2 2.9 %collective-permute-start.28 = (bf16[64,256]{1,0:T(8,128)(2,1)S(1)}, bf16[64,256]{1,0:T(8,128)(2,1)S(1)}, u32[]{:S(2)}, u32[]{:S(2)}) collective-permute-start(bf16[64,256]{1,0:T(8,128)(2,1)S(1)} %get-tuple-element.84), channel_id=1, source_target_pairs={{0,12},{4,8},{8,4},{12,0},{16,28},{20,24},{24,20},{28,16},{1,13},{... | collective-permute-start | bytes 98312 | tf_op jit(solution)/shard_map/ppermute | solution.py:534
  96.1 2.6 %collective-permute-done.32.refs_2_ = bf16[64,512]{1,0:T(8,128)(2,1)S(1)} collective-permute-done((bf16[64,512]{1,0:T(8,128)(2,1)S(1)}, bf16[64,512]{1,0:T(8,128)(2,1)S(1)}, u32[]{:S(2)}, u32[]{:S(2)}) %collective-permute-start.32) | collective-permute-done | bytes 65568 | tf_op jit(solution)/shard_map/ppermute | solution.py:531
  (77 shorter events, 29.8 us)
Async XLA Ops:
  1.4 5.6 %collective-permute-start.1 = (s32[1,8,2]{2,1,0:T(8,128)S(1)}, s32[1,8,2]{2,1,0:T(8,128)S(1)}, u32[]{:S(2)}, u32[]{:S(2)}) collective-permute-start(s32[1,8,2]{2,1,0:T(8,128)S(1)} %copy.11), channel_id=1, source_target_pairs={{0,16},{1,21},{2,26},{3,31},{4,20},{5,17},{6,30},{7,27},{8,24},{9,... | collective-permute-start | bytes 200 | tf_op jit(solution)/shard_map/ppermute | solution.py:540
  9.6 11.1 %collective-permute-start.2 = (bf16[256,256]{1,0:T(8,128)(2,1)S(1)}, bf16[256,256]{1,0:T(8,128)(2,1)S(1)}, u32[]{:S(2)}, u32[]{:S(2)}) collective-permute-start(bf16[256,256]{1,0:T(8,128)(2,1)S(1)} %get-tuple-element.49), channel_id=1, source_target_pairs={{0,0},{1,5},{2,10},{3,15},{4,4},{5,1},{6,14},{7,11},{8,8},{9,13},{... | collective-permute-start | bytes 393224 | tf_op jit(solution)/shard_map/ppermute | solution.py:540
  10.2 10.4 %collective-permute-start.3 = (bf16[256,256]{1,0:T(8,128)(2,1)S(1)}, bf16[256,256]{1,0:T(8,128)(2,1)S(1)}, u32[]{:S(2)}, u32[]{:S(2)}) collective-permute-start(bf16[256,256]{1,0:T(8,128)(2,1)S(1)} %get-tuple-element.50), channel_id=1, source_target_pairs={{0,16},{1,21},{2,26},{3,31},{4,20},{5,17},{6,30},{7,27},{8,24},{9,... | collective-permute-start | bytes 393224 | tf_op jit(solution)/shard_map/ppermute | solution.py:540
  20.7 13.4 %collective-permute-start.5 = (bf16[512,256]{1,0:T(8,128)(2,1)S(1)}, bf16[512,256]{1,0:T(8,128)(2,1)S(1)}, u32[]{:S(2)}, u32[]{:S(2)}) collective-permute-start(bf16[512,256]{1,0:T(8,128)(2,1)S(1)} %pad_maximum_fusion.refs_0_), channel_id=1, source_target_pairs={{0,2},{1,3},{2,0},{3,1},{4,6},{5,7},{6,4},{7,5},{8,10},{9,11},{10,... | collective-permute-start | bytes 786440 | tf_op jit(solution)/shard_map/ppermute | solution.py:531
  27.7 6.5 %collective-permute-start.4 = (bf16[512,256]{1,0:T(8,128)(2,1)S(1)}, bf16[512,256]{1,0:T(8,128)(2,1)S(1)}, u32[]{:S(2)}, u32[]{:S(2)}) collective-permute-start(bf16[512,256]{1,0:T(8,128)(2,1)S(1)} %pad_maximum_fusion.refs_0_), channel_id=1, source_target_pairs={{0,1},{1,0},{2,3},{3,2},{4,5},{5,4},{6,7},{7,6},{8,9},{9,8},{10,11... | collective-permute-start | bytes 786440 | tf_op jit(solution)/shard_map/ppermute | solution.py:531
  39.2 8.5 %collective-permute-start.9 = (bf16[512,256]{1,0:T(8,128)(2,1)S(1)}, bf16[512,256]{1,0:T(8,128)(2,1)S(1)}, u32[]{:S(2)}, u32[]{:S(2)}) collective-permute-start(bf16[512,256]{1,0:T(8,128)(2,1)S(1)} %add_convert_fusion), channel_id=1, source_target_pairs={{0,2},{1,3},{2,0},{3,1},{4,6},{5,7},{6,4},{7,5},{8,10},{9,11},{10,... | collective-permute-start | bytes 786440 | tf_op jit(solution)/shard_map/ppermute | solution.py:531
  41.8 5.9 %collective-permute-start.8 = (bf16[512,256]{1,0:T(8,128)(2,1)S(1)}, bf16[512,256]{1,0:T(8,128)(2,1)S(1)}, u32[]{:S(2)}, u32[]{:S(2)}) collective-permute-start(bf16[512,256]{1,0:T(8,128)(2,1)S(1)} %get-tuple-element.57), channel_id=1, source_target_pairs={{0,1},{1,0},{2,3},{3,2},{4,5},{5,4},{6,7},{7,6},{8,9},{9,8},{10,11... | collective-permute-start | bytes 786440 | tf_op jit(solution)/shard_map/ppermute | solution.py:531
  41.9 4.9 %collective-permute-start.12 = (s32[128]{0:T(128)S(1)}, s32[128]{0:T(128)S(1)}, u32[]{:S(2)}, u32[]{:S(2)}) collective-permute-start(s32[128]{0:T(128)S(1)} %get-tuple-element.59.refs_0_), channel_id=1, source_target_pairs={{0,3},{1,2},{2,1},{3,0},{4,7},{5,6},{6,5},{7,4},{8,11},{9,10},{10,... | collective-permute-start | bytes 1544 | tf_op jit(solution)/shard_map/ppermute | solution.py:531
  48.8 8.7 %collective-permute-start.13 = (bf16[256,512]{1,0:T(8,128)(2,1)S(1)}, bf16[256,512]{1,0:T(8,128)(2,1)S(1)}, u32[]{:S(2)}, u32[]{:S(2)}) collective-permute-start(bf16[256,512]{1,0:T(8,128)(2,1)S(1)} %get-tuple-element.62.even_ref), channel_id=1, source_target_pairs={{0,2},{1,3},{2,0},{3,1},{4,6},{5,7},{6,4},{7,5},{8,10},{9,11},{10,... | collective-permute-start | bytes 786440 | tf_op jit(solution)/shard_map/ppermute | solution.py:531
  52.7 4.6 %collective-permute-start.15 = (f32[64,256]{1,0:T(8,128)S(1)}, f32[64,256]{1,0:T(8,128)S(1)}, u32[]{:S(2)}, u32[]{:S(2)}) collective-permute-start(f32[64,256]{1,0:T(8,128)S(1)} %get-tuple-element.67), channel_id=1, source_target_pairs={{0,4},{4,0},{8,12},{12,8},{16,20},{20,16},{24,28},{28,24},{1,5},{5... | collective-permute-start | bytes 196616 | tf_op jit(solution)/shard_map/ppermute | solution.py:534
  57.5 4.5 %collective-permute-start.17 = (f32[64,256]{1,0:T(8,128)S(1)}, f32[64,256]{1,0:T(8,128)S(1)}, u32[]{:S(2)}, u32[]{:S(2)}) collective-permute-start(f32[64,256]{1,0:T(8,128)S(1)} %add.22), channel_id=1, source_target_pairs={{0,2},{1,3},{2,0},{3,1},{4,6},{5,7},{6,4},{7,5},{8,10},{9,11},{10,... | collective-permute-start | bytes 196616 | tf_op jit(solution)/shard_map/ppermute | solution.py:531
  62.0 4.8 %collective-permute-start.20 = (bf16[128,1024]{1,0:T(8,128)(2,1)S(1)}, bf16[128,1024]{1,0:T(8,128)(2,1)S(1)}, u32[]{:S(2)}, u32[]{:S(2)}) collective-permute-start(bf16[128,1024]{1,0:T(8,128)(2,1)S(1)} %get-tuple-element.70), channel_id=1, source_target_pairs={{0,1},{1,0},{2,3},{3,2},{4,5},{5,4},{6,7},{7,6},{8,9},{9,8},{10,11... | collective-permute-start | bytes 786440 | tf_op jit(solution)/shard_map/ppermute | solution.py:531
  62.0 4.8 %collective-permute-start.21 = (f32[64,256]{1,0:T(8,128)S(1)}, f32[64,256]{1,0:T(8,128)S(1)}, u32[]{:S(2)}, u32[]{:S(2)}) collective-permute-start(f32[64,256]{1,0:T(8,128)S(1)} %add.24), channel_id=1, source_target_pairs={{0,8},{4,12},{8,0},{12,4},{16,24},{20,28},{24,16},{28,20},{1,9},{5... | collective-permute-start | bytes 196616 | tf_op jit(solution)/shard_map/ppermute | solution.py:534
  66.9 8.8 %collective-permute-start.22 = (bf16[64,1024]{1,0:T(8,128)(2,1)S(1)}, bf16[64,1024]{1,0:T(8,128)(2,1)S(1)}, u32[]{:S(2)}, u32[]{:S(2)}) collective-permute-start(bf16[64,1024]{1,0:T(8,128)(2,1)S(1)} %add_convert_fusion.1), channel_id=1, source_target_pairs={{0,2},{1,3},{2,0},{3,1},{4,6},{5,7},{6,4},{7,5},{8,10},{9,11},{10,... | collective-permute-start | bytes 393224 | tf_op jit(solution)/shard_map/ppermute | solution.py:531
  68.7 10.4 %collective-permute-start.19 = (bf16[64,1024]{1,0:T(8,128)(2,1)S(1)}, bf16[64,1024]{1,0:T(8,128)(2,1)S(1)}, u32[]{:S(2)}, u32[]{:S(2)}) collective-permute-start(bf16[64,1024]{1,0:T(8,128)(2,1)S(1)} %add_convert_fusion.2), channel_id=1, source_target_pairs={{0,2},{1,3},{2,0},{3,1},{4,6},{5,7},{6,4},{7,5},{8,10},{9,11},{10,... | collective-permute-start | bytes 393224 | tf_op jit(solution)/shard_map/ppermute | solution.py:531
  69.4 6.3 %collective-permute-start.23 = (f32[64,256]{1,0:T(8,128)S(1)}, f32[64,256]{1,0:T(8,128)S(1)}, u32[]{:S(2)}, u32[]{:S(2)}) collective-permute-start(f32[64,256]{1,0:T(8,128)S(1)} %add.26), channel_id=1, source_target_pairs={{0,16},{4,20},{8,24},{12,28},{16,0},{20,4},{24,8},{28,12},{1,17},{... | collective-permute-start | bytes 196616 | tf_op jit(solution)/shard_map/ppermute | solution.py:534
  75.8 5.1 %collective-permute-start.24 = (bf16[64,256]{1,0:T(8,128)(2,1)S(1)}, bf16[64,256]{1,0:T(8,128)(2,1)S(1)}, u32[]{:S(2)}, u32[]{:S(2)}) collective-permute-start(bf16[64,256]{1,0:T(8,128)(2,1)S(1)} %get-tuple-element.78), channel_id=1, source_target_pairs={{0,16},{4,20},{8,24},{12,28},{16,0},{20,4},{24,8},{28,12},{1,17},{... | collective-permute-start | bytes 98312 | tf_op jit(solution)/shard_map/ppermute | solution.py:534
  77.0 5.8 %collective-permute-start.25 = (bf16[64,256]{1,0:T(8,128)(2,1)S(1)}, bf16[64,256]{1,0:T(8,128)(2,1)S(1)}, u32[]{:S(2)}, u32[]{:S(2)}) collective-permute-start(bf16[64,256]{1,0:T(8,128)(2,1)S(1)} %get-tuple-element.79), channel_id=1, source_target_pairs={{0,20},{4,16},{8,28},{12,24},{16,4},{20,0},{24,12},{28,8},{1,21},{... | collective-permute-start | bytes 98312 | tf_op jit(solution)/shard_map/ppermute | solution.py:534
  82.9 10.5 %collective-permute-start.26 = (bf16[128,256]{1,0:T(8,128)(2,1)S(1)}, bf16[128,256]{1,0:T(8,128)(2,1)S(1)}, u32[]{:S(2)}, u32[]{:S(2)}) collective-permute-start(bf16[128,256]{1,0:T(8,128)(2,1)S(1)} %get-tuple-element.82), channel_id=1, source_target_pairs={{0,4},{4,0},{8,12},{12,8},{16,20},{20,16},{24,28},{28,24},{1,5},{5... | collective-permute-start | bytes 196616 | tf_op jit(solution)/shard_map/ppermute | solution.py:534
  84.4 6.8 %collective-permute-start.29 = (bf16[64,256]{1,0:T(8,128)(2,1)S(1)}, bf16[64,256]{1,0:T(8,128)(2,1)S(1)}, u32[]{:S(2)}, u32[]{:S(2)}) collective-permute-start(bf16[64,256]{1,0:T(8,128)(2,1)S(1)} %get-tuple-element.85), channel_id=1, source_target_pairs={{0,24},{4,28},{8,16},{12,20},{16,8},{20,12},{24,0},{28,4},{1,25},{... | collective-permute-start | bytes 98312 | tf_op jit(solution)/shard_map/ppermute | solution.py:534
  85.0 6.6 %collective-permute-start.30 = (bf16[64,256]{1,0:T(8,128)(2,1)S(1)}, bf16[64,256]{1,0:T(8,128)(2,1)S(1)}, u32[]{:S(2)}, u32[]{:S(2)}) collective-permute-start(bf16[64,256]{1,0:T(8,128)(2,1)S(1)} %get-tuple-element.86), channel_id=1, source_target_pairs={{0,28},{4,24},{8,20},{12,16},{16,12},{20,8},{24,4},{28,0},{1,29},{... | collective-permute-start | bytes 98312 | tf_op jit(solution)/shard_map/ppermute | solution.py:534
  88.2 5.1 %collective-permute-start.28 = (bf16[64,256]{1,0:T(8,128)(2,1)S(1)}, bf16[64,256]{1,0:T(8,128)(2,1)S(1)}, u32[]{:S(2)}, u32[]{:S(2)}) collective-permute-start(bf16[64,256]{1,0:T(8,128)(2,1)S(1)} %get-tuple-element.84), channel_id=1, source_target_pairs={{0,12},{4,8},{8,4},{12,0},{16,28},{20,24},{24,20},{28,16},{1,13},{... | collective-permute-start | bytes 98312 | tf_op jit(solution)/shard_map/ppermute | solution.py:534
  94.1 5.8 %collective-permute-start.31 = (bf16[128,512]{1,0:T(8,128)(2,1)S(1)}, bf16[128,512]{1,0:T(8,128)(2,1)S(1)}, u32[]{:S(2)}, u32[]{:S(2)}) collective-permute-start(bf16[128,512]{1,0:T(8,128)(2,1)S(1)} %get-tuple-element.88), channel_id=1, source_target_pairs={{0,1},{1,0},{2,3},{3,2},{4,5},{5,4},{6,7},{7,6},{8,9},{9,8},{10,11... | collective-permute-start | bytes 393224 | tf_op jit(solution)/shard_map/ppermute | solution.py:531
  94.2 4.5 %collective-permute-start.32 = (bf16[64,512]{1,0:T(8,128)(2,1)S(1)}, bf16[64,512]{1,0:T(8,128)(2,1)S(1)}, u32[]{:S(2)}, u32[]{:S(2)}) collective-permute-start(bf16[64,512]{1,0:T(8,128)(2,1)S(1)} %get-tuple-element.89), channel_id=1, source_target_pairs={{0,2},{1,3},{2,0},{3,1},{4,6},{5,7},{6,4},{7,5},{8,10},{9,11},{10,... | collective-permute-start | bytes 196616 | tf_op jit(solution)/shard_map/ppermute | solution.py:531
  (15 other events, 62.1 us)

commit v7 on v6

--- a/solution.py
+++ b/solution.py
@@ -10,6 +10,7 @@
 BF16 = jnp.bfloat16
 F32 = jnp.float32
 COL_CHUNK = 16
+LIST_STEP = 4
 ROW_TILE = 256
 COL_TILE = 512
 WHOLE = pl.BlockSpec(memory_space=pltpu.VMEM)
@@ -42,9 +43,10 @@
 class Table:
     def __init__(self, slots, cells):
         self.groups = cells // COL_CHUNK
+        self.spare = cells
         self.first = 0
-        self.second = cells
-        self.older = 2 * cells
+        self.second = cells + 1
+        self.older = 2 * (cells + 1)
         self.wide_at = self.older + slots + 1
         self.wide_cell = self.wide_at + self.groups
         self.wide_next = self.wide_cell + slots
@@ -68,26 +70,37 @@
 
     out_ref[t.older + slots] = slots
 
-    def link(slot, wide):
+    live = count_ref[0]
+
+    def place(slot):
         row_high, row_low = div_rem(rows_ref[slot], quarter)
         source, c = div_rem(fetch_ref[slot], per_list)
         hi, low = div_rem(source ^ r, n_rep)
         half, hi = div_rem(hi, deep)
         row = (n_rep - 1 - (row_high ^ q)) * quarter + row_low
         col = ((half * n_rep + (low ^ q)) * deep + hi) * per_list + c
-        cell = row * all_cols + col
-        at = t.wide_at + row * chunks + div_rem(col, COL_CHUNK)[0]
+        cell = jnp.where(slot < live, row * all_cols + col, t.spare)
+        return cell, t.wide_at + row * chunks + div_rem(col, COL_CHUNK)[0]
+
+    def link(slot, cell, at, wide):
         one, two, begin = out_ref[t.first + cell], out_ref[t.second + cell], out_ref[at]
         out_ref[t.first + cell] = slot
         out_ref[t.second + cell] = one
         out_ref[t.older + slot] = one
-        full = two != slots
+        full = (two != slots) & (slot < live)
         out_ref[t.wide_cell + wide] = cell
         out_ref[t.wide_next + wide] = begin
         out_ref[at] = jnp.where(full, wide, begin)
         return wide + full.astype(jnp.int32)
 
-    lax.fori_loop(0, count_ref[0], link, jnp.int32(0))
+    def link_group(group, wide):
+        begin = group * LIST_STEP
+        places = [(begin + i, *place(begin + i)) for i in range(LIST_STEP)]
+        for slot, cell, at in places:
+            wide = link(slot, cell, at, wide)
+        return wide
+
+    lax.fori_loop(0, lax.div(live + LIST_STEP - 1, LIST_STEP), link_group, jnp.int32(0))
 
 
 def slot_lists(block_rows, block_fetch, block_count, n_row, n_rep, per_list, row_blocks):
@@ -396,48 +409,39 @@
     )(odd, even, adj, first)
 
 
-def split_body(own_ref, near_ref, far_ref, *refs, n_rep, deep, half):
-    q = lax.axis_index("rep")
-    w, outs = (None, refs) if half else (refs[0], refs[1:])
-    part, width = outs[0].shape
-    for i, out in enumerate(outs):
-        low, hi = i % n_rep, i // n_rep
-        j = low ^ q
-        cols = pl.ds(pl.multiple_of((j * deep + hi) * width, width), width)
-        far_cols = pl.ds(pl.multiple_of(((j ^ 2) * deep + hi) * width, width), width)
-        total = own_ref[part:, cols] + near_ref[part:, cols].astype(F32) + far_ref[:, far_cols].astype(F32)
-        out[:part] = total.astype(out.dtype)
-    if w is not None:
-        fold_in(outs[1], part, 0, w[...])
-
-
-def split(own, near, far, w, half, n_rep, deep):
-    part, cols = far.shape
-    count = n_rep * deep
-    width = cols // count
-    out_shape = [shape((part, width), BF16) for i in range(count)]
-    if not half:
-        out_shape[0] = shape((part, width), F32)
-        out_shape[1] = shape((part + w.size // width, width), BF16)
-    extra = [] if half else [w]
-    return pl.pallas_call(
-        functools.partial(split_body, n_rep=n_rep, deep=deep, half=half),
-        out_shape=out_shape,
-        in_specs=[WHOLE] * (3 + len(extra)),
-        out_specs=[WHOLE] * count,
-        compiler_params=params(own.size * 10),
-        cost_estimate=pl.CostEstimate(flops=own.size, bytes_accessed=own.size * 5, transcendentals=0),
-        name=f"split_{half}",
-    )(own, near, far, *extra)
+def split_body(*refs, n_rep, deep):
+    halves, out_ref = (refs[:3], refs[3:6]), refs[6]
+    r, q = lax.axis_index("row"), lax.axis_index("rep")
+    _, part, width = out_ref.shape
+    for half, (own_ref, near_ref, far_ref) in enumerate(halves):
+        for i in range(n_rep * deep):
+            low, hi = i % n_rep, i // n_rep
+            j = low ^ q
+            cols = pl.ds(pl.multiple_of((j * deep + hi) * width, width), width)
+            far_cols = pl.ds(pl.multiple_of(((j ^ 2) * deep + hi) * width, width), width)
+            total = own_ref[part:, cols] + near_ref[part:, cols].astype(F32) + far_ref[:, far_cols].astype(F32)
+            out_ref[r ^ (half * n_rep * deep + i)] = total.astype(BF16)
+
+
+def split(low, high, n_row, n_rep):
+    part, cols = low[2].shape
+    width = 2 * cols // n_row
+    return pl.pallas_call(
+        functools.partial(split_body, n_rep=n_rep, deep=n_row // n_rep // 2),
+        out_shape=shape((n_row, part, width), BF16),
+        in_specs=[WHOLE] * 6,
+        out_specs=WHOLE,
+        compiler_params=params(cols * part * 40),
+        cost_estimate=pl.CostEstimate(flops=4 * part * cols, bytes_accessed=part * cols * 20, transcendentals=0),
+        name="split",
+    )(*low, *high)
 
 
 def collect_body(*refs, n_row, n_rep, per_list, quarter, blk):
     lists = refs[:n_rep]
-    messages = refs[n_rep : n_rep + n_row]
-    w_ref = refs[n_rep + n_row]
-    outs = refs[n_rep + n_row + 1 : -3]
-    w_out, other_out, acc_ref = refs[-3:]
-    q = lax.axis_index("rep")
+    messages, w_ref, other_ref = refs[n_rep : n_rep + 3]
+    outs, acc_ref = refs[n_rep + 3 : -1], refs[-1]
+    r, q = lax.axis_index("row"), lax.axis_index("rep")
     acc_ref[...] = jnp.zeros(acc_ref.shape, F32)
     for k in range(n_row):
         j = (k % n_rep) ^ q
@@ -448,21 +452,18 @@
                 b = jnp.where(j == other, lists[other][at], b)
             cell = (lax.div(b, quarter) ^ q) * quarter + lax.rem(b, quarter)
             cols = pl.ds(pl.multiple_of(cell * blk, blk), blk)
-            acc_ref[:, cols] += messages[k][: acc_ref.shape[0], c * blk : (c + 1) * blk].astype(F32)
+            acc_ref[:, cols] += messages[r ^ k, :, c * blk : (c + 1) * blk].astype(F32)
     width = outs[0].shape[1]
     part = acc_ref.shape[0]
-    w_out[...] = w_ref[...].astype(BF16)
-    other_out[...] = fold_out(messages[1], part, 0, *w_ref.shape).astype(BF16)
     for j, out in enumerate(outs):
         out[:part] = acc_ref[:, j * width : (j + 1) * width].astype(out.dtype)
-    fold_in(outs[1], part, 0, w_out[...])
-    fold_in(outs[1], part, 1, other_out[...])
-
-
-def collect(lists, messages, w, per_list, row_blocks, blk):
+    fold_in(outs[1], part, 0, w_ref[...])
+    fold_in(outs[1], part, 1, other_ref[...])
+
+
+def collect(lists, messages, w, other, per_list, row_blocks, blk):
     n_rep = len(lists)
-    n_row = len(messages)
-    part = messages[0].shape[0]
+    n_row, part, _ = messages.shape
     quarter = row_blocks // n_rep
     body = functools.partial(
         collect_body, n_row=n_row, n_rep=n_rep, per_list=per_list, quarter=quarter, blk=blk
@@ -473,17 +474,16 @@
             shape((part, quarter * blk), F32),
             shape((part + 2 * w.size // (quarter * blk), quarter * blk), BF16),
         ]
-        + [shape((part, quarter * blk), BF16)] * (n_rep - 2)
-        + [shape(w.shape, BF16)] * 2,
-        in_specs=[SMEM] * n_rep + [WHOLE] * (n_row + 1),
-        out_specs=[WHOLE] * (n_rep + 2),
+        + [shape((part, quarter * blk), BF16)] * (n_rep - 2),
+        in_specs=[SMEM] * n_rep + [WHOLE] * 3,
+        out_specs=[WHOLE] * n_rep,
         scratch_shapes=[pltpu.VMEM((part, row_blocks * blk), F32)],
         compiler_params=params(4 << 20),
         cost_estimate=pl.CostEstimate(
             flops=part * row_blocks * blk, bytes_accessed=part * row_blocks * blk * 5, transcendentals=0
         ),
         name="collect",
-    )(*lists, *messages, w)
+    )(*lists, messages, w, other)
 
 
 def finish_body(*refs, n_rep):
@@ -548,11 +548,12 @@
     table = slot_lists(
         block_rows, block_fetch, after(block_count, outgoing), n_row, n_rep, per_list, row_blocks
     )
-    adj = densify(table, blocks, n_row, per_list, row_blocks)
     deep = n_hi // 2
-    own = after(jnp.concatenate(own, axis=0), adj)
+    own = after(jnp.concatenate(own, axis=0), table)
     far = to_rep(own, 2)
-    pieces = [own, to_rep(own, 1), far, to_rep(far, 1)]
+    near = to_rep(own, 1)
+    adj = densify(after(table, near), blocks, n_row, per_list, row_blocks)
+    pieces = [own, near, far, to_rep(after(far, adj), 1)]
 
     send3, keep2 = forward(pieces, adj, 0)
     across = (keep2 + to_rep(send3, 1).astype(F32)).astype(BF16)
@@ -572,32 +573,31 @@
     got = to_rep(w, 2)
     send_high, keep_high = back_second(grad3, grad2, adj, first, 1, n_rep, deep)
     send_high = after(send_high, got)
+    w = w + got
+    got = to_row(w, 2)
     near_high = to_rep(send_high, 1)
     send_low, keep_low = back_second(grad3, grad2, adj, after(first, send_high), 0, n_rep, deep)
-    near_low = to_rep(send_low, 1)
-    w = w + got
-    got = to_row(w, 2)
+    near_low = to_rep(after(send_low, near_high, got), 1)
     part = features // n_rep
 
     def across_sum(keep, near):
         return (keep[:part] + near[:part].astype(F32)).astype(BF16)
 
-    far_high = to_rep(across_sum(keep_high, after(near_high, send_low, got)), 2)
-    across = across_sum(keep_low, near_low)
-    far_low = to_rep(across, 2)
+    across_high = across_sum(keep_high, after(near_high, send_low))
+    across_low = across_sum(keep_low, near_low)
+    far_high = to_rep(across_high, 2)
+    far_low = to_rep(across_low, 2)
     w = w + got
-    got = to_row(after(w, across), 4)
-    high = split(keep_high, near_high, after(far_high, got), None, 1, n_rep, deep)
-    w = w + got
+    w = w + to_row(after(w, across_high, across_low), 4)
     step = 8
     while step < n_row:
         w = w + to_row(w, step)
         step *= 2
-    half_rows = n_row // 2
-    back_high = [to_row(x, half_rows + i) for i, x in enumerate(high)]
-    low = split(keep_low, near_low, after(far_low, back_high[:2]), w, 0, n_rep, deep)
-    returned = [low[0]] + [to_row(low[i], i) for i in range(1, half_rows)] + back_high
-    *grads, w, other = collect(lists, returned, w, per_list, row_blocks, blk)
+    w = w.astype(BF16)
+    other = to_row(w, 1)
+    messages = split((keep_low, near_low, far_low), (keep_high, near_high, after(far_high, w)), n_row, n_rep)
+    returned = lax.all_to_all(messages, "row", split_axis=0, concat_axis=0, tiled=True)
+    grads = collect(lists, returned, w, other, per_list, row_blocks, blk)
     node_grad, weight_grad = finish([grads[0]] + [to_rep(grads[j], j) for j in range(1, n_rep)], w, other)
     return (output, weight_grad, node_grad)
 

time: 102 us -> 99.3 us (0.974)
  waiting for transfers between devices: 32.8 us -> 31 us
    ppermute x10 -> x4, starting transfers between devices: 18 us -> 7.16 us  [to_row(): return lax.ppermute(x, 'row', xor_perm(n_row, k))]
    ppermute x20, starting transfers between devices: 16.8 us -> 22.1 us  [to_rep(): return lax.ppermute(x, 'rep', xor_perm(n_rep, j))]
    all_to_all x0 -> x1, starting transfers between devices: none -> 4.91 us  [local(): lax.all_to_all(messages, 'row', split_axis=0, concat_axis=0, tiled=True)]
    all_to_all x0 -> x1, waiting for transfers between devices: none -> 3.76 us  [local(): lax.all_to_all(messages, 'row', split_axis=0, concat_axis=0, tiled=True)]
    ppermute x10 -> x4, waiting for transfers between devices: 13.1 us -> 9.92 us  [to_row(): return lax.ppermute(x, 'row', xor_perm(n_row, k))]
    ppermute x20, waiting for transfers between devices: 19.4 us -> 16.4 us  [to_rep(): return lax.ppermute(x, 'rep', xor_perm(n_rep, j))]
  transfers between devices with their start and end apart: 34 -> 29, of which waited for: 20 -> 19; matrix products, arithmetic and copies ran while one was open for 0% -> 0% of each run, Pallas kernels for 15% -> 15%
where the time goes in v7:
time: 99.3 us; the launch traced here: 98.9 us
  starting transfers between devices  42.6 us (43%)
  waiting for transfers between devices  31 us (31%)
  Pallas kernels  22.1 us (22%)
  between operations  1.51 us (2%)
  local copies, waits for them, and re-layouts  1.47 us (1%)
    ppermute x20, starting transfers between devices, to_rep(): return lax.ppermute(x, 'rep', xor_perm(n_rep, j))  22.1 us
    ppermute x20, waiting for transfers between devices, to_rep(): return lax.ppermute(x, 'rep', xor_perm(n_rep, j))  16.4 us
    ppermute x4, waiting for transfers between devices, to_row(): return lax.ppermute(x, 'row', xor_perm(n_row, k))  9.92 us
    ppermute x4, starting transfers between devices, spread(): return lax.ppermute(x, ('row', 'rep'), perm)  8.47 us
    ppermute x4, starting transfers between devices, to_row(): return lax.ppermute(x, 'row', xor_perm(n_row, k))  7.16 us
    all_to_all x1, starting transfers between devices, local(): lax.all_to_all(messages, 'row', split_axis=0, concat_axis=0, tiled=True)  4.91 us
    pallas_call x1, Pallas kernels, densify(): pl.pallas_call(functools.partial(densify_body, all_cols=all_cols, row_blo...  4.29 us
    all_to_all x1, waiting for transfers between devices, local(): lax.all_to_all(messages, 'row', split_axis=0, concat_axis=0, tiled=True)  3.76 us
  transfers between devices with their start and end apart: 29, of which 19 were waited for; matrix products, arithmetic and copies ran while one was open for 0% of the time, Pallas kernels for 15%

profile of v7, /device:TPU:0, one launch (start us, length us, event | category | flops | bytes accessed | tf_op | source)
XLA Modules:
  0.0 98.9 jit_solution(16003342905155797369)
XLA Ops:
  1.4 4.0 %collective-permute-start.1 = (s32[1,8,2]{2,1,0:T(8,128)S(1)}, s32[1,8,2]{2,1,0:T(8,128)S(1)}, u32[]{:S(2)}, u32[]{:S(2)}) collective-permute-start(s32[1,8,2]{2,1,0:T(8,128)S(1)} %copy.11), channel_id=1, source_target_pairs={{0,16},{1,21},{2,26},{3,31},{4,20},{5,17},{6,30},{7,27},{8,24},{9,... | collective-permute-start | bytes 200 | tf_op jit(solution)/shard_map/ppermute | solution.py:540
  7.0 2.2 %pack.1 = (bf16[256,256]{1,0:T(8,128)(2,1)S(1)}, bf16[256,256]{1,0:T(8,128)(2,1)S(1)}, s32[128]{0:T(128)S(1)}) custom-call(s32[1,8,2]{2,1,0:T(8,128)S(1)} %collective-permute-done.refs_0_, s32[1,8,2]{2,1,0:T(8,128)S(1)} %collective-permute-done.1.refs_1_, bf16[2048,256]{1,0:T(8,128)(2,1)} %refs_2_.1), custom_call_target="tpu_custom_call" | custom-call | tf_op jit(solution)/shard_map/pack/pallas_call | solution.py:215
  10.1 3.0 %collective-permute-start.3 = (bf16[256,256]{1,0:T(8,128)(2,1)S(1)}, bf16[256,256]{1,0:T(8,128)(2,1)S(1)}, u32[]{:S(2)}, u32[]{:S(2)}) collective-permute-start(bf16[256,256]{1,0:T(8,128)(2,1)S(1)} %get-tuple-element.42), channel_id=1, source_target_pairs={{0,16},{1,21},{2,26},{3,31},{4,20},{5,17},{6,30},{7,27},{8,24},{9,... | collective-permute-start | bytes 393224 | tf_op jit(solution)/shard_map/ppermute | solution.py:540
  13.1 2.3 %slot_lists.1.table_ref = s32[1152]{0:T(1024)} custom-call(s32[192]{0:T(256)} %rows_ref.1, s32[192]{0:T(256)} %fetch_ref.1, s32[1]{0:T(128)S(6)} %copy.13.count_ref), custom_call_target="tpu_custom_call" | custom-call | flops 3221225472 | bytes 1536 | tf_op jit(solution)/shard_map/slot_lists/pallas_call | solution.py:116
  16.1 6.1 %collective-permute-start.4 = (bf16[512,256]{1,0:T(8,128)(2,1)S(1)}, bf16[512,256]{1,0:T(8,128)(2,1)S(1)}, u32[]{:S(2)}, u32[]{:S(2)}) collective-permute-start(bf16[512,256]{1,0:T(8,128)(2,1)S(1)} %pad_maximum_fusion.refs_0_), channel_id=1, source_target_pairs={{0,1},{1,0},{2,3},{3,2},{4,5},{5,4},{6,7},{7,6},{8,9},{9,8},{10,11... | collective-permute-start | bytes 786440 | tf_op jit(solution)/shard_map/ppermute | solution.py:531
  22.1 4.3 %collective-permute-start.5 = (bf16[512,256]{1,0:T(8,128)(2,1)S(1)}, bf16[512,256]{1,0:T(8,128)(2,1)S(1)}, u32[]{:S(2)}, u32[]{:S(2)}) collective-permute-start(bf16[512,256]{1,0:T(8,128)(2,1)S(1)} %pad_maximum_fusion.refs_0_), channel_id=1, source_target_pairs={{0,2},{1,3},{2,0},{3,1},{4,6},{5,7},{6,4},{7,5},{8,10},{9,11},{10,... | collective-permute-start | bytes 786440 | tf_op jit(solution)/shard_map/ppermute | solution.py:531
  27.1 4.3 %densify.1.refs_4_.adj_ref = bf16[2048,2048]{1,0:T(8,128)(2,1)S(1)} custom-call(s32[1152]{0:T(1024)S(1)} %copy-done.2, bf16[192,128,128]{2,1,0:T(8,128)(2,1)S(1)} %bitcast.1), custom_call_target="tpu_custom_call" | custom-call | flops 3145728 | bytes 14680064 | tf_op jit(solution)/shard_map/densify/pallas_call | solution.py:172
  31.4 1.9 %collective-permute-done.5.refs_2_ = bf16[512,256]{1,0:T(8,128)(2,1)S(1)} collective-permute-done((bf16[512,256]{1,0:T(8,128)(2,1)S(1)}, bf16[512,256]{1,0:T(8,128)(2,1)S(1)}, u32[]{:S(2)}, u32[]{:S(2)}) %collective-permute-start.5) | collective-permute-done | bytes 262176 | tf_op jit(solution)/shard_map/ppermute | solution.py:531
  34.8 1.8 %forward.2 = (bf16[512,256]{1,0:T(8,128)(2,1)S(1)}, f32[512,256]{1,0:T(8,128)S(1)}) custom-call(bf16[512,256]{1,0:T(8,128)(2,1)S(1)} %pad_maximum_fusion.refs_0_, bf16[512,256]{1,0:T(8,128)(2,1)S(1)} %collective-permute-done.4.refs_1_, bf16[512,256]{1,0:T(8,128)(2,1)S(1)} %collective-permute-done.5.refs_2_, ...), custom_call_target="tpu_custom_call" | custom-call | flops 1073741824 | bytes 5242880 | tf_op jit(solution)/shard_map/forward/pallas_call | solution.py:253
  38.4 1.8 %collective-permute-start.9 = (bf16[512,256]{1,0:T(8,128)(2,1)S(1)}, bf16[512,256]{1,0:T(8,128)(2,1)S(1)}, u32[]{:S(2)}, u32[]{:S(2)}) collective-permute-start(bf16[512,256]{1,0:T(8,128)(2,1)S(1)} %add_convert_fusion), channel_id=1, source_target_pairs={{0,2},{1,3},{2,0},{3,1},{4,6},{5,7},{6,4},{7,5},{8,10},{9,11},{10,... | collective-permute-start | bytes 786440 | tf_op jit(solution)/shard_map/ppermute | solution.py:531
  40.2 1.8 %forward.3 = (bf16[512,256]{1,0:T(8,128)(2,1)S(1)}, f32[512,256]{1,0:T(8,128)S(1)}) custom-call(bf16[512,256]{1,0:T(8,128)(2,1)S(1)} %pad_maximum_fusion.refs_0_, bf16[512,256]{1,0:T(8,128)(2,1)S(1)} %collective-permute-done.4.refs_1_, bf16[512,256]{1,0:T(8,128)(2,1)S(1)} %collective-permute-done.5.refs_2_, ...), custom_call_target="tpu_custom_call" | custom-call | flops 1073741824 | bytes 5242880 | tf_op jit(solution)/shard_map/forward/pallas_call | solution.py:253
  44.3 1.8 %collective-permute-done.12.refs_3_ = s32[128]{0:T(128)S(1)} collective-permute-done((s32[128]{0:T(128)S(1)}, s32[128]{0:T(128)S(1)}, u32[]{:S(2)}, u32[]{:S(2)}) %collective-permute-start.12) | collective-permute-done | bytes 544 | tf_op jit(solution)/shard_map/ppermute | solution.py:531
  49.8 2.3 %back_first.1 = (f32[256,2048]{1,0:T(8,128)S(1)}, f32[64,256]{1,0:T(8,128)S(1)}, f32[64,256]{1,0:T(8,128)S(1)}) custom-call(bf16[320,512]{1,0:T(8,128)(2,1)S(1)} %collective-permute-done.14.odd_ref, bf16[256,512]{1,0:T(8,128)(2,1)S(1)} %get-tuple-element.56.even_ref, bf16[2048,2048]{1,0:T(8,128)(2,1)S(1)} %densify.1.refs_4_.adj_ref, ...), custom_call_target="tpu_custom_call" | custom-call | flops 1073741824 | bytes 6291456 | tf_op jit(solution)/shard_map/back_first/pallas_call | solution.py:354
  53.7 2.7 %collective-permute-done.15 = f32[64,256]{1,0:T(8,128)S(1)} collective-permute-done((f32[64,256]{1,0:T(8,128)S(1)}, f32[64,256]{1,0:T(8,128)S(1)}, u32[]{:S(2)}, u32[]{:S(2)}) %collective-permute-start.15) | collective-permute-done | bytes 65568 | tf_op jit(solution)/shard_map/ppermute | solution.py:534
  58.5 1.8 %back_second_1.1 = (bf16[128,1024]{1,0:T(8,128)(2,1)S(1)}, f32[128,1024]{1,0:T(8,128)S(1)}) custom-call(bf16[256,512]{1,0:T(8,128)(2,1)S(1)} %collective-permute-done.16.odd_ref, bf16[256,512]{1,0:T(8,128)(2,1)S(1)} %collective-permute-done.13.even_ref, bf16[2048,2048]{1,0:T(8,128)(2,1)S(1)} %densify.1.refs_4_.adj_ref, ...), custom_call_target="tpu_custom_call" | custom-call | flops 536870912 | bytes 3932160 | tf_op jit(solution)/shard_map/back_second_1/pallas_call | solution.py:387
  61.2 2.7 %collective-permute-start.19 = (f32[64,256]{1,0:T(8,128)S(1)}, f32[64,256]{1,0:T(8,128)S(1)}, u32[]{:S(2)}, u32[]{:S(2)}) collective-permute-start(f32[64,256]{1,0:T(8,128)S(1)} %add.23), channel_id=1, source_target_pairs={{0,8},{4,12},{8,0},{12,4},{16,24},{20,28},{24,16},{28,20},{1,9},{5... | collective-permute-start | bytes 196616 | tf_op jit(solution)/shard_map/ppermute | solution.py:534
  64.0 1.8 %back_second_0.1 = (bf16[128,1024]{1,0:T(8,128)(2,1)S(1)}, f32[128,1024]{1,0:T(8,128)S(1)}) custom-call(bf16[256,512]{1,0:T(8,128)(2,1)S(1)} %collective-permute-done.16.odd_ref, bf16[256,512]{1,0:T(8,128)(2,1)S(1)} %collective-permute-done.13.even_ref, bf16[2048,2048]{1,0:T(8,128)(2,1)S(1)} %densify.1.refs_4_.adj_ref, ...), custom_call_target="tpu_custom_call" | custom-call | flops 536870912 | bytes 3932160 | tf_op jit(solution)/shard_map/back_second_0/pallas_call | solution.py:387
  71.2 3.8 %collective-permute-done.23 = f32[64,256]{1,0:T(8,128)S(1)} collective-permute-done((f32[64,256]{1,0:T(8,128)S(1)}, f32[64,256]{1,0:T(8,128)S(1)}, u32[]{:S(2)}, u32[]{:S(2)}) %collective-permute-start.23) | collective-permute-done | bytes 65568 | tf_op jit(solution)/shard_map/ppermute | solution.py:534
  78.0 4.9 %all-to-all-start = ((bf16[8,64,256]{2,1,0:T(8,128)(2,1)}), bf16[8,64,256]{2,1,0:T(8,128)(2,1)S(1)}, u32[]{:S(2)}, u32[]{:S(2)}) async-start(bf16[8,64,256]{2,1,0:T(8,128)(2,1)} %split.1), calls=%async_computation | async-start | bytes 524288 | tf_op jit(solution)/shard_map/all_to_all | solution.py:599
  82.9 2.0 %collective-permute-start.24 = (bf16[64,256]{1,0:T(8,128)(2,1)S(1)}, bf16[64,256]{1,0:T(8,128)(2,1)S(1)}, u32[]{:S(2)}, u32[]{:S(2)}) collective-permute-start(bf16[64,256]{1,0:T(8,128)(2,1)S(1)} %add_convert_fusion.3.refs_5_.refs_4_), channel_id=1, source_target_pairs={{0,4},{4,0},{8,12},{12,8},{16,20},{20,16},{24,28},{28,24},{1,5},{5... | collective-permute-start | bytes 98312 | tf_op jit(solution)/shard_map/ppermute | solution.py:534
  85.0 2.4 %collective-permute-done.24.refs_6_.refs_5_ = bf16[64,256]{1,0:T(8,128)(2,1)S(1)} collective-permute-done((bf16[64,256]{1,0:T(8,128)(2,1)S(1)}, bf16[64,256]{1,0:T(8,128)(2,1)S(1)}, u32[]{:S(2)}, u32[]{:S(2)}) %collective-permute-start.24) | collective-permute-done | bytes 32800 | tf_op jit(solution)/shard_map/ppermute | solution.py:534
  87.4 3.8 %all-to-all-done.refs_4_ = bf16[8,64,256]{2,1,0:T(8,128)(2,1)S(1)} async-done(((bf16[8,64,256]{2,1,0:T(8,128)(2,1)}), bf16[8,64,256]{2,1,0:T(8,128)(2,1)S(1)}, u32[]{:S(2)}, u32[]{:S(2)}) %all-to-all-start) | async-done | bytes 262176 | tf_op jit(solution)/shard_map/all_to_all | solution.py:599
  92.0 1.8 %collective-permute-start.26 = (bf16[64,512]{1,0:T(8,128)(2,1)S(1)}, bf16[64,512]{1,0:T(8,128)(2,1)S(1)}, u32[]{:S(2)}, u32[]{:S(2)}) collective-permute-start(bf16[64,512]{1,0:T(8,128)(2,1)S(1)} %get-tuple-element.75), channel_id=1, source_target_pairs={{0,2},{1,3},{2,0},{3,1},{4,6},{5,7},{6,4},{7,5},{8,10},{9,11},{10,... | collective-permute-start | bytes 196616 | tf_op jit(solution)/shard_map/ppermute | solution.py:531
  93.9 2.6 %collective-permute-done.26.refs_2_ = bf16[64,512]{1,0:T(8,128)(2,1)S(1)} collective-permute-done((bf16[64,512]{1,0:T(8,128)(2,1)S(1)}, bf16[64,512]{1,0:T(8,128)(2,1)S(1)}, u32[]{:S(2)}, u32[]{:S(2)}) %collective-permute-start.26) | collective-permute-done | bytes 65568 | tf_op jit(solution)/shard_map/ppermute | solution.py:531
  (66 shorter events, 29.2 us)
Async XLA Ops:
  1.4 5.6 %collective-permute-start.1 = (s32[1,8,2]{2,1,0:T(8,128)S(1)}, s32[1,8,2]{2,1,0:T(8,128)S(1)}, u32[]{:S(2)}, u32[]{:S(2)}) collective-permute-start(s32[1,8,2]{2,1,0:T(8,128)S(1)} %copy.11), channel_id=1, source_target_pairs={{0,16},{1,21},{2,26},{3,31},{4,20},{5,17},{6,30},{7,27},{8,24},{9,... | collective-permute-start | bytes 200 | tf_op jit(solution)/shard_map/ppermute | solution.py:540
  9.3 6.1 %collective-permute-start.2 = (bf16[256,256]{1,0:T(8,128)(2,1)S(1)}, bf16[256,256]{1,0:T(8,128)(2,1)S(1)}, u32[]{:S(2)}, u32[]{:S(2)}) collective-permute-start(bf16[256,256]{1,0:T(8,128)(2,1)S(1)} %get-tuple-element.41), channel_id=1, source_target_pairs={{0,0},{1,5},{2,10},{3,15},{4,4},{5,1},{6,14},{7,11},{8,8},{9,13},{... | collective-permute-start | bytes 393224 | tf_op jit(solution)/shard_map/ppermute | solution.py:540
  10.1 5.9 %collective-permute-start.3 = (bf16[256,256]{1,0:T(8,128)(2,1)S(1)}, bf16[256,256]{1,0:T(8,128)(2,1)S(1)}, u32[]{:S(2)}, u32[]{:S(2)}) collective-permute-start(bf16[256,256]{1,0:T(8,128)(2,1)S(1)} %get-tuple-element.42), channel_id=1, source_target_pairs={{0,16},{1,21},{2,26},{3,31},{4,20},{5,17},{6,30},{7,27},{8,24},{9,... | collective-permute-start | bytes 393224 | tf_op jit(solution)/shard_map/ppermute | solution.py:540
  16.1 10.4 %collective-permute-start.4 = (bf16[512,256]{1,0:T(8,128)(2,1)S(1)}, bf16[512,256]{1,0:T(8,128)(2,1)S(1)}, u32[]{:S(2)}, u32[]{:S(2)}) collective-permute-start(bf16[512,256]{1,0:T(8,128)(2,1)S(1)} %pad_maximum_fusion.refs_0_), channel_id=1, source_target_pairs={{0,1},{1,0},{2,3},{3,2},{4,5},{5,4},{6,7},{7,6},{8,9},{9,8},{10,11... | collective-permute-start | bytes 786440 | tf_op jit(solution)/shard_map/ppermute | solution.py:531
  22.1 11.2 %collective-permute-start.5 = (bf16[512,256]{1,0:T(8,128)(2,1)S(1)}, bf16[512,256]{1,0:T(8,128)(2,1)S(1)}, u32[]{:S(2)}, u32[]{:S(2)}) collective-permute-start(bf16[512,256]{1,0:T(8,128)(2,1)S(1)} %pad_maximum_fusion.refs_0_), channel_id=1, source_target_pairs={{0,2},{1,3},{2,0},{3,1},{4,6},{5,7},{6,4},{7,5},{8,10},{9,11},{10,... | collective-permute-start | bytes 786440 | tf_op jit(solution)/shard_map/ppermute | solution.py:531
  38.4 8.5 %collective-permute-start.9 = (bf16[512,256]{1,0:T(8,128)(2,1)S(1)}, bf16[512,256]{1,0:T(8,128)(2,1)S(1)}, u32[]{:S(2)}, u32[]{:S(2)}) collective-permute-start(bf16[512,256]{1,0:T(8,128)(2,1)S(1)} %add_convert_fusion), channel_id=1, source_target_pairs={{0,2},{1,3},{2,0},{3,1},{4,6},{5,7},{6,4},{7,5},{8,10},{9,11},{10,... | collective-permute-start | bytes 786440 | tf_op jit(solution)/shard_map/ppermute | solution.py:531
  42.0 4.9 %collective-permute-start.8 = (bf16[512,256]{1,0:T(8,128)(2,1)S(1)}, bf16[512,256]{1,0:T(8,128)(2,1)S(1)}, u32[]{:S(2)}, u32[]{:S(2)}) collective-permute-start(bf16[512,256]{1,0:T(8,128)(2,1)S(1)} %get-tuple-element.51), channel_id=1, source_target_pairs={{0,1},{1,0},{2,3},{3,2},{4,5},{5,4},{6,7},{7,6},{8,9},{9,8},{10,11... | collective-permute-start | bytes 786440 | tf_op jit(solution)/shard_map/ppermute | solution.py:531
  42.1 4.0 %collective-permute-start.12 = (s32[128]{0:T(128)S(1)}, s32[128]{0:T(128)S(1)}, u32[]{:S(2)}, u32[]{:S(2)}) collective-permute-start(s32[128]{0:T(128)S(1)} %get-tuple-element.53.refs_0_), channel_id=1, source_target_pairs={{0,3},{1,2},{2,1},{3,0},{4,7},{5,6},{6,5},{7,4},{8,11},{9,10},{10,... | collective-permute-start | bytes 1544 | tf_op jit(solution)/shard_map/ppermute | solution.py:531
  42.5 4.4 %collective-permute-start.11 = (s32[128]{0:T(128)S(1)}, s32[128]{0:T(128)S(1)}, u32[]{:S(2)}, u32[]{:S(2)}) collective-permute-start(s32[128]{0:T(128)S(1)} %get-tuple-element.53.refs_0_), channel_id=1, source_target_pairs={{0,2},{1,3},{2,0},{3,1},{4,6},{5,7},{6,4},{7,5},{8,10},{9,11},{10,... | collective-permute-start | bytes 1544 | tf_op jit(solution)/shard_map/ppermute | solution.py:531
  44.3 2.6 %collective-permute-start.10 = (s32[128]{0:T(128)S(1)}, s32[128]{0:T(128)S(1)}, u32[]{:S(2)}, u32[]{:S(2)}) collective-permute-start(s32[128]{0:T(128)S(1)} %get-tuple-element.53.refs_0_), channel_id=1, source_target_pairs={{0,1},{1,0},{2,3},{3,2},{4,5},{5,4},{6,7},{7,6},{8,9},{9,8},{10,11... | collective-permute-start | bytes 1544 | tf_op jit(solution)/shard_map/ppermute | solution.py:531
  48.0 1.8 %collective-permute-start.14 = (bf16[320,512]{1,0:T(8,128)(2,1)S(1)}, bf16[320,512]{1,0:T(8,128)(2,1)S(1)}, u32[]{:S(2)}, u32[]{:S(2)}) collective-permute-start(bf16[320,512]{1,0:T(8,128)(2,1)S(1)} %get-tuple-element.57), channel_id=1, source_target_pairs={{0,1},{1,0},{2,3},{3,2},{4,5},{5,4},{6,7},{7,6},{8,9},{9,8},{10,11... | collective-permute-start | bytes 983048 | tf_op jit(solution)/shard_map/ppermute | solution.py:531
  48.0 8.7 %collective-permute-start.13 = (bf16[256,512]{1,0:T(8,128)(2,1)S(1)}, bf16[256,512]{1,0:T(8,128)(2,1)S(1)}, u32[]{:S(2)}, u32[]{:S(2)}) collective-permute-start(bf16[256,512]{1,0:T(8,128)(2,1)S(1)} %get-tuple-element.56.even_ref), channel_id=1, source_target_pairs={{0,2},{1,3},{2,0},{3,1},{4,6},{5,7},{6,4},{7,5},{8,10},{9,11},{10,... | collective-permute-start | bytes 786440 | tf_op jit(solution)/shard_map/ppermute | solution.py:531
  52.1 4.3 %collective-permute-start.15 = (f32[64,256]{1,0:T(8,128)S(1)}, f32[64,256]{1,0:T(8,128)S(1)}, u32[]{:S(2)}, u32[]{:S(2)}) collective-permute-start(f32[64,256]{1,0:T(8,128)S(1)} %get-tuple-element.61), channel_id=1, source_target_pairs={{0,4},{4,0},{8,12},{12,8},{16,20},{20,16},{24,28},{28,24},{1,5},{5... | collective-permute-start | bytes 196616 | tf_op jit(solution)/shard_map/ppermute | solution.py:534
  56.7 4.5 %collective-permute-start.17 = (f32[64,256]{1,0:T(8,128)S(1)}, f32[64,256]{1,0:T(8,128)S(1)}, u32[]{:S(2)}, u32[]{:S(2)}) collective-permute-start(f32[64,256]{1,0:T(8,128)S(1)} %add.22), channel_id=1, source_target_pairs={{0,2},{1,3},{2,0},{3,1},{4,6},{5,7},{6,4},{7,5},{8,10},{9,11},{10,... | collective-permute-start | bytes 196616 | tf_op jit(solution)/shard_map/ppermute | solution.py:531
  61.2 5.5 %collective-permute-start.18 = (bf16[128,1024]{1,0:T(8,128)(2,1)S(1)}, bf16[128,1024]{1,0:T(8,128)(2,1)S(1)}, u32[]{:S(2)}, u32[]{:S(2)}) collective-permute-start(bf16[128,1024]{1,0:T(8,128)(2,1)S(1)} %get-tuple-element.64), channel_id=1, source_target_pairs={{0,1},{1,0},{2,3},{3,2},{4,5},{5,4},{6,7},{7,6},{8,9},{9,8},{10,11... | collective-permute-start | bytes 786440 | tf_op jit(solution)/shard_map/ppermute | solution.py:531
  61.2 5.5 %collective-permute-start.19 = (f32[64,256]{1,0:T(8,128)S(1)}, f32[64,256]{1,0:T(8,128)S(1)}, u32[]{:S(2)}, u32[]{:S(2)}) collective-permute-start(f32[64,256]{1,0:T(8,128)S(1)} %add.23), channel_id=1, source_target_pairs={{0,8},{4,12},{8,0},{12,4},{16,24},{20,28},{24,16},{28,20},{1,9},{5... | collective-permute-start | bytes 196616 | tf_op jit(solution)/shard_map/ppermute | solution.py:534
  68.3 6.6 %collective-permute-start.23 = (f32[64,256]{1,0:T(8,128)S(1)}, f32[64,256]{1,0:T(8,128)S(1)}, u32[]{:S(2)}, u32[]{:S(2)}) collective-permute-start(f32[64,256]{1,0:T(8,128)S(1)} %add.26), channel_id=1, source_target_pairs={{0,16},{4,20},{8,24},{12,28},{16,0},{20,4},{24,8},{28,12},{1,17},{... | collective-permute-start | bytes 196616 | tf_op jit(solution)/shard_map/ppermute | solution.py:534
  69.1 6.4 %collective-permute-start.22 = (bf16[64,1024]{1,0:T(8,128)(2,1)S(1)}, bf16[64,1024]{1,0:T(8,128)(2,1)S(1)}, u32[]{:S(2)}, u32[]{:S(2)}) collective-permute-start(bf16[64,1024]{1,0:T(8,128)(2,1)S(1)} %add_convert_fusion.1), channel_id=1, source_target_pairs={{0,2},{1,3},{2,0},{3,1},{4,6},{5,7},{6,4},{7,5},{8,10},{9,11},{10,... | collective-permute-start | bytes 393224 | tf_op jit(solution)/shard_map/ppermute | solution.py:531
  70.9 6.3 %collective-permute-start.21 = (bf16[64,1024]{1,0:T(8,128)(2,1)S(1)}, bf16[64,1024]{1,0:T(8,128)(2,1)S(1)}, u32[]{:S(2)}, u32[]{:S(2)}) collective-permute-start(bf16[64,1024]{1,0:T(8,128)(2,1)S(1)} %add_convert_fusion.2), channel_id=1, source_target_pairs={{0,2},{1,3},{2,0},{3,1},{4,6},{5,7},{6,4},{7,5},{8,10},{9,11},{10,... | collective-permute-start | bytes 393224 | tf_op jit(solution)/shard_map/ppermute | solution.py:531
  78.0 13.1 %all-to-all-start = ((bf16[8,64,256]{2,1,0:T(8,128)(2,1)}), bf16[8,64,256]{2,1,0:T(8,128)(2,1)S(1)}, u32[]{:S(2)}, u32[]{:S(2)}) async-start(bf16[8,64,256]{2,1,0:T(8,128)(2,1)} %split.1), calls=%async_computation | async-start | bytes 524288 | tf_op jit(solution)/shard_map/all_to_all | solution.py:599
  82.9 4.5 %collective-permute-start.24 = (bf16[64,256]{1,0:T(8,128)(2,1)S(1)}, bf16[64,256]{1,0:T(8,128)(2,1)S(1)}, u32[]{:S(2)}, u32[]{:S(2)}) collective-permute-start(bf16[64,256]{1,0:T(8,128)(2,1)S(1)} %add_convert_fusion.3.refs_5_.refs_4_), channel_id=1, source_target_pairs={{0,4},{4,0},{8,12},{12,8},{16,20},{20,16},{24,28},{28,24},{1,5},{5... | collective-permute-start | bytes 98312 | tf_op jit(solution)/shard_map/ppermute | solution.py:534
  91.9 5.9 %collective-permute-start.25 = (bf16[128,512]{1,0:T(8,128)(2,1)S(1)}, bf16[128,512]{1,0:T(8,128)(2,1)S(1)}, u32[]{:S(2)}, u32[]{:S(2)}) collective-permute-start(bf16[128,512]{1,0:T(8,128)(2,1)S(1)} %get-tuple-element.74), channel_id=1, source_target_pairs={{0,1},{1,0},{2,3},{3,2},{4,5},{5,4},{6,7},{7,6},{8,9},{9,8},{10,11... | collective-permute-start | bytes 393224 | tf_op jit(solution)/shard_map/ppermute | solution.py:531
  92.0 4.5 %collective-permute-start.26 = (bf16[64,512]{1,0:T(8,128)(2,1)S(1)}, bf16[64,512]{1,0:T(8,128)(2,1)S(1)}, u32[]{:S(2)}, u32[]{:S(2)}) collective-permute-start(bf16[64,512]{1,0:T(8,128)(2,1)S(1)} %get-tuple-element.75), channel_id=1, source_target_pairs={{0,2},{1,3},{2,0},{3,1},{4,6},{5,7},{6,4},{7,5},{8,10},{9,11},{10,... | collective-permute-start | bytes 196616 | tf_op jit(solution)/shard_map/ppermute | solution.py:531
  93.8 4.0 %collective-permute-start.27 = (bf16[64,512]{1,0:T(8,128)(2,1)S(1)}, bf16[64,512]{1,0:T(8,128)(2,1)S(1)}, u32[]{:S(2)}, u32[]{:S(2)}) collective-permute-start(bf16[64,512]{1,0:T(8,128)(2,1)S(1)} %get-tuple-element.76), channel_id=1, source_target_pairs={{0,3},{1,2},{2,1},{3,0},{4,7},{5,6},{6,5},{7,4},{8,11},{9,10},{10,... | collective-permute-start | bytes 196616 | tf_op jit(solution)/shard_map/ppermute | solution.py:531
  (10 other events, 62.6 us)

commit v8 on v7

--- a/solution.py
+++ b/solution.py
@@ -332,32 +332,28 @@
     )(keep, near, far, weight, cot)
 
 
-def back_first_body(odd_ref, even_ref, adj_ref, wkeep_ref, out_ref, wsend_out, wkeep_out):
+def back_first_body(odd_ref, even_ref, adj_ref, wkeep_ref, out_ref, w_out):
     features, rows = out_ref.shape[0], odd_ref.shape[1]
     out_ref[...] = dot(odd_ref[:features], adj_ref[:rows]) + dot(even_ref[...], adj_ref[rows:])
 
     @pl.when(pl.program_id(0) == 0)
     def _():
-        part = wkeep_out.shape[0]
-        mine = (lax.rem(lax.axis_index("row"), 2) ^ lax.div(lax.axis_index("rep"), 2)) == 0
-        zero = wkeep_ref[:part] + fold_out(odd_ref, features, 0, *wkeep_out.shape)
-        two = wkeep_ref[part:] + fold_out(odd_ref, features, 1, *wkeep_out.shape)
-        wkeep_out[...] = jnp.where(mine, zero, two)
-        wsend_out[...] = jnp.where(mine, two, zero)
+        part = w_out.shape[0] // 2
+        for at in range(2):
+            rows_here = slice(at * part, (at + 1) * part)
+            w_out[rows_here] = wkeep_ref[rows_here] + fold_out(odd_ref, features, at, part, features)
 
 
 def back_first(odd, even, adj, wkeep):
     rows, cols = adj.shape[0] // 2, adj.shape[1]
     features = wkeep.shape[1]
     whole = lambda x: pl.BlockSpec(x.shape, lambda i: (0, 0))
-    part = wkeep.shape[0] // 2
     return pl.pallas_call(
         back_first_body,
         grid=(cols // COL_TILE,),
-        out_shape=[shape((features, cols), F32)] + [shape((part, features), F32)] * 2,
+        out_shape=[shape((features, cols), F32), shape(wkeep.shape, F32)],
         in_specs=[whole(odd), whole(even), pl.BlockSpec((rows, COL_TILE), lambda i: (1, i)), whole(wkeep)],
-        out_specs=[pl.BlockSpec((features, COL_TILE), lambda i: (0, i))]
-        + [pl.BlockSpec((part, features), lambda i: (0, 0))] * 2,
+        out_specs=[pl.BlockSpec((features, COL_TILE), lambda i: (0, i)), whole(wkeep)],
         compiler_params=params(4 << 20),
         cost_estimate=pl.CostEstimate(
             flops=2 * rows * cols * features, bytes_accessed=adj.size + cols * features * 4, transcendentals=0
@@ -439,8 +435,8 @@
 
 def collect_body(*refs, n_row, n_rep, per_list, quarter, blk):
     lists = refs[:n_rep]
-    messages, w_ref, other_ref = refs[n_rep : n_rep + 3]
-    outs, acc_ref = refs[n_rep + 3 : -1], refs[-1]
+    messages, w_ref = refs[n_rep : n_rep + 2]
+    outs, acc_ref = refs[n_rep + 2 : -1], refs[-1]
     r, q = lax.axis_index("row"), lax.axis_index("rep")
     acc_ref[...] = jnp.zeros(acc_ref.shape, F32)
     for k in range(n_row):
@@ -457,11 +453,11 @@
     part = acc_ref.shape[0]
     for j, out in enumerate(outs):
         out[:part] = acc_ref[:, j * width : (j + 1) * width].astype(out.dtype)
-    fold_in(outs[1], part, 0, w_ref[...])
-    fold_in(outs[1], part, 1, other_ref[...])
-
-
-def collect(lists, messages, w, other, per_list, row_blocks, blk):
+        if j:
+            fold_in(out, part, 0, w_ref[...])
+
+
+def collect(lists, messages, w, per_list, row_blocks, blk):
     n_rep = len(lists)
     n_row, part, _ = messages.shape
     quarter = row_blocks // n_rep
@@ -470,12 +466,9 @@
     )
     return pl.pallas_call(
         body,
-        out_shape=[
-            shape((part, quarter * blk), F32),
-            shape((part + 2 * w.size // (quarter * blk), quarter * blk), BF16),
-        ]
-        + [shape((part, quarter * blk), BF16)] * (n_rep - 2),
-        in_specs=[SMEM] * n_rep + [WHOLE] * 3,
+        out_shape=[shape((part, quarter * blk), F32)]
+        + [shape((part + w.size // (quarter * blk), quarter * blk), BF16)] * (n_rep - 1),
+        in_specs=[SMEM] * n_rep + [WHOLE] * 2,
         out_specs=[WHOLE] * n_rep,
         scratch_shapes=[pltpu.VMEM((part, row_blocks * blk), F32)],
         compiler_params=params(4 << 20),
@@ -483,37 +476,35 @@
             flops=part * row_blocks * blk, bytes_accessed=part * row_blocks * blk * 5, transcendentals=0
         ),
         name="collect",
-    )(*lists, messages, w, other)
+    )(*lists, messages, w)
 
 
 def finish_body(*refs, n_rep):
     grads = refs[:n_rep]
-    w_ref, other_ref, node_ref, weight_ref, acc_ref = refs[n_rep:]
+    w_ref, node_ref, weight_ref, acc_ref = refs[n_rep:]
     q = lax.axis_index("rep")
     part = w_ref.shape[0]
     for j in range(n_rep):
-        acc_ref[pl.ds(pl.multiple_of((q ^ j) * part, part), part), :] = grads[j][:part].astype(F32)
-    mine = lax.rem(q, 2) + 2 * lax.rem(lax.axis_index("row"), 2)
-    near = [fold_out(grads[1], part, at, *w_ref.shape) for at in range(2)]
-    for j, piece in enumerate((w_ref[...].astype(F32), near[0], other_ref[...].astype(F32), near[1])):
-        weight_ref[pl.ds(pl.multiple_of((mine ^ j) * part, part), part), :] = piece
+        rows = pl.ds(pl.multiple_of((q ^ j) * part, part), part)
+        acc_ref[rows, :] = grads[j][:part].astype(F32)
+        weight_ref[rows, :] = fold_out(grads[j], part, 0, *w_ref.shape) if j else w_ref[...].astype(F32)
     node_ref[...] = acc_ref[...].T
 
 
-def finish(grads, w, other):
+def finish(grads, w):
     n_rep = len(grads)
     part, rows = grads[0].shape
     features = w.shape[1]
     return pl.pallas_call(
         functools.partial(finish_body, n_rep=n_rep),
         out_shape=[shape((rows, part * n_rep), F32), shape((features, features), F32)],
-        in_specs=[WHOLE] * (n_rep + 2),
+        in_specs=[WHOLE] * (n_rep + 1),
         out_specs=[WHOLE] * 2,
         scratch_shapes=[pltpu.VMEM((part * n_rep, rows), F32)],
         compiler_params=params(6 << 20),
         cost_estimate=pl.CostEstimate(flops=0, bytes_accessed=rows * part * n_rep * 8, transcendentals=0),
         name="finish",
-    )(*grads, w, other)
+    )(*grads, w)
 
 
 def local(
@@ -566,18 +557,13 @@
     output, to_near, grad0, wkeep = middle(keep0, to_rep(send1, 1), arrived, weight, out_grad, n_rep, factor)
 
     grad2 = to_rep(grad0, 2)
-    first, wsend, w = back_first(to_rep(to_near, 1), grad0, adj, wkeep)
-    w = w + to_row(wsend, 1)
-    grad2 = after(grad2, first, w)
+    first, w = back_first(to_rep(to_near, 1), grad0, adj, wkeep)
+    grad2 = after(grad2, first)
     grad3 = to_rep(grad2, 1)
-    got = to_rep(w, 2)
     send_high, keep_high = back_second(grad3, grad2, adj, first, 1, n_rep, deep)
-    send_high = after(send_high, got)
-    w = w + got
-    got = to_row(w, 2)
     near_high = to_rep(send_high, 1)
     send_low, keep_low = back_second(grad3, grad2, adj, after(first, send_high), 0, n_rep, deep)
-    near_low = to_rep(after(send_low, near_high, got), 1)
+    near_low = to_rep(after(send_low, near_high), 1)
     part = features // n_rep
 
     def across_sum(keep, near):
@@ -587,18 +573,19 @@
     across_low = across_sum(keep_low, near_low)
     far_high = to_rep(across_high, 2)
     far_low = to_rep(across_low, 2)
-    w = w + got
-    w = w + to_row(after(w, across_high, across_low), 4)
-    step = 8
+
+    got = to_row(after(w, far_high), 1)
+    messages = split((keep_low, near_low, far_low), (keep_high, near_high, far_high), n_row, n_rep)
+    returned = lax.all_to_all(messages, "row", split_axis=0, concat_axis=0, tiled=True)
+    w2 = after(w[part:] + got[part:], messages)
+    w = w[:part] + got[:part] + to_rep(w2, 2)
+    step = 2
     while step < n_row:
         w = w + to_row(w, step)
         step *= 2
     w = w.astype(BF16)
-    other = to_row(w, 1)
-    messages = split((keep_low, near_low, far_low), (keep_high, near_high, after(far_high, w)), n_row, n_rep)
-    returned = lax.all_to_all(messages, "row", split_axis=0, concat_axis=0, tiled=True)
-    grads = collect(lists, returned, w, other, per_list, row_blocks, blk)
-    node_grad, weight_grad = finish([grads[0]] + [to_rep(grads[j], j) for j in range(1, n_rep)], w, other)
+    grads = collect(lists, after(returned, w), w, per_list, row_blocks, blk)
+    node_grad, weight_grad = finish([grads[0]] + [to_rep(grads[j], j) for j in range(1, n_rep)], w)
     return (output, weight_grad, node_grad)
 
 

time: 99.3 us -> 103 us (1.037)
  starting transfers between devices: 42.6 us -> 44.9 us
  waiting for transfers between devices: 31 us -> 32.2 us
    ppermute x20, waiting for transfers between devices: 16.4 us -> 24.1 us  [to_rep(): return lax.ppermute(x, 'rep', xor_perm(n_rep, j))]
    all_to_all x1, waiting for transfers between devices: 3.76 us -> 0.01 us  [local(): lax.all_to_all(messages, 'row', split_axis=0, concat_axis=0, tiled=True)]
    ppermute x4 -> x3, waiting for transfers between devices: 9.92 us -> 7.54 us  [to_row(): return lax.ppermute(x, 'row', xor_perm(n_row, k))]
    ppermute x20, starting transfers between devices: 22.1 us -> 24.3 us  [to_rep(): return lax.ppermute(x, 'rep', xor_perm(n_rep, j))]
    ppermute x4 -> x3, starting transfers between devices: 7.16 us -> 8.14 us  [to_row(): return lax.ppermute(x, 'row', xor_perm(n_row, k))]
  transfers between devices with their start and end apart: 29 -> 28, of which waited for: 19 -> 16; matrix products, arithmetic and copies ran while one was open for 0% -> 0% of each run, Pallas kernels for 15% -> 12%
where the time goes in v8:
time: 103 us
  starting transfers between devices  44.9 us (44%)
  waiting for transfers between devices  32.2 us (31%)
  Pallas kernels  22.5 us (22%)
  between operations  1.53 us (1%)
  local copies, waits for them, and re-layouts  1.47 us (1%)
    ppermute x20, starting transfers between devices, to_rep(): return lax.ppermute(x, 'rep', xor_perm(n_rep, j))  24.3 us
    ppermute x20, waiting for transfers between devices, to_rep(): return lax.ppermute(x, 'rep', xor_perm(n_rep, j))  24.1 us
    ppermute x4, starting transfers between devices, spread(): return lax.ppermute(x, ('row', 'rep'), perm)  8.47 us
    ppermute x3, starting transfers between devices, to_row(): return lax.ppermute(x, 'row', xor_perm(n_row, k))  8.14 us
    ppermute x3, waiting for transfers between devices, to_row(): return lax.ppermute(x, 'row', xor_perm(n_row, k))  7.54 us
    pallas_call x1, Pallas kernels, densify(): pl.pallas_call(functools.partial(densify_body, all_cols=all_cols, row_blo...  4.29 us
    all_to_all x1, starting transfers between devices, local(): lax.all_to_all(messages, 'row', split_axis=0, concat_axis=0, tiled=True)  3.9 us
    pallas_call x2, Pallas kernels, forward(): pl.pallas_call(functools.partial(forward_body, n_rep=len(pieces)), grid=(...  3.67 us
  transfers between devices with their start and end apart: 28, of which 16 were waited for; matrix products, arithmetic and copies ran while one was open for 0% of the time, Pallas kernels for 12%

profile of v8, /device:TPU:0, one launch (start us, length us, event | category | flops | bytes accessed | tf_op | source)
XLA Modules:
  0.0 102.7 jit_solution(15970905546564142364)
XLA Ops:
  1.4 4.0 %collective-permute-start.1 = (s32[1,8,2]{2,1,0:T(8,128)S(1)}, s32[1,8,2]{2,1,0:T(8,128)S(1)}, u32[]{:S(2)}, u32[]{:S(2)}) collective-permute-start(s32[1,8,2]{2,1,0:T(8,128)S(1)} %copy.11), channel_id=1, source_target_pairs={{0,16},{1,21},{2,26},{3,31},{4,20},{5,17},{6,30},{7,27},{8,24},{9,... | collective-permute-start | bytes 200 | tf_op jit(solution)/shard_map/ppermute | solution.py:531
  7.0 2.2 %pack.1 = (bf16[256,256]{1,0:T(8,128)(2,1)S(1)}, bf16[256,256]{1,0:T(8,128)(2,1)S(1)}, s32[128]{0:T(128)S(1)}) custom-call(s32[1,8,2]{2,1,0:T(8,128)S(1)} %collective-permute-done.refs_0_, s32[1,8,2]{2,1,0:T(8,128)S(1)} %collective-permute-done.1.refs_1_, bf16[2048,256]{1,0:T(8,128)(2,1)} %refs_2_.1), custom_call_target="tpu_custom_call" | custom-call | tf_op jit(solution)/shard_map/pack/pallas_call | solution.py:215
  10.1 3.0 %collective-permute-start.3 = (bf16[256,256]{1,0:T(8,128)(2,1)S(1)}, bf16[256,256]{1,0:T(8,128)(2,1)S(1)}, u32[]{:S(2)}, u32[]{:S(2)}) collective-permute-start(bf16[256,256]{1,0:T(8,128)(2,1)S(1)} %get-tuple-element.41), channel_id=1, source_target_pairs={{0,16},{1,21},{2,26},{3,31},{4,20},{5,17},{6,30},{7,27},{8,24},{9,... | collective-permute-start | bytes 393224 | tf_op jit(solution)/shard_map/ppermute | solution.py:531
  13.1 2.6 %slot_lists.1.table_ref = s32[1152]{0:T(1024)} custom-call(s32[192]{0:T(256)} %rows_ref.1, s32[192]{0:T(256)} %fetch_ref.1, s32[1]{0:T(128)S(6)} %copy.13.count_ref), custom_call_target="tpu_custom_call" | custom-call | flops 3221225472 | bytes 1536 | tf_op jit(solution)/shard_map/slot_lists/pallas_call | solution.py:116
  16.1 6.1 %collective-permute-start.4 = (bf16[512,256]{1,0:T(8,128)(2,1)S(1)}, bf16[512,256]{1,0:T(8,128)(2,1)S(1)}, u32[]{:S(2)}, u32[]{:S(2)}) collective-permute-start(bf16[512,256]{1,0:T(8,128)(2,1)S(1)} %pad_maximum_fusion.refs_0_), channel_id=1, source_target_pairs={{0,1},{1,0},{2,3},{3,2},{4,5},{5,4},{6,7},{7,6},{8,9},{9,8},{10,11... | collective-permute-start | bytes 786440 | tf_op jit(solution)/shard_map/ppermute | solution.py:522
  22.1 4.3 %collective-permute-start.5 = (bf16[512,256]{1,0:T(8,128)(2,1)S(1)}, bf16[512,256]{1,0:T(8,128)(2,1)S(1)}, u32[]{:S(2)}, u32[]{:S(2)}) collective-permute-start(bf16[512,256]{1,0:T(8,128)(2,1)S(1)} %pad_maximum_fusion.refs_0_), channel_id=1, source_target_pairs={{0,2},{1,3},{2,0},{3,1},{4,6},{5,7},{6,4},{7,5},{8,10},{9,11},{10,... | collective-permute-start | bytes 786440 | tf_op jit(solution)/shard_map/ppermute | solution.py:522
  27.1 4.3 %densify.1.refs_4_.adj_ref = bf16[2048,2048]{1,0:T(8,128)(2,1)S(1)} custom-call(s32[1152]{0:T(1024)S(1)} %copy-done.2, bf16[192,128,128]{2,1,0:T(8,128)(2,1)S(1)} %bitcast.1), custom_call_target="tpu_custom_call" | custom-call | flops 3145728 | bytes 14680064 | tf_op jit(solution)/shard_map/densify/pallas_call | solution.py:172
  31.4 1.9 %collective-permute-done.5.refs_2_ = bf16[512,256]{1,0:T(8,128)(2,1)S(1)} collective-permute-done((bf16[512,256]{1,0:T(8,128)(2,1)S(1)}, bf16[512,256]{1,0:T(8,128)(2,1)S(1)}, u32[]{:S(2)}, u32[]{:S(2)}) %collective-permute-start.5) | collective-permute-done | bytes 262176 | tf_op jit(solution)/shard_map/ppermute | solution.py:522
  34.8 1.8 %forward.2 = (bf16[512,256]{1,0:T(8,128)(2,1)S(1)}, f32[512,256]{1,0:T(8,128)S(1)}) custom-call(bf16[512,256]{1,0:T(8,128)(2,1)S(1)} %pad_maximum_fusion.refs_0_, bf16[512,256]{1,0:T(8,128)(2,1)S(1)} %collective-permute-done.4.refs_1_, bf16[512,256]{1,0:T(8,128)(2,1)S(1)} %collective-permute-done.5.refs_2_, ...), custom_call_target="tpu_custom_call" | custom-call | flops 1073741824 | bytes 5242880 | tf_op jit(solution)/shard_map/forward/pallas_call | solution.py:253
  38.4 1.8 %collective-permute-start.9 = (bf16[512,256]{1,0:T(8,128)(2,1)S(1)}, bf16[512,256]{1,0:T(8,128)(2,1)S(1)}, u32[]{:S(2)}, u32[]{:S(2)}) collective-permute-start(bf16[512,256]{1,0:T(8,128)(2,1)S(1)} %add_convert_fusion), channel_id=1, source_target_pairs={{0,2},{1,3},{2,0},{3,1},{4,6},{5,7},{6,4},{7,5},{8,10},{9,11},{10,... | collective-permute-start | bytes 786440 | tf_op jit(solution)/shard_map/ppermute | solution.py:522
  40.2 1.8 %forward.3 = (bf16[512,256]{1,0:T(8,128)(2,1)S(1)}, f32[512,256]{1,0:T(8,128)S(1)}) custom-call(bf16[512,256]{1,0:T(8,128)(2,1)S(1)} %pad_maximum_fusion.refs_0_, bf16[512,256]{1,0:T(8,128)(2,1)S(1)} %collective-permute-done.4.refs_1_, bf16[512,256]{1,0:T(8,128)(2,1)S(1)} %collective-permute-done.5.refs_2_, ...), custom_call_target="tpu_custom_call" | custom-call | flops 1073741824 | bytes 5242880 | tf_op jit(solution)/shard_map/forward/pallas_call | solution.py:253
  44.3 1.8 %collective-permute-done.12.refs_3_ = s32[128]{0:T(128)S(1)} collective-permute-done((s32[128]{0:T(128)S(1)}, s32[128]{0:T(128)S(1)}, u32[]{:S(2)}, u32[]{:S(2)}) %collective-permute-start.12) | collective-permute-done | bytes 544 | tf_op jit(solution)/shard_map/ppermute | solution.py:522
  49.8 2.3 %back_first.1 = (f32[256,2048]{1,0:T(8,128)S(1)}, f32[128,256]{1,0:T(8,128)S(1)}) custom-call(bf16[320,512]{1,0:T(8,128)(2,1)S(1)} %collective-permute-done.14.odd_ref, bf16[256,512]{1,0:T(8,128)(2,1)S(1)} %get-tuple-element.55.even_ref, bf16[2048,2048]{1,0:T(8,128)(2,1)S(1)} %densify.1.refs_4_.adj_ref, f32[128,256]{1,0:T(8,128)S(1)} %get-tuple-element.57.wkeep_ref), custom_call_target="tpu_custom_call" | custom-call | flops 1073741824 | bytes 6291456 | tf_op jit(solution)/shard_map/back_first/pallas_call | solution.py:351
  52.1 4.7 %collective-permute-done.13.even_ref = bf16[256,512]{1,0:T(8,128)(2,1)S(1)} collective-permute-done((bf16[256,512]{1,0:T(8,128)(2,1)S(1)}, bf16[256,512]{1,0:T(8,128)(2,1)S(1)}, u32[]{:S(2)}, u32[]{:S(2)}) %collective-permute-start.13) | collective-permute-done | bytes 262176 | tf_op jit(solution)/shard_map/ppermute | solution.py:522
  58.3 1.8 %back_second_1.1 = (bf16[128,1024]{1,0:T(8,128)(2,1)S(1)}, f32[128,1024]{1,0:T(8,128)S(1)}) custom-call(bf16[256,512]{1,0:T(8,128)(2,1)S(1)} %collective-permute-done.15.odd_ref, bf16[256,512]{1,0:T(8,128)(2,1)S(1)} %collective-permute-done.13.even_ref, bf16[2048,2048]{1,0:T(8,128)(2,1)S(1)} %densify.1.refs_4_.adj_ref, ...), custom_call_target="tpu_custom_call" | custom-call | flops 536870912 | bytes 3932160 | tf_op jit(solution)/shard_map/back_second_1/pallas_call | solution.py:383
  60.3 1.8 %back_second_0.1 = (bf16[128,1024]{1,0:T(8,128)(2,1)S(1)}, f32[128,1024]{1,0:T(8,128)S(1)}) custom-call(bf16[256,512]{1,0:T(8,128)(2,1)S(1)} %collective-permute-done.15.odd_ref, bf16[256,512]{1,0:T(8,128)(2,1)S(1)} %collective-permute-done.13.even_ref, bf16[2048,2048]{1,0:T(8,128)(2,1)S(1)} %densify.1.refs_4_.adj_ref, ...), custom_call_target="tpu_custom_call" | custom-call | flops 536870912 | bytes 3932160 | tf_op jit(solution)/shard_map/back_second_0/pallas_call | solution.py:383
  62.6 1.8 %collective-permute-start.19 = (bf16[64,1024]{1,0:T(8,128)(2,1)S(1)}, bf16[64,1024]{1,0:T(8,128)(2,1)S(1)}, u32[]{:S(2)}, u32[]{:S(2)}) collective-permute-start(bf16[64,1024]{1,0:T(8,128)(2,1)S(1)} %add_convert_fusion.1), channel_id=1, source_target_pairs={{0,2},{1,3},{2,0},{3,1},{4,6},{5,7},{6,4},{7,5},{8,10},{9,11},{10,... | collective-permute-start | bytes 393224 | tf_op jit(solution)/shard_map/ppermute | solution.py:522
  64.5 3.8 %collective-permute-done.19.refs_5_ = bf16[64,1024]{1,0:T(8,128)(2,1)S(1)} collective-permute-done((bf16[64,1024]{1,0:T(8,128)(2,1)S(1)}, bf16[64,1024]{1,0:T(8,128)(2,1)S(1)}, u32[]{:S(2)}, u32[]{:S(2)}) %collective-permute-start.19) | collective-permute-done | bytes 131104 | tf_op jit(solution)/shard_map/ppermute | solution.py:522
  77.4 3.9 %all-to-all-start = ((bf16[8,64,256]{2,1,0:T(8,128)(2,1)}), bf16[8,64,256]{2,1,0:T(8,128)(2,1)S(1)}, u32[]{:S(2)}, u32[]{:S(2)}) async-start(bf16[8,64,256]{2,1,0:T(8,128)(2,1)} %split.1), calls=%async_computation | async-start | bytes 524288 | tf_op jit(solution)/shard_map/all_to_all | solution.py:579
  81.4 2.1 %collective-permute-start.22 = (f32[64,256]{1,0:T(8,128)S(1)}, f32[64,256]{1,0:T(8,128)S(1)}, u32[]{:S(2)}, u32[]{:S(2)}) collective-permute-start(f32[64,256]{1,0:T(8,128)S(1)} %fusion), channel_id=1, source_target_pairs={{0,8},{4,12},{8,0},{12,4},{16,24},{20,28},{24,16},{28,20},{1,9},{5... | collective-permute-start | bytes 196616 | tf_op jit(solution)/shard_map/ppermute | solution.py:525
  83.5 3.1 %collective-permute-done.22 = f32[64,256]{1,0:T(8,128)S(1)} collective-permute-done((f32[64,256]{1,0:T(8,128)S(1)}, f32[64,256]{1,0:T(8,128)S(1)}, u32[]{:S(2)}, u32[]{:S(2)}) %collective-permute-start.22) | collective-permute-done | bytes 65568 | tf_op jit(solution)/shard_map/ppermute | solution.py:525
  86.5 4.5 %collective-permute-start.23 = (f32[64,256]{1,0:T(8,128)S(1)}, f32[64,256]{1,0:T(8,128)S(1)}, u32[]{:S(2)}, u32[]{:S(2)}) collective-permute-start(f32[64,256]{1,0:T(8,128)S(1)} %add.30), channel_id=1, source_target_pairs={{0,16},{4,20},{8,24},{12,28},{16,0},{20,4},{24,8},{28,12},{1,17},{... | collective-permute-start | bytes 196616 | tf_op jit(solution)/shard_map/ppermute | solution.py:525
  91.1 2.9 %collective-permute-done.23 = f32[64,256]{1,0:T(8,128)S(1)} collective-permute-done((f32[64,256]{1,0:T(8,128)S(1)}, f32[64,256]{1,0:T(8,128)S(1)}, u32[]{:S(2)}, u32[]{:S(2)}) %collective-permute-start.23) | collective-permute-done | bytes 65568 | tf_op jit(solution)/shard_map/ppermute | solution.py:525
  96.7 3.8 %collective-permute-done.25.refs_2_ = bf16[96,512]{1,0:T(8,128)(2,1)S(1)} collective-permute-done((bf16[96,512]{1,0:T(8,128)(2,1)S(1)}, bf16[96,512]{1,0:T(8,128)(2,1)S(1)}, u32[]{:S(2)}, u32[]{:S(2)}) %collective-permute-start.25) | collective-permute-done | bytes 98336 | tf_op jit(solution)/shard_map/ppermute | solution.py:522
  (64 shorter events, 29.0 us)
Async XLA Ops:
  1.4 5.6 %collective-permute-start.1 = (s32[1,8,2]{2,1,0:T(8,128)S(1)}, s32[1,8,2]{2,1,0:T(8,128)S(1)}, u32[]{:S(2)}, u32[]{:S(2)}) collective-permute-start(s32[1,8,2]{2,1,0:T(8,128)S(1)} %copy.11), channel_id=1, source_target_pairs={{0,16},{1,21},{2,26},{3,31},{4,20},{5,17},{6,30},{7,27},{8,24},{9,... | collective-permute-start | bytes 200 | tf_op jit(solution)/shard_map/ppermute | solution.py:531
  9.3 6.4 %collective-permute-start.2 = (bf16[256,256]{1,0:T(8,128)(2,1)S(1)}, bf16[256,256]{1,0:T(8,128)(2,1)S(1)}, u32[]{:S(2)}, u32[]{:S(2)}) collective-permute-start(bf16[256,256]{1,0:T(8,128)(2,1)S(1)} %get-tuple-element.40), channel_id=1, source_target_pairs={{0,0},{1,5},{2,10},{3,15},{4,4},{5,1},{6,14},{7,11},{8,8},{9,13},{... | collective-permute-start | bytes 393224 | tf_op jit(solution)/shard_map/ppermute | solution.py:531
  10.1 5.9 %collective-permute-start.3 = (bf16[256,256]{1,0:T(8,128)(2,1)S(1)}, bf16[256,256]{1,0:T(8,128)(2,1)S(1)}, u32[]{:S(2)}, u32[]{:S(2)}) collective-permute-start(bf16[256,256]{1,0:T(8,128)(2,1)S(1)} %get-tuple-element.41), channel_id=1, source_target_pairs={{0,16},{1,21},{2,26},{3,31},{4,20},{5,17},{6,30},{7,27},{8,24},{9,... | collective-permute-start | bytes 393224 | tf_op jit(solution)/shard_map/ppermute | solution.py:531
  16.1 10.4 %collective-permute-start.4 = (bf16[512,256]{1,0:T(8,128)(2,1)S(1)}, bf16[512,256]{1,0:T(8,128)(2,1)S(1)}, u32[]{:S(2)}, u32[]{:S(2)}) collective-permute-start(bf16[512,256]{1,0:T(8,128)(2,1)S(1)} %pad_maximum_fusion.refs_0_), channel_id=1, source_target_pairs={{0,1},{1,0},{2,3},{3,2},{4,5},{5,4},{6,7},{7,6},{8,9},{9,8},{10,11... | collective-permute-start | bytes 786440 | tf_op jit(solution)/shard_map/ppermute | solution.py:522
  22.1 11.2 %collective-permute-start.5 = (bf16[512,256]{1,0:T(8,128)(2,1)S(1)}, bf16[512,256]{1,0:T(8,128)(2,1)S(1)}, u32[]{:S(2)}, u32[]{:S(2)}) collective-permute-start(bf16[512,256]{1,0:T(8,128)(2,1)S(1)} %pad_maximum_fusion.refs_0_), channel_id=1, source_target_pairs={{0,2},{1,3},{2,0},{3,1},{4,6},{5,7},{6,4},{7,5},{8,10},{9,11},{10,... | collective-permute-start | bytes 786440 | tf_op jit(solution)/shard_map/ppermute | solution.py:522
  38.4 8.5 %collective-permute-start.9 = (bf16[512,256]{1,0:T(8,128)(2,1)S(1)}, bf16[512,256]{1,0:T(8,128)(2,1)S(1)}, u32[]{:S(2)}, u32[]{:S(2)}) collective-permute-start(bf16[512,256]{1,0:T(8,128)(2,1)S(1)} %add_convert_fusion), channel_id=1, source_target_pairs={{0,2},{1,3},{2,0},{3,1},{4,6},{5,7},{6,4},{7,5},{8,10},{9,11},{10,... | collective-permute-start | bytes 786440 | tf_op jit(solution)/shard_map/ppermute | solution.py:522
  42.0 4.9 %collective-permute-start.8 = (bf16[512,256]{1,0:T(8,128)(2,1)S(1)}, bf16[512,256]{1,0:T(8,128)(2,1)S(1)}, u32[]{:S(2)}, u32[]{:S(2)}) collective-permute-start(bf16[512,256]{1,0:T(8,128)(2,1)S(1)} %get-tuple-element.50), channel_id=1, source_target_pairs={{0,1},{1,0},{2,3},{3,2},{4,5},{5,4},{6,7},{7,6},{8,9},{9,8},{10,11... | collective-permute-start | bytes 786440 | tf_op jit(solution)/shard_map/ppermute | solution.py:522
  42.1 4.0 %collective-permute-start.12 = (s32[128]{0:T(128)S(1)}, s32[128]{0:T(128)S(1)}, u32[]{:S(2)}, u32[]{:S(2)}) collective-permute-start(s32[128]{0:T(128)S(1)} %get-tuple-element.52.refs_0_), channel_id=1, source_target_pairs={{0,3},{1,2},{2,1},{3,0},{4,7},{5,6},{6,5},{7,4},{8,11},{9,10},{10,... | collective-permute-start | bytes 1544 | tf_op jit(solution)/shard_map/ppermute | solution.py:522
  42.5 4.4 %collective-permute-start.11 = (s32[128]{0:T(128)S(1)}, s32[128]{0:T(128)S(1)}, u32[]{:S(2)}, u32[]{:S(2)}) collective-permute-start(s32[128]{0:T(128)S(1)} %get-tuple-element.52.refs_0_), channel_id=1, source_target_pairs={{0,2},{1,3},{2,0},{3,1},{4,6},{5,7},{6,4},{7,5},{8,10},{9,11},{10,... | collective-permute-start | bytes 1544 | tf_op jit(solution)/shard_map/ppermute | solution.py:522
  44.3 2.6 %collective-permute-start.10 = (s32[128]{0:T(128)S(1)}, s32[128]{0:T(128)S(1)}, u32[]{:S(2)}, u32[]{:S(2)}) collective-permute-start(s32[128]{0:T(128)S(1)} %get-tuple-element.52.refs_0_), channel_id=1, source_target_pairs={{0,1},{1,0},{2,3},{3,2},{4,5},{5,4},{6,7},{7,6},{8,9},{9,8},{10,11... | collective-permute-start | bytes 1544 | tf_op jit(solution)/shard_map/ppermute | solution.py:522
  48.0 1.8 %collective-permute-start.14 = (bf16[320,512]{1,0:T(8,128)(2,1)S(1)}, bf16[320,512]{1,0:T(8,128)(2,1)S(1)}, u32[]{:S(2)}, u32[]{:S(2)}) collective-permute-start(bf16[320,512]{1,0:T(8,128)(2,1)S(1)} %get-tuple-element.56), channel_id=1, source_target_pairs={{0,1},{1,0},{2,3},{3,2},{4,5},{5,4},{6,7},{7,6},{8,9},{9,8},{10,11... | collective-permute-start | bytes 983048 | tf_op jit(solution)/shard_map/ppermute | solution.py:522
  48.0 8.7 %collective-permute-start.13 = (bf16[256,512]{1,0:T(8,128)(2,1)S(1)}, bf16[256,512]{1,0:T(8,128)(2,1)S(1)}, u32[]{:S(2)}, u32[]{:S(2)}) collective-permute-start(bf16[256,512]{1,0:T(8,128)(2,1)S(1)} %get-tuple-element.55.even_ref), channel_id=1, source_target_pairs={{0,2},{1,3},{2,0},{3,1},{4,6},{5,7},{6,4},{7,5},{8,10},{9,11},{10,... | collective-permute-start | bytes 786440 | tf_op jit(solution)/shard_map/ppermute | solution.py:522
  60.1 2.0 %collective-permute-start.16 = (bf16[128,1024]{1,0:T(8,128)(2,1)S(1)}, bf16[128,1024]{1,0:T(8,128)(2,1)S(1)}, u32[]{:S(2)}, u32[]{:S(2)}) collective-permute-start(bf16[128,1024]{1,0:T(8,128)(2,1)S(1)} %get-tuple-element.60), channel_id=1, source_target_pairs={{0,1},{1,0},{2,3},{3,2},{4,5},{5,4},{6,7},{7,6},{8,9},{9,8},{10,11... | collective-permute-start | bytes 786440 | tf_op jit(solution)/shard_map/ppermute | solution.py:522
  62.2 7.6 %collective-permute-start.17 = (bf16[128,1024]{1,0:T(8,128)(2,1)S(1)}, bf16[128,1024]{1,0:T(8,128)(2,1)S(1)}, u32[]{:S(2)}, u32[]{:S(2)}) collective-permute-start(bf16[128,1024]{1,0:T(8,128)(2,1)S(1)} %get-tuple-element.64), channel_id=1, source_target_pairs={{0,1},{1,0},{2,3},{3,2},{4,5},{5,4},{6,7},{7,6},{8,9},{9,8},{10,11... | collective-permute-start | bytes 786440 | tf_op jit(solution)/shard_map/ppermute | solution.py:522
  62.6 5.6 %collective-permute-start.19 = (bf16[64,1024]{1,0:T(8,128)(2,1)S(1)}, bf16[64,1024]{1,0:T(8,128)(2,1)S(1)}, u32[]{:S(2)}, u32[]{:S(2)}) collective-permute-start(bf16[64,1024]{1,0:T(8,128)(2,1)S(1)} %add_convert_fusion.1), channel_id=1, source_target_pairs={{0,2},{1,3},{2,0},{3,1},{4,6},{5,7},{6,4},{7,5},{8,10},{9,11},{10,... | collective-permute-start | bytes 393224 | tf_op jit(solution)/shard_map/ppermute | solution.py:522
  68.3 5.0 %collective-permute-start.20 = (f32[128,256]{1,0:T(8,128)S(1)}, f32[128,256]{1,0:T(8,128)S(1)}, u32[]{:S(2)}, u32[]{:S(2)}) collective-permute-start(f32[128,256]{1,0:T(8,128)S(1)} %get-tuple-element.68), channel_id=1, source_target_pairs={{0,4},{4,0},{8,12},{12,8},{16,20},{20,16},{24,28},{28,24},{1,5},{5... | collective-permute-start | bytes 393224 | tf_op jit(solution)/shard_map/ppermute | solution.py:525
  69.8 5.0 %collective-permute-start.18 = (bf16[64,1024]{1,0:T(8,128)(2,1)S(1)}, bf16[64,1024]{1,0:T(8,128)(2,1)S(1)}, u32[]{:S(2)}, u32[]{:S(2)}) collective-permute-start(bf16[64,1024]{1,0:T(8,128)(2,1)S(1)} %add_convert_fusion.2), channel_id=1, source_target_pairs={{0,2},{1,3},{2,0},{3,1},{4,6},{5,7},{6,4},{7,5},{8,10},{9,11},{10,... | collective-permute-start | bytes 393224 | tf_op jit(solution)/shard_map/ppermute | solution.py:522
  75.7 5.6 %collective-permute-start.21 = (f32[64,256]{1,0:T(8,128)S(1)}, f32[64,256]{1,0:T(8,128)S(1)}, u32[]{:S(2)}, u32[]{:S(2)}) collective-permute-start(f32[64,256]{1,0:T(8,128)S(1)} %slice_add_fusion), channel_id=1, source_target_pairs={{0,2},{1,3},{2,0},{3,1},{4,6},{5,7},{6,4},{7,5},{8,10},{9,11},{10,... | collective-permute-start | bytes 196616 | tf_op jit(solution)/shard_map/ppermute | solution.py:522
  77.4 16.5 %all-to-all-start = ((bf16[8,64,256]{2,1,0:T(8,128)(2,1)}), bf16[8,64,256]{2,1,0:T(8,128)(2,1)S(1)}, u32[]{:S(2)}, u32[]{:S(2)}) async-start(bf16[8,64,256]{2,1,0:T(8,128)(2,1)} %split.1), calls=%async_computation | async-start | bytes 524288 | tf_op jit(solution)/shard_map/all_to_all | solution.py:579
  81.4 5.1 %collective-permute-start.22 = (f32[64,256]{1,0:T(8,128)S(1)}, f32[64,256]{1,0:T(8,128)S(1)}, u32[]{:S(2)}, u32[]{:S(2)}) collective-permute-start(f32[64,256]{1,0:T(8,128)S(1)} %fusion), channel_id=1, source_target_pairs={{0,8},{4,12},{8,0},{12,4},{16,24},{20,28},{24,16},{28,20},{1,9},{5... | collective-permute-start | bytes 196616 | tf_op jit(solution)/shard_map/ppermute | solution.py:525
  86.5 7.4 %collective-permute-start.23 = (f32[64,256]{1,0:T(8,128)S(1)}, f32[64,256]{1,0:T(8,128)S(1)}, u32[]{:S(2)}, u32[]{:S(2)}) collective-permute-start(f32[64,256]{1,0:T(8,128)S(1)} %add.30), channel_id=1, source_target_pairs={{0,16},{4,20},{8,24},{12,28},{16,0},{20,4},{24,8},{28,12},{1,17},{... | collective-permute-start | bytes 196616 | tf_op jit(solution)/shard_map/ppermute | solution.py:525
  94.7 1.9 %collective-permute-start.24 = (bf16[96,512]{1,0:T(8,128)(2,1)S(1)}, bf16[96,512]{1,0:T(8,128)(2,1)S(1)}, u32[]{:S(2)}, u32[]{:S(2)}) collective-permute-start(bf16[96,512]{1,0:T(8,128)(2,1)S(1)} %get-tuple-element.72), channel_id=1, source_target_pairs={{0,1},{1,0},{2,3},{3,2},{4,5},{5,4},{6,7},{7,6},{8,9},{9,8},{10,11... | collective-permute-start | bytes 294920 | tf_op jit(solution)/shard_map/ppermute | solution.py:522
  94.8 5.7 %collective-permute-start.25 = (bf16[96,512]{1,0:T(8,128)(2,1)S(1)}, bf16[96,512]{1,0:T(8,128)(2,1)S(1)}, u32[]{:S(2)}, u32[]{:S(2)}) collective-permute-start(bf16[96,512]{1,0:T(8,128)(2,1)S(1)} %get-tuple-element.73), channel_id=1, source_target_pairs={{0,2},{1,3},{2,0},{3,1},{4,6},{5,7},{6,4},{7,5},{8,10},{9,11},{10,... | collective-permute-start | bytes 294920 | tf_op jit(solution)/shard_map/ppermute | solution.py:522
  95.2 6.5 %collective-permute-start.26 = (bf16[96,512]{1,0:T(8,128)(2,1)S(1)}, bf16[96,512]{1,0:T(8,128)(2,1)S(1)}, u32[]{:S(2)}, u32[]{:S(2)}) collective-permute-start(bf16[96,512]{1,0:T(8,128)(2,1)S(1)} %get-tuple-element.74), channel_id=1, source_target_pairs={{0,3},{1,2},{2,1},{3,0},{4,7},{5,6},{6,5},{7,4},{8,11},{9,10},{10,... | collective-permute-start | bytes 294920 | tf_op jit(solution)/shard_map/ppermute | solution.py:522
  (9 other events, 60.9 us)

commit v9 on v8

--- a/solution.py
+++ b/solution.py
@@ -405,32 +405,50 @@
     )(odd, even, adj, first)
 
 
-def split_body(*refs, n_rep, deep):
-    halves, out_ref = (refs[:3], refs[3:6]), refs[6]
+def across_body(low_ref, low_near, high_ref, high_near, out_ref):
+    part, cols = out_ref.shape[0], low_ref.shape[1]
+    for half, (keep, near) in enumerate(((low_ref, low_near), (high_ref, high_near))):
+        out_ref[:, half * cols : (half + 1) * cols] = (keep[:part] + near[:part].astype(F32)).astype(BF16)
+
+
+def across_sum(keep_low, near_low, keep_high, near_high):
+    rows, cols = keep_low.shape
+    return pl.pallas_call(
+        across_body,
+        out_shape=shape((rows // 2, 2 * cols), BF16),
+        in_specs=[WHOLE] * 4,
+        out_specs=WHOLE,
+        compiler_params=params(rows * cols * 14),
+        cost_estimate=pl.CostEstimate(flops=rows * cols, bytes_accessed=rows * cols * 8, transcendentals=0),
+        name="across_sum",
+    )(keep_low, near_low, keep_high, near_high)
+
+
+def split_body(low_ref, low_near, high_ref, high_near, far_ref, out_ref, *, n_rep, deep):
     r, q = lax.axis_index("row"), lax.axis_index("rep")
     _, part, width = out_ref.shape
-    for half, (own_ref, near_ref, far_ref) in enumerate(halves):
-        for i in range(n_rep * deep):
+    per_half = n_rep * deep
+    for half, (own, near) in enumerate(((low_ref, low_near), (high_ref, high_near))):
+        for i in range(per_half):
             low, hi = i % n_rep, i // n_rep
             j = low ^ q
             cols = pl.ds(pl.multiple_of((j * deep + hi) * width, width), width)
-            far_cols = pl.ds(pl.multiple_of(((j ^ 2) * deep + hi) * width, width), width)
-            total = own_ref[part:, cols] + near_ref[part:, cols].astype(F32) + far_ref[:, far_cols].astype(F32)
-            out_ref[r ^ (half * n_rep * deep + i)] = total.astype(BF16)
-
-
-def split(low, high, n_row, n_rep):
-    part, cols = low[2].shape
-    width = 2 * cols // n_row
+            far_cols = pl.ds(pl.multiple_of((half * per_half + (j ^ 2) * deep + hi) * width, width), width)
+            total = own[part:, cols] + near[part:, cols].astype(F32) + far_ref[:, far_cols].astype(F32)
+            out_ref[r ^ (half * per_half + i)] = total.astype(BF16)
+
+
+def split(keep_low, near_low, keep_high, near_high, far, n_row, n_rep):
+    part, cols = far.shape
     return pl.pallas_call(
         functools.partial(split_body, n_rep=n_rep, deep=n_row // n_rep // 2),
-        out_shape=shape((n_row, part, width), BF16),
-        in_specs=[WHOLE] * 6,
+        out_shape=shape((n_row, part, cols // n_row), BF16),
+        in_specs=[WHOLE] * 5,
         out_specs=WHOLE,
-        compiler_params=params(cols * part * 40),
-        cost_estimate=pl.CostEstimate(flops=4 * part * cols, bytes_accessed=part * cols * 20, transcendentals=0),
+        compiler_params=params(cols * part * 20),
+        cost_estimate=pl.CostEstimate(flops=2 * part * cols, bytes_accessed=part * cols * 10, transcendentals=0),
         name="split",
-    )(*low, *high)
+    )(keep_low, near_low, keep_high, near_high, far)
 
 
 def collect_body(*refs, n_row, n_rep, per_list, quarter, blk):
@@ -558,33 +576,27 @@
 
     grad2 = to_rep(grad0, 2)
     first, w = back_first(to_rep(to_near, 1), grad0, adj, wkeep)
-    grad2 = after(grad2, first)
+    w = w + to_row(w, 1)
+    grad2 = after(grad2, first, w)
     grad3 = to_rep(grad2, 1)
+    part = features // n_rep
+    got = to_rep(w[part:], 2)
     send_high, keep_high = back_second(grad3, grad2, adj, first, 1, n_rep, deep)
+    send_high = after(send_high, got)
     near_high = to_rep(send_high, 1)
     send_low, keep_low = back_second(grad3, grad2, adj, after(first, send_high), 0, n_rep, deep)
     near_low = to_rep(after(send_low, near_high), 1)
-    part = features // n_rep
-
-    def across_sum(keep, near):
-        return (keep[:part] + near[:part].astype(F32)).astype(BF16)
-
-    across_high = across_sum(keep_high, after(near_high, send_low))
-    across_low = across_sum(keep_low, near_low)
-    far_high = to_rep(across_high, 2)
-    far_low = to_rep(across_low, 2)
-
-    got = to_row(after(w, far_high), 1)
-    messages = split((keep_low, near_low, far_low), (keep_high, near_high, far_high), n_row, n_rep)
-    returned = lax.all_to_all(messages, "row", split_axis=0, concat_axis=0, tiled=True)
-    w2 = after(w[part:] + got[part:], messages)
-    w = w[:part] + got[:part] + to_rep(w2, 2)
+    across = across_sum(keep_low, near_low, keep_high, near_high)
+    far = to_rep(across, 2)
+    w = after(w[:part], across) + got
     step = 2
     while step < n_row:
         w = w + to_row(w, step)
         step *= 2
+    messages = split(keep_low, near_low, keep_high, near_high, after(far, w), n_row, n_rep)
+    returned = lax.all_to_all(messages, "row", split_axis=0, concat_axis=0, tiled=True)
     w = w.astype(BF16)
-    grads = collect(lists, after(returned, w), w, per_list, row_blocks, blk)
+    grads = collect(lists, returned, w, per_list, row_blocks, blk)
     node_grad, weight_grad = finish([grads[0]] + [to_rep(grads[j], j) for j in range(1, n_rep)], w)
     return (output, weight_grad, node_grad)
 

time: 103 us -> 98.8 us (0.959)
  blocking collectives: 0 us -> 11.2 us
  starting transfers between devices: 44.9 us -> 35.3 us
  waiting for transfers between devices: 32.2 us -> 25.9 us
    all_to_all x0 -> x1, blocking collectives: none -> 11.2 us  [local(): lax.all_to_all(messages, 'row', split_axis=0, concat_axis=0, tiled=True)]
    ppermute x20 -> x19, waiting for transfers between devices: 24.1 us -> 14.7 us  [to_rep(): return lax.ppermute(x, 'rep', xor_perm(n_rep, j))]
    all_to_all x1 -> x0, starting transfers between devices: 3.9 us -> none  [local(): lax.all_to_all(messages, 'row', split_axis=0, concat_axis=0, tiled=True)]
    ppermute x3, waiting for transfers between devices: 7.54 us -> 11 us  [to_row(): return lax.ppermute(x, 'row', xor_perm(n_row, k))]
    ppermute x20 -> x19, starting transfers between devices: 24.3 us -> 21.5 us  [to_rep(): return lax.ppermute(x, 'rep', xor_perm(n_rep, j))]
    ppermute x3, starting transfers between devices: 8.14 us -> 5.33 us  [to_row(): return lax.ppermute(x, 'row', xor_perm(n_row, k))]
  transfers between devices with their start and end apart: 28 -> 26, of which waited for: 16 -> 13; matrix products, arithmetic and copies ran while one was open for 0% -> 0% of each run, Pallas kernels for 12% -> 16%
where the time goes in v9:
time: 98.8 us; the launch traced here: 98.5 us
  starting transfers between devices  35.3 us (36%)
  waiting for transfers between devices  25.9 us (26%)
  Pallas kernels  22.9 us (23%)
  blocking collectives  11.2 us (11%)
  between operations  1.55 us (2%)
  local copies, waits for them, and re-layouts  1.49 us (2%)
    ppermute x19, starting transfers between devices, to_rep(): return lax.ppermute(x, 'rep', xor_perm(n_rep, j))  21.5 us
    ppermute x19, waiting for transfers between devices, to_rep(): return lax.ppermute(x, 'rep', xor_perm(n_rep, j))  14.7 us
    all_to_all x1, blocking collectives, local(): lax.all_to_all(messages, 'row', split_axis=0, concat_axis=0, tiled=True)  11.2 us
    ppermute x3, waiting for transfers between devices, to_row(): return lax.ppermute(x, 'row', xor_perm(n_row, k))  11 us
    ppermute x4, starting transfers between devices, spread(): return lax.ppermute(x, ('row', 'rep'), perm)  8.47 us
    ppermute x3, starting transfers between devices, to_row(): return lax.ppermute(x, 'row', xor_perm(n_row, k))  5.33 us
    pallas_call x1, Pallas kernels, densify(): pl.pallas_call(functools.partial(densify_body, all_cols=all_cols, row_blo...  4.32 us
    pallas_call x2, Pallas kernels, back_second(): pl.pallas_call(back_second_body, grid=(tiles,), out_shape=[shape((feature...  3.67 us
  transfers between devices with their start and end apart: 26, of which 13 were waited for; matrix products, arithmetic and copies ran while one was open for 0% of the time, Pallas kernels for 16%

profile of v9, /device:TPU:0, one launch (start us, length us, event | category | flops | bytes accessed | tf_op | source)
XLA Modules:
  0.0 98.5 jit_solution(17276691759905556029)
XLA Ops:
  1.4 4.0 %collective-permute-start.1 = (s32[1,8,2]{2,1,0:T(8,128)S(1)}, s32[1,8,2]{2,1,0:T(8,128)S(1)}, u32[]{:S(2)}, u32[]{:S(2)}) collective-permute-start(s32[1,8,2]{2,1,0:T(8,128)S(1)} %copy.11), channel_id=1, source_target_pairs={{0,16},{1,21},{2,26},{3,31},{4,20},{5,17},{6,30},{7,27},{8,24},{9,... | collective-permute-start | bytes 200 | tf_op jit(solution)/shard_map/ppermute | solution.py:549
  7.0 2.2 %pack.1 = (bf16[256,256]{1,0:T(8,128)(2,1)S(1)}, bf16[256,256]{1,0:T(8,128)(2,1)S(1)}, s32[128]{0:T(128)S(1)}) custom-call(s32[1,8,2]{2,1,0:T(8,128)S(1)} %collective-permute-done.refs_0_, s32[1,8,2]{2,1,0:T(8,128)S(1)} %collective-permute-done.1.refs_1_, bf16[2048,256]{1,0:T(8,128)(2,1)} %refs_2_.1), custom_call_target="tpu_custom_call" | custom-call | tf_op jit(solution)/shard_map/pack/pallas_call | solution.py:215
  10.1 3.0 %collective-permute-start.3 = (bf16[256,256]{1,0:T(8,128)(2,1)S(1)}, bf16[256,256]{1,0:T(8,128)(2,1)S(1)}, u32[]{:S(2)}, u32[]{:S(2)}) collective-permute-start(bf16[256,256]{1,0:T(8,128)(2,1)S(1)} %get-tuple-element.40), channel_id=1, source_target_pairs={{0,16},{1,21},{2,26},{3,31},{4,20},{5,17},{6,30},{7,27},{8,24},{9,... | collective-permute-start | bytes 393224 | tf_op jit(solution)/shard_map/ppermute | solution.py:549
  13.1 3.6 %slot_lists.1.table_ref = s32[1152]{0:T(1024)} custom-call(s32[192]{0:T(256)} %rows_ref.1, s32[192]{0:T(256)} %fetch_ref.1, s32[1]{0:T(128)S(6)} %copy.13.count_ref), custom_call_target="tpu_custom_call" | custom-call | flops 3221225472 | bytes 1536 | tf_op jit(solution)/shard_map/slot_lists/pallas_call | solution.py:116
  16.8 5.4 %collective-permute-start.4 = (bf16[512,256]{1,0:T(8,128)(2,1)S(1)}, bf16[512,256]{1,0:T(8,128)(2,1)S(1)}, u32[]{:S(2)}, u32[]{:S(2)}) collective-permute-start(bf16[512,256]{1,0:T(8,128)(2,1)S(1)} %pad_maximum_fusion.refs_0_), channel_id=1, source_target_pairs={{0,1},{1,0},{2,3},{3,2},{4,5},{5,4},{6,7},{7,6},{8,9},{9,8},{10,11... | collective-permute-start | bytes 786440 | tf_op jit(solution)/shard_map/ppermute | solution.py:540
  22.1 4.3 %collective-permute-start.5 = (bf16[512,256]{1,0:T(8,128)(2,1)S(1)}, bf16[512,256]{1,0:T(8,128)(2,1)S(1)}, u32[]{:S(2)}, u32[]{:S(2)}) collective-permute-start(bf16[512,256]{1,0:T(8,128)(2,1)S(1)} %pad_maximum_fusion.refs_0_), channel_id=1, source_target_pairs={{0,2},{1,3},{2,0},{3,1},{4,6},{5,7},{6,4},{7,5},{8,10},{9,11},{10,... | collective-permute-start | bytes 786440 | tf_op jit(solution)/shard_map/ppermute | solution.py:540
  27.1 4.3 %densify.1.refs_4_.adj_ref = bf16[2048,2048]{1,0:T(8,128)(2,1)S(1)} custom-call(s32[1152]{0:T(1024)S(1)} %copy-done.2, bf16[192,128,128]{2,1,0:T(8,128)(2,1)S(1)} %bitcast.1), custom_call_target="tpu_custom_call" | custom-call | flops 3145728 | bytes 14680064 | tf_op jit(solution)/shard_map/densify/pallas_call | solution.py:172
  31.5 1.9 %collective-permute-done.5.refs_2_ = bf16[512,256]{1,0:T(8,128)(2,1)S(1)} collective-permute-done((bf16[512,256]{1,0:T(8,128)(2,1)S(1)}, bf16[512,256]{1,0:T(8,128)(2,1)S(1)}, u32[]{:S(2)}, u32[]{:S(2)}) %collective-permute-start.5) | collective-permute-done | bytes 262176 | tf_op jit(solution)/shard_map/ppermute | solution.py:540
  34.8 1.8 %forward.2 = (bf16[512,256]{1,0:T(8,128)(2,1)S(1)}, f32[512,256]{1,0:T(8,128)S(1)}) custom-call(bf16[512,256]{1,0:T(8,128)(2,1)S(1)} %pad_maximum_fusion.refs_0_, bf16[512,256]{1,0:T(8,128)(2,1)S(1)} %collective-permute-done.4.refs_1_, bf16[512,256]{1,0:T(8,128)(2,1)S(1)} %collective-permute-done.5.refs_2_, ...), custom_call_target="tpu_custom_call" | custom-call | flops 1073741824 | bytes 5242880 | tf_op jit(solution)/shard_map/forward/pallas_call | solution.py:253
  38.4 1.8 %collective-permute-start.9 = (bf16[512,256]{1,0:T(8,128)(2,1)S(1)}, bf16[512,256]{1,0:T(8,128)(2,1)S(1)}, u32[]{:S(2)}, u32[]{:S(2)}) collective-permute-start(bf16[512,256]{1,0:T(8,128)(2,1)S(1)} %add_convert_fusion), channel_id=1, source_target_pairs={{0,2},{1,3},{2,0},{3,1},{4,6},{5,7},{6,4},{7,5},{8,10},{9,11},{10,... | collective-permute-start | bytes 786440 | tf_op jit(solution)/shard_map/ppermute | solution.py:540
  40.2 1.8 %forward.3 = (bf16[512,256]{1,0:T(8,128)(2,1)S(1)}, f32[512,256]{1,0:T(8,128)S(1)}) custom-call(bf16[512,256]{1,0:T(8,128)(2,1)S(1)} %pad_maximum_fusion.refs_0_, bf16[512,256]{1,0:T(8,128)(2,1)S(1)} %collective-permute-done.4.refs_1_, bf16[512,256]{1,0:T(8,128)(2,1)S(1)} %collective-permute-done.5.refs_2_, ...), custom_call_target="tpu_custom_call" | custom-call | flops 1073741824 | bytes 5242880 | tf_op jit(solution)/shard_map/forward/pallas_call | solution.py:253
  42.5 1.8 %collective-permute-start.11 = (s32[128]{0:T(128)S(1)}, s32[128]{0:T(128)S(1)}, u32[]{:S(2)}, u32[]{:S(2)}) collective-permute-start(s32[128]{0:T(128)S(1)} %get-tuple-element.51.refs_0_), channel_id=1, source_target_pairs={{0,2},{1,3},{2,0},{3,1},{4,6},{5,7},{6,4},{7,5},{8,10},{9,11},{10,... | collective-permute-start | bytes 1544 | tf_op jit(solution)/shard_map/ppermute | solution.py:540
  44.3 1.8 %collective-permute-done.12.refs_3_ = s32[128]{0:T(128)S(1)} collective-permute-done((s32[128]{0:T(128)S(1)}, s32[128]{0:T(128)S(1)}, u32[]{:S(2)}, u32[]{:S(2)}) %collective-permute-start.12) | collective-permute-done | bytes 544 | tf_op jit(solution)/shard_map/ppermute | solution.py:540
  48.0 1.7 %collective-permute-start.13 = (bf16[256,512]{1,0:T(8,128)(2,1)S(1)}, bf16[256,512]{1,0:T(8,128)(2,1)S(1)}, u32[]{:S(2)}, u32[]{:S(2)}) collective-permute-start(bf16[256,512]{1,0:T(8,128)(2,1)S(1)} %get-tuple-element.54.even_ref), channel_id=1, source_target_pairs={{0,2},{1,3},{2,0},{3,1},{4,6},{5,7},{6,4},{7,5},{8,10},{9,11},{10,... | collective-permute-start | bytes 786440 | tf_op jit(solution)/shard_map/ppermute | solution.py:540
  49.8 2.3 %back_first.1 = (f32[256,2048]{1,0:T(8,128)S(1)}, f32[128,256]{1,0:T(8,128)S(1)}) custom-call(bf16[320,512]{1,0:T(8,128)(2,1)S(1)} %collective-permute-done.14.odd_ref, bf16[256,512]{1,0:T(8,128)(2,1)S(1)} %get-tuple-element.54.even_ref, bf16[2048,2048]{1,0:T(8,128)(2,1)S(1)} %densify.1.refs_4_.adj_ref, f32[128,256]{1,0:T(8,128)S(1)} %get-tuple-element.56.wkeep_ref), custom_call_target="tpu_custom_call" | custom-call | flops 1073741824 | bytes 6291456 | tf_op jit(solution)/shard_map/back_first/pallas_call | solution.py:351
  53.6 4.1 %collective-permute-done.15 = f32[128,256]{1,0:T(8,128)S(1)} collective-permute-done((f32[128,256]{1,0:T(8,128)S(1)}, f32[128,256]{1,0:T(8,128)S(1)}, u32[]{:S(2)}, u32[]{:S(2)}) %collective-permute-start.15) | collective-permute-done | bytes 131104 | tf_op jit(solution)/shard_map/ppermute | solution.py:543
  59.4 1.8 %back_second_1.1 = (bf16[128,1024]{1,0:T(8,128)(2,1)S(1)}, f32[128,1024]{1,0:T(8,128)S(1)}) custom-call(bf16[256,512]{1,0:T(8,128)(2,1)S(1)} %collective-permute-done.16.odd_ref, bf16[256,512]{1,0:T(8,128)(2,1)S(1)} %collective-permute-done.13.even_ref, bf16[2048,2048]{1,0:T(8,128)(2,1)S(1)} %densify.1.refs_4_.adj_ref, ...), custom_call_target="tpu_custom_call" | custom-call | flops 536870912 | bytes 3932160 | tf_op jit(solution)/shard_map/back_second_1/pallas_call | solution.py:383
  62.4 1.8 %back_second_0.1 = (bf16[128,1024]{1,0:T(8,128)(2,1)S(1)}, f32[128,1024]{1,0:T(8,128)S(1)}) custom-call(bf16[256,512]{1,0:T(8,128)(2,1)S(1)} %collective-permute-done.16.odd_ref, bf16[256,512]{1,0:T(8,128)(2,1)S(1)} %collective-permute-done.13.even_ref, bf16[2048,2048]{1,0:T(8,128)(2,1)S(1)} %densify.1.refs_4_.adj_ref, ...), custom_call_target="tpu_custom_call" | custom-call | flops 536870912 | bytes 3932160 | tf_op jit(solution)/shard_map/back_second_0/pallas_call | solution.py:383
  66.0 1.7 %collective-permute-start.20 = (bf16[64,2048]{1,0:T(8,128)(2,1)S(1)}, bf16[64,2048]{1,0:T(8,128)(2,1)S(1)}, u32[]{:S(2)}, u32[]{:S(2)}) collective-permute-start(bf16[64,2048]{1,0:T(8,128)(2,1)S(1)} %across_sum.1), channel_id=1, source_target_pairs={{0,2},{1,3},{2,0},{3,1},{4,6},{5,7},{6,4},{7,5},{8,10},{9,11},{10,... | collective-permute-start | bytes 786440 | tf_op jit(solution)/shard_map/ppermute | solution.py:540
  67.7 2.8 %collective-permute-start.21 = (f32[64,256]{1,0:T(8,128)S(1)}, f32[64,256]{1,0:T(8,128)S(1)}, u32[]{:S(2)}, u32[]{:S(2)}) collective-permute-start(f32[64,256]{1,0:T(8,128)S(1)} %add.17), channel_id=1, source_target_pairs={{0,8},{4,12},{8,0},{12,4},{16,24},{20,28},{24,16},{28,20},{1,9},{5... | collective-permute-start | bytes 196616 | tf_op jit(solution)/shard_map/ppermute | solution.py:543
  70.5 2.3 %collective-permute-done.21 = f32[64,256]{1,0:T(8,128)S(1)} collective-permute-done((f32[64,256]{1,0:T(8,128)S(1)}, f32[64,256]{1,0:T(8,128)S(1)}, u32[]{:S(2)}, u32[]{:S(2)}) %collective-permute-start.21) | collective-permute-done | bytes 65568 | tf_op jit(solution)/shard_map/ppermute | solution.py:543
  73.8 4.6 %collective-permute-done.22 = f32[64,256]{1,0:T(8,128)S(1)} collective-permute-done((f32[64,256]{1,0:T(8,128)S(1)}, f32[64,256]{1,0:T(8,128)S(1)}, u32[]{:S(2)}, u32[]{:S(2)}) %collective-permute-start.22) | collective-permute-done | bytes 65568 | tf_op jit(solution)/shard_map/ppermute | solution.py:543
  78.5 11.2 %all_to_all.5.refs_4_ = bf16[8,64,256]{2,1,0:T(8,128)(2,1)S(1)} all-to-all(bf16[8,64,256]{2,1,0:T(8,128)(2,1)S(1)} %split.1), channel_id=1, replica_groups=mesh['row'=8,'rep'=4] {'row'}, dimensions={0} | all-to-all | bytes 524288 | tf_op jit(solution)/shard_map/all_to_all | solution.py:597
  92.4 3.8 %collective-permute-done.24.refs_2_ = bf16[96,512]{1,0:T(8,128)(2,1)S(1)} collective-permute-done((bf16[96,512]{1,0:T(8,128)(2,1)S(1)}, bf16[96,512]{1,0:T(8,128)(2,1)S(1)}, u32[]{:S(2)}, u32[]{:S(2)}) %collective-permute-start.24) | collective-permute-done | bytes 98336 | tf_op jit(solution)/shard_map/ppermute | solution.py:540
  (61 shorter events, 21.1 us)
Async XLA Ops:
  1.4 5.6 %collective-permute-start.1 = (s32[1,8,2]{2,1,0:T(8,128)S(1)}, s32[1,8,2]{2,1,0:T(8,128)S(1)}, u32[]{:S(2)}, u32[]{:S(2)}) collective-permute-start(s32[1,8,2]{2,1,0:T(8,128)S(1)} %copy.11), channel_id=1, source_target_pairs={{0,16},{1,21},{2,26},{3,31},{4,20},{5,17},{6,30},{7,27},{8,24},{9,... | collective-permute-start | bytes 200 | tf_op jit(solution)/shard_map/ppermute | solution.py:549
  9.3 7.5 %collective-permute-start.2 = (bf16[256,256]{1,0:T(8,128)(2,1)S(1)}, bf16[256,256]{1,0:T(8,128)(2,1)S(1)}, u32[]{:S(2)}, u32[]{:S(2)}) collective-permute-start(bf16[256,256]{1,0:T(8,128)(2,1)S(1)} %get-tuple-element.39), channel_id=1, source_target_pairs={{0,0},{1,5},{2,10},{3,15},{4,4},{5,1},{6,14},{7,11},{8,8},{9,13},{... | collective-permute-start | bytes 393224 | tf_op jit(solution)/shard_map/ppermute | solution.py:549
  10.1 6.6 %collective-permute-start.3 = (bf16[256,256]{1,0:T(8,128)(2,1)S(1)}, bf16[256,256]{1,0:T(8,128)(2,1)S(1)}, u32[]{:S(2)}, u32[]{:S(2)}) collective-permute-start(bf16[256,256]{1,0:T(8,128)(2,1)S(1)} %get-tuple-element.40), channel_id=1, source_target_pairs={{0,16},{1,21},{2,26},{3,31},{4,20},{5,17},{6,30},{7,27},{8,24},{9,... | collective-permute-start | bytes 393224 | tf_op jit(solution)/shard_map/ppermute | solution.py:549
  16.8 9.7 %collective-permute-start.4 = (bf16[512,256]{1,0:T(8,128)(2,1)S(1)}, bf16[512,256]{1,0:T(8,128)(2,1)S(1)}, u32[]{:S(2)}, u32[]{:S(2)}) collective-permute-start(bf16[512,256]{1,0:T(8,128)(2,1)S(1)} %pad_maximum_fusion.refs_0_), channel_id=1, source_target_pairs={{0,1},{1,0},{2,3},{3,2},{4,5},{5,4},{6,7},{7,6},{8,9},{9,8},{10,11... | collective-permute-start | bytes 786440 | tf_op jit(solution)/shard_map/ppermute | solution.py:540
  22.1 11.2 %collective-permute-start.5 = (bf16[512,256]{1,0:T(8,128)(2,1)S(1)}, bf16[512,256]{1,0:T(8,128)(2,1)S(1)}, u32[]{:S(2)}, u32[]{:S(2)}) collective-permute-start(bf16[512,256]{1,0:T(8,128)(2,1)S(1)} %pad_maximum_fusion.refs_0_), channel_id=1, source_target_pairs={{0,2},{1,3},{2,0},{3,1},{4,6},{5,7},{6,4},{7,5},{8,10},{9,11},{10,... | collective-permute-start | bytes 786440 | tf_op jit(solution)/shard_map/ppermute | solution.py:540
  36.7 1.6 %collective-permute-start.7 = (bf16[512,256]{1,0:T(8,128)(2,1)S(1)}, bf16[512,256]{1,0:T(8,128)(2,1)S(1)}, u32[]{:S(2)}, u32[]{:S(2)}) collective-permute-start(bf16[512,256]{1,0:T(8,128)(2,1)S(1)} %get-tuple-element.46), channel_id=1, source_target_pairs={{0,1},{1,0},{2,3},{3,2},{4,5},{5,4},{6,7},{7,6},{8,9},{9,8},{10,11... | collective-permute-start | bytes 786440 | tf_op jit(solution)/shard_map/ppermute | solution.py:540
  38.4 8.5 %collective-permute-start.9 = (bf16[512,256]{1,0:T(8,128)(2,1)S(1)}, bf16[512,256]{1,0:T(8,128)(2,1)S(1)}, u32[]{:S(2)}, u32[]{:S(2)}) collective-permute-start(bf16[512,256]{1,0:T(8,128)(2,1)S(1)} %add_convert_fusion), channel_id=1, source_target_pairs={{0,2},{1,3},{2,0},{3,1},{4,6},{5,7},{6,4},{7,5},{8,10},{9,11},{10,... | collective-permute-start | bytes 786440 | tf_op jit(solution)/shard_map/ppermute | solution.py:540
  42.0 4.9 %collective-permute-start.8 = (bf16[512,256]{1,0:T(8,128)(2,1)S(1)}, bf16[512,256]{1,0:T(8,128)(2,1)S(1)}, u32[]{:S(2)}, u32[]{:S(2)}) collective-permute-start(bf16[512,256]{1,0:T(8,128)(2,1)S(1)} %get-tuple-element.49), channel_id=1, source_target_pairs={{0,1},{1,0},{2,3},{3,2},{4,5},{5,4},{6,7},{7,6},{8,9},{9,8},{10,11... | collective-permute-start | bytes 786440 | tf_op jit(solution)/shard_map/ppermute | solution.py:540
  42.1 4.0 %collective-permute-start.12 = (s32[128]{0:T(128)S(1)}, s32[128]{0:T(128)S(1)}, u32[]{:S(2)}, u32[]{:S(2)}) collective-permute-start(s32[128]{0:T(128)S(1)} %get-tuple-element.51.refs_0_), channel_id=1, source_target_pairs={{0,3},{1,2},{2,1},{3,0},{4,7},{5,6},{6,5},{7,4},{8,11},{9,10},{10,... | collective-permute-start | bytes 1544 | tf_op jit(solution)/shard_map/ppermute | solution.py:540
  42.5 4.4 %collective-permute-start.11 = (s32[128]{0:T(128)S(1)}, s32[128]{0:T(128)S(1)}, u32[]{:S(2)}, u32[]{:S(2)}) collective-permute-start(s32[128]{0:T(128)S(1)} %get-tuple-element.51.refs_0_), channel_id=1, source_target_pairs={{0,2},{1,3},{2,0},{3,1},{4,6},{5,7},{6,4},{7,5},{8,10},{9,11},{10,... | collective-permute-start | bytes 1544 | tf_op jit(solution)/shard_map/ppermute | solution.py:540
  44.3 2.6 %collective-permute-start.10 = (s32[128]{0:T(128)S(1)}, s32[128]{0:T(128)S(1)}, u32[]{:S(2)}, u32[]{:S(2)}) collective-permute-start(s32[128]{0:T(128)S(1)} %get-tuple-element.51.refs_0_), channel_id=1, source_target_pairs={{0,1},{1,0},{2,3},{3,2},{4,5},{5,4},{6,7},{7,6},{8,9},{9,8},{10,11... | collective-permute-start | bytes 1544 | tf_op jit(solution)/shard_map/ppermute | solution.py:540
  48.0 1.8 %collective-permute-start.14 = (bf16[320,512]{1,0:T(8,128)(2,1)S(1)}, bf16[320,512]{1,0:T(8,128)(2,1)S(1)}, u32[]{:S(2)}, u32[]{:S(2)}) collective-permute-start(bf16[320,512]{1,0:T(8,128)(2,1)S(1)} %get-tuple-element.55), channel_id=1, source_target_pairs={{0,1},{1,0},{2,3},{3,2},{4,5},{5,4},{6,7},{7,6},{8,9},{9,8},{10,11... | collective-permute-start | bytes 983048 | tf_op jit(solution)/shard_map/ppermute | solution.py:540
  48.0 9.7 %collective-permute-start.13 = (bf16[256,512]{1,0:T(8,128)(2,1)S(1)}, bf16[256,512]{1,0:T(8,128)(2,1)S(1)}, u32[]{:S(2)}, u32[]{:S(2)}) collective-permute-start(bf16[256,512]{1,0:T(8,128)(2,1)S(1)} %get-tuple-element.54.even_ref), channel_id=1, source_target_pairs={{0,2},{1,3},{2,0},{3,1},{4,6},{5,7},{6,4},{7,5},{8,10},{9,11},{10,... | collective-permute-start | bytes 786440 | tf_op jit(solution)/shard_map/ppermute | solution.py:540
  52.1 5.7 %collective-permute-start.15 = (f32[128,256]{1,0:T(8,128)S(1)}, f32[128,256]{1,0:T(8,128)S(1)}, u32[]{:S(2)}, u32[]{:S(2)}) collective-permute-start(f32[128,256]{1,0:T(8,128)S(1)} %get-tuple-element.58), channel_id=1, source_target_pairs={{0,4},{4,0},{8,12},{12,8},{16,20},{20,16},{24,28},{28,24},{1,5},{5... | collective-permute-start | bytes 393224 | tf_op jit(solution)/shard_map/ppermute | solution.py:543
  57.7 1.7 %collective-permute-start.16 = (bf16[256,512]{1,0:T(8,128)(2,1)S(1)}, bf16[256,512]{1,0:T(8,128)(2,1)S(1)}, u32[]{:S(2)}, u32[]{:S(2)}) collective-permute-start(bf16[256,512]{1,0:T(8,128)(2,1)S(1)} %collective-permute-done.13.even_ref), channel_id=1, source_target_pairs={{0,1},{1,0},{2,3},{3,2},{4,5},{5,4},{6,7},{7,6},{8,9},{9,8},{10,11... | collective-permute-start | bytes 786440 | tf_op jit(solution)/shard_map/ppermute | solution.py:540
  57.8 4.6 %collective-permute-start.17 = (f32[64,256]{1,0:T(8,128)S(1)}, f32[64,256]{1,0:T(8,128)S(1)}, u32[]{:S(2)}, u32[]{:S(2)}) collective-permute-start(f32[64,256]{1,0:T(8,128)S(1)} %get-tuple-element.76), channel_id=1, source_target_pairs={{0,2},{1,3},{2,0},{3,1},{4,6},{5,7},{6,4},{7,5},{8,10},{9,11},{10,... | collective-permute-start | bytes 196616 | tf_op jit(solution)/shard_map/ppermute | solution.py:540
  62.4 1.8 %collective-permute-start.18 = (bf16[128,1024]{1,0:T(8,128)(2,1)S(1)}, bf16[128,1024]{1,0:T(8,128)(2,1)S(1)}, u32[]{:S(2)}, u32[]{:S(2)}) collective-permute-start(bf16[128,1024]{1,0:T(8,128)(2,1)S(1)} %get-tuple-element.61), channel_id=1, source_target_pairs={{0,1},{1,0},{2,3},{3,2},{4,5},{5,4},{6,7},{7,6},{8,9},{9,8},{10,11... | collective-permute-start | bytes 786440 | tf_op jit(solution)/shard_map/ppermute | solution.py:540
  64.2 1.7 %collective-permute-start.19 = (bf16[128,1024]{1,0:T(8,128)(2,1)S(1)}, bf16[128,1024]{1,0:T(8,128)(2,1)S(1)}, u32[]{:S(2)}, u32[]{:S(2)}) collective-permute-start(bf16[128,1024]{1,0:T(8,128)(2,1)S(1)} %get-tuple-element.65), channel_id=1, source_target_pairs={{0,1},{1,0},{2,3},{3,2},{4,5},{5,4},{6,7},{7,6},{8,9},{9,8},{10,11... | collective-permute-start | bytes 786440 | tf_op jit(solution)/shard_map/ppermute | solution.py:540
  66.0 12.3 %collective-permute-start.20 = (bf16[64,2048]{1,0:T(8,128)(2,1)S(1)}, bf16[64,2048]{1,0:T(8,128)(2,1)S(1)}, u32[]{:S(2)}, u32[]{:S(2)}) collective-permute-start(bf16[64,2048]{1,0:T(8,128)(2,1)S(1)} %across_sum.1), channel_id=1, source_target_pairs={{0,2},{1,3},{2,0},{3,1},{4,6},{5,7},{6,4},{7,5},{8,10},{9,11},{10,... | collective-permute-start | bytes 786440 | tf_op jit(solution)/shard_map/ppermute | solution.py:540
  67.7 5.1 %collective-permute-start.21 = (f32[64,256]{1,0:T(8,128)S(1)}, f32[64,256]{1,0:T(8,128)S(1)}, u32[]{:S(2)}, u32[]{:S(2)}) collective-permute-start(f32[64,256]{1,0:T(8,128)S(1)} %add.17), channel_id=1, source_target_pairs={{0,8},{4,12},{8,0},{12,4},{16,24},{20,28},{24,16},{28,20},{1,9},{5... | collective-permute-start | bytes 196616 | tf_op jit(solution)/shard_map/ppermute | solution.py:543
  72.8 5.6 %collective-permute-start.22 = (f32[64,256]{1,0:T(8,128)S(1)}, f32[64,256]{1,0:T(8,128)S(1)}, u32[]{:S(2)}, u32[]{:S(2)}) collective-permute-start(f32[64,256]{1,0:T(8,128)S(1)} %add.18), channel_id=1, source_target_pairs={{0,16},{4,20},{8,24},{12,28},{16,0},{20,4},{24,8},{28,12},{1,17},{... | collective-permute-start | bytes 196616 | tf_op jit(solution)/shard_map/ppermute | solution.py:543
  90.5 1.9 %collective-permute-start.23 = (bf16[96,512]{1,0:T(8,128)(2,1)S(1)}, bf16[96,512]{1,0:T(8,128)(2,1)S(1)}, u32[]{:S(2)}, u32[]{:S(2)}) collective-permute-start(bf16[96,512]{1,0:T(8,128)(2,1)S(1)} %get-tuple-element.70), channel_id=1, source_target_pairs={{0,1},{1,0},{2,3},{3,2},{4,5},{5,4},{6,7},{7,6},{8,9},{9,8},{10,11... | collective-permute-start | bytes 294920 | tf_op jit(solution)/shard_map/ppermute | solution.py:540
  90.5 5.7 %collective-permute-start.24 = (bf16[96,512]{1,0:T(8,128)(2,1)S(1)}, bf16[96,512]{1,0:T(8,128)(2,1)S(1)}, u32[]{:S(2)}, u32[]{:S(2)}) collective-permute-start(bf16[96,512]{1,0:T(8,128)(2,1)S(1)} %get-tuple-element.71), channel_id=1, source_target_pairs={{0,2},{1,3},{2,0},{3,1},{4,6},{5,7},{6,4},{7,5},{8,10},{9,11},{10,... | collective-permute-start | bytes 294920 | tf_op jit(solution)/shard_map/ppermute | solution.py:540
  91.1 6.3 %collective-permute-start.25 = (bf16[96,512]{1,0:T(8,128)(2,1)S(1)}, bf16[96,512]{1,0:T(8,128)(2,1)S(1)}, u32[]{:S(2)}, u32[]{:S(2)}) collective-permute-start(bf16[96,512]{1,0:T(8,128)(2,1)S(1)} %get-tuple-element.72), channel_id=1, source_target_pairs={{0,3},{1,2},{2,1},{3,0},{4,7},{5,6},{6,5},{7,4},{8,11},{9,10},{10,... | collective-permute-start | bytes 294920 | tf_op jit(solution)/shard_map/ppermute | solution.py:540
  (7 other events, 57.7 us)

commit v10 on v9

--- a/solution.py
+++ b/solution.py
@@ -38,6 +38,10 @@
     if n & (n - 1) == 0:
         return x >> (n.bit_length() - 1), x & (n - 1)
     return lax.div(x, n), lax.rem(x, n)
+
+
+def turned(low):
+    return ((low & 1) << 1) | (low >> 1)
 
 
 class Table:
@@ -78,7 +82,7 @@
         hi, low = div_rem(source ^ r, n_rep)
         half, hi = div_rem(hi, deep)
         row = (n_rep - 1 - (row_high ^ q)) * quarter + row_low
-        col = ((half * n_rep + (low ^ q)) * deep + hi) * per_list + c
+        col = ((half * n_rep + (turned(low) ^ q)) * deep + hi) * per_list + c
         cell = jnp.where(slot < live, row * all_cols + col, t.spare)
         return cell, t.wide_at + row * chunks + div_rem(col, COL_CHUNK)[0]
 
@@ -224,15 +228,13 @@
 
 
 def forward_body(*refs, n_rep):
-    pieces = refs[:n_rep]
-    adj_ref, send_ref, keep_ref = refs[n_rep:]
+    pieces = refs[: 2 * n_rep]
+    adj_ref, send_ref, keep_ref = refs[2 * n_rep :]
     i = pl.program_id(0)
-    depth = pieces[0].shape[0] // 2
+    depth = pieces[0].shape[0]
     total = 0.0
-    for half in range(2):
-        for j in range(n_rep):
-            at = (half * n_rep + j) * depth
-            total += dot(adj_ref[:, at : at + depth], pieces[j][half * depth : (half + 1) * depth])
+    for n, piece in enumerate(pieces):
+        total += dot(adj_ref[:, n * depth : (n + 1) * depth], piece[...])
 
     half = pl.num_programs(0) // 2
 
@@ -251,7 +253,7 @@
     tiles = rows // ROW_TILE
     half = tiles // 2
     return pl.pallas_call(
-        functools.partial(forward_body, n_rep=len(pieces)),
+        functools.partial(forward_body, n_rep=len(pieces) // 2),
         grid=(tiles,),
         out_shape=[shape((rows // 2, features), BF16), shape((rows // 2, features), F32)],
         in_specs=[pl.BlockSpec(x.shape, lambda i: (0, 0)) for x in pieces]
@@ -431,7 +433,7 @@
     for half, (own, near) in enumerate(((low_ref, low_near), (high_ref, high_near))):
         for i in range(per_half):
             low, hi = i % n_rep, i // n_rep
-            j = low ^ q
+            j = turned(low) ^ q
             cols = pl.ds(pl.multiple_of((j * deep + hi) * width, width), width)
             far_cols = pl.ds(pl.multiple_of((half * per_half + (j ^ 2) * deep + hi) * width, width), width)
             total = own[part:, cols] + near[part:, cols].astype(F32) + far_ref[:, far_cols].astype(F32)
@@ -458,7 +460,7 @@
     r, q = lax.axis_index("row"), lax.axis_index("rep")
     acc_ref[...] = jnp.zeros(acc_ref.shape, F32)
     for k in range(n_row):
-        j = (k % n_rep) ^ q
+        j = turned(k % n_rep) ^ q
         for c in range(per_list):
             at = k // n_rep * per_list + c
             b = lists[0][at]
@@ -544,7 +546,7 @@
 
     def spread(x, hi):
         perm = [
-            (r * n_rep + q, (r ^ (hi * n_rep + q)) * n_rep + q) for r in range(n_row) for q in range(n_rep)
+            (r * n_rep + q, (r ^ (hi * n_rep + turned(q))) * n_rep + q) for r in range(n_row) for q in range(n_rep)
         ]
         return lax.ppermute(x, ("row", "rep"), perm)
 
@@ -554,15 +556,18 @@
     wanted = [spread(fetch_lists, hi) for hi in range(n_hi)]
     *outgoing, own_list = pack(wanted, node_features, per_list, blk)
     own = [spread(x, hi) for hi, x in enumerate(outgoing)]
+    deep = n_hi // 2
+    low, high = [jnp.concatenate(own[half * deep : (half + 1) * deep], axis=0) for half in range(2)]
+    low_far, low_near = to_rep(low, 2), to_rep(low, 1)
     table = slot_lists(
-        block_rows, block_fetch, after(block_count, outgoing), n_row, n_rep, per_list, row_blocks
+        block_rows, block_fetch, after(block_count, low_near), n_row, n_rep, per_list, row_blocks
     )
-    deep = n_hi // 2
-    own = after(jnp.concatenate(own, axis=0), table)
-    far = to_rep(own, 2)
-    near = to_rep(own, 1)
-    adj = densify(after(table, near), blocks, n_row, per_list, row_blocks)
-    pieces = [own, near, far, to_rep(after(far, adj), 1)]
+    high = after(high, low_far, table)
+    high_far, high_near = to_rep(high, 2), to_rep(high, 1)
+    adj = densify(after(table, high_near), blocks, n_row, per_list, row_blocks)
+    low_diag = to_rep(after(low_far, high_near), 1)
+    high_diag = to_rep(after(high_far, adj), 1)
+    pieces = [low, low_near, low_far, low_diag, high, high_near, high_far, high_diag]
 
     send3, keep2 = forward(pieces, adj, 0)
     across = (keep2 + to_rep(send3, 1).astype(F32)).astype(BF16)
@@ -583,13 +588,15 @@
     got = to_rep(w[part:], 2)
     send_high, keep_high = back_second(grad3, grad2, adj, first, 1, n_rep, deep)
     send_high = after(send_high, got)
+    w = w[:part] + got
+    got = to_row(w, 2)
     near_high = to_rep(send_high, 1)
     send_low, keep_low = back_second(grad3, grad2, adj, after(first, send_high), 0, n_rep, deep)
-    near_low = to_rep(after(send_low, near_high), 1)
+    near_low = to_rep(after(send_low, near_high, got), 1)
     across = across_sum(keep_low, near_low, keep_high, near_high)
     far = to_rep(across, 2)
-    w = after(w[:part], across) + got
-    step = 2
+    w = after(w, across) + got
+    step = 4
     while step < n_row:
         w = w + to_row(w, step)
         step *= 2

time: 98.8 us -> 99.4 us (level)
  starting transfers between devices: 35.3 us -> 26.9 us
  waiting for transfers between devices: 25.9 us -> 33.4 us
  Pallas kernels: 22.9 us -> 25.1 us
    ppermute x3, starting transfers between devices: 5.33 us -> 0.63 us  [to_row(): return lax.ppermute(x, 'row', xor_perm(n_row, k))]
    ppermute x19 -> x22, waiting for transfers between devices: 14.7 us -> 18.6 us  [to_rep(): return lax.ppermute(x, 'rep', xor_perm(n_rep, j))]
    ppermute x19 -> x22, starting transfers between devices: 21.5 us -> 17.9 us  [to_rep(): return lax.ppermute(x, 'rep', xor_perm(n_rep, j))]
    ppermute x3, waiting for transfers between devices: 11 us -> 13.8 us  [to_row(): return lax.ppermute(x, 'row', xor_perm(n_row, k))]
    pallas_call x1, Pallas kernels: 3.63 us -> 5.22 us  [slot_lists(): pl.pallas_call(body, out_shape=shape((Table(slots, row_blocks * n_row * p...]
  transfers between devices with their start and end apart: 26 -> 29, of which waited for: 13 -> 16; matrix products, arithmetic and copies ran while one was open for 0% -> 0% of each run, Pallas kernels for 16% -> 18%
where the time goes in v10:
time: 99.4 us; the launch traced here: 99.6 us
  waiting for transfers between devices  33.4 us (34%)
  starting transfers between devices  26.9 us (27%)
  Pallas kernels  25.1 us (25%)
  blocking collectives  11.1 us (11%)
  between operations  1.57 us (2%)
  local copies, waits for them, and re-layouts  1.48 us (1%)
    ppermute x22, waiting for transfers between devices, to_rep(): return lax.ppermute(x, 'rep', xor_perm(n_rep, j))  18.6 us
    ppermute x22, starting transfers between devices, to_rep(): return lax.ppermute(x, 'rep', xor_perm(n_rep, j))  17.9 us
    ppermute x3, waiting for transfers between devices, to_row(): return lax.ppermute(x, 'row', xor_perm(n_row, k))  13.8 us
    all_to_all x1, blocking collectives, local(): lax.all_to_all(messages, 'row', split_axis=0, concat_axis=0, tiled=True)  11.1 us
    ppermute x4, starting transfers between devices, spread(): return lax.ppermute(x, ('row', 'rep'), perm)  8.34 us
    pallas_call x1, Pallas kernels, slot_lists(): pl.pallas_call(body, out_shape=shape((Table(slots, row_blocks * n_row * p...  5.22 us
    pallas_call x1, Pallas kernels, densify(): pl.pallas_call(functools.partial(densify_body, all_cols=all_cols, row_blo...  4.94 us
    pallas_call x2, Pallas kernels, back_second(): pl.pallas_call(back_second_body, grid=(tiles,), out_shape=[shape((feature...  3.69 us
  transfers between devices with their start and end apart: 29, of which 16 were waited for; matrix products, arithmetic and copies ran while one was open for 0% of the time, Pallas kernels for 18%

profile of v10, /device:TPU:0, one launch (start us, length us, event | category | flops | bytes accessed | tf_op | source)
XLA Modules:
  0.0 99.6 jit_solution(12063187459945030749)
XLA Ops:
  1.4 4.0 %collective-permute-start.1 = (s32[1,8,2]{2,1,0:T(8,128)S(1)}, s32[1,8,2]{2,1,0:T(8,128)S(1)}, u32[]{:S(2)}, u32[]{:S(2)}) collective-permute-start(s32[1,8,2]{2,1,0:T(8,128)S(1)} %copy.11), channel_id=1, source_target_pairs={{0,16},{1,25},{2,22},{3,31},{4,20},{5,29},{6,18},{7,27},{8,24},{9,... | collective-permute-start | bytes 200 | tf_op jit(solution)/shard_map/ppermute | solution.py:551
  7.0 2.2 %pack.1 = (bf16[256,256]{1,0:T(8,128)(2,1)S(1)}, bf16[256,256]{1,0:T(8,128)(2,1)S(1)}, s32[128]{0:T(128)S(1)}) custom-call(s32[1,8,2]{2,1,0:T(8,128)S(1)} %collective-permute-done.refs_0_, s32[1,8,2]{2,1,0:T(8,128)S(1)} %collective-permute-done.1.refs_1_, bf16[2048,256]{1,0:T(8,128)(2,1)} %refs_2_.1), custom_call_target="tpu_custom_call" | custom-call | tf_op jit(solution)/shard_map/pack/pallas_call | solution.py:219
  10.6 3.0 %collective-permute-start.5 = (bf16[256,256]{1,0:T(8,128)(2,1)S(1)}, bf16[256,256]{1,0:T(8,128)(2,1)S(1)}, u32[]{:S(2)}, u32[]{:S(2)}) collective-permute-start(bf16[256,256]{1,0:T(8,128)(2,1)S(1)} %get-tuple-element.41), channel_id=1, source_target_pairs={{0,16},{1,25},{2,22},{3,31},{4,20},{5,29},{6,18},{7,27},{8,24},{9,... | collective-permute-start | bytes 393224 | tf_op jit(solution)/shard_map/ppermute | solution.py:551
  13.6 10.3 %collective-permute-start.4 = (bf16[256,256]{1,0:T(8,128)(2,1)S(1)}, bf16[256,256]{1,0:T(8,128)(2,1)S(1)}, u32[]{:S(2)}, u32[]{:S(2)}) collective-permute-start(bf16[256,256]{1,0:T(8,128)(2,1)S(1)} %collective-permute-done.2.refs_0_), channel_id=1, source_target_pairs={{0,2},{1,3},{2,0},{3,1},{4,6},{5,7},{6,4},{7,5},{8,10},{9,11},{10,... | collective-permute-start | bytes 393224 | tf_op jit(solution)/shard_map/ppermute | solution.py:542
  23.9 5.2 %slot_lists.1.table_ref = s32[1152]{0:T(1024)} custom-call(s32[192]{0:T(256)} %rows_ref.1, s32[192]{0:T(256)} %fetch_ref.1, s32[1]{0:T(128)S(6)} %copy.13.count_ref), custom_call_target="tpu_custom_call" | custom-call | flops 3221225472 | bytes 1536 | tf_op jit(solution)/shard_map/slot_lists/pallas_call | solution.py:120
  31.4 4.9 %densify.1.refs_8_.adj_ref = bf16[2048,2048]{1,0:T(8,128)(2,1)S(1)} custom-call(s32[1152]{0:T(1024)S(1)} %copy-done.2, bf16[192,128,128]{2,1,0:T(8,128)(2,1)S(1)} %bitcast.1), custom_call_target="tpu_custom_call" | custom-call | flops 3145728 | bytes 14680064 | tf_op jit(solution)/shard_map/densify/pallas_call | solution.py:176
  36.4 1.3 %collective-permute-done.9.refs_7_ = bf16[256,256]{1,0:T(8,128)(2,1)S(1)} collective-permute-done((bf16[256,256]{1,0:T(8,128)(2,1)S(1)}, bf16[256,256]{1,0:T(8,128)(2,1)S(1)}, u32[]{:S(2)}, u32[]{:S(2)}) %collective-permute-start.9) | collective-permute-done | bytes 131104 | tf_op jit(solution)/shard_map/ppermute | solution.py:542
  37.8 1.8 %forward.2 = (bf16[512,256]{1,0:T(8,128)(2,1)S(1)}, f32[512,256]{1,0:T(8,128)S(1)}) custom-call(bf16[256,256]{1,0:T(8,128)(2,1)S(1)} %collective-permute-done.2.refs_0_, bf16[256,256]{1,0:T(8,128)(2,1)S(1)} %collective-permute-done.3.refs_1_, bf16[256,256]{1,0:T(8,128)(2,1)S(1)} %collective-permute-done.4.refs_2_, ...), custom_call_target="tpu_custom_call" | custom-call | flops 1073741824 | bytes 5242880 | tf_op jit(solution)/shard_map/forward/pallas_call | solution.py:255
  39.8 1.4 %collective-permute-done.10 = bf16[512,256]{1,0:T(8,128)(2,1)S(1)} collective-permute-done((bf16[512,256]{1,0:T(8,128)(2,1)S(1)}, bf16[512,256]{1,0:T(8,128)(2,1)S(1)}, u32[]{:S(2)}, u32[]{:S(2)}) %collective-permute-start.10) | collective-permute-done | bytes 262176 | tf_op jit(solution)/shard_map/ppermute | solution.py:542
  41.9 1.8 %forward.3 = (bf16[512,256]{1,0:T(8,128)(2,1)S(1)}, f32[512,256]{1,0:T(8,128)S(1)}) custom-call(bf16[256,256]{1,0:T(8,128)(2,1)S(1)} %collective-permute-done.2.refs_0_, bf16[256,256]{1,0:T(8,128)(2,1)S(1)} %collective-permute-done.3.refs_1_, bf16[256,256]{1,0:T(8,128)(2,1)S(1)} %collective-permute-done.4.refs_2_, ...), custom_call_target="tpu_custom_call" | custom-call | flops 1073741824 | bytes 5242880 | tf_op jit(solution)/shard_map/forward/pallas_call | solution.py:255
  43.8 1.6 %collective-permute-start.15 = (s32[128]{0:T(128)S(1)}, s32[128]{0:T(128)S(1)}, u32[]{:S(2)}, u32[]{:S(2)}) collective-permute-start(s32[128]{0:T(128)S(1)} %get-tuple-element.53.refs_0_), channel_id=1, source_target_pairs={{0,3},{1,2},{2,1},{3,0},{4,7},{5,6},{6,5},{7,4},{8,11},{9,10},{10,... | collective-permute-start | bytes 1544 | tf_op jit(solution)/shard_map/ppermute | solution.py:542
  46.0 2.9 %collective-permute-done.15.refs_3_ = s32[128]{0:T(128)S(1)} collective-permute-done((s32[128]{0:T(128)S(1)}, s32[128]{0:T(128)S(1)}, u32[]{:S(2)}, u32[]{:S(2)}) %collective-permute-start.15) | collective-permute-done | bytes 544 | tf_op jit(solution)/shard_map/ppermute | solution.py:542
  52.5 2.3 %back_first.1 = (f32[256,2048]{1,0:T(8,128)S(1)}, f32[128,256]{1,0:T(8,128)S(1)}) custom-call(bf16[320,512]{1,0:T(8,128)(2,1)S(1)} %collective-permute-done.17.odd_ref, bf16[256,512]{1,0:T(8,128)(2,1)S(1)} %get-tuple-element.56.even_ref, bf16[2048,2048]{1,0:T(8,128)(2,1)S(1)} %densify.1.refs_8_.adj_ref, f32[128,256]{1,0:T(8,128)S(1)} %get-tuple-element.58.wkeep_ref), custom_call_target="tpu_custom_call" | custom-call | flops 1073741824 | bytes 6291456 | tf_op jit(solution)/shard_map/back_first/pallas_call | solution.py:353
  55.3 5.1 %collective-permute-done.18 = f32[128,256]{1,0:T(8,128)S(1)} collective-permute-done((f32[128,256]{1,0:T(8,128)S(1)}, f32[128,256]{1,0:T(8,128)S(1)}, u32[]{:S(2)}, u32[]{:S(2)}) %collective-permute-start.18) | collective-permute-done | bytes 131104 | tf_op jit(solution)/shard_map/ppermute | solution.py:545
  62.0 1.8 %back_second_1.1 = (bf16[128,1024]{1,0:T(8,128)(2,1)S(1)}, f32[128,1024]{1,0:T(8,128)S(1)}) custom-call(bf16[256,512]{1,0:T(8,128)(2,1)S(1)} %collective-permute-done.19.odd_ref, bf16[256,512]{1,0:T(8,128)(2,1)S(1)} %collective-permute-done.16.even_ref, bf16[2048,2048]{1,0:T(8,128)(2,1)S(1)} %densify.1.refs_8_.adj_ref, ...), custom_call_target="tpu_custom_call" | custom-call | flops 536870912 | bytes 3932160 | tf_op jit(solution)/shard_map/back_second_1/pallas_call | solution.py:385
  65.1 1.8 %back_second_0.1 = (bf16[128,1024]{1,0:T(8,128)(2,1)S(1)}, f32[128,1024]{1,0:T(8,128)S(1)}) custom-call(bf16[256,512]{1,0:T(8,128)(2,1)S(1)} %collective-permute-done.19.odd_ref, bf16[256,512]{1,0:T(8,128)(2,1)S(1)} %collective-permute-done.16.even_ref, bf16[2048,2048]{1,0:T(8,128)(2,1)S(1)} %densify.1.refs_8_.adj_ref, ...), custom_call_target="tpu_custom_call" | custom-call | flops 536870912 | bytes 3932160 | tf_op jit(solution)/shard_map/back_second_0/pallas_call | solution.py:385
  67.0 2.6 %collective-permute-done.22 = f32[64,256]{1,0:T(8,128)S(1)} collective-permute-done((f32[64,256]{1,0:T(8,128)S(1)}, f32[64,256]{1,0:T(8,128)S(1)}, u32[]{:S(2)}, u32[]{:S(2)}) %collective-permute-start.22) | collective-permute-done | bytes 65568 | tf_op jit(solution)/shard_map/ppermute | solution.py:545
  69.6 1.5 %collective-permute-done.23.low_near = bf16[128,1024]{1,0:T(8,128)(2,1)S(1)} collective-permute-done((bf16[128,1024]{1,0:T(8,128)(2,1)S(1)}, bf16[128,1024]{1,0:T(8,128)(2,1)S(1)}, u32[]{:S(2)}, u32[]{:S(2)}) %collective-permute-start.23) | collective-permute-done | bytes 262176 | tf_op jit(solution)/shard_map/ppermute | solution.py:542
  71.9 6.1 %collective-permute-done.25 = f32[64,256]{1,0:T(8,128)S(1)} collective-permute-done((f32[64,256]{1,0:T(8,128)S(1)}, f32[64,256]{1,0:T(8,128)S(1)}, u32[]{:S(2)}, u32[]{:S(2)}) %collective-permute-start.25) | collective-permute-done | bytes 65568 | tf_op jit(solution)/shard_map/ppermute | solution.py:545
  78.0 1.6 %collective-permute-done.24.far_ref = bf16[64,2048]{1,0:T(8,128)(2,1)S(1)} collective-permute-done((bf16[64,2048]{1,0:T(8,128)(2,1)S(1)}, bf16[64,2048]{1,0:T(8,128)(2,1)S(1)}, u32[]{:S(2)}, u32[]{:S(2)}) %collective-permute-start.24) | collective-permute-done | bytes 262176 | tf_op jit(solution)/shard_map/ppermute | solution.py:542
  79.8 11.1 %all_to_all.5.refs_4_ = bf16[8,64,256]{2,1,0:T(8,128)(2,1)S(1)} all-to-all(bf16[8,64,256]{2,1,0:T(8,128)(2,1)S(1)} %split.1), channel_id=1, replica_groups=mesh['row'=8,'rep'=4] {'row'}, dimensions={0} | all-to-all | bytes 524288 | tf_op jit(solution)/shard_map/all_to_all | solution.py:604
  92.3 1.3 %collective-permute-start.28 = (bf16[96,512]{1,0:T(8,128)(2,1)S(1)}, bf16[96,512]{1,0:T(8,128)(2,1)S(1)}, u32[]{:S(2)}, u32[]{:S(2)}) collective-permute-start(bf16[96,512]{1,0:T(8,128)(2,1)S(1)} %get-tuple-element.74), channel_id=1, source_target_pairs={{0,3},{1,2},{2,1},{3,0},{4,7},{5,6},{6,5},{7,4},{8,11},{9,10},{10,... | collective-permute-start | bytes 294920 | tf_op jit(solution)/shard_map/ppermute | solution.py:542
  93.6 3.8 %collective-permute-done.27.refs_2_ = bf16[96,512]{1,0:T(8,128)(2,1)S(1)} collective-permute-done((bf16[96,512]{1,0:T(8,128)(2,1)S(1)}, bf16[96,512]{1,0:T(8,128)(2,1)S(1)}, u32[]{:S(2)}, u32[]{:S(2)}) %collective-permute-start.27) | collective-permute-done | bytes 98336 | tf_op jit(solution)/shard_map/ppermute | solution.py:542
  97.4 1.2 %collective-permute-done.28.refs_3_ = bf16[96,512]{1,0:T(8,128)(2,1)S(1)} collective-permute-done((bf16[96,512]{1,0:T(8,128)(2,1)S(1)}, bf16[96,512]{1,0:T(8,128)(2,1)S(1)}, u32[]{:S(2)}, u32[]{:S(2)}) %collective-permute-start.28) | collective-permute-done | bytes 98336 | tf_op jit(solution)/shard_map/ppermute | solution.py:542
  (66 shorter events, 17.1 us)
Async XLA Ops:
  1.4 5.6 %collective-permute-start.1 = (s32[1,8,2]{2,1,0:T(8,128)S(1)}, s32[1,8,2]{2,1,0:T(8,128)S(1)}, u32[]{:S(2)}, u32[]{:S(2)}) collective-permute-start(s32[1,8,2]{2,1,0:T(8,128)S(1)} %copy.11), channel_id=1, source_target_pairs={{0,16},{1,25},{2,22},{3,31},{4,20},{5,29},{6,18},{7,27},{8,24},{9,... | collective-permute-start | bytes 200 | tf_op jit(solution)/shard_map/ppermute | solution.py:551
  9.3 4.3 %collective-permute-start.2 = (bf16[256,256]{1,0:T(8,128)(2,1)S(1)}, bf16[256,256]{1,0:T(8,128)(2,1)S(1)}, u32[]{:S(2)}, u32[]{:S(2)}) collective-permute-start(bf16[256,256]{1,0:T(8,128)(2,1)S(1)} %get-tuple-element.40), channel_id=1, source_target_pairs={{0,0},{1,9},{2,6},{3,15},{4,4},{5,13},{6,2},{7,11},{8,8},{9,1},{10... | collective-permute-start | bytes 393224 | tf_op jit(solution)/shard_map/ppermute | solution.py:551
  10.6 18.5 %collective-permute-start.5 = (bf16[256,256]{1,0:T(8,128)(2,1)S(1)}, bf16[256,256]{1,0:T(8,128)(2,1)S(1)}, u32[]{:S(2)}, u32[]{:S(2)}) collective-permute-start(bf16[256,256]{1,0:T(8,128)(2,1)S(1)} %get-tuple-element.41), channel_id=1, source_target_pairs={{0,16},{1,25},{2,22},{3,31},{4,20},{5,29},{6,18},{7,27},{8,24},{9,... | collective-permute-start | bytes 393224 | tf_op jit(solution)/shard_map/ppermute | solution.py:551
  13.6 15.5 %collective-permute-start.4 = (bf16[256,256]{1,0:T(8,128)(2,1)S(1)}, bf16[256,256]{1,0:T(8,128)(2,1)S(1)}, u32[]{:S(2)}, u32[]{:S(2)}) collective-permute-start(bf16[256,256]{1,0:T(8,128)(2,1)S(1)} %collective-permute-done.2.refs_0_), channel_id=1, source_target_pairs={{0,2},{1,3},{2,0},{3,1},{4,6},{5,7},{6,4},{7,5},{8,10},{9,11},{10,... | collective-permute-start | bytes 393224 | tf_op jit(solution)/shard_map/ppermute | solution.py:542
  29.2 7.1 %collective-permute-start.8 = (bf16[256,256]{1,0:T(8,128)(2,1)S(1)}, bf16[256,256]{1,0:T(8,128)(2,1)S(1)}, u32[]{:S(2)}, u32[]{:S(2)}) collective-permute-start(bf16[256,256]{1,0:T(8,128)(2,1)S(1)} %collective-permute-done.5.refs_4_), channel_id=1, source_target_pairs={{0,2},{1,3},{2,0},{3,1},{4,6},{5,7},{6,4},{7,5},{8,10},{9,11},{10,... | collective-permute-start | bytes 393224 | tf_op jit(solution)/shard_map/ppermute | solution.py:542
  29.3 7.2 %collective-permute-start.3 = (bf16[256,256]{1,0:T(8,128)(2,1)S(1)}, bf16[256,256]{1,0:T(8,128)(2,1)S(1)}, u32[]{:S(2)}, u32[]{:S(2)}) collective-permute-start(bf16[256,256]{1,0:T(8,128)(2,1)S(1)} %collective-permute-done.2.refs_0_), channel_id=1, source_target_pairs={{0,1},{1,0},{2,3},{3,2},{4,5},{5,4},{6,7},{7,6},{8,9},{9,8},{10,11... | collective-permute-start | bytes 393224 | tf_op jit(solution)/shard_map/ppermute | solution.py:542
  30.5 5.9 %collective-permute-start.7 = (bf16[256,256]{1,0:T(8,128)(2,1)S(1)}, bf16[256,256]{1,0:T(8,128)(2,1)S(1)}, u32[]{:S(2)}, u32[]{:S(2)}) collective-permute-start(bf16[256,256]{1,0:T(8,128)(2,1)S(1)} %collective-permute-done.4.refs_2_), channel_id=1, source_target_pairs={{0,1},{1,0},{2,3},{3,2},{4,5},{5,4},{6,7},{7,6},{8,9},{9,8},{10,11... | collective-permute-start | bytes 393224 | tf_op jit(solution)/shard_map/ppermute | solution.py:542
  39.6 1.6 %collective-permute-start.10 = (bf16[512,256]{1,0:T(8,128)(2,1)S(1)}, bf16[512,256]{1,0:T(8,128)(2,1)S(1)}, u32[]{:S(2)}, u32[]{:S(2)}) collective-permute-start(bf16[512,256]{1,0:T(8,128)(2,1)S(1)} %get-tuple-element.48), channel_id=1, source_target_pairs={{0,1},{1,0},{2,3},{3,2},{4,5},{5,4},{6,7},{7,6},{8,9},{9,8},{10,11... | collective-permute-start | bytes 786440 | tf_op jit(solution)/shard_map/ppermute | solution.py:542
  41.3 8.5 %collective-permute-start.12 = (bf16[512,256]{1,0:T(8,128)(2,1)S(1)}, bf16[512,256]{1,0:T(8,128)(2,1)S(1)}, u32[]{:S(2)}, u32[]{:S(2)}) collective-permute-start(bf16[512,256]{1,0:T(8,128)(2,1)S(1)} %add_convert_fusion), channel_id=1, source_target_pairs={{0,2},{1,3},{2,0},{3,1},{4,6},{5,7},{6,4},{7,5},{8,10},{9,11},{10,... | collective-permute-start | bytes 786440 | tf_op jit(solution)/shard_map/ppermute | solution.py:542
  43.7 6.1 %collective-permute-start.11 = (bf16[512,256]{1,0:T(8,128)(2,1)S(1)}, bf16[512,256]{1,0:T(8,128)(2,1)S(1)}, u32[]{:S(2)}, u32[]{:S(2)}) collective-permute-start(bf16[512,256]{1,0:T(8,128)(2,1)S(1)} %get-tuple-element.51), channel_id=1, source_target_pairs={{0,1},{1,0},{2,3},{3,2},{4,5},{5,4},{6,7},{7,6},{8,9},{9,8},{10,11... | collective-permute-start | bytes 786440 | tf_op jit(solution)/shard_map/ppermute | solution.py:542
  43.8 5.1 %collective-permute-start.15 = (s32[128]{0:T(128)S(1)}, s32[128]{0:T(128)S(1)}, u32[]{:S(2)}, u32[]{:S(2)}) collective-permute-start(s32[128]{0:T(128)S(1)} %get-tuple-element.53.refs_0_), channel_id=1, source_target_pairs={{0,3},{1,2},{2,1},{3,0},{4,7},{5,6},{6,5},{7,4},{8,11},{9,10},{10,... | collective-permute-start | bytes 1544 | tf_op jit(solution)/shard_map/ppermute | solution.py:542
  45.4 4.4 %collective-permute-start.14 = (s32[128]{0:T(128)S(1)}, s32[128]{0:T(128)S(1)}, u32[]{:S(2)}, u32[]{:S(2)}) collective-permute-start(s32[128]{0:T(128)S(1)} %get-tuple-element.53.refs_0_), channel_id=1, source_target_pairs={{0,2},{1,3},{2,0},{3,1},{4,6},{5,7},{6,4},{7,5},{8,10},{9,11},{10,... | collective-permute-start | bytes 1544 | tf_op jit(solution)/shard_map/ppermute | solution.py:542
  46.0 3.8 %collective-permute-start.13 = (s32[128]{0:T(128)S(1)}, s32[128]{0:T(128)S(1)}, u32[]{:S(2)}, u32[]{:S(2)}) collective-permute-start(s32[128]{0:T(128)S(1)} %get-tuple-element.53.refs_0_), channel_id=1, source_target_pairs={{0,1},{1,0},{2,3},{3,2},{4,5},{5,4},{6,7},{7,6},{8,9},{9,8},{10,11... | collective-permute-start | bytes 1544 | tf_op jit(solution)/shard_map/ppermute | solution.py:542
  50.9 1.6 %collective-permute-start.17 = (bf16[320,512]{1,0:T(8,128)(2,1)S(1)}, bf16[320,512]{1,0:T(8,128)(2,1)S(1)}, u32[]{:S(2)}, u32[]{:S(2)}) collective-permute-start(bf16[320,512]{1,0:T(8,128)(2,1)S(1)} %get-tuple-element.57), channel_id=1, source_target_pairs={{0,1},{1,0},{2,3},{3,2},{4,5},{5,4},{6,7},{7,6},{8,9},{9,8},{10,11... | collective-permute-start | bytes 983048 | tf_op jit(solution)/shard_map/ppermute | solution.py:542
  50.9 9.5 %collective-permute-start.16 = (bf16[256,512]{1,0:T(8,128)(2,1)S(1)}, bf16[256,512]{1,0:T(8,128)(2,1)S(1)}, u32[]{:S(2)}, u32[]{:S(2)}) collective-permute-start(bf16[256,512]{1,0:T(8,128)(2,1)S(1)} %get-tuple-element.56.even_ref), channel_id=1, source_target_pairs={{0,2},{1,3},{2,0},{3,1},{4,6},{5,7},{6,4},{7,5},{8,10},{9,11},{10,... | collective-permute-start | bytes 786440 | tf_op jit(solution)/shard_map/ppermute | solution.py:542
  54.8 5.6 %collective-permute-start.18 = (f32[128,256]{1,0:T(8,128)S(1)}, f32[128,256]{1,0:T(8,128)S(1)}, u32[]{:S(2)}, u32[]{:S(2)}) collective-permute-start(f32[128,256]{1,0:T(8,128)S(1)} %get-tuple-element.60), channel_id=1, source_target_pairs={{0,4},{4,0},{8,12},{12,8},{16,20},{20,16},{24,28},{28,24},{1,5},{5... | collective-permute-start | bytes 393224 | tf_op jit(solution)/shard_map/ppermute | solution.py:545
  60.5 4.5 %collective-permute-start.20 = (f32[64,256]{1,0:T(8,128)S(1)}, f32[64,256]{1,0:T(8,128)S(1)}, u32[]{:S(2)}, u32[]{:S(2)}) collective-permute-start(f32[64,256]{1,0:T(8,128)S(1)} %slice.8), channel_id=1, source_target_pairs={{0,2},{1,3},{2,0},{3,1},{4,6},{5,7},{6,4},{7,5},{8,10},{9,11},{10,... | collective-permute-start | bytes 196616 | tf_op jit(solution)/shard_map/ppermute | solution.py:542
  65.0 4.6 %collective-permute-start.21 = (bf16[128,1024]{1,0:T(8,128)(2,1)S(1)}, bf16[128,1024]{1,0:T(8,128)(2,1)S(1)}, u32[]{:S(2)}, u32[]{:S(2)}) collective-permute-start(bf16[128,1024]{1,0:T(8,128)(2,1)S(1)} %get-tuple-element.63), channel_id=1, source_target_pairs={{0,1},{1,0},{2,3},{3,2},{4,5},{5,4},{6,7},{7,6},{8,9},{9,8},{10,11... | collective-permute-start | bytes 786440 | tf_op jit(solution)/shard_map/ppermute | solution.py:542
  65.1 4.6 %collective-permute-start.22 = (f32[64,256]{1,0:T(8,128)S(1)}, f32[64,256]{1,0:T(8,128)S(1)}, u32[]{:S(2)}, u32[]{:S(2)}) collective-permute-start(f32[64,256]{1,0:T(8,128)S(1)} %slice_add_fusion), channel_id=1, source_target_pairs={{0,8},{4,12},{8,0},{12,4},{16,24},{20,28},{24,16},{28,20},{1,9},{5... | collective-permute-start | bytes 196616 | tf_op jit(solution)/shard_map/ppermute | solution.py:545
  71.2 8.4 %collective-permute-start.24 = (bf16[64,2048]{1,0:T(8,128)(2,1)S(1)}, bf16[64,2048]{1,0:T(8,128)(2,1)S(1)}, u32[]{:S(2)}, u32[]{:S(2)}) collective-permute-start(bf16[64,2048]{1,0:T(8,128)(2,1)S(1)} %across_sum.1), channel_id=1, source_target_pairs={{0,2},{1,3},{2,0},{3,1},{4,6},{5,7},{6,4},{7,5},{8,10},{9,11},{10,... | collective-permute-start | bytes 786440 | tf_op jit(solution)/shard_map/ppermute | solution.py:542
  71.8 6.1 %collective-permute-start.25 = (f32[64,256]{1,0:T(8,128)S(1)}, f32[64,256]{1,0:T(8,128)S(1)}, u32[]{:S(2)}, u32[]{:S(2)}) collective-permute-start(f32[64,256]{1,0:T(8,128)S(1)} %add.18), channel_id=1, source_target_pairs={{0,16},{4,20},{8,24},{12,28},{16,0},{20,4},{24,8},{28,12},{1,17},{... | collective-permute-start | bytes 196616 | tf_op jit(solution)/shard_map/ppermute | solution.py:545
  91.6 1.9 %collective-permute-start.26 = (bf16[96,512]{1,0:T(8,128)(2,1)S(1)}, bf16[96,512]{1,0:T(8,128)(2,1)S(1)}, u32[]{:S(2)}, u32[]{:S(2)}) collective-permute-start(bf16[96,512]{1,0:T(8,128)(2,1)S(1)} %get-tuple-element.72), channel_id=1, source_target_pairs={{0,1},{1,0},{2,3},{3,2},{4,5},{5,4},{6,7},{7,6},{8,9},{9,8},{10,11... | collective-permute-start | bytes 294920 | tf_op jit(solution)/shard_map/ppermute | solution.py:542
  91.7 5.7 %collective-permute-start.27 = (bf16[96,512]{1,0:T(8,128)(2,1)S(1)}, bf16[96,512]{1,0:T(8,128)(2,1)S(1)}, u32[]{:S(2)}, u32[]{:S(2)}) collective-permute-start(bf16[96,512]{1,0:T(8,128)(2,1)S(1)} %get-tuple-element.73), channel_id=1, source_target_pairs={{0,2},{1,3},{2,0},{3,1},{4,6},{5,7},{6,4},{7,5},{8,10},{9,11},{10,... | collective-permute-start | bytes 294920 | tf_op jit(solution)/shard_map/ppermute | solution.py:542
  92.3 6.3 %collective-permute-start.28 = (bf16[96,512]{1,0:T(8,128)(2,1)S(1)}, bf16[96,512]{1,0:T(8,128)(2,1)S(1)}, u32[]{:S(2)}, u32[]{:S(2)}) collective-permute-start(bf16[96,512]{1,0:T(8,128)(2,1)S(1)} %get-tuple-element.74), channel_id=1, source_target_pairs={{0,3},{1,2},{2,1},{3,0},{4,7},{5,6},{6,5},{7,4},{8,11},{9,10},{10,... | collective-permute-start | bytes 294920 | tf_op jit(solution)/shard_map/ppermute | solution.py:542
  (10 other events, 78.1 us)

commit v11 on v10

--- a/solution.py
+++ b/solution.py
@@ -10,7 +10,6 @@
 BF16 = jnp.bfloat16
 F32 = jnp.float32
 COL_CHUNK = 16
-LIST_STEP = 4
 ROW_TILE = 256
 COL_TILE = 512
 WHOLE = pl.BlockSpec(memory_space=pltpu.VMEM)
@@ -44,129 +43,89 @@
     return ((low & 1) << 1) | (low >> 1)
 
 
-class Table:
-    def __init__(self, slots, cells):
-        self.groups = cells // COL_CHUNK
-        self.spare = cells
-        self.first = 0
-        self.second = cells + 1
-        self.older = 2 * (cells + 1)
-        self.wide_at = self.older + slots + 1
-        self.wide_cell = self.wide_at + self.groups
-        self.wide_next = self.wide_cell + slots
-        self.size = -(-(self.wide_next + slots) // 128) * 128
-
-
-def lists_body(rows_ref, fetch_ref, count_ref, out_ref, *, slots, n_rep, n_hi, per_list, quarter):
+def lists_body(slots_ref, count_ref, out_ref, *, n_rep, n_hi, per_list, quarter):
     r, q = lax.axis_index("row"), lax.axis_index("rep")
     all_cols = n_rep * n_hi * per_list
-    chunks = all_cols // COL_CHUNK
-    deep = n_hi // 2
-    t = Table(slots, n_rep * quarter * all_cols)
-
-    @pl.loop(0, t.older, unroll=16)
-    def _(at):
-        out_ref[at] = slots
-
-    @pl.loop(0, t.groups, unroll=16)
-    def _(at):
-        out_ref[t.wide_at + at] = -1
-
-    out_ref[t.older + slots] = slots
-
-    live = count_ref[0]
-
-    def place(slot):
-        row_high, row_low = div_rem(rows_ref[slot], quarter)
-        source, c = div_rem(fetch_ref[slot], per_list)
-        hi, low = div_rem(source ^ r, n_rep)
-        half, hi = div_rem(hi, deep)
-        row = (n_rep - 1 - (row_high ^ q)) * quarter + row_low
-        col = ((half * n_rep + (turned(low) ^ q)) * deep + hi) * per_list + c
-        cell = jnp.where(slot < live, row * all_cols + col, t.spare)
-        return cell, t.wide_at + row * chunks + div_rem(col, COL_CHUNK)[0]
-
-    def link(slot, cell, at, wide):
-        one, two, begin = out_ref[t.first + cell], out_ref[t.second + cell], out_ref[at]
-        out_ref[t.first + cell] = slot
-        out_ref[t.second + cell] = one
-        out_ref[t.older + slot] = one
-        full = (two != slots) & (slot < live)
-        out_ref[t.wide_cell + wide] = cell
-        out_ref[t.wide_next + wide] = begin
-        out_ref[at] = jnp.where(full, wide, begin)
-        return wide + full.astype(jnp.int32)
-
-    def link_group(group, wide):
-        begin = group * LIST_STEP
-        places = [(begin + i, *place(begin + i)) for i in range(LIST_STEP)]
-        for slot, cell, at in places:
-            wide = link(slot, cell, at, wide)
-        return wide
-
-    lax.fori_loop(0, lax.div(live + LIST_STEP - 1, LIST_STEP), link_group, jnp.int32(0))
+    cells = n_rep * quarter * all_cols
+    slots = slots_ref.shape[1]
+    row_high, row_low = div_rem(slots_ref[0:1, :], quarter)
+    source, c = div_rem(slots_ref[1:2, :], per_list)
+    hi, low = div_rem(source ^ r, n_rep)
+    half, hi = div_rem(hi, n_hi // 2)
+    row = (n_rep - 1 - (row_high ^ q)) * quarter + row_low
+    col = ((half * n_rep + (turned(low) ^ q)) * (n_hi // 2) + hi) * per_list + c
+    across = lax.broadcasted_iota(jnp.int32, (1, slots), 1)
+    cell = jnp.where(across < count_ref[0], row * all_cols + col, cells)
+    down = lax.broadcasted_iota(jnp.int32, (slots, slots), 0)
+    side = lax.broadcasted_iota(jnp.int32, (slots, slots), 1)
+    cell_down = jnp.sum(jnp.where(down == side, jnp.broadcast_to(cell, (slots, slots)), 0), axis=1, keepdims=True)
+    before = jnp.where((cell_down == cell) & (down < side), down, -1)
+    out_ref[4:5, :slots] = jnp.max(before, axis=0, keepdims=True)
+    width = 256
+    for begin in range(0, cells, width):
+        here = lax.broadcasted_iota(jnp.int32, (slots, width), 1) + begin
+        slot = lax.broadcasted_iota(jnp.int32, (slots, width), 0)
+        slot = jnp.where(cell_down == here, slot, -1)
+        for depth in range(4):
+            last = jnp.max(slot, axis=0, keepdims=True)
+            out_ref[depth : depth + 1, begin : begin + width] = last
+            slot = jnp.where(slot < last, slot, -1)
 
 
 def slot_lists(block_rows, block_fetch, block_count, n_row, n_rep, per_list, row_blocks):
-    slots = block_rows.shape[0]
+    cells = row_blocks * n_row * per_list
     body = functools.partial(
-        lists_body,
-        slots=slots,
-        n_rep=n_rep,
-        n_hi=n_row // n_rep,
-        per_list=per_list,
-        quarter=row_blocks // n_rep,
+        lists_body, n_rep=n_rep, n_hi=n_row // n_rep, per_list=per_list, quarter=row_blocks // n_rep
     )
     return pl.pallas_call(
         body,
-        out_shape=shape((Table(slots, row_blocks * n_row * per_list).size,), jnp.int32),
-        in_specs=[SMEM] * 3,
-        out_specs=SMEM,
-        compiler_params=pltpu.CompilerParams(vmem_limit_bytes=56 << 20),
-        cost_estimate=pl.CostEstimate(flops=3 << 30, bytes_accessed=8 * slots, transcendentals=0),
+        out_shape=shape((8, cells), jnp.int32),
+        in_specs=[WHOLE, SMEM],
+        out_specs=WHOLE,
+        compiler_params=params(8 << 20),
+        cost_estimate=pl.CostEstimate(flops=3 << 30, bytes_accessed=32 * cells, transcendentals=0),
         name="slot_lists",
-    )(block_rows, block_fetch, block_count)
-
-
-def densify_body(table_ref, held, out_ref, *, all_cols, row_blocks):
+    )(jnp.stack([block_rows, block_fetch]), block_count)
+
+
+def densify_body(table_ref, held, out_ref, *, all_cols):
     chunk, row_cell = pl.program_id(0), pl.program_id(1)
-    slots, blk = held.shape[0], held.shape[1]
-    t = Table(slots, row_blocks * all_cols)
+    blk = held.shape[1]
+    base = row_cell * all_cols + chunk * COL_CHUNK
     zero = jnp.zeros((blk, blk), BF16)
 
     def block(slot):
-        return jnp.where(slot < slots, held[jnp.minimum(slot, slots - 1)], zero)
-
+        return jnp.where(slot >= 0, held[jnp.maximum(slot, 0)], zero)
+
+    widest = jnp.int32(-1)
     for col in range(COL_CHUNK):
-        cell = row_cell * all_cols + chunk * COL_CHUNK + col
-        total = block(table_ref[t.first + cell]) + block(table_ref[t.second + cell])
-        out_ref[:, col * blk : (col + 1) * blk] = total
-
-    def redo(wide):
-        cell = table_ref[t.wide_cell + wide]
-        two = table_ref[t.second + cell]
-        three = table_ref[t.older + two]
-        four = table_ref[t.older + three]
-        total = held[table_ref[t.first + cell]].astype(F32) + held[two].astype(F32)
-        total = total + (held[three].astype(F32) + block(four).astype(F32))
-        col = cell - row_cell * all_cols - chunk * COL_CHUNK
-        place = (slice(None), pl.ds(pl.multiple_of(col * blk, blk), blk))
-        out_ref[place] = total.astype(BF16)
-        five = table_ref[t.older + four]
-
-        @pl.when(five < slots)
-        def _():
-            def more(carry):
-                slot, total = carry
-                return table_ref[t.older + slot], total + held[slot].astype(F32)
-
-            _, rest = lax.while_loop(lambda carry: carry[0] < slots, more, (five, total))
-            out_ref[place] = rest.astype(BF16)
-
-        return table_ref[t.wide_next + wide]
-
-    begin = table_ref[t.wide_at + row_cell * (all_cols // COL_CHUNK) + chunk]
-    lax.while_loop(lambda wide: wide >= 0, redo, begin)
+        cell = base + col
+        out_ref[:, col * blk : (col + 1) * blk] = block(table_ref[0, cell]) + block(table_ref[1, cell])
+        widest = jnp.maximum(widest, table_ref[2, cell])
+
+    @pl.when(widest >= 0)
+    def _():
+        @pl.loop(0, COL_CHUNK)
+        def _(col):
+            cell = base + col
+            one, two, three, four = (table_ref[depth, cell] for depth in range(4))
+
+            @pl.when(three >= 0)
+            def _():
+                total = held[one].astype(F32) + held[two].astype(F32)
+                total = total + (held[three].astype(F32) + block(four).astype(F32))
+                place = (slice(None), pl.ds(pl.multiple_of(col * blk, blk), blk))
+                out_ref[place] = total.astype(BF16)
+                five = jnp.where(four >= 0, table_ref[4, jnp.maximum(four, 0)], -1)
+
+                @pl.when(five >= 0)
+                def _():
+                    def more(carry):
+                        slot, total = carry
+                        return table_ref[4, slot], total + held[slot].astype(F32)
+
+                    _, rest = lax.while_loop(lambda carry: carry[0] >= 0, more, (five, total))
+                    out_ref[place] = rest.astype(BF16)
 
 
 def densify(table, blocks, n_row, per_list, row_blocks):
@@ -174,7 +133,7 @@
     all_cols = n_row * per_list
     width = COL_CHUNK * blk
     return pl.pallas_call(
-        functools.partial(densify_body, all_cols=all_cols, row_blocks=row_blocks),
+        functools.partial(densify_body, all_cols=all_cols),
         out_shape=shape((row_blocks * blk, all_cols * blk), BF16),
         grid_spec=pltpu.PrefetchScalarGridSpec(
             num_scalar_prefetch=1,
@@ -426,9 +385,11 @@
     )(keep_low, near_low, keep_high, near_high)
 
 
-def split_body(low_ref, low_near, high_ref, high_near, far_ref, out_ref, *, n_rep, deep):
+def split_body(low_ref, low_near, high_ref, high_near, far_ref, w_ref, out_ref, *, n_rep, deep):
     r, q = lax.axis_index("row"), lax.axis_index("rep")
-    _, part, width = out_ref.shape
+    part, width = far_ref.shape[0], out_ref.shape[2]
+    depth = w_ref.shape[0] // 2
+    w = w_ref[pl.ds(pl.multiple_of((r & 1) * depth, depth), depth), :].astype(BF16)
     per_half = n_rep * deep
     for half, (own, near) in enumerate(((low_ref, low_near), (high_ref, high_near))):
         for i in range(per_half):
@@ -437,26 +398,27 @@
             cols = pl.ds(pl.multiple_of((j * deep + hi) * width, width), width)
             far_cols = pl.ds(pl.multiple_of((half * per_half + (j ^ 2) * deep + hi) * width, width), width)
             total = own[part:, cols] + near[part:, cols].astype(F32) + far_ref[:, far_cols].astype(F32)
-            out_ref[r ^ (half * per_half + i)] = total.astype(BF16)
-
-
-def split(keep_low, near_low, keep_high, near_high, far, n_row, n_rep):
+            out_ref[r ^ (half * per_half + i), :part] = total.astype(BF16)
+            out_ref[r ^ (half * per_half + i), part:] = w
+
+
+def split(keep_low, near_low, keep_high, near_high, far, w, n_row, n_rep):
     part, cols = far.shape
     return pl.pallas_call(
         functools.partial(split_body, n_rep=n_rep, deep=n_row // n_rep // 2),
-        out_shape=shape((n_row, part, cols // n_row), BF16),
-        in_specs=[WHOLE] * 5,
+        out_shape=shape((n_row, part + w.shape[0] // 2, cols // n_row), BF16),
+        in_specs=[WHOLE] * 6,
         out_specs=WHOLE,
         compiler_params=params(cols * part * 20),
         cost_estimate=pl.CostEstimate(flops=2 * part * cols, bytes_accessed=part * cols * 10, transcendentals=0),
         name="split",
-    )(keep_low, near_low, keep_high, near_high, far)
+    )(keep_low, near_low, keep_high, near_high, far, w)
 
 
 def collect_body(*refs, n_row, n_rep, per_list, quarter, blk):
     lists = refs[:n_rep]
-    messages, w_ref = refs[n_rep : n_rep + 2]
-    outs, acc_ref = refs[n_rep + 2 : -1], refs[-1]
+    messages = refs[n_rep]
+    outs, w_out, acc_ref = refs[n_rep + 1 : -2], refs[-2], refs[-1]
     r, q = lax.axis_index("row"), lax.axis_index("rep")
     acc_ref[...] = jnp.zeros(acc_ref.shape, F32)
     for k in range(n_row):
@@ -468,18 +430,24 @@
                 b = jnp.where(j == other, lists[other][at], b)
             cell = (lax.div(b, quarter) ^ q) * quarter + lax.rem(b, quarter)
             cols = pl.ds(pl.multiple_of(cell * blk, blk), blk)
-            acc_ref[:, cols] += messages[r ^ k, :, c * blk : (c + 1) * blk].astype(F32)
+            acc_ref[:, cols] += messages[r ^ k, : acc_ref.shape[0], c * blk : (c + 1) * blk].astype(F32)
     width = outs[0].shape[1]
-    part = acc_ref.shape[0]
+    part, depth = acc_ref.shape[0], w_out.shape[0] // 2
+    for parity in range(2):
+        total = messages[parity, part:].astype(F32)
+        for other in range(parity + 2, n_row, 2):
+            total += messages[other, part:].astype(F32)
+        w_out[parity * depth : (parity + 1) * depth] = total.astype(BF16)
     for j, out in enumerate(outs):
         out[:part] = acc_ref[:, j * width : (j + 1) * width].astype(out.dtype)
         if j:
-            fold_in(out, part, 0, w_ref[...])
-
-
-def collect(lists, messages, w, per_list, row_blocks, blk):
+            fold_in(out, part, 0, w_out[...])
+
+
+def collect(lists, messages, part, per_list, row_blocks, blk):
     n_rep = len(lists)
-    n_row, part, _ = messages.shape
+    n_row, rows, features = messages.shape
+    depth = 2 * (rows - part)
     quarter = row_blocks // n_rep
     body = functools.partial(
         collect_body, n_row=n_row, n_rep=n_rep, per_list=per_list, quarter=quarter, blk=blk
@@ -487,16 +455,17 @@
     return pl.pallas_call(
         body,
         out_shape=[shape((part, quarter * blk), F32)]
-        + [shape((part + w.size // (quarter * blk), quarter * blk), BF16)] * (n_rep - 1),
-        in_specs=[SMEM] * n_rep + [WHOLE] * 2,
-        out_specs=[WHOLE] * n_rep,
+        + [shape((part + depth * features // (quarter * blk), quarter * blk), BF16)] * (n_rep - 1)
+        + [shape((depth, features), BF16)],
+        in_specs=[SMEM] * n_rep + [WHOLE],
+        out_specs=[WHOLE] * (n_rep + 1),
         scratch_shapes=[pltpu.VMEM((part, row_blocks * blk), F32)],
         compiler_params=params(4 << 20),
         cost_estimate=pl.CostEstimate(
             flops=part * row_blocks * blk, bytes_accessed=part * row_blocks * blk * 5, transcendentals=0
         ),
         name="collect",
-    )(*lists, messages, w)
+    )(*lists, messages)
 
 
 def finish_body(*refs, n_rep):
@@ -581,29 +550,21 @@
 
     grad2 = to_rep(grad0, 2)
     first, w = back_first(to_rep(to_near, 1), grad0, adj, wkeep)
-    w = w + to_row(w, 1)
-    grad2 = after(grad2, first, w)
+    part = features // n_rep
+    grad2 = after(grad2, first)
     grad3 = to_rep(grad2, 1)
-    part = features // n_rep
-    got = to_rep(w[part:], 2)
+    got = to_rep(after(w, grad2)[part:], 2)
     send_high, keep_high = back_second(grad3, grad2, adj, first, 1, n_rep, deep)
-    send_high = after(send_high, got)
-    w = w[:part] + got
-    got = to_row(w, 2)
     near_high = to_rep(send_high, 1)
     send_low, keep_low = back_second(grad3, grad2, adj, after(first, send_high), 0, n_rep, deep)
     near_low = to_rep(after(send_low, near_high, got), 1)
     across = across_sum(keep_low, near_low, keep_high, near_high)
     far = to_rep(across, 2)
-    w = after(w, across) + got
-    step = 4
-    while step < n_row:
-        w = w + to_row(w, step)
-        step *= 2
-    messages = split(keep_low, near_low, keep_high, near_high, after(far, w), n_row, n_rep)
+    w = after(w[:part], across) + got
+    w = w + to_row(w, 1)
+    messages = split(keep_low, near_low, keep_high, near_high, far, w, n_row, n_rep)
     returned = lax.all_to_all(messages, "row", split_axis=0, concat_axis=0, tiled=True)
-    w = w.astype(BF16)
-    grads = collect(lists, returned, w, per_list, row_blocks, blk)
+    *grads, w = collect(lists, returned, part, per_list, row_blocks, blk)
     node_grad, weight_grad = finish([grads[0]] + [to_rep(grads[j], j) for j in range(1, n_rep)], w)
     return (output, weight_grad, node_grad)
 

time: 99.4 us -> 101 us (1.016)
  starting transfers between devices: 26.9 us -> 34.9 us
  waiting for transfers between devices: 33.4 us -> 27.2 us
  Pallas kernels: 25.1 us -> 20.5 us
  blocking collectives: 11.1 us -> 15.1 us
    ppermute x3 -> x1, waiting for transfers between devices: 13.8 us -> 2.31 us  [to_row(): return lax.ppermute(x, 'row', xor_perm(n_row, k))]
    ppermute x22, starting transfers between devices: 17.9 us -> 24.5 us  [to_rep(): return lax.ppermute(x, 'rep', xor_perm(n_rep, j))]
    ppermute x22, waiting for transfers between devices: 18.6 us -> 23.9 us  [to_rep(): return lax.ppermute(x, 'rep', xor_perm(n_rep, j))]
    pallas_call x2, Pallas kernels: 10.2 us -> 5.57 us  [the longest x1 5.29 us: densify(): pl.pallas_call(functools.partial(densify_body, all_cols=all_cols), out_sh...]
    all_to_all x1, blocking collectives: 11.1 us -> 15.1 us  [local(): lax.all_to_all(messages, 'row', split_axis=0, concat_axis=0, tiled=True)]
    ppermute x3 -> x1, starting transfers between devices: 0.63 us -> 2.02 us  [to_row(): return lax.ppermute(x, 'row', xor_perm(n_row, k))]
  transfers between devices with their start and end apart: 29 -> 27, of which waited for: 16 -> 14; matrix products, arithmetic and copies ran while one was open for 0% -> 1% of each run, Pallas kernels for 18% -> 11%
where the time goes in v11:
time: 101 us
  starting transfers between devices  34.9 us (35%)
  waiting for transfers between devices  27.2 us (27%)
  Pallas kernels  20.5 us (20%)
  blocking collectives  15.1 us (15%)
  between operations  1.49 us (1%)
    ppermute x22, starting transfers between devices, to_rep(): return lax.ppermute(x, 'rep', xor_perm(n_rep, j))  24.5 us
    ppermute x22, waiting for transfers between devices, to_rep(): return lax.ppermute(x, 'rep', xor_perm(n_rep, j))  23.9 us
    all_to_all x1, blocking collectives, local(): lax.all_to_all(messages, 'row', split_axis=0, concat_axis=0, tiled=True)  15.1 us
    ppermute x4, starting transfers between devices, spread(): return lax.ppermute(x, ('row', 'rep'), perm)  8.34 us
    pallas_call x1, Pallas kernels, densify(): pl.pallas_call(functools.partial(densify_body, all_cols=all_cols), out_sh...  5.29 us
    pallas_call x2, Pallas kernels, back_second(): pl.pallas_call(back_second_body, grid=(tiles,), out_shape=[shape((feature...  3.67 us
    pallas_call x2, Pallas kernels, forward(): pl.pallas_call(functools.partial(forward_body, n_rep=len(pieces) // 2), g...  3.67 us
    ppermute x1, waiting for transfers between devices, to_row(): return lax.ppermute(x, 'row', xor_perm(n_row, k))  2.31 us
  transfers between devices with their start and end apart: 27, of which 14 were waited for; matrix products, arithmetic and copies ran while one was open for 1% of the time, Pallas kernels for 11%

profile of v11, /device:TPU:0, one launch (start us, length us, event | category | flops | bytes accessed | tf_op | source)
XLA Modules:
  0.0 100.7 jit_solution(2278617003024442573)
XLA Ops:
  1.4 4.0 %collective-permute-start.1 = (s32[1,8,2]{2,1,0:T(8,128)S(1)}, s32[1,8,2]{2,1,0:T(8,128)S(1)}, u32[]{:S(2)}, u32[]{:S(2)}) collective-permute-start(s32[1,8,2]{2,1,0:T(8,128)S(1)} %copy.11), channel_id=1, source_target_pairs={{0,16},{1,25},{2,22},{3,31},{4,20},{5,29},{6,18},{7,27},{8,24},{9,... | collective-permute-start | bytes 200 | tf_op jit(solution)/shard_map/ppermute | solution.py:520
  7.0 2.2 %pack.1 = (bf16[256,256]{1,0:T(8,128)(2,1)S(1)}, bf16[256,256]{1,0:T(8,128)(2,1)S(1)}, s32[128]{0:T(128)S(1)}) custom-call(s32[1,8,2]{2,1,0:T(8,128)S(1)} %collective-permute-done.refs_0_, s32[1,8,2]{2,1,0:T(8,128)S(1)} %collective-permute-done.1.refs_1_, bf16[2048,256]{1,0:T(8,128)(2,1)} %refs_2_.1), custom_call_target="tpu_custom_call" | custom-call | tf_op jit(solution)/shard_map/pack/pallas_call | solution.py:178
  11.3 3.0 %collective-permute-start.5 = (bf16[256,256]{1,0:T(8,128)(2,1)S(1)}, bf16[256,256]{1,0:T(8,128)(2,1)S(1)}, u32[]{:S(2)}, u32[]{:S(2)}) collective-permute-start(bf16[256,256]{1,0:T(8,128)(2,1)S(1)} %get-tuple-element.41), channel_id=1, source_target_pairs={{0,16},{1,25},{2,22},{3,31},{4,20},{5,29},{6,18},{7,27},{8,24},{9,... | collective-permute-start | bytes 393224 | tf_op jit(solution)/shard_map/ppermute | solution.py:520
  14.3 9.6 %collective-permute-start.4 = (bf16[256,256]{1,0:T(8,128)(2,1)S(1)}, bf16[256,256]{1,0:T(8,128)(2,1)S(1)}, u32[]{:S(2)}, u32[]{:S(2)}) collective-permute-start(bf16[256,256]{1,0:T(8,128)(2,1)S(1)} %collective-permute-done.2.refs_0_), channel_id=1, source_target_pairs={{0,2},{1,3},{2,0},{3,1},{4,6},{5,7},{6,4},{7,5},{8,10},{9,11},{10,... | collective-permute-start | bytes 393224 | tf_op jit(solution)/shard_map/ppermute | solution.py:511
  24.2 2.6 %collective-permute-done.4.refs_2_ = bf16[256,256]{1,0:T(8,128)(2,1)S(1)} collective-permute-done((bf16[256,256]{1,0:T(8,128)(2,1)S(1)}, bf16[256,256]{1,0:T(8,128)(2,1)S(1)}, u32[]{:S(2)}, u32[]{:S(2)}) %collective-permute-start.4) | collective-permute-done | bytes 131104 | tf_op jit(solution)/shard_map/ppermute | solution.py:511
  26.8 2.7 %collective-permute-start.8 = (bf16[256,256]{1,0:T(8,128)(2,1)S(1)}, bf16[256,256]{1,0:T(8,128)(2,1)S(1)}, u32[]{:S(2)}, u32[]{:S(2)}) collective-permute-start(bf16[256,256]{1,0:T(8,128)(2,1)S(1)} %collective-permute-done.5.refs_4_), channel_id=1, source_target_pairs={{0,2},{1,3},{2,0},{3,1},{4,6},{5,7},{6,4},{7,5},{8,10},{9,11},{10,... | collective-permute-start | bytes 393224 | tf_op jit(solution)/shard_map/ppermute | solution.py:511
  30.0 5.3 %densify.1.refs_8_.adj_ref = bf16[2048,2048]{1,0:T(8,128)(2,1)S(1)} custom-call(s32[8,256]{1,0:T(8,128)S(1)} %slot_lists.1.table_ref, bf16[192,128,128]{2,1,0:T(8,128)(2,1)S(1)} %bitcast.3), custom_call_target="tpu_custom_call" | custom-call | flops 3145728 | bytes 14680064 | tf_op jit(solution)/shard_map/densify/pallas_call | solution.py:135
  36.7 1.8 %forward.2 = (bf16[512,256]{1,0:T(8,128)(2,1)S(1)}, f32[512,256]{1,0:T(8,128)S(1)}) custom-call(bf16[256,256]{1,0:T(8,128)(2,1)S(1)} %collective-permute-done.2.refs_0_, bf16[256,256]{1,0:T(8,128)(2,1)S(1)} %collective-permute-done.3.refs_1_, bf16[256,256]{1,0:T(8,128)(2,1)S(1)} %collective-permute-done.4.refs_2_, ...), custom_call_target="tpu_custom_call" | custom-call | flops 1073741824 | bytes 5242880 | tf_op jit(solution)/shard_map/forward/pallas_call | solution.py:214
  40.3 1.7 %collective-permute-start.12 = (bf16[512,256]{1,0:T(8,128)(2,1)S(1)}, bf16[512,256]{1,0:T(8,128)(2,1)S(1)}, u32[]{:S(2)}, u32[]{:S(2)}) collective-permute-start(bf16[512,256]{1,0:T(8,128)(2,1)S(1)} %add_convert_fusion), channel_id=1, source_target_pairs={{0,2},{1,3},{2,0},{3,1},{4,6},{5,7},{6,4},{7,5},{8,10},{9,11},{10,... | collective-permute-start | bytes 786440 | tf_op jit(solution)/shard_map/ppermute | solution.py:511
  42.0 1.8 %forward.3 = (bf16[512,256]{1,0:T(8,128)(2,1)S(1)}, f32[512,256]{1,0:T(8,128)S(1)}) custom-call(bf16[256,256]{1,0:T(8,128)(2,1)S(1)} %collective-permute-done.2.refs_0_, bf16[256,256]{1,0:T(8,128)(2,1)S(1)} %collective-permute-done.3.refs_1_, bf16[256,256]{1,0:T(8,128)(2,1)S(1)} %collective-permute-done.4.refs_2_, ...), custom_call_target="tpu_custom_call" | custom-call | flops 1073741824 | bytes 5242880 | tf_op jit(solution)/shard_map/forward/pallas_call | solution.py:214
  44.4 1.7 %collective-permute-start.14 = (s32[128]{0:T(128)S(1)}, s32[128]{0:T(128)S(1)}, u32[]{:S(2)}, u32[]{:S(2)}) collective-permute-start(s32[128]{0:T(128)S(1)} %get-tuple-element.53.refs_0_), channel_id=1, source_target_pairs={{0,2},{1,3},{2,0},{3,1},{4,6},{5,7},{6,4},{7,5},{8,10},{9,11},{10,... | collective-permute-start | bytes 1544 | tf_op jit(solution)/shard_map/ppermute | solution.py:511
  46.1 2.1 %collective-permute-done.15.refs_3_ = s32[128]{0:T(128)S(1)} collective-permute-done((s32[128]{0:T(128)S(1)}, s32[128]{0:T(128)S(1)}, u32[]{:S(2)}, u32[]{:S(2)}) %collective-permute-start.15) | collective-permute-done | bytes 544 | tf_op jit(solution)/shard_map/ppermute | solution.py:511
  50.0 1.7 %collective-permute-start.16 = (bf16[256,512]{1,0:T(8,128)(2,1)S(1)}, bf16[256,512]{1,0:T(8,128)(2,1)S(1)}, u32[]{:S(2)}, u32[]{:S(2)}) collective-permute-start(bf16[256,512]{1,0:T(8,128)(2,1)S(1)} %get-tuple-element.56.even_ref), channel_id=1, source_target_pairs={{0,2},{1,3},{2,0},{3,1},{4,6},{5,7},{6,4},{7,5},{8,10},{9,11},{10,... | collective-permute-start | bytes 786440 | tf_op jit(solution)/shard_map/ppermute | solution.py:511
  51.8 2.3 %back_first.1 = (f32[256,2048]{1,0:T(8,128)S(1)}, f32[128,256]{1,0:T(8,128)S(1)}) custom-call(bf16[320,512]{1,0:T(8,128)(2,1)S(1)} %collective-permute-done.17.odd_ref, bf16[256,512]{1,0:T(8,128)(2,1)S(1)} %get-tuple-element.56.even_ref, bf16[2048,2048]{1,0:T(8,128)(2,1)S(1)} %densify.1.refs_8_.adj_ref, f32[128,256]{1,0:T(8,128)S(1)} %get-tuple-element.58.wkeep_ref), custom_call_target="tpu_custom_call" | custom-call | flops 1073741824 | bytes 6291456 | tf_op jit(solution)/shard_map/back_first/pallas_call | solution.py:312
  54.1 4.7 %collective-permute-done.16.even_ref = bf16[256,512]{1,0:T(8,128)(2,1)S(1)} collective-permute-done((bf16[256,512]{1,0:T(8,128)(2,1)S(1)}, bf16[256,512]{1,0:T(8,128)(2,1)S(1)}, u32[]{:S(2)}, u32[]{:S(2)}) %collective-permute-start.16) | collective-permute-done | bytes 262176 | tf_op jit(solution)/shard_map/ppermute | solution.py:511
  60.3 1.8 %back_second_1.1 = (bf16[128,1024]{1,0:T(8,128)(2,1)S(1)}, f32[128,1024]{1,0:T(8,128)S(1)}) custom-call(bf16[256,512]{1,0:T(8,128)(2,1)S(1)} %collective-permute-done.18.odd_ref, bf16[256,512]{1,0:T(8,128)(2,1)S(1)} %collective-permute-done.16.even_ref, bf16[2048,2048]{1,0:T(8,128)(2,1)S(1)} %densify.1.refs_8_.adj_ref, ...), custom_call_target="tpu_custom_call" | custom-call | flops 536870912 | bytes 3932160 | tf_op jit(solution)/shard_map/back_second_1/pallas_call | solution.py:344
  62.3 1.8 %collective-permute-start.20 = (f32[64,256]{1,0:T(8,128)S(1)}, f32[64,256]{1,0:T(8,128)S(1)}, u32[]{:S(2)}, u32[]{:S(2)}) collective-permute-start(f32[64,256]{1,0:T(8,128)S(1)} %slice.6), channel_id=1, source_target_pairs={{0,2},{1,3},{2,0},{3,1},{4,6},{5,7},{6,4},{7,5},{8,10},{9,11},{10,... | collective-permute-start | bytes 196616 | tf_op jit(solution)/shard_map/ppermute | solution.py:511
  64.1 1.8 %back_second_0.1 = (bf16[128,1024]{1,0:T(8,128)(2,1)S(1)}, f32[128,1024]{1,0:T(8,128)S(1)}) custom-call(bf16[256,512]{1,0:T(8,128)(2,1)S(1)} %collective-permute-done.18.odd_ref, bf16[256,512]{1,0:T(8,128)(2,1)S(1)} %collective-permute-done.16.even_ref, bf16[2048,2048]{1,0:T(8,128)(2,1)S(1)} %densify.1.refs_8_.adj_ref, ...), custom_call_target="tpu_custom_call" | custom-call | flops 536870912 | bytes 3932160 | tf_op jit(solution)/shard_map/back_second_0/pallas_call | solution.py:344
  68.3 1.8 %collective-permute-start.22 = (bf16[64,2048]{1,0:T(8,128)(2,1)S(1)}, bf16[64,2048]{1,0:T(8,128)(2,1)S(1)}, u32[]{:S(2)}, u32[]{:S(2)}) collective-permute-start(bf16[64,2048]{1,0:T(8,128)(2,1)S(1)} %across_sum.1), channel_id=1, source_target_pairs={{0,2},{1,3},{2,0},{3,1},{4,6},{5,7},{6,4},{7,5},{8,10},{9,11},{10,... | collective-permute-start | bytes 786440 | tf_op jit(solution)/shard_map/ppermute | solution.py:511
  70.1 2.0 %collective-permute-start.23 = (f32[64,256]{1,0:T(8,128)S(1)}, f32[64,256]{1,0:T(8,128)S(1)}, u32[]{:S(2)}, u32[]{:S(2)}) collective-permute-start(f32[64,256]{1,0:T(8,128)S(1)} %add.10), channel_id=1, source_target_pairs={{0,4},{4,0},{8,12},{12,8},{16,20},{20,16},{24,28},{28,24},{1,5},{5... | collective-permute-start | bytes 196616 | tf_op jit(solution)/shard_map/ppermute | solution.py:514
  72.1 2.3 %collective-permute-done.23 = f32[64,256]{1,0:T(8,128)S(1)} collective-permute-done((f32[64,256]{1,0:T(8,128)S(1)}, f32[64,256]{1,0:T(8,128)S(1)}, u32[]{:S(2)}, u32[]{:S(2)}) %collective-permute-start.23) | collective-permute-done | bytes 65568 | tf_op jit(solution)/shard_map/ppermute | solution.py:514
  74.5 2.2 %collective-permute-done.22.far_ref = bf16[64,2048]{1,0:T(8,128)(2,1)S(1)} collective-permute-done((bf16[64,2048]{1,0:T(8,128)(2,1)S(1)}, bf16[64,2048]{1,0:T(8,128)(2,1)S(1)}, u32[]{:S(2)}, u32[]{:S(2)}) %collective-permute-start.22) | collective-permute-done | bytes 262176 | tf_op jit(solution)/shard_map/ppermute | solution.py:511
  76.9 15.1 %all_to_all.5.refs_4_ = bf16[8,96,256]{2,1,0:T(8,128)(2,1)S(1)} all-to-all(bf16[8,96,256]{2,1,0:T(8,128)(2,1)S(1)} %split.1), channel_id=1, replica_groups=mesh['row'=8,'rep'=4] {'row'}, dimensions={0} | all-to-all | bytes 786432 | tf_op jit(solution)/shard_map/all_to_all | solution.py:566
  94.6 3.8 %collective-permute-done.25.refs_2_ = bf16[96,512]{1,0:T(8,128)(2,1)S(1)} collective-permute-done((bf16[96,512]{1,0:T(8,128)(2,1)S(1)}, bf16[96,512]{1,0:T(8,128)(2,1)S(1)}, u32[]{:S(2)}, u32[]{:S(2)}) %collective-permute-start.25) | collective-permute-done | bytes 98336 | tf_op jit(solution)/shard_map/ppermute | solution.py:511
  (60 shorter events, 19.2 us)
Async XLA Ops:
  1.4 5.6 %collective-permute-start.1 = (s32[1,8,2]{2,1,0:T(8,128)S(1)}, s32[1,8,2]{2,1,0:T(8,128)S(1)}, u32[]{:S(2)}, u32[]{:S(2)}) collective-permute-start(s32[1,8,2]{2,1,0:T(8,128)S(1)} %copy.11), channel_id=1, source_target_pairs={{0,16},{1,25},{2,22},{3,31},{4,20},{5,29},{6,18},{7,27},{8,24},{9,... | collective-permute-start | bytes 200 | tf_op jit(solution)/shard_map/ppermute | solution.py:520
  5.4 1.6 %collective-permute-start = (s32[1,8,2]{2,1,0:T(8,128)S(1)}, s32[1,8,2]{2,1,0:T(8,128)S(1)}, u32[]{:S(2)}, u32[]{:S(2)}) collective-permute-start(s32[1,8,2]{2,1,0:T(8,128)S(1)} %copy.11), channel_id=1, source_target_pairs={{0,0},{1,9},{2,6},{3,15},{4,4},{5,13},{6,2},{7,11},{8,8},{9,1},{10... | collective-permute-start | bytes 200 | tf_op jit(solution)/shard_map/ppermute | solution.py:520
  9.3 5.0 %collective-permute-start.2 = (bf16[256,256]{1,0:T(8,128)(2,1)S(1)}, bf16[256,256]{1,0:T(8,128)(2,1)S(1)}, u32[]{:S(2)}, u32[]{:S(2)}) collective-permute-start(bf16[256,256]{1,0:T(8,128)(2,1)S(1)} %get-tuple-element.40), channel_id=1, source_target_pairs={{0,0},{1,9},{2,6},{3,15},{4,4},{5,13},{6,2},{7,11},{8,8},{9,1},{10... | collective-permute-start | bytes 393224 | tf_op jit(solution)/shard_map/ppermute | solution.py:520
  11.3 12.9 %collective-permute-start.5 = (bf16[256,256]{1,0:T(8,128)(2,1)S(1)}, bf16[256,256]{1,0:T(8,128)(2,1)S(1)}, u32[]{:S(2)}, u32[]{:S(2)}) collective-permute-start(bf16[256,256]{1,0:T(8,128)(2,1)S(1)} %get-tuple-element.41), channel_id=1, source_target_pairs={{0,16},{1,25},{2,22},{3,31},{4,20},{5,29},{6,18},{7,27},{8,24},{9,... | collective-permute-start | bytes 393224 | tf_op jit(solution)/shard_map/ppermute | solution.py:520
  14.3 12.5 %collective-permute-start.4 = (bf16[256,256]{1,0:T(8,128)(2,1)S(1)}, bf16[256,256]{1,0:T(8,128)(2,1)S(1)}, u32[]{:S(2)}, u32[]{:S(2)}) collective-permute-start(bf16[256,256]{1,0:T(8,128)(2,1)S(1)} %collective-permute-done.2.refs_0_), channel_id=1, source_target_pairs={{0,2},{1,3},{2,0},{3,1},{4,6},{5,7},{6,4},{7,5},{8,10},{9,11},{10,... | collective-permute-start | bytes 393224 | tf_op jit(solution)/shard_map/ppermute | solution.py:511
  26.8 2.9 %collective-permute-start.6 = (bf16[256,256]{1,0:T(8,128)(2,1)S(1)}, bf16[256,256]{1,0:T(8,128)(2,1)S(1)}, u32[]{:S(2)}, u32[]{:S(2)}) collective-permute-start(bf16[256,256]{1,0:T(8,128)(2,1)S(1)} %collective-permute-done.5.refs_4_), channel_id=1, source_target_pairs={{0,1},{1,0},{2,3},{3,2},{4,5},{5,4},{6,7},{7,6},{8,9},{9,8},{10,11... | collective-permute-start | bytes 393224 | tf_op jit(solution)/shard_map/ppermute | solution.py:511
  26.8 8.5 %collective-permute-start.8 = (bf16[256,256]{1,0:T(8,128)(2,1)S(1)}, bf16[256,256]{1,0:T(8,128)(2,1)S(1)}, u32[]{:S(2)}, u32[]{:S(2)}) collective-permute-start(bf16[256,256]{1,0:T(8,128)(2,1)S(1)} %collective-permute-done.5.refs_4_), channel_id=1, source_target_pairs={{0,2},{1,3},{2,0},{3,1},{4,6},{5,7},{6,4},{7,5},{8,10},{9,11},{10,... | collective-permute-start | bytes 393224 | tf_op jit(solution)/shard_map/ppermute | solution.py:511
  29.5 5.9 %collective-permute-start.3 = (bf16[256,256]{1,0:T(8,128)(2,1)S(1)}, bf16[256,256]{1,0:T(8,128)(2,1)S(1)}, u32[]{:S(2)}, u32[]{:S(2)}) collective-permute-start(bf16[256,256]{1,0:T(8,128)(2,1)S(1)} %collective-permute-done.2.refs_0_), channel_id=1, source_target_pairs={{0,1},{1,0},{2,3},{3,2},{4,5},{5,4},{6,7},{7,6},{8,9},{9,8},{10,11... | collective-permute-start | bytes 393224 | tf_op jit(solution)/shard_map/ppermute | solution.py:511
  29.7 5.7 %collective-permute-start.7 = (bf16[256,256]{1,0:T(8,128)(2,1)S(1)}, bf16[256,256]{1,0:T(8,128)(2,1)S(1)}, u32[]{:S(2)}, u32[]{:S(2)}) collective-permute-start(bf16[256,256]{1,0:T(8,128)(2,1)S(1)} %collective-permute-done.4.refs_2_), channel_id=1, source_target_pairs={{0,1},{1,0},{2,3},{3,2},{4,5},{5,4},{6,7},{7,6},{8,9},{9,8},{10,11... | collective-permute-start | bytes 393224 | tf_op jit(solution)/shard_map/ppermute | solution.py:511
  38.6 1.6 %collective-permute-start.10 = (bf16[512,256]{1,0:T(8,128)(2,1)S(1)}, bf16[512,256]{1,0:T(8,128)(2,1)S(1)}, u32[]{:S(2)}, u32[]{:S(2)}) collective-permute-start(bf16[512,256]{1,0:T(8,128)(2,1)S(1)} %get-tuple-element.48), channel_id=1, source_target_pairs={{0,1},{1,0},{2,3},{3,2},{4,5},{5,4},{6,7},{7,6},{8,9},{9,8},{10,11... | collective-permute-start | bytes 786440 | tf_op jit(solution)/shard_map/ppermute | solution.py:511
  40.3 8.6 %collective-permute-start.12 = (bf16[512,256]{1,0:T(8,128)(2,1)S(1)}, bf16[512,256]{1,0:T(8,128)(2,1)S(1)}, u32[]{:S(2)}, u32[]{:S(2)}) collective-permute-start(bf16[512,256]{1,0:T(8,128)(2,1)S(1)} %add_convert_fusion), channel_id=1, source_target_pairs={{0,2},{1,3},{2,0},{3,1},{4,6},{5,7},{6,4},{7,5},{8,10},{9,11},{10,... | collective-permute-start | bytes 786440 | tf_op jit(solution)/shard_map/ppermute | solution.py:511
  43.9 5.1 %collective-permute-start.11 = (bf16[512,256]{1,0:T(8,128)(2,1)S(1)}, bf16[512,256]{1,0:T(8,128)(2,1)S(1)}, u32[]{:S(2)}, u32[]{:S(2)}) collective-permute-start(bf16[512,256]{1,0:T(8,128)(2,1)S(1)} %get-tuple-element.51), channel_id=1, source_target_pairs={{0,1},{1,0},{2,3},{3,2},{4,5},{5,4},{6,7},{7,6},{8,9},{9,8},{10,11... | collective-permute-start | bytes 786440 | tf_op jit(solution)/shard_map/ppermute | solution.py:511
  44.0 4.2 %collective-permute-start.15 = (s32[128]{0:T(128)S(1)}, s32[128]{0:T(128)S(1)}, u32[]{:S(2)}, u32[]{:S(2)}) collective-permute-start(s32[128]{0:T(128)S(1)} %get-tuple-element.53.refs_0_), channel_id=1, source_target_pairs={{0,3},{1,2},{2,1},{3,0},{4,7},{5,6},{6,5},{7,4},{8,11},{9,10},{10,... | collective-permute-start | bytes 1544 | tf_op jit(solution)/shard_map/ppermute | solution.py:511
  44.4 4.5 %collective-permute-start.14 = (s32[128]{0:T(128)S(1)}, s32[128]{0:T(128)S(1)}, u32[]{:S(2)}, u32[]{:S(2)}) collective-permute-start(s32[128]{0:T(128)S(1)} %get-tuple-element.53.refs_0_), channel_id=1, source_target_pairs={{0,2},{1,3},{2,0},{3,1},{4,6},{5,7},{6,4},{7,5},{8,10},{9,11},{10,... | collective-permute-start | bytes 1544 | tf_op jit(solution)/shard_map/ppermute | solution.py:511
  46.1 2.8 %collective-permute-start.13 = (s32[128]{0:T(128)S(1)}, s32[128]{0:T(128)S(1)}, u32[]{:S(2)}, u32[]{:S(2)}) collective-permute-start(s32[128]{0:T(128)S(1)} %get-tuple-element.53.refs_0_), channel_id=1, source_target_pairs={{0,1},{1,0},{2,3},{3,2},{4,5},{5,4},{6,7},{7,6},{8,9},{9,8},{10,11... | collective-permute-start | bytes 1544 | tf_op jit(solution)/shard_map/ppermute | solution.py:511
  50.0 1.8 %collective-permute-start.17 = (bf16[320,512]{1,0:T(8,128)(2,1)S(1)}, bf16[320,512]{1,0:T(8,128)(2,1)S(1)}, u32[]{:S(2)}, u32[]{:S(2)}) collective-permute-start(bf16[320,512]{1,0:T(8,128)(2,1)S(1)} %get-tuple-element.57), channel_id=1, source_target_pairs={{0,1},{1,0},{2,3},{3,2},{4,5},{5,4},{6,7},{7,6},{8,9},{9,8},{10,11... | collective-permute-start | bytes 983048 | tf_op jit(solution)/shard_map/ppermute | solution.py:511
  50.0 8.7 %collective-permute-start.16 = (bf16[256,512]{1,0:T(8,128)(2,1)S(1)}, bf16[256,512]{1,0:T(8,128)(2,1)S(1)}, u32[]{:S(2)}, u32[]{:S(2)}) collective-permute-start(bf16[256,512]{1,0:T(8,128)(2,1)S(1)} %get-tuple-element.56.even_ref), channel_id=1, source_target_pairs={{0,2},{1,3},{2,0},{3,1},{4,6},{5,7},{6,4},{7,5},{8,10},{9,11},{10,... | collective-permute-start | bytes 786440 | tf_op jit(solution)/shard_map/ppermute | solution.py:511
  62.1 4.6 %collective-permute-start.19 = (bf16[128,1024]{1,0:T(8,128)(2,1)S(1)}, bf16[128,1024]{1,0:T(8,128)(2,1)S(1)}, u32[]{:S(2)}, u32[]{:S(2)}) collective-permute-start(bf16[128,1024]{1,0:T(8,128)(2,1)S(1)} %get-tuple-element.61), channel_id=1, source_target_pairs={{0,1},{1,0},{2,3},{3,2},{4,5},{5,4},{6,7},{7,6},{8,9},{9,8},{10,11... | collective-permute-start | bytes 786440 | tf_op jit(solution)/shard_map/ppermute | solution.py:511
  62.3 4.4 %collective-permute-start.20 = (f32[64,256]{1,0:T(8,128)S(1)}, f32[64,256]{1,0:T(8,128)S(1)}, u32[]{:S(2)}, u32[]{:S(2)}) collective-permute-start(f32[64,256]{1,0:T(8,128)S(1)} %slice.6), channel_id=1, source_target_pairs={{0,2},{1,3},{2,0},{3,1},{4,6},{5,7},{6,4},{7,5},{8,10},{9,11},{10,... | collective-permute-start | bytes 196616 | tf_op jit(solution)/shard_map/ppermute | solution.py:511
  68.3 8.4 %collective-permute-start.22 = (bf16[64,2048]{1,0:T(8,128)(2,1)S(1)}, bf16[64,2048]{1,0:T(8,128)(2,1)S(1)}, u32[]{:S(2)}, u32[]{:S(2)}) collective-permute-start(bf16[64,2048]{1,0:T(8,128)(2,1)S(1)} %across_sum.1), channel_id=1, source_target_pairs={{0,2},{1,3},{2,0},{3,1},{4,6},{5,7},{6,4},{7,5},{8,10},{9,11},{10,... | collective-permute-start | bytes 786440 | tf_op jit(solution)/shard_map/ppermute | solution.py:511
  70.1 4.3 %collective-permute-start.23 = (f32[64,256]{1,0:T(8,128)S(1)}, f32[64,256]{1,0:T(8,128)S(1)}, u32[]{:S(2)}, u32[]{:S(2)}) collective-permute-start(f32[64,256]{1,0:T(8,128)S(1)} %add.10), channel_id=1, source_target_pairs={{0,4},{4,0},{8,12},{12,8},{16,20},{20,16},{24,28},{28,24},{1,5},{5... | collective-permute-start | bytes 196616 | tf_op jit(solution)/shard_map/ppermute | solution.py:514
  92.7 1.9 %collective-permute-start.24 = (bf16[96,512]{1,0:T(8,128)(2,1)S(1)}, bf16[96,512]{1,0:T(8,128)(2,1)S(1)}, u32[]{:S(2)}, u32[]{:S(2)}) collective-permute-start(bf16[96,512]{1,0:T(8,128)(2,1)S(1)} %get-tuple-element.71), channel_id=1, source_target_pairs={{0,1},{1,0},{2,3},{3,2},{4,5},{5,4},{6,7},{7,6},{8,9},{9,8},{10,11... | collective-permute-start | bytes 294920 | tf_op jit(solution)/shard_map/ppermute | solution.py:511
  92.8 5.7 %collective-permute-start.25 = (bf16[96,512]{1,0:T(8,128)(2,1)S(1)}, bf16[96,512]{1,0:T(8,128)(2,1)S(1)}, u32[]{:S(2)}, u32[]{:S(2)}) collective-permute-start(bf16[96,512]{1,0:T(8,128)(2,1)S(1)} %get-tuple-element.72), channel_id=1, source_target_pairs={{0,2},{1,3},{2,0},{3,1},{4,6},{5,7},{6,4},{7,5},{8,10},{9,11},{10,... | collective-permute-start | bytes 294920 | tf_op jit(solution)/shard_map/ppermute | solution.py:511
  94.1 5.5 %collective-permute-start.26 = (bf16[96,512]{1,0:T(8,128)(2,1)S(1)}, bf16[96,512]{1,0:T(8,128)(2,1)S(1)}, u32[]{:S(2)}, u32[]{:S(2)}) collective-permute-start(bf16[96,512]{1,0:T(8,128)(2,1)S(1)} %get-tuple-element.73), channel_id=1, source_target_pairs={{0,3},{1,2},{2,1},{3,0},{4,7},{5,6},{6,5},{7,4},{8,11},{9,10},{10,... | collective-permute-start | bytes 294920 | tf_op jit(solution)/shard_map/ppermute | solution.py:511
  (7 other events, 72.5 us)

commit v12 on v11

--- a/solution.py
+++ b/solution.py
@@ -37,10 +37,6 @@
     if n & (n - 1) == 0:
         return x >> (n.bit_length() - 1), x & (n - 1)
     return lax.div(x, n), lax.rem(x, n)
-
-
-def turned(low):
-    return ((low & 1) << 1) | (low >> 1)
 
 
 def lists_body(slots_ref, count_ref, out_ref, *, n_rep, n_hi, per_list, quarter):
@@ -53,7 +49,7 @@
     hi, low = div_rem(source ^ r, n_rep)
     half, hi = div_rem(hi, n_hi // 2)
     row = (n_rep - 1 - (row_high ^ q)) * quarter + row_low
-    col = ((half * n_rep + (turned(low) ^ q)) * (n_hi // 2) + hi) * per_list + c
+    col = ((half * n_rep + (low ^ q)) * (n_hi // 2) + hi) * per_list + c
     across = lax.broadcasted_iota(jnp.int32, (1, slots), 1)
     cell = jnp.where(across < count_ref[0], row * all_cols + col, cells)
     down = lax.broadcasted_iota(jnp.int32, (slots, slots), 0)
@@ -108,10 +104,11 @@
         @pl.loop(0, COL_CHUNK)
         def _(col):
             cell = base + col
-            one, two, three, four = (table_ref[depth, cell] for depth in range(4))
+            three = table_ref[2, cell]
 
             @pl.when(three >= 0)
             def _():
+                one, two, four = table_ref[0, cell], table_ref[1, cell], table_ref[3, cell]
                 total = held[one].astype(F32) + held[two].astype(F32)
                 total = total + (held[three].astype(F32) + block(four).astype(F32))
                 place = (slice(None), pl.ds(pl.multiple_of(col * blk, blk), blk))
@@ -187,13 +184,15 @@
 
 
 def forward_body(*refs, n_rep):
-    pieces = refs[: 2 * n_rep]
-    adj_ref, send_ref, keep_ref = refs[2 * n_rep :]
+    pieces = refs[:n_rep]
+    adj_ref, send_ref, keep_ref = refs[n_rep:]
     i = pl.program_id(0)
-    depth = pieces[0].shape[0]
+    depth = pieces[0].shape[0] // 2
     total = 0.0
-    for n, piece in enumerate(pieces):
-        total += dot(adj_ref[:, n * depth : (n + 1) * depth], piece[...])
+    for half in range(2):
+        for j in range(n_rep):
+            at = (half * n_rep + j) * depth
+            total += dot(adj_ref[:, at : at + depth], pieces[j][half * depth : (half + 1) * depth])
 
     half = pl.num_programs(0) // 2
 
@@ -212,7 +211,7 @@
     tiles = rows // ROW_TILE
     half = tiles // 2
     return pl.pallas_call(
-        functools.partial(forward_body, n_rep=len(pieces) // 2),
+        functools.partial(forward_body, n_rep=len(pieces)),
         grid=(tiles,),
         out_shape=[shape((rows // 2, features), BF16), shape((rows // 2, features), F32)],
         in_specs=[pl.BlockSpec(x.shape, lambda i: (0, 0)) for x in pieces]
@@ -394,7 +393,7 @@
     for half, (own, near) in enumerate(((low_ref, low_near), (high_ref, high_near))):
         for i in range(per_half):
             low, hi = i % n_rep, i // n_rep
-            j = turned(low) ^ q
+            j = low ^ q
             cols = pl.ds(pl.multiple_of((j * deep + hi) * width, width), width)
             far_cols = pl.ds(pl.multiple_of((half * per_half + (j ^ 2) * deep + hi) * width, width), width)
             total = own[part:, cols] + near[part:, cols].astype(F32) + far_ref[:, far_cols].astype(F32)
@@ -422,7 +421,7 @@
     r, q = lax.axis_index("row"), lax.axis_index("rep")
     acc_ref[...] = jnp.zeros(acc_ref.shape, F32)
     for k in range(n_row):
-        j = turned(k % n_rep) ^ q
+        j = (k % n_rep) ^ q
         for c in range(per_list):
             at = k // n_rep * per_list + c
             b = lists[0][at]
@@ -515,7 +514,7 @@
 
     def spread(x, hi):
         perm = [
-            (r * n_rep + q, (r ^ (hi * n_rep + turned(q))) * n_rep + q) for r in range(n_row) for q in range(n_rep)
+            (r * n_rep + q, (r ^ (hi * n_rep + q)) * n_rep + q) for r in range(n_row) for q in range(n_rep)
         ]
         return lax.ppermute(x, ("row", "rep"), perm)
 
@@ -526,25 +525,19 @@
     *outgoing, own_list = pack(wanted, node_features, per_list, blk)
     own = [spread(x, hi) for hi, x in enumerate(outgoing)]
     deep = n_hi // 2
-    low, high = [jnp.concatenate(own[half * deep : (half + 1) * deep], axis=0) for half in range(2)]
-    low_far, low_near = to_rep(low, 2), to_rep(low, 1)
-    table = slot_lists(
-        block_rows, block_fetch, after(block_count, low_near), n_row, n_rep, per_list, row_blocks
-    )
-    high = after(high, low_far, table)
-    high_far, high_near = to_rep(high, 2), to_rep(high, 1)
-    adj = densify(after(table, high_near), blocks, n_row, per_list, row_blocks)
-    low_diag = to_rep(after(low_far, high_near), 1)
-    high_diag = to_rep(after(high_far, adj), 1)
-    pieces = [low, low_near, low_far, low_diag, high, high_near, high_far, high_diag]
+    table = slot_lists(block_rows, block_fetch, block_count, n_row, n_rep, per_list, row_blocks)
+    lists = [own_list] + [to_rep(own_list, j) for j in range(1, n_rep)]
+    own = after(jnp.concatenate(own, axis=0), table, lists)
+    far = to_rep(own, 2)
+    near = to_rep(own, 1)
+    adj = densify(after(table, near), blocks, n_row, per_list, row_blocks)
+    pieces = [own, near, far, to_rep(after(far, adj), 1)]
 
     send3, keep2 = forward(pieces, adj, 0)
     across = (keep2 + to_rep(send3, 1).astype(F32)).astype(BF16)
     arrived = to_rep(across, 2)
     send1, keep0 = forward(pieces, after(adj, across), 1)
-    own_list = after(own_list, keep0)
-    lists = [own_list] + [to_rep(own_list, j) for j in range(1, n_rep)]
-    arrived = after(arrived, keep0, lists)
+    arrived = after(arrived, keep0)
     factor = float(n_row * band_rows) ** (-0.5)
     output, to_near, grad0, wkeep = middle(keep0, to_rep(send1, 1), arrived, weight, out_grad, n_rep, factor)
 
@@ -555,9 +548,10 @@
     grad3 = to_rep(grad2, 1)
     got = to_rep(after(w, grad2)[part:], 2)
     send_high, keep_high = back_second(grad3, grad2, adj, first, 1, n_rep, deep)
+    send_high = after(send_high, got)
     near_high = to_rep(send_high, 1)
     send_low, keep_low = back_second(grad3, grad2, adj, after(first, send_high), 0, n_rep, deep)
-    near_low = to_rep(after(send_low, near_high, got), 1)
+    near_low = to_rep(after(send_low, near_high), 1)
     across = across_sum(keep_low, near_low, keep_high, near_high)
     far = to_rep(across, 2)
     w = after(w[:part], across) + got

time: 101 us -> 99 us (0.980)
  starting transfers between devices: 34.9 us -> 26.3 us
  waiting for transfers between devices: 27.2 us -> 30.9 us
  Pallas kernels: 20.5 us -> 22.8 us
    ppermute x22 -> x19, starting transfers between devices: 24.5 us -> 16.7 us  [to_rep(): return lax.ppermute(x, 'rep', xor_perm(n_rep, j))]
    ppermute x22 -> x19, waiting for transfers between devices: 23.9 us -> 28.2 us  [to_rep(): return lax.ppermute(x, 'rep', xor_perm(n_rep, j))]
    pallas_call x1, Pallas kernels: 5.29 us -> 7.5 us  [densify(): pl.pallas_call(functools.partial(densify_body, all_cols=all_cols), out_sh...]
  transfers between devices with their start and end apart: 27 -> 24, of which waited for: 14 -> 14; matrix products, arithmetic and copies ran while one was open for 1% -> 1% of each run, Pallas kernels for 11% -> 16%
where the time goes in v12:
time: 99 us; the launch traced here: 98.4 us
  waiting for transfers between devices  30.9 us (31%)
  starting transfers between devices  26.3 us (27%)
  Pallas kernels  22.8 us (23%)
  blocking collectives  15.2 us (15%)
  between operations  1.51 us (2%)
    ppermute x19, waiting for transfers between devices, to_rep(): return lax.ppermute(x, 'rep', xor_perm(n_rep, j))  28.2 us
    ppermute x19, starting transfers between devices, to_rep(): return lax.ppermute(x, 'rep', xor_perm(n_rep, j))  16.7 us
    all_to_all x1, blocking collectives, local(): lax.all_to_all(messages, 'row', split_axis=0, concat_axis=0, tiled=True)  15.2 us
    ppermute x4, starting transfers between devices, spread(): return lax.ppermute(x, ('row', 'rep'), perm)  8.02 us
    pallas_call x1, Pallas kernels, densify(): pl.pallas_call(functools.partial(densify_body, all_cols=all_cols), out_sh...  7.5 us
    pallas_call x2, Pallas kernels, forward(): pl.pallas_call(functools.partial(forward_body, n_rep=len(pieces)), grid=(...  3.76 us
    pallas_call x2, Pallas kernels, back_second(): pl.pallas_call(back_second_body, grid=(tiles,), out_shape=[shape((feature...  3.68 us
    ppermute x1, waiting for transfers between devices, to_row(): return lax.ppermute(x, 'row', xor_perm(n_row, k))  2.73 us
  transfers between devices with their start and end apart: 24, of which 14 were waited for; matrix products, arithmetic and copies ran while one was open for 1% of the time, Pallas kernels for 16%

profile of v12, /device:TPU:0, one launch (start us, length us, event | category | flops | bytes accessed | tf_op | source)
XLA Modules:
  0.0 98.4 jit_solution(423255644805341683)
XLA Ops:
  1.4 4.0 %collective-permute-start.1 = (s32[1,8,2]{2,1,0:T(8,128)S(1)}, s32[1,8,2]{2,1,0:T(8,128)S(1)}, u32[]{:S(2)}, u32[]{:S(2)}) collective-permute-start(s32[1,8,2]{2,1,0:T(8,128)S(1)} %copy.11), channel_id=1, source_target_pairs={{0,16},{1,21},{2,26},{3,31},{4,20},{5,17},{6,30},{7,27},{8,24},{9,... | collective-permute-start | bytes 200 | tf_op jit(solution)/shard_map/ppermute | solution.py:519
  7.5 2.2 %pack.1 = (bf16[256,256]{1,0:T(8,128)(2,1)S(1)}, bf16[256,256]{1,0:T(8,128)(2,1)S(1)}, s32[128]{0:T(128)S(1)}) custom-call(s32[1,8,2]{2,1,0:T(8,128)S(1)} %collective-permute-done.refs_0_, s32[1,8,2]{2,1,0:T(8,128)S(1)} %collective-permute-done.1.refs_1_, bf16[2048,256]{1,0:T(8,128)(2,1)} %refs_2_.1), custom_call_target="tpu_custom_call" | custom-call | tf_op jit(solution)/shard_map/pack/pallas_call | solution.py:175
  10.5 2.5 %collective-permute-start.3 = (bf16[256,256]{1,0:T(8,128)(2,1)S(1)}, bf16[256,256]{1,0:T(8,128)(2,1)S(1)}, u32[]{:S(2)}, u32[]{:S(2)}) collective-permute-start(bf16[256,256]{1,0:T(8,128)(2,1)S(1)} %get-tuple-element.39), channel_id=1, source_target_pairs={{0,16},{1,21},{2,26},{3,31},{4,20},{5,17},{6,30},{7,27},{8,24},{9,... | collective-permute-start | bytes 393224 | tf_op jit(solution)/shard_map/ppermute | solution.py:519
  13.4 6.0 %collective-permute-start.6 = (s32[128]{0:T(128)S(1)}, s32[128]{0:T(128)S(1)}, u32[]{:S(2)}, u32[]{:S(2)}) collective-permute-start(s32[128]{0:T(128)S(1)} %get-tuple-element.40.refs_0_), channel_id=1, source_target_pairs={{0,3},{1,2},{2,1},{3,0},{4,7},{5,6},{6,5},{7,4},{8,11},{9,10},{10,... | collective-permute-start | bytes 1544 | tf_op jit(solution)/shard_map/ppermute | solution.py:510
  20.7 2.2 %collective-permute-done.5.refs_2_ = s32[128]{0:T(128)S(1)} collective-permute-done((s32[128]{0:T(128)S(1)}, s32[128]{0:T(128)S(1)}, u32[]{:S(2)}, u32[]{:S(2)}) %collective-permute-start.5) | collective-permute-done | bytes 544 | tf_op jit(solution)/shard_map/ppermute | solution.py:510
  22.9 3.6 %collective-permute-start.8 = (bf16[512,256]{1,0:T(8,128)(2,1)S(1)}, bf16[512,256]{1,0:T(8,128)(2,1)S(1)}, u32[]{:S(2)}, u32[]{:S(2)}) collective-permute-start(bf16[512,256]{1,0:T(8,128)(2,1)S(1)} %pad_maximum_fusion.refs_0_), channel_id=1, source_target_pairs={{0,2},{1,3},{2,0},{3,1},{4,6},{5,7},{6,4},{7,5},{8,10},{9,11},{10,... | collective-permute-start | bytes 786440 | tf_op jit(solution)/shard_map/ppermute | solution.py:510
  26.6 7.5 %densify.1.refs_4_.adj_ref = bf16[2048,2048]{1,0:T(8,128)(2,1)S(1)} custom-call(s32[8,256]{1,0:T(8,128)S(1)} %slot_lists.1.table_ref, bf16[192,128,128]{2,1,0:T(8,128)(2,1)S(1)} %bitcast.3), custom_call_target="tpu_custom_call" | custom-call | flops 3145728 | bytes 14680064 | tf_op jit(solution)/shard_map/densify/pallas_call | solution.py:132
  34.2 1.5 %collective-permute-done.9.refs_3_ = bf16[512,256]{1,0:T(8,128)(2,1)S(1)} collective-permute-done((bf16[512,256]{1,0:T(8,128)(2,1)S(1)}, bf16[512,256]{1,0:T(8,128)(2,1)S(1)}, u32[]{:S(2)}, u32[]{:S(2)}) %collective-permute-start.9) | collective-permute-done | bytes 262176 | tf_op jit(solution)/shard_map/ppermute | solution.py:510
  35.7 1.9 %forward.2 = (bf16[512,256]{1,0:T(8,128)(2,1)S(1)}, f32[512,256]{1,0:T(8,128)S(1)}) custom-call(bf16[512,256]{1,0:T(8,128)(2,1)S(1)} %pad_maximum_fusion.refs_0_, bf16[512,256]{1,0:T(8,128)(2,1)S(1)} %collective-permute-done.7.refs_1_, bf16[512,256]{1,0:T(8,128)(2,1)S(1)} %collective-permute-done.8.refs_2_, ...), custom_call_target="tpu_custom_call" | custom-call | flops 1073741824 | bytes 5242880 | tf_op jit(solution)/shard_map/forward/pallas_call | solution.py:213
  37.8 1.4 %collective-permute-done.10 = bf16[512,256]{1,0:T(8,128)(2,1)S(1)} collective-permute-done((bf16[512,256]{1,0:T(8,128)(2,1)S(1)}, bf16[512,256]{1,0:T(8,128)(2,1)S(1)}, u32[]{:S(2)}, u32[]{:S(2)}) %collective-permute-start.10) | collective-permute-done | bytes 262176 | tf_op jit(solution)/shard_map/ppermute | solution.py:510
  40.3 1.9 %forward.3 = (bf16[512,256]{1,0:T(8,128)(2,1)S(1)}, f32[512,256]{1,0:T(8,128)S(1)}) custom-call(bf16[512,256]{1,0:T(8,128)(2,1)S(1)} %pad_maximum_fusion.refs_0_, bf16[512,256]{1,0:T(8,128)(2,1)S(1)} %collective-permute-done.7.refs_1_, bf16[512,256]{1,0:T(8,128)(2,1)S(1)} %collective-permute-done.8.refs_2_, ...), custom_call_target="tpu_custom_call" | custom-call | flops 1073741824 | bytes 5242880 | tf_op jit(solution)/shard_map/forward/pallas_call | solution.py:213
  42.2 5.4 %collective-permute-done.12.far_ref = bf16[512,256]{1,0:T(8,128)(2,1)S(1)} collective-permute-done((bf16[512,256]{1,0:T(8,128)(2,1)S(1)}, bf16[512,256]{1,0:T(8,128)(2,1)S(1)}, u32[]{:S(2)}, u32[]{:S(2)}) %collective-permute-start.12) | collective-permute-done | bytes 262176 | tf_op jit(solution)/shard_map/ppermute | solution.py:510
  50.4 2.3 %back_first.1 = (f32[256,2048]{1,0:T(8,128)S(1)}, f32[128,256]{1,0:T(8,128)S(1)}) custom-call(bf16[320,512]{1,0:T(8,128)(2,1)S(1)} %collective-permute-done.14.odd_ref, bf16[256,512]{1,0:T(8,128)(2,1)S(1)} %get-tuple-element.51.even_ref, bf16[2048,2048]{1,0:T(8,128)(2,1)S(1)} %densify.1.refs_4_.adj_ref, f32[128,256]{1,0:T(8,128)S(1)} %get-tuple-element.53.wkeep_ref), custom_call_target="tpu_custom_call" | custom-call | flops 1073741824 | bytes 6291456 | tf_op jit(solution)/shard_map/back_first/pallas_call | solution.py:311
  52.7 4.8 %collective-permute-done.13.even_ref = bf16[256,512]{1,0:T(8,128)(2,1)S(1)} collective-permute-done((bf16[256,512]{1,0:T(8,128)(2,1)S(1)}, bf16[256,512]{1,0:T(8,128)(2,1)S(1)}, u32[]{:S(2)}, u32[]{:S(2)}) %collective-permute-start.13) | collective-permute-done | bytes 262176 | tf_op jit(solution)/shard_map/ppermute | solution.py:510
  59.0 1.8 %back_second_1.1 = (bf16[128,1024]{1,0:T(8,128)(2,1)S(1)}, f32[128,1024]{1,0:T(8,128)S(1)}) custom-call(bf16[256,512]{1,0:T(8,128)(2,1)S(1)} %collective-permute-done.15.odd_ref, bf16[256,512]{1,0:T(8,128)(2,1)S(1)} %collective-permute-done.13.even_ref, bf16[2048,2048]{1,0:T(8,128)(2,1)S(1)} %densify.1.refs_4_.adj_ref, ...), custom_call_target="tpu_custom_call" | custom-call | flops 536870912 | bytes 3932160 | tf_op jit(solution)/shard_map/back_second_1/pallas_call | solution.py:343
  62.0 1.8 %back_second_0.1 = (bf16[128,1024]{1,0:T(8,128)(2,1)S(1)}, f32[128,1024]{1,0:T(8,128)S(1)}) custom-call(bf16[256,512]{1,0:T(8,128)(2,1)S(1)} %collective-permute-done.15.odd_ref, bf16[256,512]{1,0:T(8,128)(2,1)S(1)} %collective-permute-done.13.even_ref, bf16[2048,2048]{1,0:T(8,128)(2,1)S(1)} %densify.1.refs_4_.adj_ref, ...), custom_call_target="tpu_custom_call" | custom-call | flops 536870912 | bytes 3932160 | tf_op jit(solution)/shard_map/back_second_0/pallas_call | solution.py:343
  64.4 1.2 %collective-permute-done.18.low_near = bf16[128,1024]{1,0:T(8,128)(2,1)S(1)} collective-permute-done((bf16[128,1024]{1,0:T(8,128)(2,1)S(1)}, bf16[128,1024]{1,0:T(8,128)(2,1)S(1)}, u32[]{:S(2)}, u32[]{:S(2)}) %collective-permute-start.18) | collective-permute-done | bytes 262176 | tf_op jit(solution)/shard_map/ppermute | solution.py:510
  66.7 1.6 %collective-permute-start.20 = (f32[64,256]{1,0:T(8,128)S(1)}, f32[64,256]{1,0:T(8,128)S(1)}, u32[]{:S(2)}, u32[]{:S(2)}) collective-permute-start(f32[64,256]{1,0:T(8,128)S(1)} %add.10), channel_id=1, source_target_pairs={{0,4},{4,0},{8,12},{12,8},{16,20},{20,16},{24,28},{28,24},{1,5},{5... | collective-permute-start | bytes 196616 | tf_op jit(solution)/shard_map/ppermute | solution.py:513
  68.3 2.7 %collective-permute-done.20 = f32[64,256]{1,0:T(8,128)S(1)} collective-permute-done((f32[64,256]{1,0:T(8,128)S(1)}, f32[64,256]{1,0:T(8,128)S(1)}, u32[]{:S(2)}, u32[]{:S(2)}) %collective-permute-start.20) | collective-permute-done | bytes 65568 | tf_op jit(solution)/shard_map/ppermute | solution.py:513
  71.1 3.2 %collective-permute-done.19.far_ref = bf16[64,2048]{1,0:T(8,128)(2,1)S(1)} collective-permute-done((bf16[64,2048]{1,0:T(8,128)(2,1)S(1)}, bf16[64,2048]{1,0:T(8,128)(2,1)S(1)}, u32[]{:S(2)}, u32[]{:S(2)}) %collective-permute-start.19) | collective-permute-done | bytes 262176 | tf_op jit(solution)/shard_map/ppermute | solution.py:510
  74.4 15.2 %all_to_all.5.refs_4_ = bf16[8,96,256]{2,1,0:T(8,128)(2,1)S(1)} all-to-all(bf16[8,96,256]{2,1,0:T(8,128)(2,1)S(1)} %split.1), channel_id=1, replica_groups=mesh['row'=8,'rep'=4] {'row'}, dimensions={0} | all-to-all | bytes 786432 | tf_op jit(solution)/shard_map/all_to_all | solution.py:560
  90.5 1.8 %collective-permute-start.22 = (bf16[96,512]{1,0:T(8,128)(2,1)S(1)}, bf16[96,512]{1,0:T(8,128)(2,1)S(1)}, u32[]{:S(2)}, u32[]{:S(2)}) collective-permute-start(bf16[96,512]{1,0:T(8,128)(2,1)S(1)} %get-tuple-element.68), channel_id=1, source_target_pairs={{0,2},{1,3},{2,0},{3,1},{4,6},{5,7},{6,4},{7,5},{8,10},{9,11},{10,... | collective-permute-start | bytes 294920 | tf_op jit(solution)/shard_map/ppermute | solution.py:510
  92.3 3.8 %collective-permute-done.22.refs_2_ = bf16[96,512]{1,0:T(8,128)(2,1)S(1)} collective-permute-done((bf16[96,512]{1,0:T(8,128)(2,1)S(1)}, bf16[96,512]{1,0:T(8,128)(2,1)S(1)}, u32[]{:S(2)}, u32[]{:S(2)}) %collective-permute-start.22) | collective-permute-done | bytes 98336 | tf_op jit(solution)/shard_map/ppermute | solution.py:510
  96.1 1.2 %collective-permute-done.23.refs_3_ = bf16[96,512]{1,0:T(8,128)(2,1)S(1)} collective-permute-done((bf16[96,512]{1,0:T(8,128)(2,1)S(1)}, bf16[96,512]{1,0:T(8,128)(2,1)S(1)}, u32[]{:S(2)}, u32[]{:S(2)}) %collective-permute-start.23) | collective-permute-done | bytes 98336 | tf_op jit(solution)/shard_map/ppermute | solution.py:510
  (55 shorter events, 15.2 us)
Async XLA Ops:
  1.4 6.1 %collective-permute-start.1 = (s32[1,8,2]{2,1,0:T(8,128)S(1)}, s32[1,8,2]{2,1,0:T(8,128)S(1)}, u32[]{:S(2)}, u32[]{:S(2)}) collective-permute-start(s32[1,8,2]{2,1,0:T(8,128)S(1)} %copy.11), channel_id=1, source_target_pairs={{0,16},{1,21},{2,26},{3,31},{4,20},{5,17},{6,30},{7,27},{8,24},{9,... | collective-permute-start | bytes 200 | tf_op jit(solution)/shard_map/ppermute | solution.py:519
  5.4 2.0 %collective-permute-start = (s32[1,8,2]{2,1,0:T(8,128)S(1)}, s32[1,8,2]{2,1,0:T(8,128)S(1)}, u32[]{:S(2)}, u32[]{:S(2)}) collective-permute-start(s32[1,8,2]{2,1,0:T(8,128)S(1)} %copy.11), channel_id=1, source_target_pairs={{0,0},{1,5},{2,10},{3,15},{4,4},{5,1},{6,14},{7,11},{8,8},{9,13},{... | collective-permute-start | bytes 200 | tf_op jit(solution)/shard_map/ppermute | solution.py:519
  9.7 9.9 %collective-permute-start.2 = (bf16[256,256]{1,0:T(8,128)(2,1)S(1)}, bf16[256,256]{1,0:T(8,128)(2,1)S(1)}, u32[]{:S(2)}, u32[]{:S(2)}) collective-permute-start(bf16[256,256]{1,0:T(8,128)(2,1)S(1)} %get-tuple-element.38), channel_id=1, source_target_pairs={{0,0},{1,5},{2,10},{3,15},{4,4},{5,1},{6,14},{7,11},{8,8},{9,13},{... | collective-permute-start | bytes 393224 | tf_op jit(solution)/shard_map/ppermute | solution.py:519
  10.5 9.0 %collective-permute-start.3 = (bf16[256,256]{1,0:T(8,128)(2,1)S(1)}, bf16[256,256]{1,0:T(8,128)(2,1)S(1)}, u32[]{:S(2)}, u32[]{:S(2)}) collective-permute-start(bf16[256,256]{1,0:T(8,128)(2,1)S(1)} %get-tuple-element.39), channel_id=1, source_target_pairs={{0,16},{1,21},{2,26},{3,31},{4,20},{5,17},{6,30},{7,27},{8,24},{9,... | collective-permute-start | bytes 393224 | tf_op jit(solution)/shard_map/ppermute | solution.py:519
  13.4 7.3 %collective-permute-start.6 = (s32[128]{0:T(128)S(1)}, s32[128]{0:T(128)S(1)}, u32[]{:S(2)}, u32[]{:S(2)}) collective-permute-start(s32[128]{0:T(128)S(1)} %get-tuple-element.40.refs_0_), channel_id=1, source_target_pairs={{0,3},{1,2},{2,1},{3,0},{4,7},{5,6},{6,5},{7,4},{8,11},{9,10},{10,... | collective-permute-start | bytes 1544 | tf_op jit(solution)/shard_map/ppermute | solution.py:510
  19.4 3.5 %collective-permute-start.5 = (s32[128]{0:T(128)S(1)}, s32[128]{0:T(128)S(1)}, u32[]{:S(2)}, u32[]{:S(2)}) collective-permute-start(s32[128]{0:T(128)S(1)} %get-tuple-element.40.refs_0_), channel_id=1, source_target_pairs={{0,2},{1,3},{2,0},{3,1},{4,6},{5,7},{6,4},{7,5},{8,10},{9,11},{10,... | collective-permute-start | bytes 1544 | tf_op jit(solution)/shard_map/ppermute | solution.py:510
  19.4 3.5 %collective-permute-start.4 = (s32[128]{0:T(128)S(1)}, s32[128]{0:T(128)S(1)}, u32[]{:S(2)}, u32[]{:S(2)}) collective-permute-start(s32[128]{0:T(128)S(1)} %get-tuple-element.40.refs_0_), channel_id=1, source_target_pairs={{0,1},{1,0},{2,3},{3,2},{4,5},{5,4},{6,7},{7,6},{8,9},{9,8},{10,11... | collective-permute-start | bytes 1544 | tf_op jit(solution)/shard_map/ppermute | solution.py:510
  22.9 3.6 %collective-permute-start.7 = (bf16[512,256]{1,0:T(8,128)(2,1)S(1)}, bf16[512,256]{1,0:T(8,128)(2,1)S(1)}, u32[]{:S(2)}, u32[]{:S(2)}) collective-permute-start(bf16[512,256]{1,0:T(8,128)(2,1)S(1)} %pad_maximum_fusion.refs_0_), channel_id=1, source_target_pairs={{0,1},{1,0},{2,3},{3,2},{4,5},{5,4},{6,7},{7,6},{8,9},{9,8},{10,11... | collective-permute-start | bytes 786440 | tf_op jit(solution)/shard_map/ppermute | solution.py:510
  22.9 11.1 %collective-permute-start.8 = (bf16[512,256]{1,0:T(8,128)(2,1)S(1)}, bf16[512,256]{1,0:T(8,128)(2,1)S(1)}, u32[]{:S(2)}, u32[]{:S(2)}) collective-permute-start(bf16[512,256]{1,0:T(8,128)(2,1)S(1)} %pad_maximum_fusion.refs_0_), channel_id=1, source_target_pairs={{0,2},{1,3},{2,0},{3,1},{4,6},{5,7},{6,4},{7,5},{8,10},{9,11},{10,... | collective-permute-start | bytes 786440 | tf_op jit(solution)/shard_map/ppermute | solution.py:510
  34.1 1.6 %collective-permute-start.9 = (bf16[512,256]{1,0:T(8,128)(2,1)S(1)}, bf16[512,256]{1,0:T(8,128)(2,1)S(1)}, u32[]{:S(2)}, u32[]{:S(2)}) collective-permute-start(bf16[512,256]{1,0:T(8,128)(2,1)S(1)} %collective-permute-done.8.refs_2_), channel_id=1, source_target_pairs={{0,1},{1,0},{2,3},{3,2},{4,5},{5,4},{6,7},{7,6},{8,9},{9,8},{10,11... | collective-permute-start | bytes 786440 | tf_op jit(solution)/shard_map/ppermute | solution.py:510
  37.6 1.6 %collective-permute-start.10 = (bf16[512,256]{1,0:T(8,128)(2,1)S(1)}, bf16[512,256]{1,0:T(8,128)(2,1)S(1)}, u32[]{:S(2)}, u32[]{:S(2)}) collective-permute-start(bf16[512,256]{1,0:T(8,128)(2,1)S(1)} %get-tuple-element.45), channel_id=1, source_target_pairs={{0,1},{1,0},{2,3},{3,2},{4,5},{5,4},{6,7},{7,6},{8,9},{9,8},{10,11... | collective-permute-start | bytes 786440 | tf_op jit(solution)/shard_map/ppermute | solution.py:510
  39.3 8.4 %collective-permute-start.12 = (bf16[512,256]{1,0:T(8,128)(2,1)S(1)}, bf16[512,256]{1,0:T(8,128)(2,1)S(1)}, u32[]{:S(2)}, u32[]{:S(2)}) collective-permute-start(bf16[512,256]{1,0:T(8,128)(2,1)S(1)} %add_convert_fusion), channel_id=1, source_target_pairs={{0,2},{1,3},{2,0},{3,1},{4,6},{5,7},{6,4},{7,5},{8,10},{9,11},{10,... | collective-permute-start | bytes 786440 | tf_op jit(solution)/shard_map/ppermute | solution.py:510
  42.2 5.5 %collective-permute-start.11 = (bf16[512,256]{1,0:T(8,128)(2,1)S(1)}, bf16[512,256]{1,0:T(8,128)(2,1)S(1)}, u32[]{:S(2)}, u32[]{:S(2)}) collective-permute-start(bf16[512,256]{1,0:T(8,128)(2,1)S(1)} %get-tuple-element.48), channel_id=1, source_target_pairs={{0,1},{1,0},{2,3},{3,2},{4,5},{5,4},{6,7},{7,6},{8,9},{9,8},{10,11... | collective-permute-start | bytes 786440 | tf_op jit(solution)/shard_map/ppermute | solution.py:510
  48.8 1.6 %collective-permute-start.14 = (bf16[320,512]{1,0:T(8,128)(2,1)S(1)}, bf16[320,512]{1,0:T(8,128)(2,1)S(1)}, u32[]{:S(2)}, u32[]{:S(2)}) collective-permute-start(bf16[320,512]{1,0:T(8,128)(2,1)S(1)} %get-tuple-element.52), channel_id=1, source_target_pairs={{0,1},{1,0},{2,3},{3,2},{4,5},{5,4},{6,7},{7,6},{8,9},{9,8},{10,11... | collective-permute-start | bytes 983048 | tf_op jit(solution)/shard_map/ppermute | solution.py:510
  48.8 8.7 %collective-permute-start.13 = (bf16[256,512]{1,0:T(8,128)(2,1)S(1)}, bf16[256,512]{1,0:T(8,128)(2,1)S(1)}, u32[]{:S(2)}, u32[]{:S(2)}) collective-permute-start(bf16[256,512]{1,0:T(8,128)(2,1)S(1)} %get-tuple-element.51.even_ref), channel_id=1, source_target_pairs={{0,2},{1,3},{2,0},{3,1},{4,6},{5,7},{6,4},{7,5},{8,10},{9,11},{10,... | collective-permute-start | bytes 786440 | tf_op jit(solution)/shard_map/ppermute | solution.py:510
  57.5 1.5 %collective-permute-start.15 = (bf16[256,512]{1,0:T(8,128)(2,1)S(1)}, bf16[256,512]{1,0:T(8,128)(2,1)S(1)}, u32[]{:S(2)}, u32[]{:S(2)}) collective-permute-start(bf16[256,512]{1,0:T(8,128)(2,1)S(1)} %collective-permute-done.13.even_ref), channel_id=1, source_target_pairs={{0,1},{1,0},{2,3},{3,2},{4,5},{5,4},{6,7},{7,6},{8,9},{9,8},{10,11... | collective-permute-start | bytes 786440 | tf_op jit(solution)/shard_map/ppermute | solution.py:510
  57.5 4.5 %collective-permute-start.16 = (f32[64,256]{1,0:T(8,128)S(1)}, f32[64,256]{1,0:T(8,128)S(1)}, u32[]{:S(2)}, u32[]{:S(2)}) collective-permute-start(f32[64,256]{1,0:T(8,128)S(1)} %slice.6), channel_id=1, source_target_pairs={{0,2},{1,3},{2,0},{3,1},{4,6},{5,7},{6,4},{7,5},{8,10},{9,11},{10,... | collective-permute-start | bytes 196616 | tf_op jit(solution)/shard_map/ppermute | solution.py:510
  62.0 1.8 %collective-permute-start.17 = (bf16[128,1024]{1,0:T(8,128)(2,1)S(1)}, bf16[128,1024]{1,0:T(8,128)(2,1)S(1)}, u32[]{:S(2)}, u32[]{:S(2)}) collective-permute-start(bf16[128,1024]{1,0:T(8,128)(2,1)S(1)} %get-tuple-element.59), channel_id=1, source_target_pairs={{0,1},{1,0},{2,3},{3,2},{4,5},{5,4},{6,7},{7,6},{8,9},{9,8},{10,11... | collective-permute-start | bytes 786440 | tf_op jit(solution)/shard_map/ppermute | solution.py:510
  63.8 1.7 %collective-permute-start.18 = (bf16[128,1024]{1,0:T(8,128)(2,1)S(1)}, bf16[128,1024]{1,0:T(8,128)(2,1)S(1)}, u32[]{:S(2)}, u32[]{:S(2)}) collective-permute-start(bf16[128,1024]{1,0:T(8,128)(2,1)S(1)} %get-tuple-element.63), channel_id=1, source_target_pairs={{0,1},{1,0},{2,3},{3,2},{4,5},{5,4},{6,7},{7,6},{8,9},{9,8},{10,11... | collective-permute-start | bytes 786440 | tf_op jit(solution)/shard_map/ppermute | solution.py:510
  65.6 8.7 %collective-permute-start.19 = (bf16[64,2048]{1,0:T(8,128)(2,1)S(1)}, bf16[64,2048]{1,0:T(8,128)(2,1)S(1)}, u32[]{:S(2)}, u32[]{:S(2)}) collective-permute-start(bf16[64,2048]{1,0:T(8,128)(2,1)S(1)} %across_sum.1), channel_id=1, source_target_pairs={{0,2},{1,3},{2,0},{3,1},{4,6},{5,7},{6,4},{7,5},{8,10},{9,11},{10,... | collective-permute-start | bytes 786440 | tf_op jit(solution)/shard_map/ppermute | solution.py:510
  66.7 4.3 %collective-permute-start.20 = (f32[64,256]{1,0:T(8,128)S(1)}, f32[64,256]{1,0:T(8,128)S(1)}, u32[]{:S(2)}, u32[]{:S(2)}) collective-permute-start(f32[64,256]{1,0:T(8,128)S(1)} %add.10), channel_id=1, source_target_pairs={{0,4},{4,0},{8,12},{12,8},{16,20},{20,16},{24,28},{28,24},{1,5},{5... | collective-permute-start | bytes 196616 | tf_op jit(solution)/shard_map/ppermute | solution.py:513
  90.4 1.9 %collective-permute-start.21 = (bf16[96,512]{1,0:T(8,128)(2,1)S(1)}, bf16[96,512]{1,0:T(8,128)(2,1)S(1)}, u32[]{:S(2)}, u32[]{:S(2)}) collective-permute-start(bf16[96,512]{1,0:T(8,128)(2,1)S(1)} %get-tuple-element.67), channel_id=1, source_target_pairs={{0,1},{1,0},{2,3},{3,2},{4,5},{5,4},{6,7},{7,6},{8,9},{9,8},{10,11... | collective-permute-start | bytes 294920 | tf_op jit(solution)/shard_map/ppermute | solution.py:510
  90.5 5.7 %collective-permute-start.22 = (bf16[96,512]{1,0:T(8,128)(2,1)S(1)}, bf16[96,512]{1,0:T(8,128)(2,1)S(1)}, u32[]{:S(2)}, u32[]{:S(2)}) collective-permute-start(bf16[96,512]{1,0:T(8,128)(2,1)S(1)} %get-tuple-element.68), channel_id=1, source_target_pairs={{0,2},{1,3},{2,0},{3,1},{4,6},{5,7},{6,4},{7,5},{8,10},{9,11},{10,... | collective-permute-start | bytes 294920 | tf_op jit(solution)/shard_map/ppermute | solution.py:510
  92.2 5.1 %collective-permute-start.23 = (bf16[96,512]{1,0:T(8,128)(2,1)S(1)}, bf16[96,512]{1,0:T(8,128)(2,1)S(1)}, u32[]{:S(2)}, u32[]{:S(2)}) collective-permute-start(bf16[96,512]{1,0:T(8,128)(2,1)S(1)} %get-tuple-element.69), channel_id=1, source_target_pairs={{0,3},{1,2},{2,1},{3,0},{4,7},{5,6},{6,5},{7,4},{8,11},{9,10},{10,... | collective-permute-start | bytes 294920 | tf_op jit(solution)/shard_map/ppermute | solution.py:510
  (4 other events, 53.1 us)

commit v13 on v12

--- a/solution.py
+++ b/solution.py
@@ -10,6 +10,7 @@
 BF16 = jnp.bfloat16
 F32 = jnp.float32
 COL_CHUNK = 16
+W_SHARE = 4
 ROW_TILE = 256
 COL_TILE = 512
 WHOLE = pl.BlockSpec(memory_space=pltpu.VMEM)
@@ -387,8 +388,8 @@
 def split_body(low_ref, low_near, high_ref, high_near, far_ref, w_ref, out_ref, *, n_rep, deep):
     r, q = lax.axis_index("row"), lax.axis_index("rep")
     part, width = far_ref.shape[0], out_ref.shape[2]
-    depth = w_ref.shape[0] // 2
-    w = w_ref[pl.ds(pl.multiple_of((r & 1) * depth, depth), depth), :].astype(BF16)
+    depth = w_ref.shape[0] // W_SHARE
+    w = w_ref[pl.ds(pl.multiple_of((r & (W_SHARE - 1)) * depth, depth), depth), :].astype(BF16)
     per_half = n_rep * deep
     for half, (own, near) in enumerate(((low_ref, low_near), (high_ref, high_near))):
         for i in range(per_half):
@@ -405,7 +406,7 @@
     part, cols = far.shape
     return pl.pallas_call(
         functools.partial(split_body, n_rep=n_rep, deep=n_row // n_rep // 2),
-        out_shape=shape((n_row, part + w.shape[0] // 2, cols // n_row), BF16),
+        out_shape=shape((n_row, part + w.shape[0] // W_SHARE, cols // n_row), BF16),
         in_specs=[WHOLE] * 6,
         out_specs=WHOLE,
         compiler_params=params(cols * part * 20),
@@ -431,10 +432,10 @@
             cols = pl.ds(pl.multiple_of(cell * blk, blk), blk)
             acc_ref[:, cols] += messages[r ^ k, : acc_ref.shape[0], c * blk : (c + 1) * blk].astype(F32)
     width = outs[0].shape[1]
-    part, depth = acc_ref.shape[0], w_out.shape[0] // 2
-    for parity in range(2):
+    part, depth = acc_ref.shape[0], w_out.shape[0] // W_SHARE
+    for parity in range(W_SHARE):
         total = messages[parity, part:].astype(F32)
-        for other in range(parity + 2, n_row, 2):
+        for other in range(parity + W_SHARE, n_row, W_SHARE):
             total += messages[other, part:].astype(F32)
         w_out[parity * depth : (parity + 1) * depth] = total.astype(BF16)
     for j, out in enumerate(outs):
@@ -446,7 +447,7 @@
 def collect(lists, messages, part, per_list, row_blocks, blk):
     n_rep = len(lists)
     n_row, rows, features = messages.shape
-    depth = 2 * (rows - part)
+    depth = W_SHARE * (rows - part)
     quarter = row_blocks // n_rep
     body = functools.partial(
         collect_body, n_row=n_row, n_rep=n_rep, per_list=per_list, quarter=quarter, blk=blk
@@ -555,7 +556,8 @@
     across = across_sum(keep_low, near_low, keep_high, near_high)
     far = to_rep(across, 2)
     w = after(w[:part], across) + got
-    w = w + to_row(w, 1)
+    for step in (1, 2):
+        w = w + to_row(w, step)
     messages = split(keep_low, near_low, keep_high, near_high, far, w, n_row, n_rep)
     returned = lax.all_to_all(messages, "row", split_axis=0, concat_axis=0, tiled=True)
     *grads, w = collect(lists, returned, part, per_list, row_blocks, blk)

time: 99 us -> 98.3 us (level)
  starting transfers between devices: 26.3 us -> 32.3 us
  Pallas kernels: 22.8 us -> 20.6 us
  blocking collectives: 15.2 us -> 13.1 us
  waiting for transfers between devices: 30.9 us -> 29.1 us
    ppermute x19, waiting for transfers between devices: 28.2 us -> 24.1 us  [to_rep(): return lax.ppermute(x, 'rep', xor_perm(n_rep, j))]
    ppermute x19, starting transfers between devices: 16.7 us -> 19.8 us  [to_rep(): return lax.ppermute(x, 'rep', xor_perm(n_rep, j))]
    ppermute x1 -> x2, starting transfers between devices: 1.6 us -> 4.47 us  [to_row(): return lax.ppermute(x, 'row', xor_perm(n_row, k))]
    ppermute x1 -> x2, waiting for transfers between devices: 2.73 us -> 4.98 us  [to_row(): return lax.ppermute(x, 'row', xor_perm(n_row, k))]
    pallas_call x1, Pallas kernels: 7.5 us -> 5.26 us  [densify(): pl.pallas_call(functools.partial(densify_body, all_cols=all_cols), out_sh...]
    all_to_all x1, blocking collectives: 15.2 us -> 13.1 us  [local(): lax.all_to_all(messages, 'row', split_axis=0, concat_axis=0, tiled=True)]
  transfers between devices with their start and end apart: 24 -> 25, of which waited for: 14 -> 13; matrix products, arithmetic and copies ran while one was open for 1% -> 1% of each run, Pallas kernels for 16% -> 14%
where the time goes in v13:
time: 98.3 us; the launch traced here: 98.2 us
  starting transfers between devices  32.3 us (33%)
  waiting for transfers between devices  29.1 us (30%)
  Pallas kernels  20.6 us (21%)
  blocking collectives  13.1 us (13%)
  between operations  1.51 us (2%)
    ppermute x19, waiting for transfers between devices, to_rep(): return lax.ppermute(x, 'rep', xor_perm(n_rep, j))  24.1 us
    ppermute x19, starting transfers between devices, to_rep(): return lax.ppermute(x, 'rep', xor_perm(n_rep, j))  19.8 us
    all_to_all x1, blocking collectives, local(): lax.all_to_all(messages, 'row', split_axis=0, concat_axis=0, tiled=True)  13.1 us
    ppermute x4, starting transfers between devices, spread(): return lax.ppermute(x, ('row', 'rep'), perm)  8.02 us
    pallas_call x1, Pallas kernels, densify(): pl.pallas_call(functools.partial(densify_body, all_cols=all_cols), out_sh...  5.26 us
    ppermute x2, waiting for transfers between devices, to_row(): return lax.ppermute(x, 'row', xor_perm(n_row, k))  4.98 us
    ppermute x2, starting transfers between devices, to_row(): return lax.ppermute(x, 'row', xor_perm(n_row, k))  4.47 us
    pallas_call x2, Pallas kernels, forward(): pl.pallas_call(functools.partial(forward_body, n_rep=len(pieces)), grid=(...  3.76 us
  transfers between devices with their start and end apart: 25, of which 13 were waited for; matrix products, arithmetic and copies ran while one was open for 1% of the time, Pallas kernels for 14%

profile of v13, /device:TPU:0, one launch (start us, length us, event | category | flops | bytes accessed | tf_op | source)
XLA Modules:
  0.0 98.2 jit_solution(5246401048013994577)
XLA Ops:
  1.4 4.0 %collective-permute-start.1 = (s32[1,8,2]{2,1,0:T(8,128)S(1)}, s32[1,8,2]{2,1,0:T(8,128)S(1)}, u32[]{:S(2)}, u32[]{:S(2)}) collective-permute-start(s32[1,8,2]{2,1,0:T(8,128)S(1)} %copy.11), channel_id=1, source_target_pairs={{0,16},{1,21},{2,26},{3,31},{4,20},{5,17},{6,30},{7,27},{8,24},{9,... | collective-permute-start | bytes 200 | tf_op jit(solution)/shard_map/ppermute | solution.py:520
  7.5 2.2 %pack.1 = (bf16[256,256]{1,0:T(8,128)(2,1)S(1)}, bf16[256,256]{1,0:T(8,128)(2,1)S(1)}, s32[128]{0:T(128)S(1)}) custom-call(s32[1,8,2]{2,1,0:T(8,128)S(1)} %collective-permute-done.refs_0_, s32[1,8,2]{2,1,0:T(8,128)S(1)} %collective-permute-done.1.refs_1_, bf16[2048,256]{1,0:T(8,128)(2,1)} %refs_2_.1), custom_call_target="tpu_custom_call" | custom-call | tf_op jit(solution)/shard_map/pack/pallas_call | solution.py:176
  10.5 2.5 %collective-permute-start.3 = (bf16[256,256]{1,0:T(8,128)(2,1)S(1)}, bf16[256,256]{1,0:T(8,128)(2,1)S(1)}, u32[]{:S(2)}, u32[]{:S(2)}) collective-permute-start(bf16[256,256]{1,0:T(8,128)(2,1)S(1)} %get-tuple-element.39), channel_id=1, source_target_pairs={{0,16},{1,21},{2,26},{3,31},{4,20},{5,17},{6,30},{7,27},{8,24},{9,... | collective-permute-start | bytes 393224 | tf_op jit(solution)/shard_map/ppermute | solution.py:520
  13.4 6.0 %collective-permute-start.6 = (s32[128]{0:T(128)S(1)}, s32[128]{0:T(128)S(1)}, u32[]{:S(2)}, u32[]{:S(2)}) collective-permute-start(s32[128]{0:T(128)S(1)} %get-tuple-element.40.refs_0_), channel_id=1, source_target_pairs={{0,3},{1,2},{2,1},{3,0},{4,7},{5,6},{6,5},{7,4},{8,11},{9,10},{10,... | collective-permute-start | bytes 1544 | tf_op jit(solution)/shard_map/ppermute | solution.py:511
  20.7 2.2 %collective-permute-done.5.refs_2_ = s32[128]{0:T(128)S(1)} collective-permute-done((s32[128]{0:T(128)S(1)}, s32[128]{0:T(128)S(1)}, u32[]{:S(2)}, u32[]{:S(2)}) %collective-permute-start.5) | collective-permute-done | bytes 544 | tf_op jit(solution)/shard_map/ppermute | solution.py:511
  22.9 3.6 %collective-permute-start.8 = (bf16[512,256]{1,0:T(8,128)(2,1)S(1)}, bf16[512,256]{1,0:T(8,128)(2,1)S(1)}, u32[]{:S(2)}, u32[]{:S(2)}) collective-permute-start(bf16[512,256]{1,0:T(8,128)(2,1)S(1)} %pad_maximum_fusion.refs_0_), channel_id=1, source_target_pairs={{0,2},{1,3},{2,0},{3,1},{4,6},{5,7},{6,4},{7,5},{8,10},{9,11},{10,... | collective-permute-start | bytes 786440 | tf_op jit(solution)/shard_map/ppermute | solution.py:511
  26.6 5.3 %densify.1.refs_4_.adj_ref = bf16[2048,2048]{1,0:T(8,128)(2,1)S(1)} custom-call(s32[8,256]{1,0:T(8,128)S(1)} %slot_lists.1.table_ref, bf16[192,128,128]{2,1,0:T(8,128)(2,1)S(1)} %bitcast.3), custom_call_target="tpu_custom_call" | custom-call | flops 3145728 | bytes 14680064 | tf_op jit(solution)/shard_map/densify/pallas_call | solution.py:133
  34.9 1.9 %forward.2 = (bf16[512,256]{1,0:T(8,128)(2,1)S(1)}, f32[512,256]{1,0:T(8,128)S(1)}) custom-call(bf16[512,256]{1,0:T(8,128)(2,1)S(1)} %pad_maximum_fusion.refs_0_, bf16[512,256]{1,0:T(8,128)(2,1)S(1)} %collective-permute-done.7.refs_1_, bf16[512,256]{1,0:T(8,128)(2,1)S(1)} %collective-permute-done.8.refs_2_, ...), custom_call_target="tpu_custom_call" | custom-call | flops 1073741824 | bytes 5242880 | tf_op jit(solution)/shard_map/forward/pallas_call | solution.py:214
  38.5 1.8 %collective-permute-start.12 = (bf16[512,256]{1,0:T(8,128)(2,1)S(1)}, bf16[512,256]{1,0:T(8,128)(2,1)S(1)}, u32[]{:S(2)}, u32[]{:S(2)}) collective-permute-start(bf16[512,256]{1,0:T(8,128)(2,1)S(1)} %add_convert_fusion), channel_id=1, source_target_pairs={{0,2},{1,3},{2,0},{3,1},{4,6},{5,7},{6,4},{7,5},{8,10},{9,11},{10,... | collective-permute-start | bytes 786440 | tf_op jit(solution)/shard_map/ppermute | solution.py:511
  40.3 1.9 %forward.3 = (bf16[512,256]{1,0:T(8,128)(2,1)S(1)}, f32[512,256]{1,0:T(8,128)S(1)}) custom-call(bf16[512,256]{1,0:T(8,128)(2,1)S(1)} %pad_maximum_fusion.refs_0_, bf16[512,256]{1,0:T(8,128)(2,1)S(1)} %collective-permute-done.7.refs_1_, bf16[512,256]{1,0:T(8,128)(2,1)S(1)} %collective-permute-done.8.refs_2_, ...), custom_call_target="tpu_custom_call" | custom-call | flops 1073741824 | bytes 5242880 | tf_op jit(solution)/shard_map/forward/pallas_call | solution.py:214
  42.2 4.6 %collective-permute-done.12.far_ref = bf16[512,256]{1,0:T(8,128)(2,1)S(1)} collective-permute-done((bf16[512,256]{1,0:T(8,128)(2,1)S(1)}, bf16[512,256]{1,0:T(8,128)(2,1)S(1)}, u32[]{:S(2)}, u32[]{:S(2)}) %collective-permute-start.12) | collective-permute-done | bytes 262176 | tf_op jit(solution)/shard_map/ppermute | solution.py:511
  48.0 1.7 %collective-permute-start.13 = (bf16[256,512]{1,0:T(8,128)(2,1)S(1)}, bf16[256,512]{1,0:T(8,128)(2,1)S(1)}, u32[]{:S(2)}, u32[]{:S(2)}) collective-permute-start(bf16[256,512]{1,0:T(8,128)(2,1)S(1)} %get-tuple-element.51.even_ref), channel_id=1, source_target_pairs={{0,2},{1,3},{2,0},{3,1},{4,6},{5,7},{6,4},{7,5},{8,10},{9,11},{10,... | collective-permute-start | bytes 786440 | tf_op jit(solution)/shard_map/ppermute | solution.py:511
  49.7 2.3 %back_first.1 = (f32[256,2048]{1,0:T(8,128)S(1)}, f32[128,256]{1,0:T(8,128)S(1)}) custom-call(bf16[320,512]{1,0:T(8,128)(2,1)S(1)} %collective-permute-done.14.odd_ref, bf16[256,512]{1,0:T(8,128)(2,1)S(1)} %get-tuple-element.51.even_ref, bf16[2048,2048]{1,0:T(8,128)(2,1)S(1)} %densify.1.refs_4_.adj_ref, f32[128,256]{1,0:T(8,128)S(1)} %get-tuple-element.53.wkeep_ref), custom_call_target="tpu_custom_call" | custom-call | flops 1073741824 | bytes 6291456 | tf_op jit(solution)/shard_map/back_first/pallas_call | solution.py:312
  52.0 4.7 %collective-permute-done.13.even_ref = bf16[256,512]{1,0:T(8,128)(2,1)S(1)} collective-permute-done((bf16[256,512]{1,0:T(8,128)(2,1)S(1)}, bf16[256,512]{1,0:T(8,128)(2,1)S(1)}, u32[]{:S(2)}, u32[]{:S(2)}) %collective-permute-start.13) | collective-permute-done | bytes 262176 | tf_op jit(solution)/shard_map/ppermute | solution.py:511
  56.7 1.8 %collective-permute-start.16 = (f32[64,256]{1,0:T(8,128)S(1)}, f32[64,256]{1,0:T(8,128)S(1)}, u32[]{:S(2)}, u32[]{:S(2)}) collective-permute-start(f32[64,256]{1,0:T(8,128)S(1)} %slice.6), channel_id=1, source_target_pairs={{0,2},{1,3},{2,0},{3,1},{4,6},{5,7},{6,4},{7,5},{8,10},{9,11},{10,... | collective-permute-start | bytes 196616 | tf_op jit(solution)/shard_map/ppermute | solution.py:511
  58.5 1.8 %back_second_1.1 = (bf16[128,1024]{1,0:T(8,128)(2,1)S(1)}, f32[128,1024]{1,0:T(8,128)S(1)}) custom-call(bf16[256,512]{1,0:T(8,128)(2,1)S(1)} %collective-permute-done.15.odd_ref, bf16[256,512]{1,0:T(8,128)(2,1)S(1)} %collective-permute-done.13.even_ref, bf16[2048,2048]{1,0:T(8,128)(2,1)S(1)} %densify.1.refs_4_.adj_ref, ...), custom_call_target="tpu_custom_call" | custom-call | flops 536870912 | bytes 3932160 | tf_op jit(solution)/shard_map/back_second_1/pallas_call | solution.py:344
  61.2 1.8 %back_second_0.1 = (bf16[128,1024]{1,0:T(8,128)(2,1)S(1)}, f32[128,1024]{1,0:T(8,128)S(1)}) custom-call(bf16[256,512]{1,0:T(8,128)(2,1)S(1)} %collective-permute-done.15.odd_ref, bf16[256,512]{1,0:T(8,128)(2,1)S(1)} %collective-permute-done.13.even_ref, bf16[2048,2048]{1,0:T(8,128)(2,1)S(1)} %densify.1.refs_4_.adj_ref, ...), custom_call_target="tpu_custom_call" | custom-call | flops 536870912 | bytes 3932160 | tf_op jit(solution)/shard_map/back_second_0/pallas_call | solution.py:344
  64.8 1.9 %collective-permute-start.19 = (bf16[64,2048]{1,0:T(8,128)(2,1)S(1)}, bf16[64,2048]{1,0:T(8,128)(2,1)S(1)}, u32[]{:S(2)}, u32[]{:S(2)}) collective-permute-start(bf16[64,2048]{1,0:T(8,128)(2,1)S(1)} %across_sum.1), channel_id=1, source_target_pairs={{0,2},{1,3},{2,0},{3,1},{4,6},{5,7},{6,4},{7,5},{8,10},{9,11},{10,... | collective-permute-start | bytes 786440 | tf_op jit(solution)/shard_map/ppermute | solution.py:511
  66.7 1.6 %collective-permute-start.20 = (f32[64,256]{1,0:T(8,128)S(1)}, f32[64,256]{1,0:T(8,128)S(1)}, u32[]{:S(2)}, u32[]{:S(2)}) collective-permute-start(f32[64,256]{1,0:T(8,128)S(1)} %add.13), channel_id=1, source_target_pairs={{0,4},{4,0},{8,12},{12,8},{16,20},{20,16},{24,28},{28,24},{1,5},{5... | collective-permute-start | bytes 196616 | tf_op jit(solution)/shard_map/ppermute | solution.py:514
  68.3 2.7 %collective-permute-done.20 = f32[64,256]{1,0:T(8,128)S(1)} collective-permute-done((f32[64,256]{1,0:T(8,128)S(1)}, f32[64,256]{1,0:T(8,128)S(1)}, u32[]{:S(2)}, u32[]{:S(2)}) %collective-permute-start.20) | collective-permute-done | bytes 65568 | tf_op jit(solution)/shard_map/ppermute | solution.py:514
  71.1 2.9 %collective-permute-start.21 = (f32[64,256]{1,0:T(8,128)S(1)}, f32[64,256]{1,0:T(8,128)S(1)}, u32[]{:S(2)}, u32[]{:S(2)}) collective-permute-start(f32[64,256]{1,0:T(8,128)S(1)} %add.14), channel_id=1, source_target_pairs={{0,8},{4,12},{8,0},{12,4},{16,24},{20,28},{24,16},{28,20},{1,9},{5... | collective-permute-start | bytes 196616 | tf_op jit(solution)/shard_map/ppermute | solution.py:514
  73.9 2.2 %collective-permute-done.21 = f32[64,256]{1,0:T(8,128)S(1)} collective-permute-done((f32[64,256]{1,0:T(8,128)S(1)}, f32[64,256]{1,0:T(8,128)S(1)}, u32[]{:S(2)}, u32[]{:S(2)}) %collective-permute-start.21) | collective-permute-done | bytes 65568 | tf_op jit(solution)/shard_map/ppermute | solution.py:514
  76.4 13.1 %all_to_all.5.refs_4_ = bf16[8,80,256]{2,1,0:T(8,128)(2,1)S(1)} all-to-all(bf16[8,80,256]{2,1,0:T(8,128)(2,1)S(1)} %split.1), channel_id=1, replica_groups=mesh['row'=8,'rep'=4] {'row'}, dimensions={0} | all-to-all | bytes 655360 | tf_op jit(solution)/shard_map/all_to_all | solution.py:562
  92.1 3.8 %collective-permute-done.23.refs_2_ = bf16[96,512]{1,0:T(8,128)(2,1)S(1)} collective-permute-done((bf16[96,512]{1,0:T(8,128)(2,1)S(1)}, bf16[96,512]{1,0:T(8,128)(2,1)S(1)}, u32[]{:S(2)}, u32[]{:S(2)}) %collective-permute-start.23) | collective-permute-done | bytes 98336 | tf_op jit(solution)/shard_map/ppermute | solution.py:511
  (58 shorter events, 18.2 us)
Async XLA Ops:
  1.4 6.1 %collective-permute-start.1 = (s32[1,8,2]{2,1,0:T(8,128)S(1)}, s32[1,8,2]{2,1,0:T(8,128)S(1)}, u32[]{:S(2)}, u32[]{:S(2)}) collective-permute-start(s32[1,8,2]{2,1,0:T(8,128)S(1)} %copy.11), channel_id=1, source_target_pairs={{0,16},{1,21},{2,26},{3,31},{4,20},{5,17},{6,30},{7,27},{8,24},{9,... | collective-permute-start | bytes 200 | tf_op jit(solution)/shard_map/ppermute | solution.py:520
  5.4 2.0 %collective-permute-start = (s32[1,8,2]{2,1,0:T(8,128)S(1)}, s32[1,8,2]{2,1,0:T(8,128)S(1)}, u32[]{:S(2)}, u32[]{:S(2)}) collective-permute-start(s32[1,8,2]{2,1,0:T(8,128)S(1)} %copy.11), channel_id=1, source_target_pairs={{0,0},{1,5},{2,10},{3,15},{4,4},{5,1},{6,14},{7,11},{8,8},{9,13},{... | collective-permute-start | bytes 200 | tf_op jit(solution)/shard_map/ppermute | solution.py:520
  9.7 9.9 %collective-permute-start.2 = (bf16[256,256]{1,0:T(8,128)(2,1)S(1)}, bf16[256,256]{1,0:T(8,128)(2,1)S(1)}, u32[]{:S(2)}, u32[]{:S(2)}) collective-permute-start(bf16[256,256]{1,0:T(8,128)(2,1)S(1)} %get-tuple-element.38), channel_id=1, source_target_pairs={{0,0},{1,5},{2,10},{3,15},{4,4},{5,1},{6,14},{7,11},{8,8},{9,13},{... | collective-permute-start | bytes 393224 | tf_op jit(solution)/shard_map/ppermute | solution.py:520
  10.5 9.0 %collective-permute-start.3 = (bf16[256,256]{1,0:T(8,128)(2,1)S(1)}, bf16[256,256]{1,0:T(8,128)(2,1)S(1)}, u32[]{:S(2)}, u32[]{:S(2)}) collective-permute-start(bf16[256,256]{1,0:T(8,128)(2,1)S(1)} %get-tuple-element.39), channel_id=1, source_target_pairs={{0,16},{1,21},{2,26},{3,31},{4,20},{5,17},{6,30},{7,27},{8,24},{9,... | collective-permute-start | bytes 393224 | tf_op jit(solution)/shard_map/ppermute | solution.py:520
  13.4 7.3 %collective-permute-start.6 = (s32[128]{0:T(128)S(1)}, s32[128]{0:T(128)S(1)}, u32[]{:S(2)}, u32[]{:S(2)}) collective-permute-start(s32[128]{0:T(128)S(1)} %get-tuple-element.40.refs_0_), channel_id=1, source_target_pairs={{0,3},{1,2},{2,1},{3,0},{4,7},{5,6},{6,5},{7,4},{8,11},{9,10},{10,... | collective-permute-start | bytes 1544 | tf_op jit(solution)/shard_map/ppermute | solution.py:511
  19.4 3.5 %collective-permute-start.5 = (s32[128]{0:T(128)S(1)}, s32[128]{0:T(128)S(1)}, u32[]{:S(2)}, u32[]{:S(2)}) collective-permute-start(s32[128]{0:T(128)S(1)} %get-tuple-element.40.refs_0_), channel_id=1, source_target_pairs={{0,2},{1,3},{2,0},{3,1},{4,6},{5,7},{6,4},{7,5},{8,10},{9,11},{10,... | collective-permute-start | bytes 1544 | tf_op jit(solution)/shard_map/ppermute | solution.py:511
  19.4 3.5 %collective-permute-start.4 = (s32[128]{0:T(128)S(1)}, s32[128]{0:T(128)S(1)}, u32[]{:S(2)}, u32[]{:S(2)}) collective-permute-start(s32[128]{0:T(128)S(1)} %get-tuple-element.40.refs_0_), channel_id=1, source_target_pairs={{0,1},{1,0},{2,3},{3,2},{4,5},{5,4},{6,7},{7,6},{8,9},{9,8},{10,11... | collective-permute-start | bytes 1544 | tf_op jit(solution)/shard_map/ppermute | solution.py:511
  22.9 3.6 %collective-permute-start.7 = (bf16[512,256]{1,0:T(8,128)(2,1)S(1)}, bf16[512,256]{1,0:T(8,128)(2,1)S(1)}, u32[]{:S(2)}, u32[]{:S(2)}) collective-permute-start(bf16[512,256]{1,0:T(8,128)(2,1)S(1)} %pad_maximum_fusion.refs_0_), channel_id=1, source_target_pairs={{0,1},{1,0},{2,3},{3,2},{4,5},{5,4},{6,7},{7,6},{8,9},{9,8},{10,11... | collective-permute-start | bytes 786440 | tf_op jit(solution)/shard_map/ppermute | solution.py:511
  22.9 10.4 %collective-permute-start.8 = (bf16[512,256]{1,0:T(8,128)(2,1)S(1)}, bf16[512,256]{1,0:T(8,128)(2,1)S(1)}, u32[]{:S(2)}, u32[]{:S(2)}) collective-permute-start(bf16[512,256]{1,0:T(8,128)(2,1)S(1)} %pad_maximum_fusion.refs_0_), channel_id=1, source_target_pairs={{0,2},{1,3},{2,0},{3,1},{4,6},{5,7},{6,4},{7,5},{8,10},{9,11},{10,... | collective-permute-start | bytes 786440 | tf_op jit(solution)/shard_map/ppermute | solution.py:511
  36.8 1.6 %collective-permute-start.10 = (bf16[512,256]{1,0:T(8,128)(2,1)S(1)}, bf16[512,256]{1,0:T(8,128)(2,1)S(1)}, u32[]{:S(2)}, u32[]{:S(2)}) collective-permute-start(bf16[512,256]{1,0:T(8,128)(2,1)S(1)} %get-tuple-element.45), channel_id=1, source_target_pairs={{0,1},{1,0},{2,3},{3,2},{4,5},{5,4},{6,7},{7,6},{8,9},{9,8},{10,11... | collective-permute-start | bytes 786440 | tf_op jit(solution)/shard_map/ppermute | solution.py:511
  38.5 8.4 %collective-permute-start.12 = (bf16[512,256]{1,0:T(8,128)(2,1)S(1)}, bf16[512,256]{1,0:T(8,128)(2,1)S(1)}, u32[]{:S(2)}, u32[]{:S(2)}) collective-permute-start(bf16[512,256]{1,0:T(8,128)(2,1)S(1)} %add_convert_fusion), channel_id=1, source_target_pairs={{0,2},{1,3},{2,0},{3,1},{4,6},{5,7},{6,4},{7,5},{8,10},{9,11},{10,... | collective-permute-start | bytes 786440 | tf_op jit(solution)/shard_map/ppermute | solution.py:511
  42.2 4.7 %collective-permute-start.11 = (bf16[512,256]{1,0:T(8,128)(2,1)S(1)}, bf16[512,256]{1,0:T(8,128)(2,1)S(1)}, u32[]{:S(2)}, u32[]{:S(2)}) collective-permute-start(bf16[512,256]{1,0:T(8,128)(2,1)S(1)} %get-tuple-element.48), channel_id=1, source_target_pairs={{0,1},{1,0},{2,3},{3,2},{4,5},{5,4},{6,7},{7,6},{8,9},{9,8},{10,11... | collective-permute-start | bytes 786440 | tf_op jit(solution)/shard_map/ppermute | solution.py:511
  48.0 1.7 %collective-permute-start.14 = (bf16[320,512]{1,0:T(8,128)(2,1)S(1)}, bf16[320,512]{1,0:T(8,128)(2,1)S(1)}, u32[]{:S(2)}, u32[]{:S(2)}) collective-permute-start(bf16[320,512]{1,0:T(8,128)(2,1)S(1)} %get-tuple-element.52), channel_id=1, source_target_pairs={{0,1},{1,0},{2,3},{3,2},{4,5},{5,4},{6,7},{7,6},{8,9},{9,8},{10,11... | collective-permute-start | bytes 983048 | tf_op jit(solution)/shard_map/ppermute | solution.py:511
  48.0 8.7 %collective-permute-start.13 = (bf16[256,512]{1,0:T(8,128)(2,1)S(1)}, bf16[256,512]{1,0:T(8,128)(2,1)S(1)}, u32[]{:S(2)}, u32[]{:S(2)}) collective-permute-start(bf16[256,512]{1,0:T(8,128)(2,1)S(1)} %get-tuple-element.51.even_ref), channel_id=1, source_target_pairs={{0,2},{1,3},{2,0},{3,1},{4,6},{5,7},{6,4},{7,5},{8,10},{9,11},{10,... | collective-permute-start | bytes 786440 | tf_op jit(solution)/shard_map/ppermute | solution.py:511
  56.7 1.8 %collective-permute-start.15 = (bf16[256,512]{1,0:T(8,128)(2,1)S(1)}, bf16[256,512]{1,0:T(8,128)(2,1)S(1)}, u32[]{:S(2)}, u32[]{:S(2)}) collective-permute-start(bf16[256,512]{1,0:T(8,128)(2,1)S(1)} %collective-permute-done.13.even_ref), channel_id=1, source_target_pairs={{0,1},{1,0},{2,3},{3,2},{4,5},{5,4},{6,7},{7,6},{8,9},{9,8},{10,11... | collective-permute-start | bytes 786440 | tf_op jit(solution)/shard_map/ppermute | solution.py:511
  56.7 4.5 %collective-permute-start.16 = (f32[64,256]{1,0:T(8,128)S(1)}, f32[64,256]{1,0:T(8,128)S(1)}, u32[]{:S(2)}, u32[]{:S(2)}) collective-permute-start(f32[64,256]{1,0:T(8,128)S(1)} %slice.6), channel_id=1, source_target_pairs={{0,2},{1,3},{2,0},{3,1},{4,6},{5,7},{6,4},{7,5},{8,10},{9,11},{10,... | collective-permute-start | bytes 196616 | tf_op jit(solution)/shard_map/ppermute | solution.py:511
  61.2 1.8 %collective-permute-start.17 = (bf16[128,1024]{1,0:T(8,128)(2,1)S(1)}, bf16[128,1024]{1,0:T(8,128)(2,1)S(1)}, u32[]{:S(2)}, u32[]{:S(2)}) collective-permute-start(bf16[128,1024]{1,0:T(8,128)(2,1)S(1)} %get-tuple-element.59), channel_id=1, source_target_pairs={{0,1},{1,0},{2,3},{3,2},{4,5},{5,4},{6,7},{7,6},{8,9},{9,8},{10,11... | collective-permute-start | bytes 786440 | tf_op jit(solution)/shard_map/ppermute | solution.py:511
  63.1 1.7 %collective-permute-start.18 = (bf16[128,1024]{1,0:T(8,128)(2,1)S(1)}, bf16[128,1024]{1,0:T(8,128)(2,1)S(1)}, u32[]{:S(2)}, u32[]{:S(2)}) collective-permute-start(bf16[128,1024]{1,0:T(8,128)(2,1)S(1)} %get-tuple-element.63), channel_id=1, source_target_pairs={{0,1},{1,0},{2,3},{3,2},{4,5},{5,4},{6,7},{7,6},{8,9},{9,8},{10,11... | collective-permute-start | bytes 786440 | tf_op jit(solution)/shard_map/ppermute | solution.py:511
  64.8 11.4 %collective-permute-start.19 = (bf16[64,2048]{1,0:T(8,128)(2,1)S(1)}, bf16[64,2048]{1,0:T(8,128)(2,1)S(1)}, u32[]{:S(2)}, u32[]{:S(2)}) collective-permute-start(bf16[64,2048]{1,0:T(8,128)(2,1)S(1)} %across_sum.1), channel_id=1, source_target_pairs={{0,2},{1,3},{2,0},{3,1},{4,6},{5,7},{6,4},{7,5},{8,10},{9,11},{10,... | collective-permute-start | bytes 786440 | tf_op jit(solution)/shard_map/ppermute | solution.py:511
  66.7 4.3 %collective-permute-start.20 = (f32[64,256]{1,0:T(8,128)S(1)}, f32[64,256]{1,0:T(8,128)S(1)}, u32[]{:S(2)}, u32[]{:S(2)}) collective-permute-start(f32[64,256]{1,0:T(8,128)S(1)} %add.13), channel_id=1, source_target_pairs={{0,4},{4,0},{8,12},{12,8},{16,20},{20,16},{24,28},{28,24},{1,5},{5... | collective-permute-start | bytes 196616 | tf_op jit(solution)/shard_map/ppermute | solution.py:514
  71.1 5.1 %collective-permute-start.21 = (f32[64,256]{1,0:T(8,128)S(1)}, f32[64,256]{1,0:T(8,128)S(1)}, u32[]{:S(2)}, u32[]{:S(2)}) collective-permute-start(f32[64,256]{1,0:T(8,128)S(1)} %add.14), channel_id=1, source_target_pairs={{0,8},{4,12},{8,0},{12,4},{16,24},{20,28},{24,16},{28,20},{1,9},{5... | collective-permute-start | bytes 196616 | tf_op jit(solution)/shard_map/ppermute | solution.py:514
  90.2 1.9 %collective-permute-start.22 = (bf16[96,512]{1,0:T(8,128)(2,1)S(1)}, bf16[96,512]{1,0:T(8,128)(2,1)S(1)}, u32[]{:S(2)}, u32[]{:S(2)}) collective-permute-start(bf16[96,512]{1,0:T(8,128)(2,1)S(1)} %get-tuple-element.67), channel_id=1, source_target_pairs={{0,1},{1,0},{2,3},{3,2},{4,5},{5,4},{6,7},{7,6},{8,9},{9,8},{10,11... | collective-permute-start | bytes 294920 | tf_op jit(solution)/shard_map/ppermute | solution.py:511
  90.3 5.7 %collective-permute-start.23 = (bf16[96,512]{1,0:T(8,128)(2,1)S(1)}, bf16[96,512]{1,0:T(8,128)(2,1)S(1)}, u32[]{:S(2)}, u32[]{:S(2)}) collective-permute-start(bf16[96,512]{1,0:T(8,128)(2,1)S(1)} %get-tuple-element.68), channel_id=1, source_target_pairs={{0,2},{1,3},{2,0},{3,1},{4,6},{5,7},{6,4},{7,5},{8,10},{9,11},{10,... | collective-permute-start | bytes 294920 | tf_op jit(solution)/shard_map/ppermute | solution.py:511
  91.3 5.9 %collective-permute-start.24 = (bf16[96,512]{1,0:T(8,128)(2,1)S(1)}, bf16[96,512]{1,0:T(8,128)(2,1)S(1)}, u32[]{:S(2)}, u32[]{:S(2)}) collective-permute-start(bf16[96,512]{1,0:T(8,128)(2,1)S(1)} %get-tuple-element.69), channel_id=1, source_target_pairs={{0,3},{1,2},{2,1},{3,0},{4,7},{5,6},{6,5},{7,4},{8,11},{9,10},{10,... | collective-permute-start | bytes 294920 | tf_op jit(solution)/shard_map/ppermute | solution.py:511
  (5 other events, 54.6 us)

commit v14 on v13

--- a/solution.py
+++ b/solution.py
@@ -526,7 +526,8 @@
     *outgoing, own_list = pack(wanted, node_features, per_list, blk)
     own = [spread(x, hi) for hi, x in enumerate(outgoing)]
     deep = n_hi // 2
-    table = slot_lists(block_rows, block_fetch, block_count, n_row, n_rep, per_list, row_blocks)
+    table = slot_lists(after(block_rows, own_list), block_fetch, block_count, n_row, n_rep, per_list, row_blocks)
+    own_list = after(own_list, table)
     lists = [own_list] + [to_rep(own_list, j) for j in range(1, n_rep)]
     own = after(jnp.concatenate(own, axis=0), table, lists)
     far = to_rep(own, 2)

time: 98.3 us -> 98 us (level)
  transfers between devices with their start and end apart: 25 -> 25, of which waited for: 13 -> 14; matrix products, arithmetic and copies ran while one was open for 1% -> 1% of each run, Pallas kernels for 14% -> 13%
where the time goes in v14:
time: 98 us; the launch traced here: 97.7 us
  starting transfers between devices  31.9 us (33%)
  waiting for transfers between devices  30 us (31%)
  Pallas kernels  20 us (20%)
  blocking collectives  12.7 us (13%)
  between operations  1.48 us (2%)
    ppermute x19, waiting for transfers between devices, to_rep(): return lax.ppermute(x, 'rep', xor_perm(n_rep, j))  24.7 us
    ppermute x19, starting transfers between devices, to_rep(): return lax.ppermute(x, 'rep', xor_perm(n_rep, j))  19.1 us
    all_to_all x1, blocking collectives, local(): lax.all_to_all(messages, 'row', split_axis=0, concat_axis=0, tiled=True)  12.7 us
    ppermute x4, starting transfers between devices, spread(): return lax.ppermute(x, ('row', 'rep'), perm)  8.47 us
    ppermute x2, waiting for transfers between devices, to_row(): return lax.ppermute(x, 'row', xor_perm(n_row, k))  4.99 us
    pallas_call x1, Pallas kernels, densify(): pl.pallas_call(functools.partial(densify_body, all_cols=all_cols), out_sh...  4.69 us
    ppermute x2, starting transfers between devices, to_row(): return lax.ppermute(x, 'row', xor_perm(n_row, k))  4.32 us
    pallas_call x2, Pallas kernels, forward(): pl.pallas_call(functools.partial(forward_body, n_rep=len(pieces)), grid=(...  3.76 us
  transfers between devices with their start and end apart: 25, of which 14 were waited for; matrix products, arithmetic and copies ran while one was open for 1% of the time, Pallas kernels for 13%

profile of v14, /device:TPU:0, one launch (start us, length us, event | category | flops | bytes accessed | tf_op | source)
XLA Modules:
  0.0 97.7 jit_solution(2250063970312910502)
XLA Ops:
  1.4 4.0 %collective-permute-start.1 = (s32[1,8,2]{2,1,0:T(8,128)S(1)}, s32[1,8,2]{2,1,0:T(8,128)S(1)}, u32[]{:S(2)}, u32[]{:S(2)}) collective-permute-start(s32[1,8,2]{2,1,0:T(8,128)S(1)} %copy.11), channel_id=1, source_target_pairs={{0,16},{1,21},{2,26},{3,31},{4,20},{5,17},{6,30},{7,27},{8,24},{9,... | collective-permute-start | bytes 200 | tf_op jit(solution)/shard_map/ppermute | solution.py:520
  7.0 2.2 %pack.1 = (bf16[256,256]{1,0:T(8,128)(2,1)S(1)}, bf16[256,256]{1,0:T(8,128)(2,1)S(1)}, s32[128]{0:T(128)S(1)}) custom-call(s32[1,8,2]{2,1,0:T(8,128)S(1)} %collective-permute-done.refs_0_, s32[1,8,2]{2,1,0:T(8,128)S(1)} %collective-permute-done.1.refs_1_, bf16[2048,256]{1,0:T(8,128)(2,1)} %refs_2_.1), custom_call_target="tpu_custom_call" | custom-call | tf_op jit(solution)/shard_map/pack/pallas_call | solution.py:176
  10.1 3.0 %collective-permute-start.3 = (bf16[256,256]{1,0:T(8,128)(2,1)S(1)}, bf16[256,256]{1,0:T(8,128)(2,1)S(1)}, u32[]{:S(2)}, u32[]{:S(2)}) collective-permute-start(bf16[256,256]{1,0:T(8,128)(2,1)S(1)} %get-tuple-element.41), channel_id=1, source_target_pairs={{0,16},{1,21},{2,26},{3,31},{4,20},{5,17},{6,30},{7,27},{8,24},{9,... | collective-permute-start | bytes 393224 | tf_op jit(solution)/shard_map/ppermute | solution.py:520
  14.1 6.0 %collective-permute-start.6 = (s32[128]{0:T(128)S(1)}, s32[128]{0:T(128)S(1)}, u32[]{:S(2)}, u32[]{:S(2)}) collective-permute-start(s32[128]{0:T(128)S(1)} %get-tuple-element.44.refs_0_), channel_id=1, source_target_pairs={{0,3},{1,2},{2,1},{3,0},{4,7},{5,6},{6,5},{7,4},{8,11},{9,10},{10,... | collective-permute-start | bytes 1544 | tf_op jit(solution)/shard_map/ppermute | solution.py:511
  21.4 2.2 %collective-permute-done.5.refs_2_ = s32[128]{0:T(128)S(1)} collective-permute-done((s32[128]{0:T(128)S(1)}, s32[128]{0:T(128)S(1)}, u32[]{:S(2)}, u32[]{:S(2)}) %collective-permute-start.5) | collective-permute-done | bytes 544 | tf_op jit(solution)/shard_map/ppermute | solution.py:511
  23.6 2.8 %collective-permute-start.8 = (bf16[512,256]{1,0:T(8,128)(2,1)S(1)}, bf16[512,256]{1,0:T(8,128)(2,1)S(1)}, u32[]{:S(2)}, u32[]{:S(2)}) collective-permute-start(bf16[512,256]{1,0:T(8,128)(2,1)S(1)} %pad_maximum_fusion.refs_0_), channel_id=1, source_target_pairs={{0,2},{1,3},{2,0},{3,1},{4,6},{5,7},{6,4},{7,5},{8,10},{9,11},{10,... | collective-permute-start | bytes 786440 | tf_op jit(solution)/shard_map/ppermute | solution.py:511
  26.5 4.7 %densify.1.refs_4_.adj_ref = bf16[2048,2048]{1,0:T(8,128)(2,1)S(1)} custom-call(s32[8,256]{1,0:T(8,128)S(1)} %slot_lists.1.table_ref, bf16[192,128,128]{2,1,0:T(8,128)(2,1)S(1)} %bitcast.3), custom_call_target="tpu_custom_call" | custom-call | flops 3145728 | bytes 14680064 | tf_op jit(solution)/shard_map/densify/pallas_call | solution.py:133
  31.2 2.2 %collective-permute-done.8.refs_2_ = bf16[512,256]{1,0:T(8,128)(2,1)S(1)} collective-permute-done((bf16[512,256]{1,0:T(8,128)(2,1)S(1)}, bf16[512,256]{1,0:T(8,128)(2,1)S(1)}, u32[]{:S(2)}, u32[]{:S(2)}) %collective-permute-start.8) | collective-permute-done | bytes 262176 | tf_op jit(solution)/shard_map/ppermute | solution.py:511
  34.9 1.9 %forward.2 = (bf16[512,256]{1,0:T(8,128)(2,1)S(1)}, f32[512,256]{1,0:T(8,128)S(1)}) custom-call(bf16[512,256]{1,0:T(8,128)(2,1)S(1)} %pad_maximum_fusion.refs_0_, bf16[512,256]{1,0:T(8,128)(2,1)S(1)} %collective-permute-done.7.refs_1_, bf16[512,256]{1,0:T(8,128)(2,1)S(1)} %collective-permute-done.8.refs_2_, ...), custom_call_target="tpu_custom_call" | custom-call | flops 1073741824 | bytes 5242880 | tf_op jit(solution)/shard_map/forward/pallas_call | solution.py:214
  38.5 1.8 %collective-permute-start.12 = (bf16[512,256]{1,0:T(8,128)(2,1)S(1)}, bf16[512,256]{1,0:T(8,128)(2,1)S(1)}, u32[]{:S(2)}, u32[]{:S(2)}) collective-permute-start(bf16[512,256]{1,0:T(8,128)(2,1)S(1)} %add_convert_fusion), channel_id=1, source_target_pairs={{0,2},{1,3},{2,0},{3,1},{4,6},{5,7},{6,4},{7,5},{8,10},{9,11},{10,... | collective-permute-start | bytes 786440 | tf_op jit(solution)/shard_map/ppermute | solution.py:511
  40.3 1.9 %forward.3 = (bf16[512,256]{1,0:T(8,128)(2,1)S(1)}, f32[512,256]{1,0:T(8,128)S(1)}) custom-call(bf16[512,256]{1,0:T(8,128)(2,1)S(1)} %pad_maximum_fusion.refs_0_, bf16[512,256]{1,0:T(8,128)(2,1)S(1)} %collective-permute-done.7.refs_1_, bf16[512,256]{1,0:T(8,128)(2,1)S(1)} %collective-permute-done.8.refs_2_, ...), custom_call_target="tpu_custom_call" | custom-call | flops 1073741824 | bytes 5242880 | tf_op jit(solution)/shard_map/forward/pallas_call | solution.py:214
  42.2 4.8 %collective-permute-done.12.far_ref = bf16[512,256]{1,0:T(8,128)(2,1)S(1)} collective-permute-done((bf16[512,256]{1,0:T(8,128)(2,1)S(1)}, bf16[512,256]{1,0:T(8,128)(2,1)S(1)}, u32[]{:S(2)}, u32[]{:S(2)}) %collective-permute-start.12) | collective-permute-done | bytes 262176 | tf_op jit(solution)/shard_map/ppermute | solution.py:511
  48.1 1.6 %collective-permute-start.13 = (bf16[256,512]{1,0:T(8,128)(2,1)S(1)}, bf16[256,512]{1,0:T(8,128)(2,1)S(1)}, u32[]{:S(2)}, u32[]{:S(2)}) collective-permute-start(bf16[256,512]{1,0:T(8,128)(2,1)S(1)} %get-tuple-element.55.even_ref), channel_id=1, source_target_pairs={{0,2},{1,3},{2,0},{3,1},{4,6},{5,7},{6,4},{7,5},{8,10},{9,11},{10,... | collective-permute-start | bytes 786440 | tf_op jit(solution)/shard_map/ppermute | solution.py:511
  49.7 2.3 %back_first.1 = (f32[256,2048]{1,0:T(8,128)S(1)}, f32[128,256]{1,0:T(8,128)S(1)}) custom-call(bf16[320,512]{1,0:T(8,128)(2,1)S(1)} %collective-permute-done.14.odd_ref, bf16[256,512]{1,0:T(8,128)(2,1)S(1)} %get-tuple-element.55.even_ref, bf16[2048,2048]{1,0:T(8,128)(2,1)S(1)} %densify.1.refs_4_.adj_ref, f32[128,256]{1,0:T(8,128)S(1)} %get-tuple-element.57.wkeep_ref), custom_call_target="tpu_custom_call" | custom-call | flops 1073741824 | bytes 6291456 | tf_op jit(solution)/shard_map/back_first/pallas_call | solution.py:312
  52.0 4.8 %collective-permute-done.13.even_ref = bf16[256,512]{1,0:T(8,128)(2,1)S(1)} collective-permute-done((bf16[256,512]{1,0:T(8,128)(2,1)S(1)}, bf16[256,512]{1,0:T(8,128)(2,1)S(1)}, u32[]{:S(2)}, u32[]{:S(2)}) %collective-permute-start.13) | collective-permute-done | bytes 262176 | tf_op jit(solution)/shard_map/ppermute | solution.py:511
  56.8 1.7 %collective-permute-start.16 = (f32[64,256]{1,0:T(8,128)S(1)}, f32[64,256]{1,0:T(8,128)S(1)}, u32[]{:S(2)}, u32[]{:S(2)}) collective-permute-start(f32[64,256]{1,0:T(8,128)S(1)} %slice.6), channel_id=1, source_target_pairs={{0,2},{1,3},{2,0},{3,1},{4,6},{5,7},{6,4},{7,5},{8,10},{9,11},{10,... | collective-permute-start | bytes 196616 | tf_op jit(solution)/shard_map/ppermute | solution.py:511
  58.5 1.8 %back_second_1.1 = (bf16[128,1024]{1,0:T(8,128)(2,1)S(1)}, f32[128,1024]{1,0:T(8,128)S(1)}) custom-call(bf16[256,512]{1,0:T(8,128)(2,1)S(1)} %collective-permute-done.15.odd_ref, bf16[256,512]{1,0:T(8,128)(2,1)S(1)} %collective-permute-done.13.even_ref, bf16[2048,2048]{1,0:T(8,128)(2,1)S(1)} %densify.1.refs_4_.adj_ref, ...), custom_call_target="tpu_custom_call" | custom-call | flops 536870912 | bytes 3932160 | tf_op jit(solution)/shard_map/back_second_1/pallas_call | solution.py:344
  61.3 1.8 %back_second_0.1 = (bf16[128,1024]{1,0:T(8,128)(2,1)S(1)}, f32[128,1024]{1,0:T(8,128)S(1)}) custom-call(bf16[256,512]{1,0:T(8,128)(2,1)S(1)} %collective-permute-done.15.odd_ref, bf16[256,512]{1,0:T(8,128)(2,1)S(1)} %collective-permute-done.13.even_ref, bf16[2048,2048]{1,0:T(8,128)(2,1)S(1)} %densify.1.refs_4_.adj_ref, ...), custom_call_target="tpu_custom_call" | custom-call | flops 536870912 | bytes 3932160 | tf_op jit(solution)/shard_map/back_second_0/pallas_call | solution.py:344
  65.0 1.8 %collective-permute-start.19 = (bf16[64,2048]{1,0:T(8,128)(2,1)S(1)}, bf16[64,2048]{1,0:T(8,128)(2,1)S(1)}, u32[]{:S(2)}, u32[]{:S(2)}) collective-permute-start(bf16[64,2048]{1,0:T(8,128)(2,1)S(1)} %across_sum.1), channel_id=1, source_target_pairs={{0,2},{1,3},{2,0},{3,1},{4,6},{5,7},{6,4},{7,5},{8,10},{9,11},{10,... | collective-permute-start | bytes 786440 | tf_op jit(solution)/shard_map/ppermute | solution.py:511
  68.3 2.7 %collective-permute-done.20 = f32[64,256]{1,0:T(8,128)S(1)} collective-permute-done((f32[64,256]{1,0:T(8,128)S(1)}, f32[64,256]{1,0:T(8,128)S(1)}, u32[]{:S(2)}, u32[]{:S(2)}) %collective-permute-start.20) | collective-permute-done | bytes 65568 | tf_op jit(solution)/shard_map/ppermute | solution.py:514
  71.1 2.7 %collective-permute-start.21 = (f32[64,256]{1,0:T(8,128)S(1)}, f32[64,256]{1,0:T(8,128)S(1)}, u32[]{:S(2)}, u32[]{:S(2)}) collective-permute-start(f32[64,256]{1,0:T(8,128)S(1)} %add.14), channel_id=1, source_target_pairs={{0,8},{4,12},{8,0},{12,4},{16,24},{20,28},{24,16},{28,20},{1,9},{5... | collective-permute-start | bytes 196616 | tf_op jit(solution)/shard_map/ppermute | solution.py:514
  73.8 2.2 %collective-permute-done.21 = f32[64,256]{1,0:T(8,128)S(1)} collective-permute-done((f32[64,256]{1,0:T(8,128)S(1)}, f32[64,256]{1,0:T(8,128)S(1)}, u32[]{:S(2)}, u32[]{:S(2)}) %collective-permute-start.21) | collective-permute-done | bytes 65568 | tf_op jit(solution)/shard_map/ppermute | solution.py:514
  76.2 12.7 %all_to_all.5.refs_4_ = bf16[8,80,256]{2,1,0:T(8,128)(2,1)S(1)} all-to-all(bf16[8,80,256]{2,1,0:T(8,128)(2,1)S(1)} %split.1), channel_id=1, replica_groups=mesh['row'=8,'rep'=4] {'row'}, dimensions={0} | all-to-all | bytes 655360 | tf_op jit(solution)/shard_map/all_to_all | solution.py:563
  91.6 3.8 %collective-permute-done.23.refs_2_ = bf16[96,512]{1,0:T(8,128)(2,1)S(1)} collective-permute-done((bf16[96,512]{1,0:T(8,128)(2,1)S(1)}, bf16[96,512]{1,0:T(8,128)(2,1)S(1)}, u32[]{:S(2)}, u32[]{:S(2)}) %collective-permute-start.23) | collective-permute-done | bytes 98336 | tf_op jit(solution)/shard_map/ppermute | solution.py:511
  (58 shorter events, 18.6 us)
Async XLA Ops:
  1.4 5.6 %collective-permute-start.1 = (s32[1,8,2]{2,1,0:T(8,128)S(1)}, s32[1,8,2]{2,1,0:T(8,128)S(1)}, u32[]{:S(2)}, u32[]{:S(2)}) collective-permute-start(s32[1,8,2]{2,1,0:T(8,128)S(1)} %copy.11), channel_id=1, source_target_pairs={{0,16},{1,21},{2,26},{3,31},{4,20},{5,17},{6,30},{7,27},{8,24},{9,... | collective-permute-start | bytes 200 | tf_op jit(solution)/shard_map/ppermute | solution.py:520
  5.4 1.6 %collective-permute-start = (s32[1,8,2]{2,1,0:T(8,128)S(1)}, s32[1,8,2]{2,1,0:T(8,128)S(1)}, u32[]{:S(2)}, u32[]{:S(2)}) collective-permute-start(s32[1,8,2]{2,1,0:T(8,128)S(1)} %copy.11), channel_id=1, source_target_pairs={{0,0},{1,5},{2,10},{3,15},{4,4},{5,1},{6,14},{7,11},{8,8},{9,13},{... | collective-permute-start | bytes 200 | tf_op jit(solution)/shard_map/ppermute | solution.py:520
  9.3 11.0 %collective-permute-start.2 = (bf16[256,256]{1,0:T(8,128)(2,1)S(1)}, bf16[256,256]{1,0:T(8,128)(2,1)S(1)}, u32[]{:S(2)}, u32[]{:S(2)}) collective-permute-start(bf16[256,256]{1,0:T(8,128)(2,1)S(1)} %get-tuple-element.40), channel_id=1, source_target_pairs={{0,0},{1,5},{2,10},{3,15},{4,4},{5,1},{6,14},{7,11},{8,8},{9,13},{... | collective-permute-start | bytes 393224 | tf_op jit(solution)/shard_map/ppermute | solution.py:520
  10.1 10.2 %collective-permute-start.3 = (bf16[256,256]{1,0:T(8,128)(2,1)S(1)}, bf16[256,256]{1,0:T(8,128)(2,1)S(1)}, u32[]{:S(2)}, u32[]{:S(2)}) collective-permute-start(bf16[256,256]{1,0:T(8,128)(2,1)S(1)} %get-tuple-element.41), channel_id=1, source_target_pairs={{0,16},{1,21},{2,26},{3,31},{4,20},{5,17},{6,30},{7,27},{8,24},{9,... | collective-permute-start | bytes 393224 | tf_op jit(solution)/shard_map/ppermute | solution.py:520
  14.1 7.3 %collective-permute-start.6 = (s32[128]{0:T(128)S(1)}, s32[128]{0:T(128)S(1)}, u32[]{:S(2)}, u32[]{:S(2)}) collective-permute-start(s32[128]{0:T(128)S(1)} %get-tuple-element.44.refs_0_), channel_id=1, source_target_pairs={{0,3},{1,2},{2,1},{3,0},{4,7},{5,6},{6,5},{7,4},{8,11},{9,10},{10,... | collective-permute-start | bytes 1544 | tf_op jit(solution)/shard_map/ppermute | solution.py:511
  20.1 3.5 %collective-permute-start.5 = (s32[128]{0:T(128)S(1)}, s32[128]{0:T(128)S(1)}, u32[]{:S(2)}, u32[]{:S(2)}) collective-permute-start(s32[128]{0:T(128)S(1)} %get-tuple-element.44.refs_0_), channel_id=1, source_target_pairs={{0,2},{1,3},{2,0},{3,1},{4,6},{5,7},{6,4},{7,5},{8,10},{9,11},{10,... | collective-permute-start | bytes 1544 | tf_op jit(solution)/shard_map/ppermute | solution.py:511
  20.1 3.5 %collective-permute-start.4 = (s32[128]{0:T(128)S(1)}, s32[128]{0:T(128)S(1)}, u32[]{:S(2)}, u32[]{:S(2)}) collective-permute-start(s32[128]{0:T(128)S(1)} %get-tuple-element.44.refs_0_), channel_id=1, source_target_pairs={{0,1},{1,0},{2,3},{3,2},{4,5},{5,4},{6,7},{7,6},{8,9},{9,8},{10,11... | collective-permute-start | bytes 1544 | tf_op jit(solution)/shard_map/ppermute | solution.py:511
  23.6 2.8 %collective-permute-start.7 = (bf16[512,256]{1,0:T(8,128)(2,1)S(1)}, bf16[512,256]{1,0:T(8,128)(2,1)S(1)}, u32[]{:S(2)}, u32[]{:S(2)}) collective-permute-start(bf16[512,256]{1,0:T(8,128)(2,1)S(1)} %pad_maximum_fusion.refs_0_), channel_id=1, source_target_pairs={{0,1},{1,0},{2,3},{3,2},{4,5},{5,4},{6,7},{7,6},{8,9},{9,8},{10,11... | collective-permute-start | bytes 786440 | tf_op jit(solution)/shard_map/ppermute | solution.py:511
  23.6 9.7 %collective-permute-start.8 = (bf16[512,256]{1,0:T(8,128)(2,1)S(1)}, bf16[512,256]{1,0:T(8,128)(2,1)S(1)}, u32[]{:S(2)}, u32[]{:S(2)}) collective-permute-start(bf16[512,256]{1,0:T(8,128)(2,1)S(1)} %pad_maximum_fusion.refs_0_), channel_id=1, source_target_pairs={{0,2},{1,3},{2,0},{3,1},{4,6},{5,7},{6,4},{7,5},{8,10},{9,11},{10,... | collective-permute-start | bytes 786440 | tf_op jit(solution)/shard_map/ppermute | solution.py:511
  36.8 1.6 %collective-permute-start.10 = (bf16[512,256]{1,0:T(8,128)(2,1)S(1)}, bf16[512,256]{1,0:T(8,128)(2,1)S(1)}, u32[]{:S(2)}, u32[]{:S(2)}) collective-permute-start(bf16[512,256]{1,0:T(8,128)(2,1)S(1)} %get-tuple-element.49), channel_id=1, source_target_pairs={{0,1},{1,0},{2,3},{3,2},{4,5},{5,4},{6,7},{7,6},{8,9},{9,8},{10,11... | collective-permute-start | bytes 786440 | tf_op jit(solution)/shard_map/ppermute | solution.py:511
  38.5 8.5 %collective-permute-start.12 = (bf16[512,256]{1,0:T(8,128)(2,1)S(1)}, bf16[512,256]{1,0:T(8,128)(2,1)S(1)}, u32[]{:S(2)}, u32[]{:S(2)}) collective-permute-start(bf16[512,256]{1,0:T(8,128)(2,1)S(1)} %add_convert_fusion), channel_id=1, source_target_pairs={{0,2},{1,3},{2,0},{3,1},{4,6},{5,7},{6,4},{7,5},{8,10},{9,11},{10,... | collective-permute-start | bytes 786440 | tf_op jit(solution)/shard_map/ppermute | solution.py:511
  42.2 4.8 %collective-permute-start.11 = (bf16[512,256]{1,0:T(8,128)(2,1)S(1)}, bf16[512,256]{1,0:T(8,128)(2,1)S(1)}, u32[]{:S(2)}, u32[]{:S(2)}) collective-permute-start(bf16[512,256]{1,0:T(8,128)(2,1)S(1)} %get-tuple-element.52), channel_id=1, source_target_pairs={{0,1},{1,0},{2,3},{3,2},{4,5},{5,4},{6,7},{7,6},{8,9},{9,8},{10,11... | collective-permute-start | bytes 786440 | tf_op jit(solution)/shard_map/ppermute | solution.py:511
  48.1 1.6 %collective-permute-start.14 = (bf16[320,512]{1,0:T(8,128)(2,1)S(1)}, bf16[320,512]{1,0:T(8,128)(2,1)S(1)}, u32[]{:S(2)}, u32[]{:S(2)}) collective-permute-start(bf16[320,512]{1,0:T(8,128)(2,1)S(1)} %get-tuple-element.56), channel_id=1, source_target_pairs={{0,1},{1,0},{2,3},{3,2},{4,5},{5,4},{6,7},{7,6},{8,9},{9,8},{10,11... | collective-permute-start | bytes 983048 | tf_op jit(solution)/shard_map/ppermute | solution.py:511
  48.1 8.7 %collective-permute-start.13 = (bf16[256,512]{1,0:T(8,128)(2,1)S(1)}, bf16[256,512]{1,0:T(8,128)(2,1)S(1)}, u32[]{:S(2)}, u32[]{:S(2)}) collective-permute-start(bf16[256,512]{1,0:T(8,128)(2,1)S(1)} %get-tuple-element.55.even_ref), channel_id=1, source_target_pairs={{0,2},{1,3},{2,0},{3,1},{4,6},{5,7},{6,4},{7,5},{8,10},{9,11},{10,... | collective-permute-start | bytes 786440 | tf_op jit(solution)/shard_map/ppermute | solution.py:511
  56.8 1.7 %collective-permute-start.15 = (bf16[256,512]{1,0:T(8,128)(2,1)S(1)}, bf16[256,512]{1,0:T(8,128)(2,1)S(1)}, u32[]{:S(2)}, u32[]{:S(2)}) collective-permute-start(bf16[256,512]{1,0:T(8,128)(2,1)S(1)} %collective-permute-done.13.even_ref), channel_id=1, source_target_pairs={{0,1},{1,0},{2,3},{3,2},{4,5},{5,4},{6,7},{7,6},{8,9},{9,8},{10,11... | collective-permute-start | bytes 786440 | tf_op jit(solution)/shard_map/ppermute | solution.py:511
  56.8 4.5 %collective-permute-start.16 = (f32[64,256]{1,0:T(8,128)S(1)}, f32[64,256]{1,0:T(8,128)S(1)}, u32[]{:S(2)}, u32[]{:S(2)}) collective-permute-start(f32[64,256]{1,0:T(8,128)S(1)} %slice.6), channel_id=1, source_target_pairs={{0,2},{1,3},{2,0},{3,1},{4,6},{5,7},{6,4},{7,5},{8,10},{9,11},{10,... | collective-permute-start | bytes 196616 | tf_op jit(solution)/shard_map/ppermute | solution.py:511
  61.3 1.8 %collective-permute-start.17 = (bf16[128,1024]{1,0:T(8,128)(2,1)S(1)}, bf16[128,1024]{1,0:T(8,128)(2,1)S(1)}, u32[]{:S(2)}, u32[]{:S(2)}) collective-permute-start(bf16[128,1024]{1,0:T(8,128)(2,1)S(1)} %get-tuple-element.63), channel_id=1, source_target_pairs={{0,1},{1,0},{2,3},{3,2},{4,5},{5,4},{6,7},{7,6},{8,9},{9,8},{10,11... | collective-permute-start | bytes 786440 | tf_op jit(solution)/shard_map/ppermute | solution.py:511
  63.2 1.7 %collective-permute-start.18 = (bf16[128,1024]{1,0:T(8,128)(2,1)S(1)}, bf16[128,1024]{1,0:T(8,128)(2,1)S(1)}, u32[]{:S(2)}, u32[]{:S(2)}) collective-permute-start(bf16[128,1024]{1,0:T(8,128)(2,1)S(1)} %get-tuple-element.67), channel_id=1, source_target_pairs={{0,1},{1,0},{2,3},{3,2},{4,5},{5,4},{6,7},{7,6},{8,9},{9,8},{10,11... | collective-permute-start | bytes 786440 | tf_op jit(solution)/shard_map/ppermute | solution.py:511
  65.0 11.1 %collective-permute-start.19 = (bf16[64,2048]{1,0:T(8,128)(2,1)S(1)}, bf16[64,2048]{1,0:T(8,128)(2,1)S(1)}, u32[]{:S(2)}, u32[]{:S(2)}) collective-permute-start(bf16[64,2048]{1,0:T(8,128)(2,1)S(1)} %across_sum.1), channel_id=1, source_target_pairs={{0,2},{1,3},{2,0},{3,1},{4,6},{5,7},{6,4},{7,5},{8,10},{9,11},{10,... | collective-permute-start | bytes 786440 | tf_op jit(solution)/shard_map/ppermute | solution.py:511
  66.7 4.3 %collective-permute-start.20 = (f32[64,256]{1,0:T(8,128)S(1)}, f32[64,256]{1,0:T(8,128)S(1)}, u32[]{:S(2)}, u32[]{:S(2)}) collective-permute-start(f32[64,256]{1,0:T(8,128)S(1)} %add.13), channel_id=1, source_target_pairs={{0,4},{4,0},{8,12},{12,8},{16,20},{20,16},{24,28},{28,24},{1,5},{5... | collective-permute-start | bytes 196616 | tf_op jit(solution)/shard_map/ppermute | solution.py:514
  71.1 5.0 %collective-permute-start.21 = (f32[64,256]{1,0:T(8,128)S(1)}, f32[64,256]{1,0:T(8,128)S(1)}, u32[]{:S(2)}, u32[]{:S(2)}) collective-permute-start(f32[64,256]{1,0:T(8,128)S(1)} %add.14), channel_id=1, source_target_pairs={{0,8},{4,12},{8,0},{12,4},{16,24},{20,28},{24,16},{28,20},{1,9},{5... | collective-permute-start | bytes 196616 | tf_op jit(solution)/shard_map/ppermute | solution.py:514
  89.7 1.9 %collective-permute-start.22 = (bf16[96,512]{1,0:T(8,128)(2,1)S(1)}, bf16[96,512]{1,0:T(8,128)(2,1)S(1)}, u32[]{:S(2)}, u32[]{:S(2)}) collective-permute-start(bf16[96,512]{1,0:T(8,128)(2,1)S(1)} %get-tuple-element.71), channel_id=1, source_target_pairs={{0,1},{1,0},{2,3},{3,2},{4,5},{5,4},{6,7},{7,6},{8,9},{9,8},{10,11... | collective-permute-start | bytes 294920 | tf_op jit(solution)/shard_map/ppermute | solution.py:511
  89.8 5.7 %collective-permute-start.23 = (bf16[96,512]{1,0:T(8,128)(2,1)S(1)}, bf16[96,512]{1,0:T(8,128)(2,1)S(1)}, u32[]{:S(2)}, u32[]{:S(2)}) collective-permute-start(bf16[96,512]{1,0:T(8,128)(2,1)S(1)} %get-tuple-element.72), channel_id=1, source_target_pairs={{0,2},{1,3},{2,0},{3,1},{4,6},{5,7},{6,4},{7,5},{8,10},{9,11},{10,... | collective-permute-start | bytes 294920 | tf_op jit(solution)/shard_map/ppermute | solution.py:511
  91.0 5.6 %collective-permute-start.24 = (bf16[96,512]{1,0:T(8,128)(2,1)S(1)}, bf16[96,512]{1,0:T(8,128)(2,1)S(1)}, u32[]{:S(2)}, u32[]{:S(2)}) collective-permute-start(bf16[96,512]{1,0:T(8,128)(2,1)S(1)} %get-tuple-element.73), channel_id=1, source_target_pairs={{0,3},{1,2},{2,1},{3,0},{4,7},{5,6},{6,5},{7,4},{8,11},{9,10},{10,... | collective-permute-start | bytes 294920 | tf_op jit(solution)/shard_map/ppermute | solution.py:511
  (5 other events, 51.9 us)
